TPU v7x, 32 devices: a whole 2x2x4 slice. The times are simulated.
32 devices in a mesh: groups: 2 (over y), inst: 4 (over z), tp: 4 (over x, core).
Axes of the slice: x: 2, y: 2, z: 4, core: 2. Of those that a mesh axis runs over, the one named last changes fastest.
Arguments:
- queries: bfloat16 [32, 128, 8192], P(('groups', 'inst'), None, 'tp'), parts along dimension 0, may hold values from -16 to 16
- kv_new: bfloat16 [32, 8, 128, 256], P(('groups', 'inst'), None, 'tp'), parts along dimension 0, may hold values from -16 to 16
- prompt_spans: int32 [8], P('groups'), parts along dimension 0, may hold values from 1 to 8, 16 in all
- prompt_tail: int32 [8], P('groups'), parts along dimension 0, may hold values from 1 to 128
- span_plan: int32 [32], P('groups'), parts along dimension 0, may hold values from 0 to 15, each once
- decode_owner: int32 [8], P('groups'), parts along dimension 0, may hold values from 0 to 3, as said below
Outputs:
- attended: bfloat16 [32, 128, 8192], P(('groups', 'inst'), None, 'tp'), parts along dimension 0
- owner_cache: bfloat16 [64, 8, 128, 256], P(('groups', 'inst'), None, 'tp'), parts along dimension 0
There are 2 independent parts, one for each index of `groups`. A program takes and returns all parts, laid end to end along the dimension named above; each array names one. Nothing has to cross between parts.
Inputs may be any that keep to these rules, and one draw needn't show every extreme that they name: `prompt_spans`: they sum to 16. `decode_owner`: distinct instances.
All inputs are finite; a program needn't handle non-finite values.
Results may differ from a plain program's by a relative error of at most 0.0036.
Values may be sent and summed in bfloat16 or wider, within the bound.
No kernel may reach another device: no remote copies, remote signals or barrier semaphores. Data moves between devices by JAX's collectives and lax.ppermute only.
A program may use at most 64 MiB of HBM per device.

v0:
```python
import math

import jax
import jax.numpy as jnp
from jax import lax
from jax.sharding import PartitionSpec as P

HEADS = 64
KVH = 8


def span_meta(prompt_spans, prompt_tail, span_plan, span_total, span_len):
    span_ids = jnp.arange(span_total, dtype=jnp.int32)
    prompt_ends = jnp.cumsum(prompt_spans)
    prompt_count = prompt_spans.shape[0]
    prompt_of = jnp.sum((span_ids[:, None] >= prompt_ends[None, :]).astype(jnp.int32), axis=1)
    belongs = prompt_of[:, None] == jnp.arange(prompt_count, dtype=jnp.int32)[None, :]
    prompt_first = prompt_ends - prompt_spans
    index_of = span_ids - jnp.sum(jnp.where(belongs, prompt_first[None, :], 0), axis=1)
    lengths = (prompt_spans - 1) * span_len + prompt_tail
    length_of = jnp.sum(jnp.where(belongs, lengths[None, :], 0), axis=1)
    plan_hits = span_plan[:, None] == span_ids[None, :]

    def lookup(values):
        return jnp.sum(jnp.where(plan_hits, values[None, :], 0), axis=1)

    return (lookup(prompt_of), lookup(index_of), lookup(length_of))


def body(queries, kv_new, prompt_spans, prompt_tail, span_plan, decode_owner):
    tp_size = lax.axis_size("tp")
    inst_size = lax.axis_size("inst")
    tp_index = lax.axis_index("tp")
    inst_index = lax.axis_index("inst")
    slot_count, span_len, row_width = queries.shape
    kv_heads = kv_new.shape[1]
    slice_len = kv_new.shape[2]
    head_dim = kv_new.shape[3] // 2
    local_heads = row_width // head_dim
    group_size = HEADS // KVH
    kv_local = max(1, kv_heads // tp_size)
    per_head = local_heads // kv_local
    span_total = slot_count * inst_size
    longest = span_total // 2
    prompt_count = prompt_spans.shape[0]
    score_scale = 1.0 / math.sqrt(head_dim)
    slot_prompt, slot_index, slot_length = span_meta(
        prompt_spans, prompt_tail, span_plan, span_total, span_len
    )
    offsets = jnp.arange(span_len, dtype=jnp.int32)
    own_first = inst_index * slot_count
    own_prompt = lax.dynamic_slice_in_dim(slot_prompt, own_first, slot_count)
    own_index = lax.dynamic_slice_in_dim(slot_index, own_first, slot_count)
    own_length = lax.dynamic_slice_in_dim(slot_length, own_first, slot_count)
    query_pos = (own_index[:, None] * span_len + offsets[None, :]).reshape(-1)
    query_live = query_pos < jnp.repeat(own_length, span_len)
    query_prompt = jnp.repeat(own_prompt, span_len)
    row_count = slot_count * span_len
    query_rows = queries.reshape(row_count, kv_local, per_head, head_dim)
    first_head = tp_index * local_heads // group_size
    starting = (
        jnp.full((row_count, kv_local, per_head), -1e30, jnp.float32),
        jnp.zeros((row_count, kv_local, per_head), jnp.float32),
        jnp.zeros((row_count, kv_local, per_head, head_dim), jnp.float32),
    )

    def attend_span(running, entries):
        key_span, key_prompt, key_index, key_length = entries
        key_pos = key_index * span_len + offsets
        allowed = (query_prompt[:, None] == key_prompt) & (key_pos[None, :] <= query_pos[:, None])
        allowed = allowed & (key_pos < key_length)[None, :] & query_live[:, None]
        wide_allowed = allowed[:, None, None, :]
        old_max, old_sum, old_mix = running
        scores = (
            jnp.einsum(
                "rkgd,kcd->rkgc",
                query_rows,
                key_span[:, :, :head_dim],
                preferred_element_type=jnp.float32,
            )
            * score_scale
        )
        masked = jnp.where(wide_allowed, scores, -1e30)
        new_max = jnp.maximum(old_max, jnp.max(masked, axis=-1))
        rescale = jnp.exp(old_max - new_max)
        weights = jnp.where(wide_allowed, jnp.exp(masked - new_max[..., None]), 0.0)
        new_sum = old_sum * rescale + jnp.sum(weights, axis=-1)
        new_mix = old_mix * rescale[..., None] + jnp.einsum(
            "rkgc,kcd->rkgd",
            weights.astype(jnp.bfloat16),
            key_span[:, :, head_dim:],
            preferred_element_type=jnp.float32,
        )
        running = (new_max, new_sum, new_mix)
        return (running, None)

    empty_cache = jnp.zeros((longest, kv_heads, slice_len, 2 * head_dim), jnp.bfloat16)
    whole = lax.all_gather(kv_new, "tp", axis=2, tiled=True)
    own_heads = lax.dynamic_slice_in_dim(whole, first_head, kv_local, 1)
    running = starting
    page_block = lax.all_gather(own_heads, "inst", axis=0, tiled=True)
    page_prompt = slot_prompt
    page_index = slot_index
    running, unused = lax.scan(
        attend_span, running, (page_block, page_prompt, page_index, slot_length)
    )
    page_block = lax.all_gather(kv_new, "inst", axis=0, tiled=True)
    page_count = page_block.shape[0]
    page_prompt = slot_prompt
    page_index = slot_index
    owner_hits = page_prompt[:, None] == jnp.arange(prompt_count, dtype=jnp.int32)[None, :]
    owners = jnp.sum(jnp.where(owner_hits, decode_owner[None, :], 0), axis=1)
    target = owners * longest + page_index - inst_index * longest
    select = (target[None, :] == jnp.arange(longest, dtype=jnp.int32)[:, None]).astype(jnp.bfloat16)
    placed = jnp.einsum(
        "ok,kx->ox", select, page_block.reshape(page_count, -1), preferred_element_type=jnp.float32
    ).astype(jnp.bfloat16)
    owner_cache = placed.reshape(empty_cache.shape)
    final_max, final_sum, final_mix = running
    divisor = jnp.where(query_live[:, None, None], final_sum, 1.0)
    result = jnp.where(query_live[:, None, None, None], final_mix / divisor[..., None], 0.0)
    attended = result.reshape(slot_count, span_len, row_width).astype(jnp.bfloat16)
    return (attended, owner_cache)


def solution(mesh):
    placed = (
        P(("groups", "inst"), None, "tp"),
        P(("groups", "inst"), None, "tp", None),
        P("groups"),
        P("groups"),
        P("groups"),
        P("groups"),
    )
    return jax.shard_map(
        body,
        mesh=mesh,
        in_specs=placed,
        out_specs=(P(("groups", "inst"), None, "tp"), P(("groups", "inst"), None, "tp", None)),
        check_vma=False,
    )
```

profile of v0, /device:TPU:5, one launch (start us, length us, event | category | flops | bytes accessed | tf_op | source)
XLA Modules:
  0.0 414.9 jit_solution(8254731939756340436)
XLA Ops:
  8.7 25.1 %all-gather.4.cloned.1.call-done = bf16[4,8,128,256]{3,2,1,0:T(8,128)(2,1)} async-done(((bf16[4,8,32,256]{3,2,1,0:T(8,128)(2,1)}), bf16[4,8,128,256]{3,2,1,0:T(8,128)(2,1)}) %all-gather.4.cloned.1.call-update) | async-done | bytes 2097168 | tf_op jit(solution)/shard_map/all_gather | solution.py:98
  41.5 39.5 %all-gather.8.cloned.1.call-done = bf16[16,8,32,256]{3,2,1,0:T(8,128)(2,1)} async-done(((bf16[4,8,32,256]{3,2,1,0:T(8,128)(2,1)}), bf16[16,8,32,256]{3,2,1,0:T(8,128)(2,1)}) %all-gather.8.cloned.1.call-update) | async-done | bytes 2097168 | tf_op jit(solution)/shard_map/all_gather | solution.py:107
  85.3 42.4 %all-gather.6.cloned.1.call-done = bf16[16,2,128,256]{3,2,1,0:T(8,128)(2,1)} async-done(((bf16[4,2,128,256]{3,2,1,0:T(8,128)(2,1)}), bf16[16,2,128,256]{3,2,1,0:T(8,128)(2,1)}) %all-gather.6.cloned.1.call-update) | async-done | bytes 2097168 | tf_op jit(solution)/shard_map/all_gather | solution.py:101
  127.8 271.5 %while.17 = (s32[]{:T(128)}, f32[512,2,8]{0,2,1:T(8,128)S(1)}, f32[512,2,8]{0,2,1:T(8,128)S(1)}, f32[512,2,8,128]{0,3,2,1:T(8,128)}, s32[16]{0:T(128)S(1)}, /*in...) while((s32[]{:T(128)}, f32[512,2,8]{0,2,1:T(8,128)S(1)}, ...), condition=%wide.region_10.11_spmd.clone.clone.clone, body=%wide.region_7.10_spmd.clone.clone.clone.sunk | while | flops 553953152 | bytes 41033280 | solution.py:104
  135.5 3.4 fusion.41
  138.9 3.8 bitcast_add_fusion.2
  150.4 3.4 fusion.41
  153.9 5.9 %bitcast_add_fusion.2 = f32[512,2,8,128]{0,3,2,1:T(8,128)} fusion(f32[512,2,8,128]{0,3,2,1:T(8,128)} %get-tuple-element.371, f32[2,128,512,8]{2,1,3,0:T(8,128)S(1)} %copy-done, f32[512,2,8]{0,2,1:T(8,128)S(1)} %get-tuple-element.352, f32[512,2,8]{0,2,1:T(8,128)S(1)} %select_maximum_fusion.2, pred[]{:T(512)S(6)} %compare.7, ...), kind=kOutput, calls=%fused_computation.4.clone.1 | convolution fusion | flops 276824064 | bytes 12779521 | tf_op jit(solution)/shard_map/while/body/eval_jaxpr/rkgc,kcd->rkgd/dot_general | solution.py:88
  167.5 3.4 fusion.41
  171.0 5.9 %bitcast_add_fusion.2 = f32[512,2,8,128]{0,3,2,1:T(8,128)} fusion(f32[512,2,8,128]{0,3,2,1:T(8,128)} %get-tuple-element.371, f32[2,128,512,8]{2,1,3,0:T(8,128)S(1)} %copy-done, f32[512,2,8]{0,2,1:T(8,128)S(1)} %get-tuple-element.352, f32[512,2,8]{0,2,1:T(8,128)S(1)} %select_maximum_fusion.2, pred[]{:T(512)S(6)} %compare.7, ...), kind=kOutput, calls=%fused_computation.4.clone.1 | convolution fusion | flops 276824064 | bytes 12779521 | tf_op jit(solution)/shard_map/while/body/eval_jaxpr/rkgc,kcd->rkgd/dot_general | solution.py:88
  188.1 5.9 %bitcast_add_fusion.2 = f32[512,2,8,128]{0,3,2,1:T(8,128)} fusion(f32[512,2,8,128]{0,3,2,1:T(8,128)} %get-tuple-element.371, f32[2,128,512,8]{2,1,3,0:T(8,128)S(1)} %copy-done, f32[512,2,8]{0,2,1:T(8,128)S(1)} %get-tuple-element.352, f32[512,2,8]{0,2,1:T(8,128)S(1)} %select_maximum_fusion.2, pred[]{:T(512)S(6)} %compare.7, ...), kind=kOutput, calls=%fused_computation.4.clone.1 | convolution fusion | flops 276824064 | bytes 12779521 | tf_op jit(solution)/shard_map/while/body/eval_jaxpr/rkgc,kcd->rkgd/dot_general | solution.py:88
  205.2 5.9 %bitcast_add_fusion.2 = f32[512,2,8,128]{0,3,2,1:T(8,128)} fusion(f32[512,2,8,128]{0,3,2,1:T(8,128)} %get-tuple-element.371, f32[2,128,512,8]{2,1,3,0:T(8,128)S(1)} %copy-done, f32[512,2,8]{0,2,1:T(8,128)S(1)} %get-tuple-element.352, f32[512,2,8]{0,2,1:T(8,128)S(1)} %select_maximum_fusion.2, pred[]{:T(512)S(6)} %compare.7, ...), kind=kOutput, calls=%fused_computation.4.clone.1 | convolution fusion | flops 276824064 | bytes 12779521 | tf_op jit(solution)/shard_map/while/body/eval_jaxpr/rkgc,kcd->rkgd/dot_general | solution.py:88
  222.3 5.9 %bitcast_add_fusion.2 = f32[512,2,8,128]{0,3,2,1:T(8,128)} fusion(f32[512,2,8,128]{0,3,2,1:T(8,128)} %get-tuple-element.371, f32[2,128,512,8]{2,1,3,0:T(8,128)S(1)} %copy-done, f32[512,2,8]{0,2,1:T(8,128)S(1)} %get-tuple-element.352, f32[512,2,8]{0,2,1:T(8,128)S(1)} %select_maximum_fusion.2, pred[]{:T(512)S(6)} %compare.7, ...), kind=kOutput, calls=%fused_computation.4.clone.1 | convolution fusion | flops 276824064 | bytes 12779521 | tf_op jit(solution)/shard_map/while/body/eval_jaxpr/rkgc,kcd->rkgd/dot_general | solution.py:88
  239.4 5.9 %bitcast_add_fusion.2 = f32[512,2,8,128]{0,3,2,1:T(8,128)} fusion(f32[512,2,8,128]{0,3,2,1:T(8,128)} %get-tuple-element.371, f32[2,128,512,8]{2,1,3,0:T(8,128)S(1)} %copy-done, f32[512,2,8]{0,2,1:T(8,128)S(1)} %get-tuple-element.352, f32[512,2,8]{0,2,1:T(8,128)S(1)} %select_maximum_fusion.2, pred[]{:T(512)S(6)} %compare.7, ...), kind=kOutput, calls=%fused_computation.4.clone.1 | convolution fusion | flops 276824064 | bytes 12779521 | tf_op jit(solution)/shard_map/while/body/eval_jaxpr/rkgc,kcd->rkgd/dot_general | solution.py:88
  256.5 5.9 %bitcast_add_fusion.2 = f32[512,2,8,128]{0,3,2,1:T(8,128)} fusion(f32[512,2,8,128]{0,3,2,1:T(8,128)} %get-tuple-element.371, f32[2,128,512,8]{2,1,3,0:T(8,128)S(1)} %copy-done, f32[512,2,8]{0,2,1:T(8,128)S(1)} %get-tuple-element.352, f32[512,2,8]{0,2,1:T(8,128)S(1)} %select_maximum_fusion.2, pred[]{:T(512)S(6)} %compare.7, ...), kind=kOutput, calls=%fused_computation.4.clone.1 | convolution fusion | flops 276824064 | bytes 12779521 | tf_op jit(solution)/shard_map/while/body/eval_jaxpr/rkgc,kcd->rkgd/dot_general | solution.py:88
  273.6 5.9 %bitcast_add_fusion.2 = f32[512,2,8,128]{0,3,2,1:T(8,128)} fusion(f32[512,2,8,128]{0,3,2,1:T(8,128)} %get-tuple-element.371, f32[2,128,512,8]{2,1,3,0:T(8,128)S(1)} %copy-done, f32[512,2,8]{0,2,1:T(8,128)S(1)} %get-tuple-element.352, f32[512,2,8]{0,2,1:T(8,128)S(1)} %select_maximum_fusion.2, pred[]{:T(512)S(6)} %compare.7, ...), kind=kOutput, calls=%fused_computation.4.clone.1 | convolution fusion | flops 276824064 | bytes 12779521 | tf_op jit(solution)/shard_map/while/body/eval_jaxpr/rkgc,kcd->rkgd/dot_general | solution.py:88
  290.7 5.9 %bitcast_add_fusion.2 = f32[512,2,8,128]{0,3,2,1:T(8,128)} fusion(f32[512,2,8,128]{0,3,2,1:T(8,128)} %get-tuple-element.371, f32[2,128,512,8]{2,1,3,0:T(8,128)S(1)} %copy-done, f32[512,2,8]{0,2,1:T(8,128)S(1)} %get-tuple-element.352, f32[512,2,8]{0,2,1:T(8,128)S(1)} %select_maximum_fusion.2, pred[]{:T(512)S(6)} %compare.7, ...), kind=kOutput, calls=%fused_computation.4.clone.1 | convolution fusion | flops 276824064 | bytes 12779521 | tf_op jit(solution)/shard_map/while/body/eval_jaxpr/rkgc,kcd->rkgd/dot_general | solution.py:88
  307.8 5.9 %bitcast_add_fusion.2 = f32[512,2,8,128]{0,3,2,1:T(8,128)} fusion(f32[512,2,8,128]{0,3,2,1:T(8,128)} %get-tuple-element.371, f32[2,128,512,8]{2,1,3,0:T(8,128)S(1)} %copy-done, f32[512,2,8]{0,2,1:T(8,128)S(1)} %get-tuple-element.352, f32[512,2,8]{0,2,1:T(8,128)S(1)} %select_maximum_fusion.2, pred[]{:T(512)S(6)} %compare.7, ...), kind=kOutput, calls=%fused_computation.4.clone.1 | convolution fusion | flops 276824064 | bytes 12779521 | tf_op jit(solution)/shard_map/while/body/eval_jaxpr/rkgc,kcd->rkgd/dot_general | solution.py:88
  324.9 5.9 %bitcast_add_fusion.2 = f32[512,2,8,128]{0,3,2,1:T(8,128)} fusion(f32[512,2,8,128]{0,3,2,1:T(8,128)} %get-tuple-element.371, f32[2,128,512,8]{2,1,3,0:T(8,128)S(1)} %copy-done, f32[512,2,8]{0,2,1:T(8,128)S(1)} %get-tuple-element.352, f32[512,2,8]{0,2,1:T(8,128)S(1)} %select_maximum_fusion.2, pred[]{:T(512)S(6)} %compare.7, ...), kind=kOutput, calls=%fused_computation.4.clone.1 | convolution fusion | flops 276824064 | bytes 12779521 | tf_op jit(solution)/shard_map/while/body/eval_jaxpr/rkgc,kcd->rkgd/dot_general | solution.py:88
  342.0 5.9 %bitcast_add_fusion.2 = f32[512,2,8,128]{0,3,2,1:T(8,128)} fusion(f32[512,2,8,128]{0,3,2,1:T(8,128)} %get-tuple-element.371, f32[2,128,512,8]{2,1,3,0:T(8,128)S(1)} %copy-done, f32[512,2,8]{0,2,1:T(8,128)S(1)} %get-tuple-element.352, f32[512,2,8]{0,2,1:T(8,128)S(1)} %select_maximum_fusion.2, pred[]{:T(512)S(6)} %compare.7, ...), kind=kOutput, calls=%fused_computation.4.clone.1 | convolution fusion | flops 276824064 | bytes 12779521 | tf_op jit(solution)/shard_map/while/body/eval_jaxpr/rkgc,kcd->rkgd/dot_general | solution.py:88
  359.1 5.9 %bitcast_add_fusion.2 = f32[512,2,8,128]{0,3,2,1:T(8,128)} fusion(f32[512,2,8,128]{0,3,2,1:T(8,128)} %get-tuple-element.371, f32[2,128,512,8]{2,1,3,0:T(8,128)S(1)} %copy-done, f32[512,2,8]{0,2,1:T(8,128)S(1)} %get-tuple-element.352, f32[512,2,8]{0,2,1:T(8,128)S(1)} %select_maximum_fusion.2, pred[]{:T(512)S(6)} %compare.7, ...), kind=kOutput, calls=%fused_computation.4.clone.1 | convolution fusion | flops 276824064 | bytes 12779521 | tf_op jit(solution)/shard_map/while/body/eval_jaxpr/rkgc,kcd->rkgd/dot_general | solution.py:88
  376.2 5.9 %bitcast_add_fusion.2 = f32[512,2,8,128]{0,3,2,1:T(8,128)} fusion(f32[512,2,8,128]{0,3,2,1:T(8,128)} %get-tuple-element.371, f32[2,128,512,8]{2,1,3,0:T(8,128)S(1)} %copy-done, f32[512,2,8]{0,2,1:T(8,128)S(1)} %get-tuple-element.352, f32[512,2,8]{0,2,1:T(8,128)S(1)} %select_maximum_fusion.2, pred[]{:T(512)S(6)} %compare.7, ...), kind=kOutput, calls=%fused_computation.4.clone.1 | convolution fusion | flops 276824064 | bytes 12779521 | tf_op jit(solution)/shard_map/while/body/eval_jaxpr/rkgc,kcd->rkgd/dot_general | solution.py:88
  393.3 5.9 %bitcast_add_fusion.2 = f32[512,2,8,128]{0,3,2,1:T(8,128)} fusion(f32[512,2,8,128]{0,3,2,1:T(8,128)} %get-tuple-element.371, f32[2,128,512,8]{2,1,3,0:T(8,128)S(1)} %copy-done, f32[512,2,8]{0,2,1:T(8,128)S(1)} %get-tuple-element.352, f32[512,2,8]{0,2,1:T(8,128)S(1)} %select_maximum_fusion.2, pred[]{:T(512)S(6)} %compare.7, ...), kind=kOutput, calls=%fused_computation.4.clone.1 | convolution fusion | flops 276824064 | bytes 12779521 | tf_op jit(solution)/shard_map/while/body/eval_jaxpr/rkgc,kcd->rkgd/dot_general | solution.py:88
  404.2 4.3 %copy.30 = bf16[4,128,2048]{2,1,0:T(8,128)(2,1)} copy(bf16[4,128,2048]{1,0,2:T(4,128)(2,1)} %reshape.184) | data formatting | bytes 4194304 | tf_op jit(solution)/shard_map/convert_element_type | solution.py:122
  (301 shorter events, 175.9 us)
Async XLA Ops:
  7.2 26.6 %all-gather.4.cloned.1.call-start = ((), (), s32[]{:S(2)}) async-start(), calls=%async_computation | async-start | bytes 2621440 | tf_op jit(solution)/shard_map/all_gather | solution.py:98
  7.9 73.0 %all-gather.8.cloned.1.call-start = ((), (), s32[]{:S(2)}) async-start(), calls=%async_computation.2 | async-start | bytes 2621440 | tf_op jit(solution)/shard_map/all_gather | solution.py:107
  8.6 119.1 %all-gather.6.cloned.1.call-start = ((), (), s32[]{:S(2)}) async-start(), calls=%async_computation.1 | async-start | bytes 2621440 | tf_op jit(solution)/shard_map/all_gather | solution.py:101
  38.4 2.9 copy-start.1
  135.5 3.4 copy-start
  150.4 3.4 copy-start
  167.5 3.4 copy-start
  184.6 3.4 copy-start
  201.7 3.4 copy-start
  218.8 3.4 copy-start
  235.9 3.4 copy-start
  253.0 3.4 copy-start
  270.1 3.4 copy-start
  287.2 3.4 copy-start
  304.3 3.4 copy-start
  321.4 3.4 copy-start
  338.5 3.4 copy-start
  355.6 3.4 copy-start
  372.7 3.4 copy-start
  389.8 3.4 copy-start
Sparse Core Ops, SparseCore 0:
  9.6 24.1 all-gather.3
  35.4 45.5 all-gather.7
  83.1 44.6 all-gather.5
where the time goes:
time: 418 us; the launch traced here: 415 us
  matrix products  138 us (33%)
  waiting for transfers between devices  108 us (26%)
  other arithmetic  84.6 us (20%)
  local copies, waits for them, and re-layouts  58.7 us (14%)
  between operations  13.8 us (3%)
  loops' own time  11.1 us (3%)
    dot_general x16, matrix products, attend_span(): jnp.einsum('rkgc,kcd->rkgd', weights.astype(jnp.bfloat16), key_span[:, :,...  92.8 us
    reduce_sum x16, other arithmetic, attend_span(): new_sum = old_sum * rescale + jnp.sum(weights, axis=-1)  54.2 us
    dot_general x16, matrix products, attend_span(): jnp.einsum('rkgd,kcd->rkgc', query_rows, key_span[:, :, :head_dim], prefe...  45.1 us
    all_gather x1, waiting for transfers between devices, body(): page_block = lax.all_gather(own_heads, 'inst', axis=0, tiled=True)  42.4 us
    all_gather x1, waiting for transfers between devices, body(): page_block = lax.all_gather(kv_new, 'inst', axis=0, tiled=True)  39.5 us
    dynamic_slice x48, local copies, waits for them, and re-layouts, body(): lax.scan(attend_span, running, (page_block, page_prompt, page_index, slot...  28.4 us
    all_gather x1, waiting for transfers between devices, body(): whole = lax.all_gather(kv_new, 'tp', axis=2, tiled=True)  25.1 us
    squeeze x16, local copies, waits for them, and re-layouts, body(): lax.scan(attend_span, running, (page_block, page_prompt, page_index, slot...  14.7 us
  transfers between devices with their start and end apart: 3, of which 3 were waited for; matrix products, arithmetic and copies ran while one was open for 3% of the time, Pallas kernels for 0%

commit v1 on v0

v1 whole, which is shorter than its diff:
```python
import functools
import math

import jax
import jax.numpy as jnp
from jax import lax
from jax.experimental import pallas as pl
from jax.experimental.pallas import tpu as pltpu
from jax.sharding import PartitionSpec as P

HEADS = 64
KVH = 8
LOG2E = 1.4426950408889634


def read_plan(spans_ref, plan_ref, place_ref, slot):
    span = plan_ref[slot]
    prompt = jnp.int32(0)
    first = jnp.int32(0)
    end = jnp.int32(0)
    for p in range(spans_ref.shape[0]):
        end = end + spans_ref[p]
        later = span >= end
        prompt = jnp.where(later, p + 1, prompt)
        first = jnp.where(later, end, first)
    return prompt, first, span


def attend_kernel(
    spans_ref, tail_ref, plan_ref, owner_ref, inst_ref,
    q_ref, kv_ref, pages_ref, out_ref, cache_ref,
    place_ref, acc_ref, max_ref, zero_ref, sems,
    *, kv_local, per_head, head_dim, span_len, slot_count, span_total, longest,
):
    step = pl.program_id(0)
    inst = inst_ref[0]
    prompt_count = spans_ref.shape[0]
    scale = LOG2E / math.sqrt(head_dim)

    def cache_copies(act):
        mine = jnp.int32(0)
        first = jnp.int32(0)
        count = jnp.int32(0)
        start = jnp.int32(0)
        for p in range(prompt_count):
            hit = owner_ref[p] == inst
            first = jnp.where(hit, start, first)
            count = jnp.where(hit, spans_ref[p], count)
            start = start + spans_ref[p]

        def row(r, unused):
            @pl.when(r < count)
            def _():
                page = place_ref[jnp.minimum(first + r, span_total - 1)]
                act(pltpu.make_async_copy(pages_ref.at[page], cache_ref.at[r], sems.at[r]))

            @pl.when(r >= count)
            def _():
                act(pltpu.make_async_copy(zero_ref, cache_ref.at[r], sems.at[r]))

            return unused

        lax.fori_loop(0, longest, row, 0)

    @pl.when(step == 0)
    def _():
        def put(g, unused):
            place_ref[plan_ref[g]] = g
            return unused

        lax.fori_loop(0, span_total, put, 0)
        zero_ref[...] = jnp.zeros_like(zero_ref)
        cache_copies(lambda copy: copy.start())

    prompt, first, span = read_plan(spans_ref, plan_ref, place_ref, inst * slot_count + step)
    index = span - first
    length = jnp.int32(0)
    for p in range(prompt_count):
        length = jnp.where(
            prompt == p, (spans_ref[p] - 1) * span_len + tail_ref[p], length
        )
    live_rows = length - index * span_len
    ones = jnp.ones((span_len, head_dim), jnp.bfloat16)
    row_ids = lax.broadcasted_iota(jnp.int32, (span_len, span_len), 0)
    col_ids = lax.broadcasted_iota(jnp.int32, (span_len, span_len), 1)
    causal = row_ids >= col_ids
    live = row_ids[:, :head_dim] < live_rows

    def load(pages, g):
        blocks = [kv_ref[page, g] for page in pages]
        keys = [b[:, :head_dim] for b in blocks]
        values = [jnp.concatenate([b[:, head_dim:], ones], axis=1) for b in blocks]
        if len(pages) == 1:
            return keys[0], values[0]
        return jnp.concatenate(keys, axis=0), jnp.concatenate(values, axis=0)

    def scores_of(g, h, keys):
        head = g * per_head + h
        q = q_ref[0, :, head * head_dim:(head + 1) * head_dim]
        return lax.dot_general(
            q, keys, (((1,), (1,)), ((), ())), preferred_element_type=jnp.float32
        ) * scale

    def begin(pages):
        for g in range(kv_local):
            keys, values = load(pages, g)
            for h in range(per_head):
                head = g * per_head + h
                s = scores_of(g, h, keys)
                tail = jnp.where(causal, s[:, -span_len:], -1e30)
                s = tail if len(pages) == 1 else jnp.concatenate([s[:, :span_len], tail], axis=1)
                top = jnp.max(s, axis=1, keepdims=True)
                w = jnp.exp2(s - top).astype(jnp.bfloat16)
                acc_ref[head] = jnp.dot(w, values, preferred_element_type=jnp.float32)
                max_ref[head] = jnp.broadcast_to(top, (span_len, head_dim))

    def more(pages):
        for g in range(kv_local):
            keys, values = load(pages, g)
            for h in range(per_head):
                head = g * per_head + h
                s = scores_of(g, h, keys)
                old = max_ref[head]
                top = jnp.maximum(old, jnp.max(s, axis=1, keepdims=True))
                rescale = jnp.exp2(old - top)
                wide = jnp.concatenate([top] * len(pages), axis=1)
                w = jnp.exp2(s - wide).astype(jnp.bfloat16)
                acc_ref[head] = acc_ref[head] * jnp.concatenate(
                    [rescale, rescale], axis=1
                ) + jnp.dot(w, values, preferred_element_type=jnp.float32)
                max_ref[head] = top

    own = inst * slot_count + step
    odd = lax.rem(index, 2)

    @pl.when(odd == 0)
    def _():
        begin([own])

    @pl.when(odd == 1)
    def _():
        begin([place_ref[first], own])

    def pair(j, unused):
        at = first + odd + 2 * j
        more([place_ref[at], place_ref[at + 1]])
        return unused

    lax.fori_loop(0, index // 2, pair, 0)

    for head in range(kv_local * per_head):
        total = acc_ref[head]
        mixed = total[:, :head_dim] / total[:, head_dim:]
        out_ref[0, :, head * head_dim:(head + 1) * head_dim] = jnp.where(
            live, mixed, 0.0
        ).astype(jnp.bfloat16)

    @pl.when(step == slot_count - 1)
    def _():
        cache_copies(lambda copy: copy.wait())


def body(queries, kv_new, prompt_spans, prompt_tail, span_plan, decode_owner):
    tp_size = lax.axis_size("tp")
    inst_size = lax.axis_size("inst")
    inst_index = lax.axis_index("inst")
    slot_count, span_len, row_width = queries.shape
    kv_heads, slice_len, width = kv_new.shape[1:]
    head_dim = width // 2
    local_heads = row_width // head_dim
    kv_local = max(1, kv_heads // tp_size)
    per_head = local_heads // kv_local
    span_total = slot_count * inst_size
    longest = span_total // 2
    pages = lax.all_gather(kv_new, "inst", axis=0, tiled=True)
    if tp_size > kv_heads:
        sent = jnp.repeat(pages, tp_size // kv_heads, axis=1)
    else:
        sent = pages
    own_heads = lax.all_to_all(sent, "tp", split_axis=1, concat_axis=2, tiled=True)
    kernel = functools.partial(
        attend_kernel,
        kv_local=kv_local,
        per_head=per_head,
        head_dim=head_dim,
        span_len=span_len,
        slot_count=slot_count,
        span_total=span_total,
        longest=longest,
    )
    work = slot_count * span_total // 4 * local_heads * span_len * span_len
    attended, owner_cache = pl.pallas_call(
        kernel,
        grid_spec=pltpu.PrefetchScalarGridSpec(
            num_scalar_prefetch=5,
            grid=(slot_count,),
            in_specs=[
                pl.BlockSpec((1, span_len, row_width), lambda i, *_: (i, 0, 0)),
                pl.BlockSpec(own_heads.shape, lambda i, *_: (0, 0, 0, 0)),
                pl.BlockSpec(memory_space=pl.ANY),
            ],
            out_specs=[
                pl.BlockSpec((1, span_len, row_width), lambda i, *_: (i, 0, 0)),
                pl.BlockSpec(memory_space=pl.ANY),
            ],
            scratch_shapes=[
                pltpu.SMEM((span_total,), jnp.int32),
                pltpu.VMEM((local_heads, span_len, 2 * head_dim), jnp.float32),
                pltpu.VMEM((local_heads, span_len, head_dim), jnp.float32),
                pltpu.VMEM((kv_heads, slice_len, width), jnp.bfloat16),
                pltpu.SemaphoreType.DMA((longest,)),
            ],
        ),
        out_shape=[
            jax.ShapeDtypeStruct(queries.shape, jnp.bfloat16),
            jax.ShapeDtypeStruct((longest, kv_heads, slice_len, width), jnp.bfloat16),
        ],
        cost_estimate=pl.CostEstimate(
            flops=4 * work * head_dim, bytes_accessed=8 << 20, transcendentals=work
        ),
        compiler_params=pltpu.CompilerParams(vmem_limit_bytes=48 << 20),
    )(
        prompt_spans, prompt_tail, span_plan, decode_owner,
        jnp.reshape(inst_index.astype(jnp.int32), (1,)),
        queries, own_heads, pages,
    )
    return (attended, owner_cache)


def solution(mesh):
    placed = (
        P(("groups", "inst"), None, "tp"),
        P(("groups", "inst"), None, "tp", None),
        P("groups"),
        P("groups"),
        P("groups"),
        P("groups"),
    )
    return jax.shard_map(
        body,
        mesh=mesh,
        in_specs=placed,
        out_specs=(P(("groups", "inst"), None, "tp"), P(("groups", "inst"), None, "tp", None)),
        check_vma=False,
    )
```

time: 418 us -> 132 us (0.32)
  matrix products: 138 us -> 0 us
  other arithmetic: 84.6 us -> 0 us
  local copies, waits for them, and re-layouts: 58.7 us -> 4.73 us
  Pallas kernels: 0 us -> 34.5 us
  waiting for transfers between devices: 108 us -> 74.4 us
  loops' own time: 11.1 us -> 0 us
  starting transfers between devices: 0.11 us -> 4.29 us
    dot_general x33 -> x0, matrix products: 138 us -> none  [the longest x16 92.8 us: attend_span(): jnp.einsum('rkgc,kcd->rkgd', weights.astype(jnp.bfloat16), key_span[:, :,...]
    all_gather x3 -> x1, waiting for transfers between devices: 107 us -> 48.8 us  [body(): pages = lax.all_gather(kv_new, 'inst', axis=0, tiled=True)]
    reduce_sum x20 -> x0, other arithmetic: 55.3 us -> none  [the longest x16 54.2 us: attend_span(): new_sum = old_sum * rescale + jnp.sum(weights, axis=-1)]
    pallas_call x0 -> x1, Pallas kernels: none -> 34.5 us  [body(): pl.pallas_call(kernel, grid_spec=pltpu.PrefetchScalarGridSpec(num_scalar_...]
    dynamic_slice x51 -> x0, local copies, waits for them, and re-layouts: 30.4 us -> none  [the longest x48 28.4 us: body(): lax.scan(attend_span, running, (page_block, page_prompt, page_index, slot...]
    all_to_all x0 -> x1, waiting for transfers between devices: none -> 24.8 us  [body(): lax.all_to_all(sent, 'tp', split_axis=1, concat_axis=2, tiled=True)]
    squeeze x16 -> x0, local copies, waits for them, and re-layouts: 14.7 us -> none  [body(): lax.scan(attend_span, running, (page_block, page_prompt, page_index, slot...]
    lt x33 -> x0, other arithmetic: 11.2 us -> none  [the longest x16 9.93 us: attend_span(): allowed = allowed & (key_pos < key_length)[None, :] & query_live[:, None]]
  transfers between devices with their start and end apart: 3 -> 2, of which waited for: 3 -> 2; matrix products, arithmetic and copies ran while one was open for 3% -> 0% of each run, Pallas kernels for 0% -> 0%
where the time goes in v1:
time: 132 us
  waiting for transfers between devices  74.4 us (56%)
  Pallas kernels  34.5 us (26%)
  between operations  14.1 us (11%)
  local copies, waits for them, and re-layouts  4.73 us (4%)
  starting transfers between devices  4.29 us (3%)
    all_gather x1, waiting for transfers between devices, body(): pages = lax.all_gather(kv_new, 'inst', axis=0, tiled=True)  48.8 us
    pallas_call x1, Pallas kernels, body(): pl.pallas_call(kernel, grid_spec=pltpu.PrefetchScalarGridSpec(num_scalar_...  34.5 us
    all_to_all x1, waiting for transfers between devices, body(): lax.all_to_all(sent, 'tp', split_axis=1, concat_axis=2, tiled=True)  24.8 us
    all_to_all x1, starting transfers between devices, body(): lax.all_to_all(sent, 'tp', split_axis=1, concat_axis=2, tiled=True)  4.25 us
    all_gather x1, local copies, waits for them, and re-layouts, body(): pages = lax.all_gather(kv_new, 'inst', axis=0, tiled=True)  3.15 us
  transfers between devices with their start and end apart: 2, of which 2 were waited for; matrix products, arithmetic and copies ran while one was open for 0% of the time, Pallas kernels for 0%

profile of v1, /device:TPU:5, one launch (start us, length us, event | category | flops | bytes accessed | tf_op | source)
XLA Modules:
  0.0 131.9 jit_solution(14350149151682763819)
XLA Ops:
  7.2 0.0 all-gather.2.cloned.1.call-start
  7.2 0.7 all-gather.2.cloned.1.call-update
  7.9 48.8 %all-gather.2.cloned.1.call-done.pages_ref = bf16[16,8,32,256]{3,2,1,0:T(8,128)(2,1)} async-done(((bf16[4,8,32,256]{3,2,1,0:T(8,128)(2,1)}), bf16[16,8,32,256]{3,2,1,0:T(8,128)(2,1)}) %all-gather.2.cloned.1.call-update) | async-done | bytes 2097168 | tf_op jit(solution)/shard_map/all_gather | solution.py:175
  56.7 3.1 %copy.9 = bf16[16,8,32,256]{3,2,0,1:T(8,128)(2,1)} copy(bf16[16,8,32,256]{3,2,1,0:T(8,128)(2,1)} %all-gather.2.cloned.1.call-done.pages_ref) | data formatting | bytes 4194304 | tf_op jit(solution)/shard_map/all_gather | solution.py:175
  59.9 4.3 %all-to-all-start = ((bf16[16,8,32,256]{3,2,0,1:T(8,128)(2,1)}), bf16[16,8,32,256]{3,2,0,1:T(8,128)(2,1)S(1)}, u32[]{:S(2)}, u32[]{:S(2)}) async-start(bf16[16,8,32,256]{3,2,0,1:T(8,128)(2,1)} %copy.9), calls=%async_computation | async-start | bytes 4194304 | tf_op jit(solution)/shard_map/all_to_all | solution.py:180
  64.1 24.8 %all-to-all-done = bf16[16,8,32,256]{3,2,0,1:T(8,128)(2,1)S(1)} async-done(((bf16[16,8,32,256]{3,2,0,1:T(8,128)(2,1)}), bf16[16,8,32,256]{3,2,0,1:T(8,128)(2,1)S(1)}, u32[]{:S(2)}, u32[]{:S(2)}) %all-to-all-start) | async-done | bytes 2097184 | tf_op jit(solution)/shard_map/all_to_all | solution.py:180
  89.0 0.0 copy-start
  89.0 0.0 copy-start.1
  89.0 0.0 copy-start.2
  89.0 0.0 copy-start.3
  89.0 0.0 copy-start.4
  89.0 0.2 copy.10
  89.2 1.3 %copy-done = bf16[4,128,2048]{2,1,0:T(8,128)(2,1)S(1)} copy-done((bf16[4,128,2048]{2,1,0:T(8,128)(2,1)S(1)}, bf16[4,128,2048]{2,1,0:T(8,128)(2,1)}, u32[]{:S(2)}) %copy-start) | copy-done | bytes 2097176
  90.6 0.0 copy-done.1
  90.6 0.0 copy-done.2
  90.6 0.0 copy-done.3
  90.6 0.0 copy-done.4
  90.6 34.5 %shard_map.77 = (bf16[4,128,2048]{2,1,0:T(8,128)(2,1)}, bf16[8,8,32,256]{3,2,1,0:T(8,128)(2,1)}) custom-call(s32[4]{0:T(128)S(1)} %copy-done.1, s32[4]{0:T(128)S(1)} %copy-done.2, s32[16]{0:T(128)S(1)} %copy-done.3, s32[4]{0:T(128)S(1)} %copy-done.4, s32[1]{0:T(128)} %bitcast.inst_ref, bf16[4,128,2048]{2,1,0:T(8,128)(2,1)S(1)} %copy-done, ...), custom_call_target="tpu_custom_call" | custom-call | flops 2147483648 | bytes 8388608 | tf_op jit(solution)/shard_map/pallas_call | solution.py:192
Async XLA Ops:
  7.2 49.6 %all-gather.2.cloned.1.call-start = ((), (), s32[]{:S(2)}) async-start(), calls=%async_computation.1 | async-start | bytes 2621440 | tf_op jit(solution)/shard_map/all_gather | solution.py:175
  59.9 29.1 %all-to-all-start = ((bf16[16,8,32,256]{3,2,0,1:T(8,128)(2,1)}), bf16[16,8,32,256]{3,2,0,1:T(8,128)(2,1)S(1)}, u32[]{:S(2)}, u32[]{:S(2)}) async-start(bf16[16,8,32,256]{3,2,0,1:T(8,128)(2,1)} %copy.9), calls=%async_computation | async-start | bytes 4194304 | tf_op jit(solution)/shard_map/all_to_all | solution.py:180
  89.0 1.6 %copy-start = (bf16[4,128,2048]{2,1,0:T(8,128)(2,1)S(1)}, bf16[4,128,2048]{2,1,0:T(8,128)(2,1)}, u32[]{:S(2)}) copy-start(bf16[4,128,2048]{2,1,0:T(8,128)(2,1)} %q_ref.1) | copy-start | bytes 6291460
  89.0 1.6 %copy-start.1 = (s32[4]{0:T(128)S(1)}, s32[4]{0:T(128)}, u32[]{:S(2)}) copy-start(s32[4]{0:T(128)} %spans_ref.1) | copy-start | bytes 52
  89.0 1.6 %copy-start.2 = (s32[4]{0:T(128)S(1)}, s32[4]{0:T(128)}, u32[]{:S(2)}) copy-start(s32[4]{0:T(128)} %tail_ref.1) | copy-start | bytes 52
  89.0 1.6 %copy-start.3 = (s32[16]{0:T(128)S(1)}, s32[16]{0:T(128)}, u32[]{:S(2)}) copy-start(s32[16]{0:T(128)} %plan_ref.1) | copy-start | bytes 196
  89.0 1.6 %copy-start.4 = (s32[4]{0:T(128)S(1)}, s32[4]{0:T(128)}, u32[]{:S(2)}) copy-start(s32[4]{0:T(128)} %owner_ref.1) | copy-start | bytes 52
Sparse Core Ops, SparseCore 0:
  9.6 47.1 all-gather.1

commit v2 on v1

v2 whole, which is shorter than its diff:
```python
import functools
import math

import jax
import jax.numpy as jnp
from jax import lax
from jax.experimental import pallas as pl
from jax.experimental.pallas import tpu as pltpu
from jax.sharding import PartitionSpec as P

HEADS = 64
KVH = 8
LOG2E = 1.4426950408889634


def source_of(unit, inst, inst_size):
    if unit == 0:
        return inst
    step, late = unit_steps(inst_size)[unit - 1]
    if not late:
        return jnp.where(inst <= inst_size - 1 - step, inst + step, inst - step)
    far = inst_size - step
    middle = (inst >= step) & (inst <= inst_size - 1 - step)
    return jnp.where(middle, inst - step, jnp.where(inst <= step - 1, inst + far, inst - far))


def unit_steps(inst_size):
    near = [(s, False) for s in range(1, inst_size // 2 + 1)]
    late = [(s, True) for s in range((inst_size - 1) // 2, 0, -1)]
    return near + late


def attend_kernel(
    spans_ref, tail_ref, plan_ref, owner_ref, where_ref, *refs,
    inst_size, tp_size, kv_local, per_head, head_dim, span_len, slot_count, longest,
):
    q_ref = refs[0]
    unit_refs = refs[1:1 + inst_size]
    part_refs = refs[1 + inst_size:1 + inst_size + inst_size * (tp_size - 1)]
    (out_ref, cache_ref, place_ref, kv_ref, s_ref, p_ref, acc_ref, max_ref, zero_ref,
     page_sems, part_sems) = refs[1 + inst_size + inst_size * (tp_size - 1):]
    step = pl.program_id(0)
    inst = where_ref[0]
    tp = where_ref[1]
    prompt_count = spans_ref.shape[0]
    span_total = slot_count * inst_size
    slice_len = span_len // tp_size
    rows = per_head * span_len
    scale = LOG2E / math.sqrt(head_dim)
    sources = [source_of(u, inst, inst_size) for u in range(inst_size)]
    first_head = tp * (kv_local * per_head) // (HEADS // KVH)

    def part_copies(act):
        for u in range(inst_size):
            slots = pl.ds(sources[u] * slot_count, slot_count)
            for j in range(tp_size):
                if j == 0:
                    src = unit_refs[u].at[:, pl.ds(first_head, kv_local)]
                else:
                    src = part_refs[u * (tp_size - 1) + j - 1]
                at = pl.multiple_of((tp ^ j) * slice_len, slice_len)
                act(pltpu.make_async_copy(
                    src, kv_ref.at[slots, :, pl.ds(at, slice_len)], part_sems.at[u, j]
                ))

    def cache_copies(act):
        first = jnp.int32(0)
        count = jnp.int32(0)
        start = jnp.int32(0)
        for p in range(prompt_count):
            hit = owner_ref[p] == inst
            first = jnp.where(hit, start, first)
            count = jnp.where(hit, spans_ref[p], count)
            start = start + spans_ref[p]

        def row(r, unused):
            page = place_ref[jnp.minimum(first + r, span_total - 1)]
            source = page // slot_count
            slot = page - source * slot_count
            for u in range(inst_size):
                @pl.when((r < count) & (source == sources[u]))
                def _():
                    act(pltpu.make_async_copy(
                        unit_refs[u].at[slot], cache_ref.at[r], page_sems.at[r]
                    ))

            @pl.when(r >= count)
            def _():
                act(pltpu.make_async_copy(zero_ref, cache_ref.at[r], page_sems.at[r]))

            return unused

        lax.fori_loop(0, longest, row, 0)

    @pl.when(step == 0)
    def _():
        part_copies(lambda copy: copy.start())

        def put(g, unused):
            place_ref[plan_ref[g]] = g
            return unused

        lax.fori_loop(0, span_total, put, 0)
        zero_ref[...] = jnp.zeros_like(zero_ref)
        cache_copies(lambda copy: copy.start())
        part_copies(lambda copy: copy.wait())

    own = inst * slot_count + step
    span = plan_ref[own]
    first = jnp.int32(0)
    end = jnp.int32(0)
    length = jnp.int32(0)
    for p in range(prompt_count):
        start = end
        end = end + spans_ref[p]
        inside = (span >= start) & (span < end)
        first = jnp.where(inside, start, first)
        length = jnp.where(inside, (spans_ref[p] - 1) * span_len + tail_ref[p], length)
    index = span - first
    live_rows = length - index * span_len
    ones = jnp.ones((span_len, head_dim), jnp.bfloat16)
    row_ids = lax.broadcasted_iota(jnp.int32, (span_len, span_len), 0)
    col_ids = lax.broadcasted_iota(jnp.int32, (span_len, span_len), 1)
    causal = row_ids >= col_ids

    def key_block(pages, g):
        return jnp.concatenate([kv_ref[page, g, :, :head_dim] for page in pages], axis=0)

    def value_block(pages, g):
        return jnp.concatenate(
            [
                jnp.concatenate([kv_ref[page, g, :, head_dim:], ones], axis=1)
                for page in pages
            ],
            axis=0,
        )

    def attend(pages, begin):
        wide = len(pages) * span_len
        for g in range(kv_local):
            q = jnp.concatenate(
                [
                    q_ref[0, :, (g * per_head + h) * head_dim:(g * per_head + h + 1) * head_dim]
                    for h in range(per_head)
                ],
                axis=0,
            )
            s_ref[g, :, :wide] = lax.dot_general(
                q, key_block(pages, g), (((1,), (1,)), ((), ())),
                preferred_element_type=jnp.float32,
            )
        for g in range(kv_local):
            rescales = []
            for h in range(per_head):
                at = slice(h * span_len, (h + 1) * span_len)
                s = s_ref[g, at, :wide] * scale
                if begin:
                    own_part = jnp.where(causal, s[:, wide - span_len:], -1e30)
                    if len(pages) > 1:
                        s = jnp.concatenate([s[:, :wide - span_len], own_part], axis=1)
                    else:
                        s = own_part
                top = jnp.max(s, axis=1, keepdims=True)
                if begin:
                    top = jnp.broadcast_to(top, (span_len, head_dim))
                else:
                    old = max_ref[g, at]
                    top = jnp.maximum(old, top)
                    rescales.append(jnp.exp2(old - top))
                max_ref[g, at] = top
                p_ref[g, at, :wide] = jnp.exp2(
                    s - jnp.concatenate([top] * len(pages), axis=1)
                ).astype(jnp.bfloat16)
            mixed = jnp.dot(
                p_ref[g, :, :wide], value_block(pages, g), preferred_element_type=jnp.float32
            )
            if begin:
                acc_ref[g] = mixed
            else:
                for h in range(per_head):
                    at = slice(h * span_len, (h + 1) * span_len)
                    acc_ref[g, at] = acc_ref[g, at] * jnp.concatenate(
                        [rescales[h], rescales[h]], axis=1
                    ) + mixed[at]

    odd = lax.rem(index, 2)

    @pl.when(odd == 0)
    def _():
        attend([own], True)

    @pl.when(odd == 1)
    def _():
        attend([place_ref[first], own], True)

    def pair(j, unused):
        at = first + odd + 2 * j
        attend([place_ref[at], place_ref[at + 1]], False)
        return unused

    lax.fori_loop(0, index // 2, pair, 0)

    live = lax.broadcasted_iota(jnp.int32, (span_len, head_dim), 0) < live_rows
    for g in range(kv_local):
        for h in range(per_head):
            head = g * per_head + h
            total = acc_ref[g, h * span_len:(h + 1) * span_len]
            out_ref[0, :, head * head_dim:(head + 1) * head_dim] = jnp.where(
                live, total[:, :head_dim] / total[:, head_dim:], 0.0
            ).astype(jnp.bfloat16)

    @pl.when(step == slot_count - 1)
    def _():
        cache_copies(lambda copy: copy.wait())


def gather_units(kv_new, inst_index, inst_size):
    up, down = [kv_new], [kv_new]
    for s in range(1, inst_size):
        up.append(lax.ppermute(up[-1], "inst", [(i, i + 1) for i in range(s - 1, inst_size - 1)]))
        down.append(lax.ppermute(down[-1], "inst", [(i + 1, i) for i in range(inst_size - s)]))
    units = [kv_new]
    for step, late in unit_steps(inst_size):
        far = inst_size - step
        if not late:
            unit = jnp.where(inst_index <= inst_size - 1 - step, down[step], up[step])
        else:
            middle = (inst_index >= step) & (inst_index <= inst_size - 1 - step)
            unit = jnp.where(
                middle, up[step], jnp.where(inst_index <= step - 1, down[far], up[far])
            )
        units.append(unit)
    return units


def body(queries, kv_new, prompt_spans, prompt_tail, span_plan, decode_owner):
    tp_size = lax.axis_size("tp")
    inst_size = lax.axis_size("inst")
    tp_index = lax.axis_index("tp")
    inst_index = lax.axis_index("inst")
    slot_count, span_len, row_width = queries.shape
    kv_heads, slice_len, width = kv_new.shape[1:]
    head_dim = width // 2
    local_heads = row_width // head_dim
    kv_local = max(1, kv_heads // tp_size)
    per_head = local_heads // kv_local
    span_total = slot_count * inst_size
    longest = span_total // 2
    units = gather_units(kv_new, inst_index, inst_size)
    parts = []
    for unit in units:
        for j in range(1, tp_size):
            head = (tp_index ^ j) * local_heads // (HEADS // KVH)
            sent = lax.dynamic_slice_in_dim(unit, head, kv_local, 1)
            parts.append(lax.ppermute(sent, "tp", [(t, t ^ j) for t in range(tp_size)]))
    kernel = functools.partial(
        attend_kernel,
        inst_size=inst_size,
        tp_size=tp_size,
        kv_local=kv_local,
        per_head=per_head,
        head_dim=head_dim,
        span_len=span_len,
        slot_count=slot_count,
        longest=longest,
    )
    work = slot_count * span_total // 4 * local_heads * span_len * span_len
    anywhere = pl.BlockSpec(memory_space=pl.ANY)
    by_slot = pl.BlockSpec((1, span_len, row_width), lambda i, *_: (i, 0, 0))
    rows = per_head * span_len
    return pl.pallas_call(
        kernel,
        grid_spec=pltpu.PrefetchScalarGridSpec(
            num_scalar_prefetch=5,
            grid=(slot_count,),
            in_specs=[by_slot] + [anywhere] * (len(units) + len(parts)),
            out_specs=[by_slot, anywhere],
            scratch_shapes=[
                pltpu.SMEM((span_total,), jnp.int32),
                pltpu.VMEM((span_total, kv_local, span_len, width), jnp.bfloat16),
                pltpu.VMEM((kv_local, rows, 2 * span_len), jnp.float32),
                pltpu.VMEM((kv_local, rows, 2 * span_len), jnp.bfloat16),
                pltpu.VMEM((kv_local, rows, 2 * head_dim), jnp.float32),
                pltpu.VMEM((kv_local, rows, head_dim), jnp.float32),
                pltpu.VMEM((kv_heads, slice_len, width), jnp.bfloat16),
                pltpu.SemaphoreType.DMA((longest,)),
                pltpu.SemaphoreType.DMA((inst_size, tp_size)),
            ],
        ),
        out_shape=[
            jax.ShapeDtypeStruct(queries.shape, jnp.bfloat16),
            jax.ShapeDtypeStruct((longest, kv_heads, slice_len, width), jnp.bfloat16),
        ],
        cost_estimate=pl.CostEstimate(
            flops=4 * work * head_dim, bytes_accessed=8 << 20, transcendentals=work
        ),
        compiler_params=pltpu.CompilerParams(vmem_limit_bytes=40 << 20),
    )(
        prompt_spans, prompt_tail, span_plan, decode_owner,
        jnp.stack([inst_index, tp_index]).astype(jnp.int32),
        queries, *units, *parts,
    )


def solution(mesh):
    placed = (
        P(("groups", "inst"), None, "tp"),
        P(("groups", "inst"), None, "tp", None),
        P("groups"),
        P("groups"),
        P("groups"),
        P("groups"),
    )
    return jax.shard_map(
        body,
        mesh=mesh,
        in_specs=placed,
        out_specs=(P(("groups", "inst"), None, "tp"), P(("groups", "inst"), None, "tp", None)),
        check_vma=False,
    )
```

time: 132 us -> 77.1 us (0.58)
  waiting for transfers between devices: 74.4 us -> 35.8 us
  Pallas kernels: 34.5 us -> 12.9 us
  starting transfers between devices: 4.29 us -> 25.1 us
  between operations: 14.1 us -> 0.89 us
  local copies, waits for them, and re-layouts: 4.73 us -> 1.93 us
    all_gather x1 -> x0, waiting for transfers between devices: 48.8 us -> none  [body(): pages = lax.all_gather(kv_new, 'inst', axis=0, tiled=True)]
    ppermute x0 -> x18, waiting for transfers between devices: none -> 35.8 us  [the longest x3 18.6 us: gather_units(): lax.ppermute(down[-1], 'inst', [(i + 1, i) for i in range(inst_size - s)])]
    ppermute x0 -> x18, starting transfers between devices: none -> 25.1 us  [the longest x12 16.7 us: body(): parts.append(lax.ppermute(sent, 'tp', [(t, t ^ j) for t in range(tp_size)]))]
    all_to_all x1 -> x0, waiting for transfers between devices: 24.8 us -> none  [body(): lax.all_to_all(sent, 'tp', split_axis=1, concat_axis=2, tiled=True)]
    pallas_call x1, Pallas kernels: 34.5 us -> 12.9 us  [body(): pl.pallas_call(kernel, grid_spec=pltpu.PrefetchScalarGridSpec(num_scalar_...]
    all_to_all x1 -> x0, starting transfers between devices: 4.25 us -> none  [body(): lax.all_to_all(sent, 'tp', split_axis=1, concat_axis=2, tiled=True)]
    all_gather x1 -> x0, local copies, waits for them, and re-layouts: 3.15 us -> none  [body(): pages = lax.all_gather(kv_new, 'inst', axis=0, tiled=True)]
    dynamic_slice x0 -> x4, local copies, waits for them, and re-layouts: none -> 1.91 us  [body(): sent = lax.dynamic_slice_in_dim(unit, head, kv_local, 1)]
  transfers between devices with their start and end apart: 2 -> 18, of which waited for: 2 -> 8; matrix products, arithmetic and copies ran while one was open for 0% -> 3% of each run, Pallas kernels for 0% -> 0%
where the time goes in v2:
time: 77.1 us; the launch traced here: 76.9 us
  waiting for transfers between devices  35.8 us (46%)
  starting transfers between devices  25.1 us (33%)
  Pallas kernels  12.9 us (17%)
  local copies, waits for them, and re-layouts  1.93 us (3%)
  between operations  0.89 us (1%)
    ppermute x3, waiting for transfers between devices, gather_units(): lax.ppermute(down[-1], 'inst', [(i + 1, i) for i in range(inst_size - s)])  18.6 us
    ppermute x12, starting transfers between devices, body(): parts.append(lax.ppermute(sent, 'tp', [(t, t ^ j) for t in range(tp_size)]))  16.7 us
    pallas_call x1, Pallas kernels, body(): pl.pallas_call(kernel, grid_spec=pltpu.PrefetchScalarGridSpec(num_scalar_...  12.9 us
    ppermute x3, waiting for transfers between devices, gather_units(): lax.ppermute(up[-1], 'inst', [(i, i + 1) for i in range(s - 1, inst_size...  9.56 us
    ppermute x12, waiting for transfers between devices, body(): parts.append(lax.ppermute(sent, 'tp', [(t, t ^ j) for t in range(tp_size)]))  7.72 us
    ppermute x3, starting transfers between devices, gather_units(): lax.ppermute(up[-1], 'inst', [(i, i + 1) for i in range(s - 1, inst_size...  4.61 us
    ppermute x3, starting transfers between devices, gather_units(): lax.ppermute(down[-1], 'inst', [(i + 1, i) for i in range(inst_size - s)])  3.85 us
    dynamic_slice x4, local copies, waits for them, and re-layouts, body(): sent = lax.dynamic_slice_in_dim(unit, head, kv_local, 1)  1.91 us
  transfers between devices with their start and end apart: 18, of which 8 were waited for; matrix products, arithmetic and copies ran while one was open for 3% of the time, Pallas kernels for 0%

profile of v2, /device:TPU:5, one launch (start us, length us, event | category | flops | bytes accessed | tf_op | source)
XLA Modules:
  0.0 76.9 jit_solution(13335983740957049877)
XLA Ops:
  0.6 3.2 %collective-permute-start.1 = (bf16[4,8,32,256]{3,2,1,0:T(8,128)(2,1)}, bf16[4,8,32,256]{3,2,1,0:T(8,128)(2,1)S(1)}, u32[]{:S(2)}, u32[]{:S(2)}) collective-permute-start(bf16[4,8,32,256]{3,2,1,0:T(8,128)(2,1)} %refs_1_.1), channel_id=1, source_target_pairs={{0,4},{4,8},{8,12},{1,5},{5,9},{9,13},{2,6},{6,10},{10,14},{3,7},{... | collective-permute-start | bytes 1572872 | tf_op jit(solution)/shard_map/ppermute | solution.py:220
  3.9 1.3 %collective-permute-start = (bf16[4,8,32,256]{3,2,1,0:T(8,128)(2,1)}, bf16[4,8,32,256]{3,2,1,0:T(8,128)(2,1)S(1)}, u32[]{:S(2)}, u32[]{:S(2)}) collective-permute-start(bf16[4,8,32,256]{3,2,1,0:T(8,128)(2,1)} %refs_1_.1), channel_id=1, source_target_pairs={{4,0},{8,4},{12,8},{5,1},{9,5},{13,9},{6,2},{10,6},{14,10},{7,3},{... | collective-permute-start | bytes 1572872 | tf_op jit(solution)/shard_map/ppermute | solution.py:221
  5.2 9.6 %collective-permute-done.1 = bf16[4,8,32,256]{3,2,1,0:T(8,128)(2,1)S(1)} collective-permute-done((bf16[4,8,32,256]{3,2,1,0:T(8,128)(2,1)}, bf16[4,8,32,256]{3,2,1,0:T(8,128)(2,1)S(1)}, u32[]{:S(2)}, u32[]{:S(2)}) %collective-permute-start.1) | collective-permute-done | bytes 524320 | tf_op jit(solution)/shard_map/ppermute | solution.py:220
  14.7 0.7 collective-permute-start.3
  15.4 3.0 %collective-permute-done = bf16[4,8,32,256]{3,2,1,0:T(8,128)(2,1)S(1)} collective-permute-done((bf16[4,8,32,256]{3,2,1,0:T(8,128)(2,1)}, bf16[4,8,32,256]{3,2,1,0:T(8,128)(2,1)S(1)}, u32[]{:S(2)}, u32[]{:S(2)}) %collective-permute-start) | collective-permute-done | bytes 524320 | tf_op jit(solution)/shard_map/ppermute | solution.py:221
  18.5 1.3 %collective-permute-start.2 = (bf16[4,8,32,256]{3,2,1,0:T(8,128)(2,1)S(1)}, bf16[4,8,32,256]{3,2,1,0:T(8,128)(2,1)S(1)}, u32[]{:S(2)}, u32[]{:S(2)}) collective-permute-start(bf16[4,8,32,256]{3,2,1,0:T(8,128)(2,1)S(1)} %collective-permute-done), channel_id=1, source_target_pairs={{4,0},{8,4},{5,1},{9,5},{6,2},{10,6},{7,3},{11,7},{20,16},{24,20},... | collective-permute-start | bytes 1572872 | tf_op jit(solution)/shard_map/ppermute | solution.py:221
  19.8 0.7 collective-permute-start.5
  20.5 11.8 %collective-permute-done.2 = bf16[4,8,32,256]{3,2,1,0:T(8,128)(2,1)S(1)} collective-permute-done((bf16[4,8,32,256]{3,2,1,0:T(8,128)(2,1)S(1)}, bf16[4,8,32,256]{3,2,1,0:T(8,128)(2,1)S(1)}, u32[]{:S(2)}, u32[]{:S(2)}) %collective-permute-start.2) | collective-permute-done | bytes 524320 | tf_op jit(solution)/shard_map/ppermute | solution.py:221
  32.2 1.3 %collective-permute-start.4 = (bf16[4,8,32,256]{3,2,1,0:T(8,128)(2,1)S(1)}, bf16[4,8,32,256]{3,2,1,0:T(8,128)(2,1)S(1)}, u32[]{:S(2)}, u32[]{:S(2)}) collective-permute-start(bf16[4,8,32,256]{3,2,1,0:T(8,128)(2,1)S(1)} %collective-permute-done.2), channel_id=1, source_target_pairs={{4,0},{5,1},{6,2},{7,3},{20,16},{21,17},{22,18},{23,19}} | collective-permute-start | bytes 1572872 | tf_op jit(solution)/shard_map/ppermute | solution.py:221
  33.6 1.8 %constant_dynamic-slice_fusion.9 = (bf16[4,2,32,256]{3,2,1,0:T(8,128)(2,1)}, bf16[4,2,32,256]{3,2,1,0:T(8,128)(2,1)}, bf16[4,2,32,256]{3,2,1,0:T(8,128)(2,1)}) fusion(bf16[4,8,32,256]{3,2,1,0:T(8,128)(2,1)} %refs_1_.1, s32[]{:T(128)S(6)} %select_n.77, s32[]{:T(128)S(6)} %select_n.75, s32[]{:T(128)S(6)} %select_n.73), kind=kLoop, calls=%fused_computation.12 | loop fusion | bytes 786444 | tf_op jit(solution)/shard_map/dynamic_slice | solution.py:254
  35.4 3.7 %collective-permute-start.8 = (bf16[4,2,32,256]{3,2,1,0:T(8,128)(2,1)}, bf16[4,2,32,256]{3,2,1,0:T(8,128)(2,1)S(1)}, u32[]{:S(2)}, u32[]{:S(2)}) collective-permute-start(bf16[4,2,32,256]{3,2,1,0:T(8,128)(2,1)} %get-tuple-element.11), channel_id=1, source_target_pairs={{0,3},{1,2},{2,1},{3,0},{4,7},{5,6},{6,5},{7,4},{8,11},{9,10},{10,... | collective-permute-start | bytes 393224 | tf_op jit(solution)/shard_map/ppermute | solution.py:255
  39.7 1.5 %collective-permute-start.14 = (bf16[4,2,32,256]{3,2,1,0:T(8,128)(2,1)S(1)}, bf16[4,2,32,256]{3,2,1,0:T(8,128)(2,1)S(1)}, u32[]{:S(2)}, u32[]{:S(2)}) collective-permute-start(bf16[4,2,32,256]{3,2,1,0:T(8,128)(2,1)S(1)} %get-tuple-element.5), channel_id=1, source_target_pairs={{0,3},{1,2},{2,1},{3,0},{4,7},{5,6},{6,5},{7,4},{8,11},{9,10},{10,... | collective-permute-start | bytes 393224 | tf_op jit(solution)/shard_map/ppermute | solution.py:255
  41.2 3.7 %collective-permute-done.4 = bf16[4,8,32,256]{3,2,1,0:T(8,128)(2,1)S(1)} collective-permute-done((bf16[4,8,32,256]{3,2,1,0:T(8,128)(2,1)S(1)}, bf16[4,8,32,256]{3,2,1,0:T(8,128)(2,1)S(1)}, u32[]{:S(2)}, u32[]{:S(2)}) %collective-permute-start.4) | collective-permute-done | bytes 524320 | tf_op jit(solution)/shard_map/ppermute | solution.py:221
  44.9 1.3 %collective-permute-start.13 = (bf16[4,2,32,256]{3,2,1,0:T(8,128)(2,1)S(1)}, bf16[4,2,32,256]{3,2,1,0:T(8,128)(2,1)S(1)}, u32[]{:S(2)}, u32[]{:S(2)}) collective-permute-start(bf16[4,2,32,256]{3,2,1,0:T(8,128)(2,1)S(1)} %get-tuple-element.6), channel_id=1, source_target_pairs={{0,2},{1,3},{2,0},{3,1},{4,6},{5,7},{6,4},{7,5},{8,10},{9,11},{10,... | collective-permute-start | bytes 393224 | tf_op jit(solution)/shard_map/ppermute | solution.py:255
  46.4 3.9 %collective-permute-start.12 = (bf16[4,2,32,256]{3,2,1,0:T(8,128)(2,1)S(1)}, bf16[4,2,32,256]{3,2,1,0:T(8,128)(2,1)S(1)}, u32[]{:S(2)}, u32[]{:S(2)}) collective-permute-start(bf16[4,2,32,256]{3,2,1,0:T(8,128)(2,1)S(1)} %get-tuple-element.7), channel_id=1, source_target_pairs={{0,1},{1,0},{2,3},{3,2},{4,5},{5,4},{6,7},{7,6},{8,9},{9,8},{10,11... | collective-permute-start | bytes 393224 | tf_op jit(solution)/shard_map/ppermute | solution.py:255
  50.5 1.3 %collective-permute-start.16 = (bf16[4,2,32,256]{3,2,1,0:T(8,128)(2,1)S(1)}, bf16[4,2,32,256]{3,2,1,0:T(8,128)(2,1)S(1)}, u32[]{:S(2)}, u32[]{:S(2)}) collective-permute-start(bf16[4,2,32,256]{3,2,1,0:T(8,128)(2,1)S(1)} %get-tuple-element.3), channel_id=1, source_target_pairs={{0,2},{1,3},{2,0},{3,1},{4,6},{5,7},{6,4},{7,5},{8,10},{9,11},{10,... | collective-permute-start | bytes 393224 | tf_op jit(solution)/shard_map/ppermute | solution.py:255
  51.8 0.7 collective-permute-start.15
  52.5 3.2 %collective-permute-start.11 = (bf16[4,2,32,256]{3,2,1,0:T(8,128)(2,1)S(1)}, bf16[4,2,32,256]{3,2,1,0:T(8,128)(2,1)S(1)}, u32[]{:S(2)}, u32[]{:S(2)}) collective-permute-start(bf16[4,2,32,256]{3,2,1,0:T(8,128)(2,1)S(1)} %get-tuple-element.8), channel_id=1, source_target_pairs={{0,3},{1,2},{2,1},{3,0},{4,7},{5,6},{6,5},{7,4},{8,11},{9,10},{10,... | collective-permute-start | bytes 393224 | tf_op jit(solution)/shard_map/ppermute | solution.py:255
  55.7 0.3 collective-permute-done.17.refs_16_
  56.0 0.4 collective-permute-start.9
  56.5 1.8 %collective-permute-done.16.refs_15_ = bf16[4,2,32,256]{3,2,1,0:T(8,128)(2,1)S(1)} collective-permute-done((bf16[4,2,32,256]{3,2,1,0:T(8,128)(2,1)S(1)}, bf16[4,2,32,256]{3,2,1,0:T(8,128)(2,1)S(1)}, u32[]{:S(2)}, u32[]{:S(2)}) %collective-permute-start.16) | collective-permute-done | bytes 131104 | tf_op jit(solution)/shard_map/ppermute | solution.py:255
  58.3 3.3 %collective-permute-done.11.refs_10_ = bf16[4,2,32,256]{3,2,1,0:T(8,128)(2,1)S(1)} collective-permute-done((bf16[4,2,32,256]{3,2,1,0:T(8,128)(2,1)S(1)}, bf16[4,2,32,256]{3,2,1,0:T(8,128)(2,1)S(1)}, u32[]{:S(2)}, u32[]{:S(2)}) %collective-permute-start.11) | collective-permute-done | bytes 131104 | tf_op jit(solution)/shard_map/ppermute | solution.py:255
  61.6 2.3 %collective-permute-done.10.refs_9_ = bf16[4,2,32,256]{3,2,1,0:T(8,128)(2,1)S(1)} collective-permute-done((bf16[4,2,32,256]{3,2,1,0:T(8,128)(2,1)S(1)}, bf16[4,2,32,256]{3,2,1,0:T(8,128)(2,1)S(1)}, u32[]{:S(2)}, u32[]{:S(2)}) %collective-permute-start.10) | collective-permute-done | bytes 131104 | tf_op jit(solution)/shard_map/ppermute | solution.py:255
  64.0 12.9 %shard_map.77 = (bf16[4,128,2048]{2,1,0:T(8,128)(2,1)}, bf16[8,8,32,256]{3,2,1,0:T(8,128)(2,1)}) custom-call(s32[4]{0:T(128)S(1)} %copy-done.2, s32[4]{0:T(128)S(1)} %copy-done.3, s32[16]{0:T(128)S(1)} %copy-done.4, s32[4]{0:T(128)S(1)} %copy-done.5, s32[2]{0:T(128)S(1)} %pad_add_fusion.where_ref, bf16[4,128,2048]{2,1,0:T(8,128)(2,1)S(1)} %copy-done.1, ...), custom_call_target="tpu_custom_call" | custom-call | flops 2147483648 | bytes 8388608 | tf_op jit(solution)/shard_map/pallas_call | solution.py:271
  (32 shorter events, 1.0 us)
Async XLA Ops:
  0.6 14.1 %collective-permute-start.1 = (bf16[4,8,32,256]{3,2,1,0:T(8,128)(2,1)}, bf16[4,8,32,256]{3,2,1,0:T(8,128)(2,1)S(1)}, u32[]{:S(2)}, u32[]{:S(2)}) collective-permute-start(bf16[4,8,32,256]{3,2,1,0:T(8,128)(2,1)} %refs_1_.1), channel_id=1, source_target_pairs={{0,4},{4,8},{8,12},{1,5},{5,9},{9,13},{2,6},{6,10},{10,14},{3,7},{... | collective-permute-start | bytes 1572872 | tf_op jit(solution)/shard_map/ppermute | solution.py:220
  3.9 14.6 %collective-permute-start = (bf16[4,8,32,256]{3,2,1,0:T(8,128)(2,1)}, bf16[4,8,32,256]{3,2,1,0:T(8,128)(2,1)S(1)}, u32[]{:S(2)}, u32[]{:S(2)}) collective-permute-start(bf16[4,8,32,256]{3,2,1,0:T(8,128)(2,1)} %refs_1_.1), channel_id=1, source_target_pairs={{4,0},{8,4},{12,8},{5,1},{9,5},{13,9},{6,2},{10,6},{14,10},{7,3},{... | collective-permute-start | bytes 1572872 | tf_op jit(solution)/shard_map/ppermute | solution.py:221
  14.7 5.0 %collective-permute-start.3 = (bf16[4,8,32,256]{3,2,1,0:T(8,128)(2,1)S(1)}, bf16[4,8,32,256]{3,2,1,0:T(8,128)(2,1)S(1)}, u32[]{:S(2)}, u32[]{:S(2)}) collective-permute-start(bf16[4,8,32,256]{3,2,1,0:T(8,128)(2,1)S(1)} %collective-permute-done.1), channel_id=1, source_target_pairs={{4,8},{8,12},{5,9},{9,13},{6,10},{10,14},{7,11},{11,15},{20,24},{2... | collective-permute-start | bytes 1572872 | tf_op jit(solution)/shard_map/ppermute | solution.py:220
  18.5 13.8 %collective-permute-start.2 = (bf16[4,8,32,256]{3,2,1,0:T(8,128)(2,1)S(1)}, bf16[4,8,32,256]{3,2,1,0:T(8,128)(2,1)S(1)}, u32[]{:S(2)}, u32[]{:S(2)}) collective-permute-start(bf16[4,8,32,256]{3,2,1,0:T(8,128)(2,1)S(1)} %collective-permute-done), channel_id=1, source_target_pairs={{4,0},{8,4},{5,1},{9,5},{6,2},{10,6},{7,3},{11,7},{20,16},{24,20},... | collective-permute-start | bytes 1572872 | tf_op jit(solution)/shard_map/ppermute | solution.py:221
  19.8 19.9 %collective-permute-start.5 = (bf16[4,8,32,256]{3,2,1,0:T(8,128)(2,1)S(1)}, bf16[4,8,32,256]{3,2,1,0:T(8,128)(2,1)S(1)}, u32[]{:S(2)}, u32[]{:S(2)}) collective-permute-start(bf16[4,8,32,256]{3,2,1,0:T(8,128)(2,1)S(1)} %collective-permute-done.3), channel_id=1, source_target_pairs={{8,12},{9,13},{10,14},{11,15},{24,28},{25,29},{26,30},{27,31}} | collective-permute-start | bytes 1572872 | tf_op jit(solution)/shard_map/ppermute | solution.py:220
  32.2 12.7 %collective-permute-start.4 = (bf16[4,8,32,256]{3,2,1,0:T(8,128)(2,1)S(1)}, bf16[4,8,32,256]{3,2,1,0:T(8,128)(2,1)S(1)}, u32[]{:S(2)}, u32[]{:S(2)}) collective-permute-start(bf16[4,8,32,256]{3,2,1,0:T(8,128)(2,1)S(1)} %collective-permute-done.2), channel_id=1, source_target_pairs={{4,0},{5,1},{6,2},{7,3},{20,16},{21,17},{22,18},{23,19}} | collective-permute-start | bytes 1572872 | tf_op jit(solution)/shard_map/ppermute | solution.py:221
  35.4 11.0 %collective-permute-start.8 = (bf16[4,2,32,256]{3,2,1,0:T(8,128)(2,1)}, bf16[4,2,32,256]{3,2,1,0:T(8,128)(2,1)S(1)}, u32[]{:S(2)}, u32[]{:S(2)}) collective-permute-start(bf16[4,2,32,256]{3,2,1,0:T(8,128)(2,1)} %get-tuple-element.11), channel_id=1, source_target_pairs={{0,3},{1,2},{2,1},{3,0},{4,7},{5,6},{6,5},{7,4},{8,11},{9,10},{10,... | collective-permute-start | bytes 393224 | tf_op jit(solution)/shard_map/ppermute | solution.py:255
  39.1 11.1 %collective-permute-start.7 = (bf16[4,2,32,256]{3,2,1,0:T(8,128)(2,1)}, bf16[4,2,32,256]{3,2,1,0:T(8,128)(2,1)S(1)}, u32[]{:S(2)}, u32[]{:S(2)}) collective-permute-start(bf16[4,2,32,256]{3,2,1,0:T(8,128)(2,1)} %get-tuple-element.12), channel_id=1, source_target_pairs={{0,2},{1,3},{2,0},{3,1},{4,6},{5,7},{6,4},{7,5},{8,10},{9,11},{10,... | collective-permute-start | bytes 393224 | tf_op jit(solution)/shard_map/ppermute | solution.py:255
  39.4 11.2 %collective-permute-start.6 = (bf16[4,2,32,256]{3,2,1,0:T(8,128)(2,1)}, bf16[4,2,32,256]{3,2,1,0:T(8,128)(2,1)S(1)}, u32[]{:S(2)}, u32[]{:S(2)}) collective-permute-start(bf16[4,2,32,256]{3,2,1,0:T(8,128)(2,1)} %get-tuple-element.13), channel_id=1, source_target_pairs={{0,1},{1,0},{2,3},{3,2},{4,5},{5,4},{6,7},{7,6},{8,9},{9,8},{10,11... | collective-permute-start | bytes 393224 | tf_op jit(solution)/shard_map/ppermute | solution.py:255
  39.7 12.2 %collective-permute-start.14 = (bf16[4,2,32,256]{3,2,1,0:T(8,128)(2,1)S(1)}, bf16[4,2,32,256]{3,2,1,0:T(8,128)(2,1)S(1)}, u32[]{:S(2)}, u32[]{:S(2)}) collective-permute-start(bf16[4,2,32,256]{3,2,1,0:T(8,128)(2,1)S(1)} %get-tuple-element.5), channel_id=1, source_target_pairs={{0,3},{1,2},{2,1},{3,0},{4,7},{5,6},{6,5},{7,4},{8,11},{9,10},{10,... | collective-permute-start | bytes 393224 | tf_op jit(solution)/shard_map/ppermute | solution.py:255
  44.9 19.1 %copy-start = (bf16[4,8,32,256]{3,2,1,0:T(8,128)(2,1)S(1)}, bf16[4,8,32,256]{3,2,1,0:T(8,128)(2,1)}, u32[]{:S(2)}) copy-start(bf16[4,8,32,256]{3,2,1,0:T(8,128)(2,1)} %refs_1_.1) | copy-start | bytes 1572868
  44.9 19.1 %copy-start.1 = (bf16[4,128,2048]{2,1,0:T(8,128)(2,1)S(1)}, bf16[4,128,2048]{2,1,0:T(8,128)(2,1)}, u32[]{:S(2)}) copy-start(bf16[4,128,2048]{2,1,0:T(8,128)(2,1)} %refs_0_.1) | copy-start | bytes 6291460
  44.9 19.1 %copy-start.2 = (s32[4]{0:T(128)S(1)}, s32[4]{0:T(128)}, u32[]{:S(2)}) copy-start(s32[4]{0:T(128)} %spans_ref.1) | copy-start | bytes 52
  44.9 19.1 %copy-start.3 = (s32[4]{0:T(128)S(1)}, s32[4]{0:T(128)}, u32[]{:S(2)}) copy-start(s32[4]{0:T(128)} %tail_ref.1) | copy-start | bytes 52
  44.9 19.1 %copy-start.4 = (s32[16]{0:T(128)S(1)}, s32[16]{0:T(128)}, u32[]{:S(2)}) copy-start(s32[16]{0:T(128)} %plan_ref.1) | copy-start | bytes 196
  44.9 19.1 %copy-start.5 = (s32[4]{0:T(128)S(1)}, s32[4]{0:T(128)}, u32[]{:S(2)}) copy-start(s32[4]{0:T(128)} %owner_ref.1) | copy-start | bytes 52
  44.9 7.6 %collective-permute-start.13 = (bf16[4,2,32,256]{3,2,1,0:T(8,128)(2,1)S(1)}, bf16[4,2,32,256]{3,2,1,0:T(8,128)(2,1)S(1)}, u32[]{:S(2)}, u32[]{:S(2)}) collective-permute-start(bf16[4,2,32,256]{3,2,1,0:T(8,128)(2,1)S(1)} %get-tuple-element.6), channel_id=1, source_target_pairs={{0,2},{1,3},{2,0},{3,1},{4,6},{5,7},{6,4},{7,5},{8,10},{9,11},{10,... | collective-permute-start | bytes 393224 | tf_op jit(solution)/shard_map/ppermute | solution.py:255
  46.4 9.4 %collective-permute-start.12 = (bf16[4,2,32,256]{3,2,1,0:T(8,128)(2,1)S(1)}, bf16[4,2,32,256]{3,2,1,0:T(8,128)(2,1)S(1)}, u32[]{:S(2)}, u32[]{:S(2)}) collective-permute-start(bf16[4,2,32,256]{3,2,1,0:T(8,128)(2,1)S(1)} %get-tuple-element.7), channel_id=1, source_target_pairs={{0,1},{1,0},{2,3},{3,2},{4,5},{5,4},{6,7},{7,6},{8,9},{9,8},{10,11... | collective-permute-start | bytes 393224 | tf_op jit(solution)/shard_map/ppermute | solution.py:255
  50.3 5.8 %collective-permute-start.17 = (bf16[4,2,32,256]{3,2,1,0:T(8,128)(2,1)S(1)}, bf16[4,2,32,256]{3,2,1,0:T(8,128)(2,1)S(1)}, u32[]{:S(2)}, u32[]{:S(2)}) collective-permute-start(bf16[4,2,32,256]{3,2,1,0:T(8,128)(2,1)S(1)} %get-tuple-element.2), channel_id=1, source_target_pairs={{0,3},{1,2},{2,1},{3,0},{4,7},{5,6},{6,5},{7,4},{8,11},{9,10},{10,... | collective-permute-start | bytes 393224 | tf_op jit(solution)/shard_map/ppermute | solution.py:255
  50.5 7.8 %collective-permute-start.16 = (bf16[4,2,32,256]{3,2,1,0:T(8,128)(2,1)S(1)}, bf16[4,2,32,256]{3,2,1,0:T(8,128)(2,1)S(1)}, u32[]{:S(2)}, u32[]{:S(2)}) collective-permute-start(bf16[4,2,32,256]{3,2,1,0:T(8,128)(2,1)S(1)} %get-tuple-element.3), channel_id=1, source_target_pairs={{0,2},{1,3},{2,0},{3,1},{4,6},{5,7},{6,4},{7,5},{8,10},{9,11},{10,... | collective-permute-start | bytes 393224 | tf_op jit(solution)/shard_map/ppermute | solution.py:255
  51.8 6.5 %collective-permute-start.15 = (bf16[4,2,32,256]{3,2,1,0:T(8,128)(2,1)S(1)}, bf16[4,2,32,256]{3,2,1,0:T(8,128)(2,1)S(1)}, u32[]{:S(2)}, u32[]{:S(2)}) collective-permute-start(bf16[4,2,32,256]{3,2,1,0:T(8,128)(2,1)S(1)} %get-tuple-element.4), channel_id=1, source_target_pairs={{0,1},{1,0},{2,3},{3,2},{4,5},{5,4},{6,7},{7,6},{8,9},{9,8},{10,11... | collective-permute-start | bytes 393224 | tf_op jit(solution)/shard_map/ppermute | solution.py:255
  52.5 9.1 %collective-permute-start.11 = (bf16[4,2,32,256]{3,2,1,0:T(8,128)(2,1)S(1)}, bf16[4,2,32,256]{3,2,1,0:T(8,128)(2,1)S(1)}, u32[]{:S(2)}, u32[]{:S(2)}) collective-permute-start(bf16[4,2,32,256]{3,2,1,0:T(8,128)(2,1)S(1)} %get-tuple-element.8), channel_id=1, source_target_pairs={{0,3},{1,2},{2,1},{3,0},{4,7},{5,6},{6,5},{7,4},{8,11},{9,10},{10,... | collective-permute-start | bytes 393224 | tf_op jit(solution)/shard_map/ppermute | solution.py:255
  55.7 8.2 %collective-permute-start.10 = (bf16[4,2,32,256]{3,2,1,0:T(8,128)(2,1)S(1)}, bf16[4,2,32,256]{3,2,1,0:T(8,128)(2,1)S(1)}, u32[]{:S(2)}, u32[]{:S(2)}) collective-permute-start(bf16[4,2,32,256]{3,2,1,0:T(8,128)(2,1)S(1)} %get-tuple-element.9), channel_id=1, source_target_pairs={{0,2},{1,3},{2,0},{3,1},{4,6},{5,7},{6,4},{7,5},{8,10},{9,11},{10,... | collective-permute-start | bytes 393224 | tf_op jit(solution)/shard_map/ppermute | solution.py:255
  56.0 7.9 %collective-permute-start.9 = (bf16[4,2,32,256]{3,2,1,0:T(8,128)(2,1)S(1)}, bf16[4,2,32,256]{3,2,1,0:T(8,128)(2,1)S(1)}, u32[]{:S(2)}, u32[]{:S(2)}) collective-permute-start(bf16[4,2,32,256]{3,2,1,0:T(8,128)(2,1)S(1)} %get-tuple-element.10), channel_id=1, source_target_pairs={{0,1},{1,0},{2,3},{3,2},{4,5},{5,4},{6,7},{7,6},{8,9},{9,8},{10,11... | collective-permute-start | bytes 393224 | tf_op jit(solution)/shard_map/ppermute | solution.py:255

commit v3 on v2

--- a/solution.py
+++ b/solution.py
@@ -13,55 +13,35 @@
 LOG2E = 1.4426950408889634
 
 
-def source_of(unit, inst, inst_size):
-    if unit == 0:
-        return inst
-    step, late = unit_steps(inst_size)[unit - 1]
-    if not late:
-        return jnp.where(inst <= inst_size - 1 - step, inst + step, inst - step)
-    far = inst_size - step
-    middle = (inst >= step) & (inst <= inst_size - 1 - step)
-    return jnp.where(middle, inst - step, jnp.where(inst <= step - 1, inst + far, inst - far))
-
-
-def unit_steps(inst_size):
-    near = [(s, False) for s in range(1, inst_size // 2 + 1)]
-    late = [(s, True) for s in range((inst_size - 1) // 2, 0, -1)]
-    return near + late
-
-
 def attend_kernel(
-    spans_ref, tail_ref, plan_ref, owner_ref, where_ref, *refs,
-    inst_size, tp_size, kv_local, per_head, head_dim, span_len, slot_count, longest,
+    spans_ref, tail_ref, plan_ref, owner_ref, place_at_ref, *refs,
+    hops, parts, inst_size, tp_size, kv_local, per_head, head_dim, span_len, slot_count, longest,
 ):
     q_ref = refs[0]
-    unit_refs = refs[1:1 + inst_size]
-    part_refs = refs[1 + inst_size:1 + inst_size + inst_size * (tp_size - 1)]
+    hop_refs = refs[1:1 + len(hops)]
+    part_refs = refs[1 + len(hops):1 + len(hops) + len(parts)]
     (out_ref, cache_ref, place_ref, kv_ref, s_ref, p_ref, acc_ref, max_ref, zero_ref,
-     page_sems, part_sems) = refs[1 + inst_size + inst_size * (tp_size - 1):]
+     page_sems, part_sems) = refs[1 + len(hops) + len(parts):]
     step = pl.program_id(0)
-    inst = where_ref[0]
-    tp = where_ref[1]
+    inst = place_at_ref[0]
+    tp = place_at_ref[1]
     prompt_count = spans_ref.shape[0]
     span_total = slot_count * inst_size
     slice_len = span_len // tp_size
     rows = per_head * span_len
     scale = LOG2E / math.sqrt(head_dim)
-    sources = [source_of(u, inst, inst_size) for u in range(inst_size)]
-    first_head = tp * (kv_local * per_head) // (HEADS // KVH)
 
     def part_copies(act):
-        for u in range(inst_size):
-            slots = pl.ds(sources[u] * slot_count, slot_count)
-            for j in range(tp_size):
-                if j == 0:
-                    src = unit_refs[u].at[:, pl.ds(first_head, kv_local)]
-                else:
-                    src = part_refs[u * (tp_size - 1) + j - 1]
-                at = pl.multiple_of((tp ^ j) * slice_len, slice_len)
+        for n, (pieces, j) in enumerate(parts):
+            at = pl.ds(pl.multiple_of((tp ^ j) * slice_len, slice_len), slice_len)
+            begin = 0
+            for m, (hop, first_slot, size) in enumerate(pieces):
+                slots = pl.ds(place_at_ref[2 + hop] * slot_count + first_slot, size)
                 act(pltpu.make_async_copy(
-                    src, kv_ref.at[slots, :, pl.ds(at, slice_len)], part_sems.at[u, j]
+                    part_refs[n].at[begin:begin + size], kv_ref.at[slots, :, at],
+                    part_sems.at[n, m],
                 ))
+                begin += size
 
     def cache_copies(act):
         first = jnp.int32(0)
@@ -75,13 +55,15 @@
 
         def row(r, unused):
             page = place_ref[jnp.minimum(first + r, span_total - 1)]
-            source = page // slot_count
-            slot = page - source * slot_count
-            for u in range(inst_size):
-                @pl.when((r < count) & (source == sources[u]))
+            for n, (hop, first_slot, size) in enumerate(hops):
+                source = place_at_ref[2 + hop]
+                slot = page - source * slot_count - first_slot
+                here = (source >= 0) & (slot >= 0) & (slot < size)
+
+                @pl.when((r < count) & here)
                 def _():
                     act(pltpu.make_async_copy(
-                        unit_refs[u].at[slot], cache_ref.at[r], page_sems.at[r]
+                        hop_refs[n].at[slot], cache_ref.at[r], page_sems.at[r]
                     ))
 
             @pl.when(r >= count)
@@ -214,23 +196,77 @@
         cache_copies(lambda copy: copy.wait())
 
 
-def gather_units(kv_new, inst_index, inst_size):
-    up, down = [kv_new], [kv_new]
-    for s in range(1, inst_size):
-        up.append(lax.ppermute(up[-1], "inst", [(i, i + 1) for i in range(s - 1, inst_size - 1)]))
-        down.append(lax.ppermute(down[-1], "inst", [(i + 1, i) for i in range(inst_size - s)]))
-    units = [kv_new]
-    for step, late in unit_steps(inst_size):
-        far = inst_size - step
-        if not late:
-            unit = jnp.where(inst_index <= inst_size - 1 - step, down[step], up[step])
-        else:
-            middle = (inst_index >= step) & (inst_index <= inst_size - 1 - step)
-            unit = jnp.where(
-                middle, up[step], jnp.where(inst_index <= step - 1, down[far], up[far])
-            )
-        units.append(unit)
-    return units
+def after(values, earlier):
+    return lax.optimization_barrier((list(values), list(earlier)))[0]
+
+
+def move_pages(kv_new, kv_local):
+    inst_size = lax.axis_size("inst")
+    tp_size = lax.axis_size("tp")
+    inst = lax.axis_index("inst")
+    tp = lax.axis_index("tp")
+    slot_count, kv_heads = kv_new.shape[:2]
+    sources = [list(range(inst_size))]
+    hops = [((0, 0, slot_count), kv_new)]
+    parts = []
+
+    def along(x, pairs):
+        return lax.ppermute(x, "inst", pairs)
+
+    def exchange(*pieces):
+        names = [name for name, _ in pieces]
+        found = []
+        for j in range(tp_size):
+            head = ((tp ^ j) * kv_heads) // tp_size
+            sent = [lax.dynamic_slice_in_dim(x, head, kv_local, 1) for _, x in pieces]
+            sent = jnp.concatenate(sent, axis=0) if len(sent) > 1 else sent[0]
+            if j:
+                sent = lax.ppermute(sent, "tp", [(t, t ^ j) for t in range(tp_size)])
+            found.append(((names, j), sent))
+        parts.extend(found)
+        return [x for _, x in found]
+
+    if inst_size != 4 or slot_count % 2:
+        exchange(hops[0])
+        for s in range(1, inst_size):
+            sources.append([(i - s) % inst_size for i in range(inst_size)])
+            pairs = [(i, (i + s) % inst_size) for i in range(inst_size)]
+            hops.append(((s, 0, slot_count), along(kv_new, pairs)))
+            exchange(hops[-1])
+        return hops, parts, sources
+
+    half = slot_count // 2
+    sources += [[-1, 0, 1, 2], [1, 2, 3, -1], [-1, -1, 0, 1], [2, 3, -1, -1], [3, -1, -1, 0]]
+    far, first, last = 6, 7, 8
+    sources += [[2, 3, 0, 1], [1, 0, 3, 2], [3, 2, 1, 0]]
+    mine = [kv_new[:half], kv_new[half:]]
+    got = []
+    for n in range(2):
+        up2 = along(mine[n], [(0, 2), (1, 3)])
+        down2 = along(mine[n], [(2, 0), (3, 1)])
+        up1 = along(mine[n], [(0, 1), (1, 2), (2, 3)])
+        down1 = along(mine[n], [(1, 0), (2, 1), (3, 2)])
+        got.append((up1, down1, up2, down2))
+        for hop, x in enumerate(got[-1], 1):
+            hops.append(((hop, n * half, half), x))
+    waiting = exchange(hops[0])
+    lasts = []
+    for n in range(2):
+        up1, down1, up2, down2 = got[n]
+        at = n * half
+        two = after([jnp.where(inst < 2, down2, up2)], waiting)[0]
+        handed = along(two, [(2, 3), (1, 0)])
+        hops.append(((5, at, half), handed))
+        one = jnp.where((inst == 0) | (inst == 2), down1, up1)
+        waiting = exchange(((far, at, half), two), ((first, at, half), one))
+        lasts.append((up1, down1, handed))
+        if n == 0:
+            before = waiting
+    for n in range(2):
+        up1, down1, handed = after(lasts[n], before)
+        end = jnp.where(inst == 1, down1, jnp.where(inst == 2, up1, handed))
+        before = exchange(((last, n * half, half), end)) + waiting
+    return hops, parts, sources
 
 
 def body(queries, kv_new, prompt_spans, prompt_tail, span_plan, decode_owner):
@@ -246,15 +282,12 @@
     per_head = local_heads // kv_local
     span_total = slot_count * inst_size
     longest = span_total // 2
-    units = gather_units(kv_new, inst_index, inst_size)
-    parts = []
-    for unit in units:
-        for j in range(1, tp_size):
-            head = (tp_index ^ j) * local_heads // (HEADS // KVH)
-            sent = lax.dynamic_slice_in_dim(unit, head, kv_local, 1)
-            parts.append(lax.ppermute(sent, "tp", [(t, t ^ j) for t in range(tp_size)]))
+    hops, parts, sources = move_pages(kv_new, kv_local)
+    own_sources = lax.dynamic_index_in_dim(jnp.asarray(sources, jnp.int32), inst_index, 1, False)
     kernel = functools.partial(
         attend_kernel,
+        hops=[name for name, _ in hops],
+        parts=[name for name, _ in parts],
         inst_size=inst_size,
         tp_size=tp_size,
         kv_local=kv_local,
@@ -273,7 +306,7 @@
         grid_spec=pltpu.PrefetchScalarGridSpec(
             num_scalar_prefetch=5,
             grid=(slot_count,),
-            in_specs=[by_slot] + [anywhere] * (len(units) + len(parts)),
+            in_specs=[by_slot] + [anywhere] * (len(hops) + len(parts)),
             out_specs=[by_slot, anywhere],
             scratch_shapes=[
                 pltpu.SMEM((span_total,), jnp.int32),
@@ -284,7 +317,7 @@
                 pltpu.VMEM((kv_local, rows, head_dim), jnp.float32),
                 pltpu.VMEM((kv_heads, slice_len, width), jnp.bfloat16),
                 pltpu.SemaphoreType.DMA((longest,)),
-                pltpu.SemaphoreType.DMA((inst_size, tp_size)),
+                pltpu.SemaphoreType.DMA((len(parts), max(len(x[0][0]) for x in parts))),
             ],
         ),
         out_shape=[
@@ -297,8 +330,8 @@
         compiler_params=pltpu.CompilerParams(vmem_limit_bytes=40 << 20),
     )(
         prompt_spans, prompt_tail, span_plan, decode_owner,
-        jnp.stack([inst_index, tp_index]).astype(jnp.int32),
-        queries, *units, *parts,
+        jnp.concatenate([jnp.stack([inst_index, tp_index]).astype(jnp.int32), own_sources]),
+        queries, *[x for _, x in hops], *[x for _, x in parts],
     )
 
 

time: 77.1 us -> 83.3 us (1.080)
  the two profiles are of different devices: /device:TPU:5 before, /device:TPU:21 now
where the time goes in v3:
time: 83.3 us; the launch traced here: 84 us
  starting transfers between devices  45 us (54%)
  waiting for transfers between devices  18.8 us (23%)
  Pallas kernels  15.5 us (19%)
  local copies, waits for them, and re-layouts  3.11 us (4%)
  between operations  1.11 us (1%)
    ppermute x10, starting transfers between devices, along(): return lax.ppermute(x, 'inst', pairs)  29 us
    ppermute x15, starting transfers between devices, exchange(): sent = lax.ppermute(sent, 'tp', [(t, t ^ j) for t in range(tp_size)])  16 us
    pallas_call x1, Pallas kernels, body(): pl.pallas_call(kernel, grid_spec=pltpu.PrefetchScalarGridSpec(num_scalar_...  15.5 us
    ppermute x10, waiting for transfers between devices, along(): return lax.ppermute(x, 'inst', pairs)  9.62 us
    ppermute x15, waiting for transfers between devices, exchange(): sent = lax.ppermute(sent, 'tp', [(t, t ^ j) for t in range(tp_size)])  9.21 us
  transfers between devices with their start and end apart: 25, of which 9 were waited for; matrix products, arithmetic and copies ran while one was open for 3% of the time, Pallas kernels for 0%

profile of v3, /device:TPU:21, one launch (start us, length us, event | category | flops | bytes accessed | tf_op | source)
XLA Modules:
  0.0 84.0 jit_solution(14079016709752709812)
XLA Ops:
  1.7 2.0 %collective-permute-start.3 = (bf16[2,8,32,256]{3,2,1,0:T(8,128)(2,1)S(1)}, bf16[2,8,32,256]{3,2,1,0:T(8,128)(2,1)S(1)}, u32[]{:S(2)}, u32[]{:S(2)}) collective-permute-start(bf16[2,8,32,256]{3,2,1,0:T(8,128)(2,1)S(1)} %get-tuple-element.23), channel_id=1, source_target_pairs={{8,0},{12,4},{9,1},{13,5},{10,2},{14,6},{11,3},{15,7},{24,16},{28,... | collective-permute-start | bytes 786440 | tf_op jit(solution)/shard_map/ppermute | solution.py:214
  3.7 1.3 %collective-permute-start.2 = (bf16[2,8,32,256]{3,2,1,0:T(8,128)(2,1)S(1)}, bf16[2,8,32,256]{3,2,1,0:T(8,128)(2,1)S(1)}, u32[]{:S(2)}, u32[]{:S(2)}) collective-permute-start(bf16[2,8,32,256]{3,2,1,0:T(8,128)(2,1)S(1)} %get-tuple-element.23), channel_id=1, source_target_pairs={{0,8},{4,12},{1,9},{5,13},{2,10},{6,14},{3,11},{7,15},{16,24},{20,... | collective-permute-start | bytes 786440 | tf_op jit(solution)/shard_map/ppermute | solution.py:214
  5.0 5.0 %collective-permute-start.1 = (bf16[2,8,32,256]{3,2,1,0:T(8,128)(2,1)S(1)}, bf16[2,8,32,256]{3,2,1,0:T(8,128)(2,1)S(1)}, u32[]{:S(2)}, u32[]{:S(2)}) collective-permute-start(bf16[2,8,32,256]{3,2,1,0:T(8,128)(2,1)S(1)} %get-tuple-element.23), channel_id=1, source_target_pairs={{4,0},{8,4},{12,8},{5,1},{9,5},{13,9},{6,2},{10,6},{14,10},{7,3},{... | collective-permute-start | bytes 786440 | tf_op jit(solution)/shard_map/ppermute | solution.py:214
  10.0 1.9 %collective-permute-start = (bf16[2,8,32,256]{3,2,1,0:T(8,128)(2,1)S(1)}, bf16[2,8,32,256]{3,2,1,0:T(8,128)(2,1)S(1)}, u32[]{:S(2)}, u32[]{:S(2)}) collective-permute-start(bf16[2,8,32,256]{3,2,1,0:T(8,128)(2,1)S(1)} %get-tuple-element.23), channel_id=1, source_target_pairs={{0,4},{4,8},{8,12},{1,5},{5,9},{9,13},{2,6},{6,10},{10,14},{3,7},{... | collective-permute-start | bytes 786440 | tf_op jit(solution)/shard_map/ppermute | solution.py:214
  13.2 2.7 %collective-permute-start.10 = (bf16[4,2,32,256]{3,2,1,0:T(8,128)(2,1)S(1)}, bf16[4,2,32,256]{3,2,1,0:T(8,128)(2,1)S(1)}, u32[]{:S(2)}, u32[]{:S(2)}) collective-permute-start(bf16[4,2,32,256]{3,2,1,0:T(8,128)(2,1)S(1)} %get-tuple-element.18), channel_id=1, source_target_pairs={{0,3},{1,2},{2,1},{3,0},{4,7},{5,6},{6,5},{7,4},{8,11},{9,10},{10,... | collective-permute-start | bytes 393224 | tf_op jit(solution)/shard_map/ppermute | solution.py:224
  16.8 1.6 %collective-permute-start.8 = (bf16[4,2,32,256]{3,2,1,0:T(8,128)(2,1)S(1)}, bf16[4,2,32,256]{3,2,1,0:T(8,128)(2,1)S(1)}, u32[]{:S(2)}, u32[]{:S(2)}) collective-permute-start(bf16[4,2,32,256]{3,2,1,0:T(8,128)(2,1)S(1)} %get-tuple-element.20), channel_id=1, source_target_pairs={{0,1},{1,0},{2,3},{3,2},{4,5},{5,4},{6,7},{7,6},{8,9},{9,8},{10,11... | collective-permute-start | bytes 393224 | tf_op jit(solution)/shard_map/ppermute | solution.py:224
  18.5 1.6 %collective-permute-done.10.refs_15_ = bf16[4,2,32,256]{3,2,1,0:T(8,128)(2,1)S(1)} collective-permute-done((bf16[4,2,32,256]{3,2,1,0:T(8,128)(2,1)S(1)}, bf16[4,2,32,256]{3,2,1,0:T(8,128)(2,1)S(1)}, u32[]{:S(2)}, u32[]{:S(2)}) %collective-permute-start.10) | collective-permute-done | bytes 131104 | tf_op jit(solution)/shard_map/ppermute | solution.py:224
  20.1 3.6 %collective-permute-start.7 = (bf16[2,8,32,256]{3,2,1,0:T(8,128)(2,1)S(1)}, bf16[2,8,32,256]{3,2,1,0:T(8,128)(2,1)S(1)}, u32[]{:S(2)}, u32[]{:S(2)}) collective-permute-start(bf16[2,8,32,256]{3,2,1,0:T(8,128)(2,1)S(1)} %get-tuple-element.22), channel_id=1, source_target_pairs={{8,0},{12,4},{9,1},{13,5},{10,2},{14,6},{11,3},{15,7},{24,16},{28,... | collective-permute-start | bytes 786440 | tf_op jit(solution)/shard_map/ppermute | solution.py:214
  23.8 1.3 %collective-permute-start.6 = (bf16[2,8,32,256]{3,2,1,0:T(8,128)(2,1)S(1)}, bf16[2,8,32,256]{3,2,1,0:T(8,128)(2,1)S(1)}, u32[]{:S(2)}, u32[]{:S(2)}) collective-permute-start(bf16[2,8,32,256]{3,2,1,0:T(8,128)(2,1)S(1)} %get-tuple-element.22), channel_id=1, source_target_pairs={{0,8},{4,12},{1,9},{5,13},{2,10},{6,14},{3,11},{7,15},{16,24},{20,... | collective-permute-start | bytes 786440 | tf_op jit(solution)/shard_map/ppermute | solution.py:214
  25.1 5.0 %collective-permute-start.5 = (bf16[2,8,32,256]{3,2,1,0:T(8,128)(2,1)S(1)}, bf16[2,8,32,256]{3,2,1,0:T(8,128)(2,1)S(1)}, u32[]{:S(2)}, u32[]{:S(2)}) collective-permute-start(bf16[2,8,32,256]{3,2,1,0:T(8,128)(2,1)S(1)} %get-tuple-element.22), channel_id=1, source_target_pairs={{4,0},{8,4},{12,8},{5,1},{9,5},{13,9},{6,2},{10,6},{14,10},{7,3},{... | collective-permute-start | bytes 786440 | tf_op jit(solution)/shard_map/ppermute | solution.py:214
  30.1 1.9 %collective-permute-start.4 = (bf16[2,8,32,256]{3,2,1,0:T(8,128)(2,1)S(1)}, bf16[2,8,32,256]{3,2,1,0:T(8,128)(2,1)S(1)}, u32[]{:S(2)}, u32[]{:S(2)}) collective-permute-start(bf16[2,8,32,256]{3,2,1,0:T(8,128)(2,1)S(1)} %get-tuple-element.22), channel_id=1, source_target_pairs={{0,4},{4,8},{8,12},{1,5},{5,9},{9,13},{2,6},{6,10},{10,14},{3,7},{... | collective-permute-start | bytes 786440 | tf_op jit(solution)/shard_map/ppermute | solution.py:214
  32.1 1.3 %collective-permute-start.11 = (bf16[2,8,32,256]{3,2,1,0:T(8,128)(2,1)S(1)}, bf16[2,8,32,256]{3,2,1,0:T(8,128)(2,1)S(1)}, u32[]{:S(2)}, u32[]{:S(2)}) collective-permute-start(bf16[2,8,32,256]{3,2,1,0:T(8,128)(2,1)S(1)} %broadcast_select_fusion.3), channel_id=1, source_target_pairs={{8,12},{4,0},{9,13},{5,1},{10,14},{6,2},{11,15},{7,3},{24,28},{20,... | collective-permute-start | bytes 786440 | tf_op jit(solution)/shard_map/ppermute | solution.py:214
  33.5 1.3 %collective-permute-done.7.refs_9_ = bf16[2,8,32,256]{3,2,1,0:T(8,128)(2,1)S(1)} collective-permute-done((bf16[2,8,32,256]{3,2,1,0:T(8,128)(2,1)S(1)}, bf16[2,8,32,256]{3,2,1,0:T(8,128)(2,1)S(1)}, u32[]{:S(2)}, u32[]{:S(2)}) %collective-permute-start.7) | collective-permute-done | bytes 262176 | tf_op jit(solution)/shard_map/ppermute | solution.py:214
  34.8 1.8 %collective-permute-start.12 = (bf16[4,2,32,256]{3,2,1,0:T(8,128)(2,1)S(1)}, bf16[4,2,32,256]{3,2,1,0:T(8,128)(2,1)S(1)}, u32[]{:S(2)}, u32[]{:S(2)}) collective-permute-start(bf16[4,2,32,256]{3,2,1,0:T(8,128)(2,1)S(1)} %pad_maximum_fusion.1), channel_id=1, source_target_pairs={{0,1},{1,0},{2,3},{3,2},{4,5},{5,4},{6,7},{7,6},{8,9},{9,8},{10,11... | collective-permute-start | bytes 393224 | tf_op jit(solution)/shard_map/ppermute | solution.py:224
  36.7 3.7 %collective-permute-done.5.refs_7_ = bf16[2,8,32,256]{3,2,1,0:T(8,128)(2,1)S(1)} collective-permute-done((bf16[2,8,32,256]{3,2,1,0:T(8,128)(2,1)S(1)}, bf16[2,8,32,256]{3,2,1,0:T(8,128)(2,1)S(1)}, u32[]{:S(2)}, u32[]{:S(2)}) %collective-permute-start.5) | collective-permute-done | bytes 262176 | tf_op jit(solution)/shard_map/ppermute | solution.py:214
  41.4 4.6 %collective-permute-done.4.refs_6_ = bf16[2,8,32,256]{3,2,1,0:T(8,128)(2,1)S(1)} collective-permute-done((bf16[2,8,32,256]{3,2,1,0:T(8,128)(2,1)S(1)}, bf16[2,8,32,256]{3,2,1,0:T(8,128)(2,1)S(1)}, u32[]{:S(2)}, u32[]{:S(2)}) %collective-permute-start.4) | collective-permute-done | bytes 262176 | tf_op jit(solution)/shard_map/ppermute | solution.py:214
  46.2 5.7 %collective-permute-start.15 = (bf16[2,8,32,256]{3,2,1,0:T(8,128)(2,1)S(1)}, bf16[2,8,32,256]{3,2,1,0:T(8,128)(2,1)S(1)}, u32[]{:S(2)}, u32[]{:S(2)}) collective-permute-start(bf16[2,8,32,256]{3,2,1,0:T(8,128)(2,1)S(1)} %broadcast_select_fusion.2), channel_id=1, source_target_pairs={{8,12},{4,0},{9,13},{5,1},{10,14},{6,2},{11,15},{7,3},{24,28},{20,... | collective-permute-start | bytes 786440 | tf_op jit(solution)/shard_map/ppermute | solution.py:214
  52.4 2.0 %collective-permute-start.18 = (bf16[4,2,32,256]{3,2,1,0:T(8,128)(2,1)S(1)}, bf16[4,2,32,256]{3,2,1,0:T(8,128)(2,1)S(1)}, u32[]{:S(2)}, u32[]{:S(2)}) collective-permute-start(bf16[4,2,32,256]{3,2,1,0:T(8,128)(2,1)S(1)} %pad_maximum_fusion.7), channel_id=1, source_target_pairs={{0,3},{1,2},{2,1},{3,0},{4,7},{5,6},{6,5},{7,4},{8,11},{9,10},{10,... | collective-permute-start | bytes 393224 | tf_op jit(solution)/shard_map/ppermute | solution.py:224
  56.8 2.3 %collective-permute-start.19 = (bf16[2,2,32,256]{3,2,1,0:T(8,128)(2,1)S(1)}, bf16[2,2,32,256]{3,2,1,0:T(8,128)(2,1)S(1)}, u32[]{:S(2)}, u32[]{:S(2)}) collective-permute-start(bf16[2,2,32,256]{3,2,1,0:T(8,128)(2,1)S(1)} %get-tuple-element.30), channel_id=1, source_target_pairs={{0,1},{1,0},{2,3},{3,2},{4,5},{5,4},{6,7},{7,6},{8,9},{9,8},{10,11... | collective-permute-start | bytes 196616 | tf_op jit(solution)/shard_map/ppermute | solution.py:224
  59.1 2.1 %collective-permute-done.18.refs_23_ = bf16[4,2,32,256]{3,2,1,0:T(8,128)(2,1)S(1)} collective-permute-done((bf16[4,2,32,256]{3,2,1,0:T(8,128)(2,1)S(1)}, bf16[4,2,32,256]{3,2,1,0:T(8,128)(2,1)S(1)}, u32[]{:S(2)}, u32[]{:S(2)}) %collective-permute-start.18) | collective-permute-done | bytes 131104 | tf_op jit(solution)/shard_map/ppermute | solution.py:224
  62.4 1.5 %collective-permute-start.24 = (bf16[2,2,32,256]{3,2,1,0:T(8,128)(2,1)S(1)}, bf16[2,2,32,256]{3,2,1,0:T(8,128)(2,1)S(1)}, u32[]{:S(2)}, u32[]{:S(2)}) collective-permute-start(bf16[2,2,32,256]{3,2,1,0:T(8,128)(2,1)S(1)} %get-tuple-element.24), channel_id=1, source_target_pairs={{0,3},{1,2},{2,1},{3,0},{4,7},{5,6},{6,5},{7,4},{8,11},{9,10},{10,... | collective-permute-start | bytes 196616 | tf_op jit(solution)/shard_map/ppermute | solution.py:224
  64.0 1.3 %collective-permute-start.23 = (bf16[2,2,32,256]{3,2,1,0:T(8,128)(2,1)S(1)}, bf16[2,2,32,256]{3,2,1,0:T(8,128)(2,1)S(1)}, u32[]{:S(2)}, u32[]{:S(2)}) collective-permute-start(bf16[2,2,32,256]{3,2,1,0:T(8,128)(2,1)S(1)} %get-tuple-element.25), channel_id=1, source_target_pairs={{0,2},{1,3},{2,0},{3,1},{4,6},{5,7},{6,4},{7,5},{8,10},{9,11},{10,... | collective-permute-start | bytes 196616 | tf_op jit(solution)/shard_map/ppermute | solution.py:224
  66.5 1.9 %collective-permute-done.23.refs_30_ = bf16[2,2,32,256]{3,2,1,0:T(8,128)(2,1)S(1)} collective-permute-done((bf16[2,2,32,256]{3,2,1,0:T(8,128)(2,1)S(1)}, bf16[2,2,32,256]{3,2,1,0:T(8,128)(2,1)S(1)}, u32[]{:S(2)}, u32[]{:S(2)}) %collective-permute-start.23) | collective-permute-done | bytes 65568 | tf_op jit(solution)/shard_map/ppermute | solution.py:224
  68.5 15.5 %shard_map.86 = (bf16[4,128,2048]{2,1,0:T(8,128)(2,1)}, bf16[8,8,32,256]{3,2,1,0:T(8,128)(2,1)}) custom-call(s32[4]{0:T(128)S(1)} %copy-done.2, s32[4]{0:T(128)S(1)} %copy-done.3, s32[16]{0:T(128)S(1)} %copy-done.4, s32[4]{0:T(128)S(1)} %copy-done.5, s32[11]{0:T(128)S(1)} %pad_add_fusion.place_at_ref, bf16[4,128,2048]{2,1,0:T(8,128)(2,1)S(1)} %copy-done.1, ...), custom_call_target="tpu_custom_call" | custom-call | flops 2147483648 | bytes 8388608 | tf_op jit(solution)/shard_map/pallas_call | solution.py:304
  (63 shorter events, 9.9 us)
Async XLA Ops:
  1.7 14.9 %collective-permute-start.3 = (bf16[2,8,32,256]{3,2,1,0:T(8,128)(2,1)S(1)}, bf16[2,8,32,256]{3,2,1,0:T(8,128)(2,1)S(1)}, u32[]{:S(2)}, u32[]{:S(2)}) collective-permute-start(bf16[2,8,32,256]{3,2,1,0:T(8,128)(2,1)S(1)} %get-tuple-element.23), channel_id=1, source_target_pairs={{8,0},{12,4},{9,1},{13,5},{10,2},{14,6},{11,3},{15,7},{24,16},{28,... | collective-permute-start | bytes 786440 | tf_op jit(solution)/shard_map/ppermute | solution.py:214
  3.7 13.1 %collective-permute-start.2 = (bf16[2,8,32,256]{3,2,1,0:T(8,128)(2,1)S(1)}, bf16[2,8,32,256]{3,2,1,0:T(8,128)(2,1)S(1)}, u32[]{:S(2)}, u32[]{:S(2)}) collective-permute-start(bf16[2,8,32,256]{3,2,1,0:T(8,128)(2,1)S(1)} %get-tuple-element.23), channel_id=1, source_target_pairs={{0,8},{4,12},{1,9},{5,13},{2,10},{6,14},{3,11},{7,15},{16,24},{20,... | collective-permute-start | bytes 786440 | tf_op jit(solution)/shard_map/ppermute | solution.py:214
  5.0 25.2 %collective-permute-start.1 = (bf16[2,8,32,256]{3,2,1,0:T(8,128)(2,1)S(1)}, bf16[2,8,32,256]{3,2,1,0:T(8,128)(2,1)S(1)}, u32[]{:S(2)}, u32[]{:S(2)}) collective-permute-start(bf16[2,8,32,256]{3,2,1,0:T(8,128)(2,1)S(1)} %get-tuple-element.23), channel_id=1, source_target_pairs={{4,0},{8,4},{12,8},{5,1},{9,5},{13,9},{6,2},{10,6},{14,10},{7,3},{... | collective-permute-start | bytes 786440 | tf_op jit(solution)/shard_map/ppermute | solution.py:214
  10.0 22.1 %collective-permute-start = (bf16[2,8,32,256]{3,2,1,0:T(8,128)(2,1)S(1)}, bf16[2,8,32,256]{3,2,1,0:T(8,128)(2,1)S(1)}, u32[]{:S(2)}, u32[]{:S(2)}) collective-permute-start(bf16[2,8,32,256]{3,2,1,0:T(8,128)(2,1)S(1)} %get-tuple-element.23), channel_id=1, source_target_pairs={{0,4},{4,8},{8,12},{1,5},{5,9},{9,13},{2,6},{6,10},{10,14},{3,7},{... | collective-permute-start | bytes 786440 | tf_op jit(solution)/shard_map/ppermute | solution.py:214
  13.2 6.9 %collective-permute-start.10 = (bf16[4,2,32,256]{3,2,1,0:T(8,128)(2,1)S(1)}, bf16[4,2,32,256]{3,2,1,0:T(8,128)(2,1)S(1)}, u32[]{:S(2)}, u32[]{:S(2)}) collective-permute-start(bf16[4,2,32,256]{3,2,1,0:T(8,128)(2,1)S(1)} %get-tuple-element.18), channel_id=1, source_target_pairs={{0,3},{1,2},{2,1},{3,0},{4,7},{5,6},{6,5},{7,4},{8,11},{9,10},{10,... | collective-permute-start | bytes 393224 | tf_op jit(solution)/shard_map/ppermute | solution.py:224
  16.6 7.2 %collective-permute-start.9 = (bf16[4,2,32,256]{3,2,1,0:T(8,128)(2,1)S(1)}, bf16[4,2,32,256]{3,2,1,0:T(8,128)(2,1)S(1)}, u32[]{:S(2)}, u32[]{:S(2)}) collective-permute-start(bf16[4,2,32,256]{3,2,1,0:T(8,128)(2,1)S(1)} %get-tuple-element.19), channel_id=1, source_target_pairs={{0,2},{1,3},{2,0},{3,1},{4,6},{5,7},{6,4},{7,5},{8,10},{9,11},{10,... | collective-permute-start | bytes 393224 | tf_op jit(solution)/shard_map/ppermute | solution.py:224
  16.8 8.3 %collective-permute-start.8 = (bf16[4,2,32,256]{3,2,1,0:T(8,128)(2,1)S(1)}, bf16[4,2,32,256]{3,2,1,0:T(8,128)(2,1)S(1)}, u32[]{:S(2)}, u32[]{:S(2)}) collective-permute-start(bf16[4,2,32,256]{3,2,1,0:T(8,128)(2,1)S(1)} %get-tuple-element.20), channel_id=1, source_target_pairs={{0,1},{1,0},{2,3},{3,2},{4,5},{5,4},{6,7},{7,6},{8,9},{9,8},{10,11... | collective-permute-start | bytes 393224 | tf_op jit(solution)/shard_map/ppermute | solution.py:224
  20.1 14.7 %collective-permute-start.7 = (bf16[2,8,32,256]{3,2,1,0:T(8,128)(2,1)S(1)}, bf16[2,8,32,256]{3,2,1,0:T(8,128)(2,1)S(1)}, u32[]{:S(2)}, u32[]{:S(2)}) collective-permute-start(bf16[2,8,32,256]{3,2,1,0:T(8,128)(2,1)S(1)} %get-tuple-element.22), channel_id=1, source_target_pairs={{8,0},{12,4},{9,1},{13,5},{10,2},{14,6},{11,3},{15,7},{24,16},{28,... | collective-permute-start | bytes 786440 | tf_op jit(solution)/shard_map/ppermute | solution.py:214
  23.8 12.9 %collective-permute-start.6 = (bf16[2,8,32,256]{3,2,1,0:T(8,128)(2,1)S(1)}, bf16[2,8,32,256]{3,2,1,0:T(8,128)(2,1)S(1)}, u32[]{:S(2)}, u32[]{:S(2)}) collective-permute-start(bf16[2,8,32,256]{3,2,1,0:T(8,128)(2,1)S(1)} %get-tuple-element.22), channel_id=1, source_target_pairs={{0,8},{4,12},{1,9},{5,13},{2,10},{6,14},{3,11},{7,15},{16,24},{20,... | collective-permute-start | bytes 786440 | tf_op jit(solution)/shard_map/ppermute | solution.py:214
  25.1 15.3 %collective-permute-start.5 = (bf16[2,8,32,256]{3,2,1,0:T(8,128)(2,1)S(1)}, bf16[2,8,32,256]{3,2,1,0:T(8,128)(2,1)S(1)}, u32[]{:S(2)}, u32[]{:S(2)}) collective-permute-start(bf16[2,8,32,256]{3,2,1,0:T(8,128)(2,1)S(1)} %get-tuple-element.22), channel_id=1, source_target_pairs={{4,0},{8,4},{12,8},{5,1},{9,5},{13,9},{6,2},{10,6},{14,10},{7,3},{... | collective-permute-start | bytes 786440 | tf_op jit(solution)/shard_map/ppermute | solution.py:214
  30.1 15.9 %collective-permute-start.4 = (bf16[2,8,32,256]{3,2,1,0:T(8,128)(2,1)S(1)}, bf16[2,8,32,256]{3,2,1,0:T(8,128)(2,1)S(1)}, u32[]{:S(2)}, u32[]{:S(2)}) collective-permute-start(bf16[2,8,32,256]{3,2,1,0:T(8,128)(2,1)S(1)} %get-tuple-element.22), channel_id=1, source_target_pairs={{0,4},{4,8},{8,12},{1,5},{5,9},{9,13},{2,6},{6,10},{10,14},{3,7},{... | collective-permute-start | bytes 786440 | tf_op jit(solution)/shard_map/ppermute | solution.py:214
  32.1 22.3 %collective-permute-start.11 = (bf16[2,8,32,256]{3,2,1,0:T(8,128)(2,1)S(1)}, bf16[2,8,32,256]{3,2,1,0:T(8,128)(2,1)S(1)}, u32[]{:S(2)}, u32[]{:S(2)}) collective-permute-start(bf16[2,8,32,256]{3,2,1,0:T(8,128)(2,1)S(1)} %broadcast_select_fusion.3), channel_id=1, source_target_pairs={{8,12},{4,0},{9,13},{5,1},{10,14},{6,2},{11,15},{7,3},{24,28},{20,... | collective-permute-start | bytes 786440 | tf_op jit(solution)/shard_map/ppermute | solution.py:214
  34.8 11.4 %collective-permute-start.12 = (bf16[4,2,32,256]{3,2,1,0:T(8,128)(2,1)S(1)}, bf16[4,2,32,256]{3,2,1,0:T(8,128)(2,1)S(1)}, u32[]{:S(2)}, u32[]{:S(2)}) collective-permute-start(bf16[4,2,32,256]{3,2,1,0:T(8,128)(2,1)S(1)} %pad_maximum_fusion.1), channel_id=1, source_target_pairs={{0,1},{1,0},{2,3},{3,2},{4,5},{5,4},{6,7},{7,6},{8,9},{9,8},{10,11... | collective-permute-start | bytes 393224 | tf_op jit(solution)/shard_map/ppermute | solution.py:224
  36.6 9.5 %collective-permute-start.13 = (bf16[4,2,32,256]{3,2,1,0:T(8,128)(2,1)S(1)}, bf16[4,2,32,256]{3,2,1,0:T(8,128)(2,1)S(1)}, u32[]{:S(2)}, u32[]{:S(2)}) collective-permute-start(bf16[4,2,32,256]{3,2,1,0:T(8,128)(2,1)S(1)} %pad_maximum_fusion.2), channel_id=1, source_target_pairs={{0,2},{1,3},{2,0},{3,1},{4,6},{5,7},{6,4},{7,5},{8,10},{9,11},{10,... | collective-permute-start | bytes 393224 | tf_op jit(solution)/shard_map/ppermute | solution.py:224
  40.4 5.8 %collective-permute-start.14 = (bf16[4,2,32,256]{3,2,1,0:T(8,128)(2,1)S(1)}, bf16[4,2,32,256]{3,2,1,0:T(8,128)(2,1)S(1)}, u32[]{:S(2)}, u32[]{:S(2)}) collective-permute-start(bf16[4,2,32,256]{3,2,1,0:T(8,128)(2,1)S(1)} %pad_maximum_fusion.3), channel_id=1, source_target_pairs={{0,3},{1,2},{2,1},{3,0},{4,7},{5,6},{6,5},{7,4},{8,11},{9,10},{10,... | collective-permute-start | bytes 393224 | tf_op jit(solution)/shard_map/ppermute | solution.py:224
  46.2 16.1 %collective-permute-start.15 = (bf16[2,8,32,256]{3,2,1,0:T(8,128)(2,1)S(1)}, bf16[2,8,32,256]{3,2,1,0:T(8,128)(2,1)S(1)}, u32[]{:S(2)}, u32[]{:S(2)}) collective-permute-start(bf16[2,8,32,256]{3,2,1,0:T(8,128)(2,1)S(1)} %broadcast_select_fusion.2), channel_id=1, source_target_pairs={{8,12},{4,0},{9,13},{5,1},{10,14},{6,2},{11,15},{7,3},{24,28},{20,... | collective-permute-start | bytes 786440 | tf_op jit(solution)/shard_map/ppermute | solution.py:214
  52.1 4.6 %collective-permute-start.17 = (bf16[4,2,32,256]{3,2,1,0:T(8,128)(2,1)S(1)}, bf16[4,2,32,256]{3,2,1,0:T(8,128)(2,1)S(1)}, u32[]{:S(2)}, u32[]{:S(2)}) collective-permute-start(bf16[4,2,32,256]{3,2,1,0:T(8,128)(2,1)S(1)} %pad_maximum_fusion.6), channel_id=1, source_target_pairs={{0,2},{1,3},{2,0},{3,1},{4,6},{5,7},{6,4},{7,5},{8,10},{9,11},{10,... | collective-permute-start | bytes 393224 | tf_op jit(solution)/shard_map/ppermute | solution.py:224
  52.4 8.8 %collective-permute-start.18 = (bf16[4,2,32,256]{3,2,1,0:T(8,128)(2,1)S(1)}, bf16[4,2,32,256]{3,2,1,0:T(8,128)(2,1)S(1)}, u32[]{:S(2)}, u32[]{:S(2)}) collective-permute-start(bf16[4,2,32,256]{3,2,1,0:T(8,128)(2,1)S(1)} %pad_maximum_fusion.7), channel_id=1, source_target_pairs={{0,3},{1,2},{2,1},{3,0},{4,7},{5,6},{6,5},{7,4},{8,11},{9,10},{10,... | collective-permute-start | bytes 393224 | tf_op jit(solution)/shard_map/ppermute | solution.py:224
  54.5 7.8 %collective-permute-start.21 = (bf16[2,2,32,256]{3,2,1,0:T(8,128)(2,1)S(1)}, bf16[2,2,32,256]{3,2,1,0:T(8,128)(2,1)S(1)}, u32[]{:S(2)}, u32[]{:S(2)}) collective-permute-start(bf16[2,2,32,256]{3,2,1,0:T(8,128)(2,1)S(1)} %get-tuple-element.28), channel_id=1, source_target_pairs={{0,3},{1,2},{2,1},{3,0},{4,7},{5,6},{6,5},{7,4},{8,11},{9,10},{10,... | collective-permute-start | bytes 196616 | tf_op jit(solution)/shard_map/ppermute | solution.py:224
  54.6 7.7 %collective-permute-start.20 = (bf16[2,2,32,256]{3,2,1,0:T(8,128)(2,1)S(1)}, bf16[2,2,32,256]{3,2,1,0:T(8,128)(2,1)S(1)}, u32[]{:S(2)}, u32[]{:S(2)}) collective-permute-start(bf16[2,2,32,256]{3,2,1,0:T(8,128)(2,1)S(1)} %get-tuple-element.29), channel_id=1, source_target_pairs={{0,2},{1,3},{2,0},{3,1},{4,6},{5,7},{6,4},{7,5},{8,10},{9,11},{10,... | collective-permute-start | bytes 196616 | tf_op jit(solution)/shard_map/ppermute | solution.py:224
  56.8 5.6 %collective-permute-start.19 = (bf16[2,2,32,256]{3,2,1,0:T(8,128)(2,1)S(1)}, bf16[2,2,32,256]{3,2,1,0:T(8,128)(2,1)S(1)}, u32[]{:S(2)}, u32[]{:S(2)}) collective-permute-start(bf16[2,2,32,256]{3,2,1,0:T(8,128)(2,1)S(1)} %get-tuple-element.30), channel_id=1, source_target_pairs={{0,1},{1,0},{2,3},{3,2},{4,5},{5,4},{6,7},{7,6},{8,9},{9,8},{10,11... | collective-permute-start | bytes 196616 | tf_op jit(solution)/shard_map/ppermute | solution.py:224
  62.4 4.1 %collective-permute-start.24 = (bf16[2,2,32,256]{3,2,1,0:T(8,128)(2,1)S(1)}, bf16[2,2,32,256]{3,2,1,0:T(8,128)(2,1)S(1)}, u32[]{:S(2)}, u32[]{:S(2)}) collective-permute-start(bf16[2,2,32,256]{3,2,1,0:T(8,128)(2,1)S(1)} %get-tuple-element.24), channel_id=1, source_target_pairs={{0,3},{1,2},{2,1},{3,0},{4,7},{5,6},{6,5},{7,4},{8,11},{9,10},{10,... | collective-permute-start | bytes 196616 | tf_op jit(solution)/shard_map/ppermute | solution.py:224
  64.0 4.5 %collective-permute-start.23 = (bf16[2,2,32,256]{3,2,1,0:T(8,128)(2,1)S(1)}, bf16[2,2,32,256]{3,2,1,0:T(8,128)(2,1)S(1)}, u32[]{:S(2)}, u32[]{:S(2)}) collective-permute-start(bf16[2,2,32,256]{3,2,1,0:T(8,128)(2,1)S(1)} %get-tuple-element.25), channel_id=1, source_target_pairs={{0,2},{1,3},{2,0},{3,1},{4,6},{5,7},{6,4},{7,5},{8,10},{9,11},{10,... | collective-permute-start | bytes 196616 | tf_op jit(solution)/shard_map/ppermute | solution.py:224
  65.2 3.3 %collective-permute-start.22 = (bf16[2,2,32,256]{3,2,1,0:T(8,128)(2,1)S(1)}, bf16[2,2,32,256]{3,2,1,0:T(8,128)(2,1)S(1)}, u32[]{:S(2)}, u32[]{:S(2)}) collective-permute-start(bf16[2,2,32,256]{3,2,1,0:T(8,128)(2,1)S(1)} %get-tuple-element.26), channel_id=1, source_target_pairs={{0,1},{1,0},{2,3},{3,2},{4,5},{5,4},{6,7},{7,6},{8,9},{9,8},{10,11... | collective-permute-start | bytes 196616 | tf_op jit(solution)/shard_map/ppermute | solution.py:224
  (7 other events, 101.8 us)

commit v4 on v3

--- a/solution.py
+++ b/solution.py
@@ -226,7 +226,7 @@
         parts.extend(found)
         return [x for _, x in found]
 
-    if inst_size != 4 or slot_count % 2:
+    if inst_size != 4:
         exchange(hops[0])
         for s in range(1, inst_size):
             sources.append([(i - s) % inst_size for i in range(inst_size)])
@@ -235,37 +235,26 @@
             exchange(hops[-1])
         return hops, parts, sources
 
-    half = slot_count // 2
-    sources += [[-1, 0, 1, 2], [1, 2, 3, -1], [-1, -1, 0, 1], [2, 3, -1, -1], [3, -1, -1, 0]]
-    far, first, last = 6, 7, 8
-    sources += [[2, 3, 0, 1], [1, 0, 3, 2], [3, 2, 1, 0]]
-    mine = [kv_new[:half], kv_new[half:]]
-    got = []
-    for n in range(2):
-        up2 = along(mine[n], [(0, 2), (1, 3)])
-        down2 = along(mine[n], [(2, 0), (3, 1)])
-        up1 = along(mine[n], [(0, 1), (1, 2), (2, 3)])
-        down1 = along(mine[n], [(1, 0), (2, 1), (3, 2)])
-        got.append((up1, down1, up2, down2))
-        for hop, x in enumerate(got[-1], 1):
-            hops.append(((hop, n * half, half), x))
+    middle = (inst == 1) | (inst == 2)
+    sources += [[1, 0, 3, 2], [-1, 2, 1, -1], [-1, 3, 0, -1], [2, -1, -1, 1], [3, -1, -1, 0]]
+    second, third = 6, 7
+    sources += [[2, 2, 1, 1], [3, 3, 0, 0]]
+    whole = slot_count
+    outer = along(kv_new, [(0, 1), (1, 0), (2, 3), (3, 2)])
+    inner = along(kv_new, [(1, 2), (2, 1)])
     waiting = exchange(hops[0])
-    lasts = []
-    for n in range(2):
-        up1, down1, up2, down2 = got[n]
-        at = n * half
-        two = after([jnp.where(inst < 2, down2, up2)], waiting)[0]
-        handed = along(two, [(2, 3), (1, 0)])
-        hops.append(((5, at, half), handed))
-        one = jnp.where((inst == 0) | (inst == 2), down1, up1)
-        waiting = exchange(((far, at, half), two), ((first, at, half), one))
-        lasts.append((up1, down1, handed))
-        if n == 0:
-            before = waiting
-    for n in range(2):
-        up1, down1, handed = after(lasts[n], before)
-        end = jnp.where(inst == 1, down1, jnp.where(inst == 2, up1, handed))
-        before = exchange(((last, n * half, half), end)) + waiting
+    outer_on, inner_on = after([outer, inner], waiting)
+    crossed = along(outer_on, [(1, 2), (2, 1)])
+    inner_ends = along(inner_on, [(1, 0), (2, 3)])
+    waiting = exchange(((1, 0, whole), outer_on))
+    crossed_on = after([crossed], waiting)[0]
+    crossed_ends = along(crossed_on, [(1, 0), (2, 3)])
+    two = jnp.where(middle, inner, inner_ends)
+    waiting = exchange(((second, 0, whole), two))
+    three = after([jnp.where(middle, crossed, crossed_ends)], waiting)[0]
+    exchange(((third, 0, whole), three))
+    for hop, x in enumerate((outer, inner, crossed, inner_ends, crossed_ends), 1):
+        hops.append(((hop, 0, whole), x))
     return hops, parts, sources
 
 

time: 83.3 us -> 66.3 us (0.80)
  the two profiles are of different devices: /device:TPU:21 before, /device:TPU:5 now
where the time goes in v4:
time: 66.3 us; the launch traced here: 65.2 us
  waiting for transfers between devices  28.2 us (43%)
  starting transfers between devices  22 us (33%)
  Pallas kernels  11.3 us (17%)
  local copies, waits for them, and re-layouts  2.67 us (4%)
  between operations  0.85 us (1%)
    ppermute x12, waiting for transfers between devices, exchange(): sent = lax.ppermute(sent, 'tp', [(t, t ^ j) for t in range(tp_size)])  18.2 us
    ppermute x12, starting transfers between devices, exchange(): sent = lax.ppermute(sent, 'tp', [(t, t ^ j) for t in range(tp_size)])  14.2 us
    pallas_call x1, Pallas kernels, body(): pl.pallas_call(kernel, grid_spec=pltpu.PrefetchScalarGridSpec(num_scalar_...  11.3 us
    ppermute x5, waiting for transfers between devices, along(): return lax.ppermute(x, 'inst', pairs)  10 us
    ppermute x5, starting transfers between devices, along(): return lax.ppermute(x, 'inst', pairs)  7.82 us
  transfers between devices with their start and end apart: 17, of which 9 were waited for; matrix products, arithmetic and copies ran while one was open for 3% of the time, Pallas kernels for 0%

profile of v4, /device:TPU:5, one launch (start us, length us, event | category | flops | bytes accessed | tf_op | source)
XLA Modules:
  0.0 65.2 jit_solution(18199638676585705888)
XLA Ops:
  0.6 0.7 %collective-permute-start.1 = (bf16[4,8,32,256]{3,2,1,0:T(8,128)(2,1)}, bf16[4,8,32,256]{3,2,1,0:T(8,128)(2,1)S(1)}, u32[]{:S(2)}, u32[]{:S(2)}) collective-permute-start(bf16[4,8,32,256]{3,2,1,0:T(8,128)(2,1)} %refs_1_.1), channel_id=1, source_target_pairs={{4,8},{8,4},{5,9},{9,5},{6,10},{10,6},{7,11},{11,7},{20,24},{24,20... | collective-permute-start | bytes 1572872 | tf_op jit(solution)/shard_map/ppermute | solution.py:214
  1.3 3.9 %collective-permute-start = (bf16[4,8,32,256]{3,2,1,0:T(8,128)(2,1)}, bf16[4,8,32,256]{3,2,1,0:T(8,128)(2,1)S(1)}, u32[]{:S(2)}, u32[]{:S(2)}) collective-permute-start(bf16[4,8,32,256]{3,2,1,0:T(8,128)(2,1)} %refs_1_.1), channel_id=1, source_target_pairs={{0,4},{4,0},{8,12},{12,8},{1,5},{5,1},{9,13},{13,9},{2,6},{6,2},{1... | collective-permute-start | bytes 1572872 | tf_op jit(solution)/shard_map/ppermute | solution.py:214
  5.2 1.1 %constant_dynamic-slice_fusion.12 = (bf16[4,2,32,256]{3,2,1,0:T(8,128)(2,1)S(1)}, bf16[4,2,32,256]{3,2,1,0:T(8,128)(2,1)S(1)}, bf16[4,2,32,256]{3,2,1,0:T(8,128)(2,1)S(1)}, bf16[4,2,32,256]{3,2,1,0:T(8,128)(2,1)S(1)}) fusion(bf16[4,8,32,256]{3,2,1,0:T(8,128)(2,1)} %refs_1_.1, s32[]{:T(128)S(6)} %select_n.74, s32[]{:T(128)S(6)} %select_n.72, ...), kind=kLoop, calls=%fused_computation.14 | loop fusion | bytes 1048592 | tf_op jit(solution)/shard_map/dynamic_slice | solution.py:221
  6.3 2.4 %collective-permute-start.4 = (bf16[4,2,32,256]{3,2,1,0:T(8,128)(2,1)S(1)}, bf16[4,2,32,256]{3,2,1,0:T(8,128)(2,1)S(1)}, u32[]{:S(2)}, u32[]{:S(2)}) collective-permute-start(bf16[4,2,32,256]{3,2,1,0:T(8,128)(2,1)S(1)} %get-tuple-element.22), channel_id=1, source_target_pairs={{0,3},{1,2},{2,1},{3,0},{4,7},{5,6},{6,5},{7,4},{8,11},{9,10},{10,... | collective-permute-start | bytes 393224 | tf_op jit(solution)/shard_map/ppermute | solution.py:224
  8.7 0.3 collective-permute-start.3
  9.2 3.9 %collective-permute-done.4.refs_10_ = bf16[4,2,32,256]{3,2,1,0:T(8,128)(2,1)S(1)} collective-permute-done((bf16[4,2,32,256]{3,2,1,0:T(8,128)(2,1)S(1)}, bf16[4,2,32,256]{3,2,1,0:T(8,128)(2,1)S(1)}, u32[]{:S(2)}, u32[]{:S(2)}) %collective-permute-start.4) | collective-permute-done | bytes 131104 | tf_op jit(solution)/shard_map/ppermute | solution.py:224
  13.1 2.7 %collective-permute-done.3.refs_9_ = bf16[4,2,32,256]{3,2,1,0:T(8,128)(2,1)S(1)} collective-permute-done((bf16[4,2,32,256]{3,2,1,0:T(8,128)(2,1)S(1)}, bf16[4,2,32,256]{3,2,1,0:T(8,128)(2,1)S(1)}, u32[]{:S(2)}, u32[]{:S(2)}) %collective-permute-start.3) | collective-permute-done | bytes 131104 | tf_op jit(solution)/shard_map/ppermute | solution.py:224
  15.8 0.9 %collective-permute-done.refs_2_ = bf16[4,8,32,256]{3,2,1,0:T(8,128)(2,1)S(1)} collective-permute-done((bf16[4,8,32,256]{3,2,1,0:T(8,128)(2,1)}, bf16[4,8,32,256]{3,2,1,0:T(8,128)(2,1)S(1)}, u32[]{:S(2)}, u32[]{:S(2)}) %collective-permute-start) | collective-permute-done | bytes 524320 | tf_op jit(solution)/shard_map/ppermute | solution.py:214
  16.8 0.7 %collective-permute-start.5 = (bf16[4,8,32,256]{3,2,1,0:T(8,128)(2,1)S(1)}, bf16[4,8,32,256]{3,2,1,0:T(8,128)(2,1)S(1)}, u32[]{:S(2)}, u32[]{:S(2)}) collective-permute-start(bf16[4,8,32,256]{3,2,1,0:T(8,128)(2,1)S(1)} %collective-permute-done.refs_2_), channel_id=1, source_target_pairs={{4,8},{8,4},{5,9},{9,5},{6,10},{10,6},{7,11},{11,7},{20,24},{24,20... | collective-permute-start | bytes 1572872 | tf_op jit(solution)/shard_map/ppermute | solution.py:214
  17.4 1.3 %collective-permute-start.6 = (bf16[4,8,32,256]{3,2,1,0:T(8,128)(2,1)S(1)}, bf16[4,8,32,256]{3,2,1,0:T(8,128)(2,1)S(1)}, u32[]{:S(2)}, u32[]{:S(2)}) collective-permute-start(bf16[4,8,32,256]{3,2,1,0:T(8,128)(2,1)S(1)} %collective-permute-done.1.refs_3_), channel_id=1, source_target_pairs={{4,0},{8,12},{5,1},{9,13},{6,2},{10,14},{7,3},{11,15},{20,16},{24,... | collective-permute-start | bytes 1572872 | tf_op jit(solution)/shard_map/ppermute | solution.py:214
  18.8 2.7 %collective-permute-start.9 = (bf16[4,2,32,256]{3,2,1,0:T(8,128)(2,1)S(1)}, bf16[4,2,32,256]{3,2,1,0:T(8,128)(2,1)S(1)}, u32[]{:S(2)}, u32[]{:S(2)}) collective-permute-start(bf16[4,2,32,256]{3,2,1,0:T(8,128)(2,1)S(1)} %get-tuple-element.18), channel_id=1, source_target_pairs={{0,3},{1,2},{2,1},{3,0},{4,7},{5,6},{6,5},{7,4},{8,11},{9,10},{10,... | collective-permute-start | bytes 393224 | tf_op jit(solution)/shard_map/ppermute | solution.py:224
  22.0 3.9 %collective-permute-done.9.refs_14_ = bf16[4,2,32,256]{3,2,1,0:T(8,128)(2,1)S(1)} collective-permute-done((bf16[4,2,32,256]{3,2,1,0:T(8,128)(2,1)S(1)}, bf16[4,2,32,256]{3,2,1,0:T(8,128)(2,1)S(1)}, u32[]{:S(2)}, u32[]{:S(2)}) %collective-permute-start.9) | collective-permute-done | bytes 131104 | tf_op jit(solution)/shard_map/ppermute | solution.py:224
  25.9 2.7 %collective-permute-done.8.refs_13_ = bf16[4,2,32,256]{3,2,1,0:T(8,128)(2,1)S(1)} collective-permute-done((bf16[4,2,32,256]{3,2,1,0:T(8,128)(2,1)S(1)}, bf16[4,2,32,256]{3,2,1,0:T(8,128)(2,1)S(1)}, u32[]{:S(2)}, u32[]{:S(2)}) %collective-permute-start.8) | collective-permute-done | bytes 131104 | tf_op jit(solution)/shard_map/ppermute | solution.py:224
  28.6 0.7 %copy-done.2 = bf16[4,2,32,256]{3,2,1,0:T(8,128)(2,1)} copy-done((bf16[4,2,32,256]{3,2,1,0:T(8,128)(2,1)}, bf16[4,2,32,256]{3,2,1,0:T(8,128)(2,1)S(1)}, u32[]{:S(2)}) %copy-start.2) | copy-done | bytes 131096
  29.2 1.3 %collective-permute-start.10 = (bf16[4,8,32,256]{3,2,1,0:T(8,128)(2,1)S(1)}, bf16[4,8,32,256]{3,2,1,0:T(8,128)(2,1)S(1)}, u32[]{:S(2)}, u32[]{:S(2)}) collective-permute-start(bf16[4,8,32,256]{3,2,1,0:T(8,128)(2,1)S(1)} %collective-permute-done.5.refs_4_), channel_id=1, source_target_pairs={{4,0},{8,12},{5,1},{9,13},{6,2},{10,14},{7,3},{11,15},{20,16},{24,... | collective-permute-start | bytes 1572872 | tf_op jit(solution)/shard_map/ppermute | solution.py:214
  30.5 0.9 %collective-permute-done.6.refs_5_ = bf16[4,8,32,256]{3,2,1,0:T(8,128)(2,1)S(1)} collective-permute-done((bf16[4,8,32,256]{3,2,1,0:T(8,128)(2,1)S(1)}, bf16[4,8,32,256]{3,2,1,0:T(8,128)(2,1)S(1)}, u32[]{:S(2)}, u32[]{:S(2)}) %collective-permute-start.6) | collective-permute-done | bytes 524320 | tf_op jit(solution)/shard_map/ppermute | solution.py:214
  31.7 3.9 %collective-permute-start.13 = (bf16[4,2,32,256]{3,2,1,0:T(8,128)(2,1)S(1)}, bf16[4,2,32,256]{3,2,1,0:T(8,128)(2,1)S(1)}, u32[]{:S(2)}, u32[]{:S(2)}) collective-permute-start(bf16[4,2,32,256]{3,2,1,0:T(8,128)(2,1)S(1)} %get-tuple-element.14), channel_id=1, source_target_pairs={{0,3},{1,2},{2,1},{3,0},{4,7},{5,6},{6,5},{7,4},{8,11},{9,10},{10,... | collective-permute-start | bytes 393224 | tf_op jit(solution)/shard_map/ppermute | solution.py:224
  36.0 8.1 %collective-permute-done.10.refs_6_ = bf16[4,8,32,256]{3,2,1,0:T(8,128)(2,1)S(1)} collective-permute-done((bf16[4,8,32,256]{3,2,1,0:T(8,128)(2,1)S(1)}, bf16[4,8,32,256]{3,2,1,0:T(8,128)(2,1)S(1)}, u32[]{:S(2)}, u32[]{:S(2)}) %collective-permute-start.10) | collective-permute-done | bytes 524320 | tf_op jit(solution)/shard_map/ppermute | solution.py:214
  44.3 2.7 %collective-permute-start.16 = (bf16[4,2,32,256]{3,2,1,0:T(8,128)(2,1)S(1)}, bf16[4,2,32,256]{3,2,1,0:T(8,128)(2,1)S(1)}, u32[]{:S(2)}, u32[]{:S(2)}) collective-permute-start(bf16[4,2,32,256]{3,2,1,0:T(8,128)(2,1)S(1)} %get-tuple-element.10), channel_id=1, source_target_pairs={{0,3},{1,2},{2,1},{3,0},{4,7},{5,6},{6,5},{7,4},{8,11},{9,10},{10,... | collective-permute-start | bytes 393224 | tf_op jit(solution)/shard_map/ppermute | solution.py:224
  47.0 1.1 %collective-permute-start.15 = (bf16[4,2,32,256]{3,2,1,0:T(8,128)(2,1)S(1)}, bf16[4,2,32,256]{3,2,1,0:T(8,128)(2,1)S(1)}, u32[]{:S(2)}, u32[]{:S(2)}) collective-permute-start(bf16[4,2,32,256]{3,2,1,0:T(8,128)(2,1)S(1)} %get-tuple-element.11), channel_id=1, source_target_pairs={{0,2},{1,3},{2,0},{3,1},{4,6},{5,7},{6,4},{7,5},{8,10},{9,11},{10,... | collective-permute-start | bytes 393224 | tf_op jit(solution)/shard_map/ppermute | solution.py:224
  48.1 0.7 %fusion = s32[8]{0:T(128)S(1)} fusion(s32[8,4]{0,1:T(4,128)} %constant.81.clone, s32[]{:T(128)S(6)} %select_n.66), kind=kLoop, calls=%fused_computation.19 | loop fusion | bytes 68 | tf_op jit(solution)/shard_map/jit(dynamic_index_in_dim)/squeeze | solution.py:275
  48.9 1.7 %collective-permute-done.16.refs_22_ = bf16[4,2,32,256]{3,2,1,0:T(8,128)(2,1)S(1)} collective-permute-done((bf16[4,2,32,256]{3,2,1,0:T(8,128)(2,1)S(1)}, bf16[4,2,32,256]{3,2,1,0:T(8,128)(2,1)S(1)}, u32[]{:S(2)}, u32[]{:S(2)}) %collective-permute-start.16) | collective-permute-done | bytes 131104 | tf_op jit(solution)/shard_map/ppermute | solution.py:224
  50.5 3.3 %collective-permute-done.15.refs_21_ = bf16[4,2,32,256]{3,2,1,0:T(8,128)(2,1)S(1)} collective-permute-done((bf16[4,2,32,256]{3,2,1,0:T(8,128)(2,1)S(1)}, bf16[4,2,32,256]{3,2,1,0:T(8,128)(2,1)S(1)}, u32[]{:S(2)}, u32[]{:S(2)}) %collective-permute-start.15) | collective-permute-done | bytes 131104 | tf_op jit(solution)/shard_map/ppermute | solution.py:224
  53.9 11.3 %shard_map.86 = (bf16[4,128,2048]{2,1,0:T(8,128)(2,1)}, bf16[8,8,32,256]{3,2,1,0:T(8,128)(2,1)}) custom-call(s32[4]{0:T(128)S(1)} %copy-done.4, s32[4]{0:T(128)S(1)} %copy-done.5, s32[16]{0:T(128)S(1)} %copy-done.6, s32[4]{0:T(128)S(1)} %copy-done.7, s32[10]{0:T(128)S(1)} %pad_add_fusion.place_at_ref, bf16[4,128,2048]{2,1,0:T(8,128)(2,1)S(1)} %copy-done.1, ...), custom_call_target="tpu_custom_call" | custom-call | flops 2147483648 | bytes 8388608 | tf_op jit(solution)/shard_map/pallas_call | solution.py:293
  (35 shorter events, 1.6 us)
Async XLA Ops:
  0.6 15.2 %collective-permute-start.1 = (bf16[4,8,32,256]{3,2,1,0:T(8,128)(2,1)}, bf16[4,8,32,256]{3,2,1,0:T(8,128)(2,1)S(1)}, u32[]{:S(2)}, u32[]{:S(2)}) collective-permute-start(bf16[4,8,32,256]{3,2,1,0:T(8,128)(2,1)} %refs_1_.1), channel_id=1, source_target_pairs={{4,8},{8,4},{5,9},{9,5},{6,10},{10,6},{7,11},{11,7},{20,24},{24,20... | collective-permute-start | bytes 1572872 | tf_op jit(solution)/shard_map/ppermute | solution.py:214
  1.3 15.4 %collective-permute-start = (bf16[4,8,32,256]{3,2,1,0:T(8,128)(2,1)}, bf16[4,8,32,256]{3,2,1,0:T(8,128)(2,1)S(1)}, u32[]{:S(2)}, u32[]{:S(2)}) collective-permute-start(bf16[4,8,32,256]{3,2,1,0:T(8,128)(2,1)} %refs_1_.1), channel_id=1, source_target_pairs={{0,4},{4,0},{8,12},{12,8},{1,5},{5,1},{9,13},{13,9},{2,6},{6,2},{1... | collective-permute-start | bytes 1572872 | tf_op jit(solution)/shard_map/ppermute | solution.py:214
  6.3 6.7 %collective-permute-start.4 = (bf16[4,2,32,256]{3,2,1,0:T(8,128)(2,1)S(1)}, bf16[4,2,32,256]{3,2,1,0:T(8,128)(2,1)S(1)}, u32[]{:S(2)}, u32[]{:S(2)}) collective-permute-start(bf16[4,2,32,256]{3,2,1,0:T(8,128)(2,1)S(1)} %get-tuple-element.22), channel_id=1, source_target_pairs={{0,3},{1,2},{2,1},{3,0},{4,7},{5,6},{6,5},{7,4},{8,11},{9,10},{10,... | collective-permute-start | bytes 393224 | tf_op jit(solution)/shard_map/ppermute | solution.py:224
  8.7 7.1 %collective-permute-start.3 = (bf16[4,2,32,256]{3,2,1,0:T(8,128)(2,1)S(1)}, bf16[4,2,32,256]{3,2,1,0:T(8,128)(2,1)S(1)}, u32[]{:S(2)}, u32[]{:S(2)}) collective-permute-start(bf16[4,2,32,256]{3,2,1,0:T(8,128)(2,1)S(1)} %get-tuple-element.23), channel_id=1, source_target_pairs={{0,2},{1,3},{2,0},{3,1},{4,6},{5,7},{6,4},{7,5},{8,10},{9,11},{10,... | collective-permute-start | bytes 393224 | tf_op jit(solution)/shard_map/ppermute | solution.py:224
  9.0 6.8 %collective-permute-start.2 = (bf16[4,2,32,256]{3,2,1,0:T(8,128)(2,1)S(1)}, bf16[4,2,32,256]{3,2,1,0:T(8,128)(2,1)S(1)}, u32[]{:S(2)}, u32[]{:S(2)}) collective-permute-start(bf16[4,2,32,256]{3,2,1,0:T(8,128)(2,1)S(1)} %get-tuple-element.24), channel_id=1, source_target_pairs={{0,1},{1,0},{2,3},{3,2},{4,5},{5,4},{6,7},{7,6},{8,9},{9,8},{10,11... | collective-permute-start | bytes 393224 | tf_op jit(solution)/shard_map/ppermute | solution.py:224
  16.8 12.5 %collective-permute-start.5 = (bf16[4,8,32,256]{3,2,1,0:T(8,128)(2,1)S(1)}, bf16[4,8,32,256]{3,2,1,0:T(8,128)(2,1)S(1)}, u32[]{:S(2)}, u32[]{:S(2)}) collective-permute-start(bf16[4,8,32,256]{3,2,1,0:T(8,128)(2,1)S(1)} %collective-permute-done.refs_2_), channel_id=1, source_target_pairs={{4,8},{8,4},{5,9},{9,5},{6,10},{10,6},{7,11},{11,7},{20,24},{24,20... | collective-permute-start | bytes 1572872 | tf_op jit(solution)/shard_map/ppermute | solution.py:214
  17.4 14.0 %collective-permute-start.6 = (bf16[4,8,32,256]{3,2,1,0:T(8,128)(2,1)S(1)}, bf16[4,8,32,256]{3,2,1,0:T(8,128)(2,1)S(1)}, u32[]{:S(2)}, u32[]{:S(2)}) collective-permute-start(bf16[4,8,32,256]{3,2,1,0:T(8,128)(2,1)S(1)} %collective-permute-done.1.refs_3_), channel_id=1, source_target_pairs={{4,0},{8,12},{5,1},{9,13},{6,2},{10,14},{7,3},{11,15},{20,16},{24,... | collective-permute-start | bytes 1572872 | tf_op jit(solution)/shard_map/ppermute | solution.py:214
  18.8 7.1 %collective-permute-start.9 = (bf16[4,2,32,256]{3,2,1,0:T(8,128)(2,1)S(1)}, bf16[4,2,32,256]{3,2,1,0:T(8,128)(2,1)S(1)}, u32[]{:S(2)}, u32[]{:S(2)}) collective-permute-start(bf16[4,2,32,256]{3,2,1,0:T(8,128)(2,1)S(1)} %get-tuple-element.18), channel_id=1, source_target_pairs={{0,3},{1,2},{2,1},{3,0},{4,7},{5,6},{6,5},{7,4},{8,11},{9,10},{10,... | collective-permute-start | bytes 393224 | tf_op jit(solution)/shard_map/ppermute | solution.py:224
  21.5 7.1 %collective-permute-start.8 = (bf16[4,2,32,256]{3,2,1,0:T(8,128)(2,1)S(1)}, bf16[4,2,32,256]{3,2,1,0:T(8,128)(2,1)S(1)}, u32[]{:S(2)}, u32[]{:S(2)}) collective-permute-start(bf16[4,2,32,256]{3,2,1,0:T(8,128)(2,1)S(1)} %get-tuple-element.19), channel_id=1, source_target_pairs={{0,2},{1,3},{2,0},{3,1},{4,6},{5,7},{6,4},{7,5},{8,10},{9,11},{10,... | collective-permute-start | bytes 393224 | tf_op jit(solution)/shard_map/ppermute | solution.py:224
  21.8 6.8 %collective-permute-start.7 = (bf16[4,2,32,256]{3,2,1,0:T(8,128)(2,1)S(1)}, bf16[4,2,32,256]{3,2,1,0:T(8,128)(2,1)S(1)}, u32[]{:S(2)}, u32[]{:S(2)}) collective-permute-start(bf16[4,2,32,256]{3,2,1,0:T(8,128)(2,1)S(1)} %get-tuple-element.20), channel_id=1, source_target_pairs={{0,1},{1,0},{2,3},{3,2},{4,5},{5,4},{6,7},{7,6},{8,9},{9,8},{10,11... | collective-permute-start | bytes 393224 | tf_op jit(solution)/shard_map/ppermute | solution.py:224
  29.2 14.9 %collective-permute-start.10 = (bf16[4,8,32,256]{3,2,1,0:T(8,128)(2,1)S(1)}, bf16[4,8,32,256]{3,2,1,0:T(8,128)(2,1)S(1)}, u32[]{:S(2)}, u32[]{:S(2)}) collective-permute-start(bf16[4,8,32,256]{3,2,1,0:T(8,128)(2,1)S(1)} %collective-permute-done.5.refs_4_), channel_id=1, source_target_pairs={{4,0},{8,12},{5,1},{9,13},{6,2},{10,14},{7,3},{11,15},{20,16},{24,... | collective-permute-start | bytes 1572872 | tf_op jit(solution)/shard_map/ppermute | solution.py:214
  31.5 22.3 %copy-start = (bf16[4,8,32,256]{3,2,1,0:T(8,128)(2,1)S(1)}, bf16[4,8,32,256]{3,2,1,0:T(8,128)(2,1)}, u32[]{:S(2)}) copy-start(bf16[4,8,32,256]{3,2,1,0:T(8,128)(2,1)} %refs_1_.1) | copy-start | bytes 1572868
  31.5 22.3 %copy-start.1 = (bf16[4,128,2048]{2,1,0:T(8,128)(2,1)S(1)}, bf16[4,128,2048]{2,1,0:T(8,128)(2,1)}, u32[]{:S(2)}) copy-start(bf16[4,128,2048]{2,1,0:T(8,128)(2,1)} %refs_0_.1) | copy-start | bytes 6291460
  31.5 22.3 %copy-start.3 = (bf16[4,2,32,256]{3,2,1,0:T(8,128)(2,1)S(1)}, bf16[4,2,32,256]{3,2,1,0:T(8,128)(2,1)}, u32[]{:S(2)}) copy-start(bf16[4,2,32,256]{3,2,1,0:T(8,128)(2,1)} %copy-done.2) | copy-start | bytes 393220
  31.6 22.3 %copy-start.4 = (s32[4]{0:T(128)S(1)}, s32[4]{0:T(128)}, u32[]{:S(2)}) copy-start(s32[4]{0:T(128)} %spans_ref.1) | copy-start | bytes 52
  31.6 22.3 %copy-start.5 = (s32[4]{0:T(128)S(1)}, s32[4]{0:T(128)}, u32[]{:S(2)}) copy-start(s32[4]{0:T(128)} %tail_ref.1) | copy-start | bytes 52
  31.6 22.3 %copy-start.6 = (s32[16]{0:T(128)S(1)}, s32[16]{0:T(128)}, u32[]{:S(2)}) copy-start(s32[16]{0:T(128)} %plan_ref.1) | copy-start | bytes 196
  31.6 22.3 %copy-start.7 = (s32[4]{0:T(128)S(1)}, s32[4]{0:T(128)}, u32[]{:S(2)}) copy-start(s32[4]{0:T(128)} %owner_ref.1) | copy-start | bytes 52
  31.7 12.6 %collective-permute-start.13 = (bf16[4,2,32,256]{3,2,1,0:T(8,128)(2,1)S(1)}, bf16[4,2,32,256]{3,2,1,0:T(8,128)(2,1)S(1)}, u32[]{:S(2)}, u32[]{:S(2)}) collective-permute-start(bf16[4,2,32,256]{3,2,1,0:T(8,128)(2,1)S(1)} %get-tuple-element.14), channel_id=1, source_target_pairs={{0,3},{1,2},{2,1},{3,0},{4,7},{5,6},{6,5},{7,4},{8,11},{9,10},{10,... | collective-permute-start | bytes 393224 | tf_op jit(solution)/shard_map/ppermute | solution.py:224
  35.5 8.7 %collective-permute-start.12 = (bf16[4,2,32,256]{3,2,1,0:T(8,128)(2,1)S(1)}, bf16[4,2,32,256]{3,2,1,0:T(8,128)(2,1)S(1)}, u32[]{:S(2)}, u32[]{:S(2)}) collective-permute-start(bf16[4,2,32,256]{3,2,1,0:T(8,128)(2,1)S(1)} %get-tuple-element.15), channel_id=1, source_target_pairs={{0,2},{1,3},{2,0},{3,1},{4,6},{5,7},{6,4},{7,5},{8,10},{9,11},{10,... | collective-permute-start | bytes 393224 | tf_op jit(solution)/shard_map/ppermute | solution.py:224
  35.8 8.4 %collective-permute-start.11 = (bf16[4,2,32,256]{3,2,1,0:T(8,128)(2,1)S(1)}, bf16[4,2,32,256]{3,2,1,0:T(8,128)(2,1)S(1)}, u32[]{:S(2)}, u32[]{:S(2)}) collective-permute-start(bf16[4,2,32,256]{3,2,1,0:T(8,128)(2,1)S(1)} %get-tuple-element.16), channel_id=1, source_target_pairs={{0,1},{1,0},{2,3},{3,2},{4,5},{5,4},{6,7},{7,6},{8,9},{9,8},{10,11... | collective-permute-start | bytes 393224 | tf_op jit(solution)/shard_map/ppermute | solution.py:224
  44.3 6.2 %collective-permute-start.16 = (bf16[4,2,32,256]{3,2,1,0:T(8,128)(2,1)S(1)}, bf16[4,2,32,256]{3,2,1,0:T(8,128)(2,1)S(1)}, u32[]{:S(2)}, u32[]{:S(2)}) collective-permute-start(bf16[4,2,32,256]{3,2,1,0:T(8,128)(2,1)S(1)} %get-tuple-element.10), channel_id=1, source_target_pairs={{0,3},{1,2},{2,1},{3,0},{4,7},{5,6},{6,5},{7,4},{8,11},{9,10},{10,... | collective-permute-start | bytes 393224 | tf_op jit(solution)/shard_map/ppermute | solution.py:224
  47.0 6.9 %collective-permute-start.15 = (bf16[4,2,32,256]{3,2,1,0:T(8,128)(2,1)S(1)}, bf16[4,2,32,256]{3,2,1,0:T(8,128)(2,1)S(1)}, u32[]{:S(2)}, u32[]{:S(2)}) collective-permute-start(bf16[4,2,32,256]{3,2,1,0:T(8,128)(2,1)S(1)} %get-tuple-element.11), channel_id=1, source_target_pairs={{0,2},{1,3},{2,0},{3,1},{4,6},{5,7},{6,4},{7,5},{8,10},{9,11},{10,... | collective-permute-start | bytes 393224 | tf_op jit(solution)/shard_map/ppermute | solution.py:224
  48.1 5.8 %collective-permute-start.14 = (bf16[4,2,32,256]{3,2,1,0:T(8,128)(2,1)S(1)}, bf16[4,2,32,256]{3,2,1,0:T(8,128)(2,1)S(1)}, u32[]{:S(2)}, u32[]{:S(2)}) collective-permute-start(bf16[4,2,32,256]{3,2,1,0:T(8,128)(2,1)S(1)} %get-tuple-element.12), channel_id=1, source_target_pairs={{0,1},{1,0},{2,3},{3,2},{4,5},{5,4},{6,7},{7,6},{8,9},{9,8},{10,11... | collective-permute-start | bytes 393224 | tf_op jit(solution)/shard_map/ppermute | solution.py:224
  (1 other events, 0.7 us)

commit v5 on v4

v5 whole, which is shorter than its diff:
```python
import functools
import math

import jax
import jax.numpy as jnp
from jax import lax
from jax.experimental import pallas as pl
from jax.experimental.pallas import tpu as pltpu
from jax.sharding import PartitionSpec as P

HEADS = 64
KVH = 8
LOG2E = 1.4426950408889634


def attend_kernel(
    spans_ref, tail_ref, plan_ref, owner_ref, place_at_ref, *refs,
    covers, hops, parts, first_call, last_call,
    inst_size, tp_size, kv_local, per_head, head_dim, span_len, slot_count, longest,
):
    refs = list(refs)

    def take(count):
        taken = refs[:count]
        del refs[:count]
        return taken

    (q_ref,) = take(1)
    mixed_ref, total_ref = (None, None) if first_call else take(2)
    hop_refs = take(len(hops))
    part_refs = take(len(parts))
    if last_call:
        out_ref, cache_ref = take(2)
    else:
        out_ref, next_total_ref = take(2)
    place_ref, list_ref, kv_ref, s_ref, p_ref, acc_ref, max_ref, part_sems = take(8)
    if last_call:
        zero_ref, page_sems = take(2)
    step = pl.program_id(0)
    inst = place_at_ref[0]
    tp = place_at_ref[1]
    prompt_count = spans_ref.shape[0]
    span_total = slot_count * inst_size
    slice_len = span_len // tp_size
    scale = LOG2E / math.sqrt(head_dim)

    def part_copies(act):
        for n, (pieces, j) in enumerate(parts):
            at = pl.ds(pl.multiple_of((tp ^ j) * slice_len, slice_len), slice_len)
            begin = 0
            for m, (hop, first_slot, size) in enumerate(pieces):
                slots = pl.ds(place_at_ref[2 + hop] * slot_count + first_slot, size)
                act(pltpu.make_async_copy(
                    part_refs[n].at[begin:begin + size], kv_ref.at[slots, :, at],
                    part_sems.at[n, m],
                ))
                begin += size

    def cache_copies(act):
        first = jnp.int32(0)
        count = jnp.int32(0)
        start = jnp.int32(0)
        for p in range(prompt_count):
            hit = owner_ref[p] == inst
            first = jnp.where(hit, start, first)
            count = jnp.where(hit, spans_ref[p], count)
            start = start + spans_ref[p]

        def row(r, unused):
            page = place_ref[jnp.minimum(first + r, span_total - 1)]
            for n, (hop, first_slot, size) in enumerate(hops):
                source = place_at_ref[2 + hop]
                slot = page - source * slot_count - first_slot
                here = (source >= 0) & (slot >= 0) & (slot < size)

                @pl.when((r < count) & here)
                def _():
                    act(pltpu.make_async_copy(
                        hop_refs[n].at[slot], cache_ref.at[r], page_sems.at[r]
                    ))

            @pl.when(r >= count)
            def _():
                act(pltpu.make_async_copy(zero_ref, cache_ref.at[r], page_sems.at[r]))

            return unused

        lax.fori_loop(0, longest, row, 0)

    @pl.when(step == 0)
    def _():
        part_copies(lambda copy: copy.start())

        def put(g, unused):
            place_ref[plan_ref[g]] = g
            return unused

        lax.fori_loop(0, span_total, put, 0)
        if last_call:
            zero_ref[...] = jnp.zeros_like(zero_ref)
            cache_copies(lambda copy: copy.start())
        part_copies(lambda copy: copy.wait())

    own = inst * slot_count + step
    span = plan_ref[own]
    first = jnp.int32(0)
    end = jnp.int32(0)
    length = jnp.int32(0)
    for p in range(prompt_count):
        start = end
        end = end + spans_ref[p]
        inside = (span >= start) & (span < end)
        first = jnp.where(inside, start, first)
        length = jnp.where(inside, (spans_ref[p] - 1) * span_len + tail_ref[p], length)
    live_rows = length - (span - first) * span_len

    def look(k, count):
        page = place_ref[k]
        source = page // slot_count
        covered = jnp.bool_(False)
        for hop in covers:
            covered = covered | (place_at_ref[2 + hop] == source)
        list_ref[count] = page
        return count + covered.astype(jnp.int32)

    count = lax.fori_loop(first, span, look, jnp.int32(0))

    ones = jnp.ones((span_len, head_dim), jnp.bfloat16)
    row_ids = lax.broadcasted_iota(jnp.int32, (span_len, span_len), 0)
    col_ids = lax.broadcasted_iota(jnp.int32, (span_len, span_len), 1)
    causal = row_ids >= col_ids

    def rows_of(h):
        return slice(h * span_len, (h + 1) * span_len)

    def key_block(pages, g):
        return jnp.concatenate([kv_ref[page, g, :, :head_dim] for page in pages], axis=0)

    def value_block(pages, g):
        return jnp.concatenate(
            [
                jnp.concatenate([kv_ref[page, g, :, head_dim:], ones], axis=1)
                for page in pages
            ],
            axis=0,
        )

    def attend(pages, since):
        wide = len(pages) * span_len
        for g in range(kv_local):
            q = jnp.concatenate(
                [
                    q_ref[0, :, (g * per_head + h) * head_dim:(g * per_head + h + 1) * head_dim]
                    for h in range(per_head)
                ],
                axis=0,
            )
            s_ref[g, :, :wide] = lax.dot_general(
                q, key_block(pages, g), (((1,), (1,)), ((), ())),
                preferred_element_type=jnp.float32,
            )
        for g in range(kv_local):
            rescales = []
            for h in range(per_head):
                at = rows_of(h)
                s = s_ref[g, at, :wide] * scale
                if since == "start":
                    own_part = jnp.where(causal, s[:, wide - span_len:], -1e30)
                    if len(pages) > 1:
                        s = jnp.concatenate([s[:, :wide - span_len], own_part], axis=1)
                    else:
                        s = own_part
                top = jnp.max(s, axis=1, keepdims=True)
                if since == "start":
                    top = jnp.broadcast_to(top, (span_len, head_dim))
                else:
                    old = total_ref[0, g, at] if since == "given" else max_ref[g, at]
                    top = jnp.maximum(old, top)
                    rescales.append(jnp.exp2(old - top))
                max_ref[g, at] = top
                p_ref[g, at, :wide] = jnp.exp2(
                    s - jnp.concatenate([top] * len(pages), axis=1)
                ).astype(jnp.bfloat16)
            mixed = jnp.dot(
                p_ref[g, :, :wide], value_block(pages, g), preferred_element_type=jnp.float32
            )
            if since == "start":
                acc_ref[g] = mixed
                continue
            for h in range(per_head):
                at = rows_of(h)
                if since == "given":
                    old = jnp.concatenate([mixed_ref[0, g, at] * rescales[h], rescales[h]], axis=1)
                else:
                    old = acc_ref[g, at] * jnp.concatenate([rescales[h], rescales[h]], axis=1)
                acc_ref[g, at] = old + mixed[at]

    def pairs(begin):
        def pair(j, unused):
            at = begin + 2 * j
            attend([list_ref[at], list_ref[at + 1]], "here")
            return unused

        lax.fori_loop(0, (count - begin) // 2, pair, 0)

    live = lax.broadcasted_iota(jnp.int32, (span_len, head_dim), 0) < live_rows

    def put_out(g, h, mixed):
        head = g * per_head + h
        out_ref[0, :, head * head_dim:(head + 1) * head_dim] = jnp.where(
            live, mixed, 0.0
        ).astype(jnp.bfloat16)

    def finish():
        for g in range(kv_local):
            for h in range(per_head):
                at = rows_of(h)
                total = acc_ref[g, at, head_dim:]
                mixed = acc_ref[g, at, :head_dim] / total
                if last_call:
                    put_out(g, h, mixed)
                else:
                    out_ref[0, g, at] = mixed
                    next_total_ref[0, g, at] = max_ref[g, at] + jnp.log(total) * LOG2E

    if first_call:
        odd = lax.rem(count, 2)

        @pl.when(odd == 0)
        def _():
            attend([own], "start")

        @pl.when(odd == 1)
        def _():
            attend([list_ref[0], own], "start")

        pairs(odd)
        finish()
    else:
        used = 2 - lax.rem(count, 2)

        @pl.when(count == 0)
        def _():
            for g in range(kv_local):
                for h in range(per_head):
                    put_out(g, h, mixed_ref[0, g, rows_of(h)])

        @pl.when(count > 0)
        def _():
            @pl.when(used == 1)
            def _():
                attend([list_ref[0]], "given")

            @pl.when(used == 2)
            def _():
                attend([list_ref[0], list_ref[1]], "given")

            pairs(used)
            finish()

    if last_call:
        @pl.when(step == slot_count - 1)
        def _():
            cache_copies(lambda copy: copy.wait())


def after(values, earlier):
    return lax.optimization_barrier((list(values), list(earlier)))[0]


def move_pages(kv_new, kv_local, attend):
    inst_size = lax.axis_size("inst")
    tp_size = lax.axis_size("tp")
    inst = lax.axis_index("inst")
    tp = lax.axis_index("tp")
    slot_count, kv_heads = kv_new.shape[:2]
    sources = [list(range(inst_size))]
    hops = [((0, 0, slot_count), kv_new)]
    parts = []

    def along(x, pairs):
        return lax.ppermute(x, "inst", pairs)

    def exchange(*pieces):
        names = [name for name, _ in pieces]
        found = []
        for j in range(tp_size):
            head = ((tp ^ j) * kv_heads) // tp_size
            sent = [lax.dynamic_slice_in_dim(x, head, kv_local, 1) for _, x in pieces]
            sent = jnp.concatenate(sent, axis=0) if len(sent) > 1 else sent[0]
            if j:
                sent = lax.ppermute(sent, "tp", [(t, t ^ j) for t in range(tp_size)])
            found.append(((names, j), sent))
        parts.extend(found)
        return [x for _, x in found]

    if inst_size != 4:
        exchange(hops[0])
        for s in range(1, inst_size):
            sources.append([(i - s) % inst_size for i in range(inst_size)])
            pairs = [(i, (i + s) % inst_size) for i in range(inst_size)]
            hops.append(((s, 0, slot_count), along(kv_new, pairs)))
            exchange(hops[-1])
        return [], (list(range(inst_size)), parts, sources), hops

    middle = (inst == 1) | (inst == 2)
    sources += [[1, 0, 3, 2], [-1, 2, 1, -1], [-1, 3, 0, -1], [2, -1, -1, 1], [3, -1, -1, 0]]
    second, third = 6, 7
    sources += [[2, 2, 1, 1], [3, 3, 0, 0]]
    whole = slot_count
    half = slot_count // 2
    outer = along(kv_new, [(0, 1), (1, 0), (2, 3), (3, 2)])
    inner = along(kv_new, [(1, 2), (2, 1)])
    waiting = exchange(hops[0])
    outer_on, inner_on = after([outer, inner], waiting)
    crossed = along(outer_on, [(1, 2), (2, 1)])
    inner_ends = along(inner_on, [(1, 0), (2, 3)])
    waiting = exchange(((1, 0, whole), outer_on))
    early = len(parts)
    state = attend([0, 1], parts, sources)
    crossed_on = after([crossed], waiting)[0]
    crossed_half = lax.optimization_barrier([crossed_on[:half], crossed_on[half:]])
    crossed_ends = [along(x, [(1, 0), (2, 3)]) for x in crossed_half]
    two = jnp.where(middle, inner, inner_ends)
    waiting = exchange(((second, 0, whole), two))
    waiting = waiting + list(state)
    for n in range(2):
        three = jnp.where(middle, crossed_half[n], crossed_ends[n])
        three = after([three], waiting)[0]
        exchange(((third, n * half, half), three))
        hops.append(((5, n * half, half), crossed_ends[n]))
    for hop, x in enumerate((outer, inner, crossed, inner_ends), 1):
        hops.append(((hop, 0, whole), x))
    return state, ([second, third], parts[early:], sources), hops


def body(queries, kv_new, prompt_spans, prompt_tail, span_plan, decode_owner):
    tp_size = lax.axis_size("tp")
    inst_size = lax.axis_size("inst")
    tp_index = lax.axis_index("tp")
    inst_index = lax.axis_index("inst")
    slot_count, span_len, row_width = queries.shape
    kv_heads, slice_len, width = kv_new.shape[1:]
    head_dim = width // 2
    local_heads = row_width // head_dim
    kv_local = max(1, kv_heads // tp_size)
    per_head = local_heads // kv_local
    span_total = slot_count * inst_size
    longest = span_total // 2
    anywhere = pl.BlockSpec(memory_space=pl.ANY)
    by_slot = pl.BlockSpec((1, span_len, row_width), lambda i, *_: (i, 0, 0))
    rows = per_head * span_len
    state_shape = (slot_count, kv_local, rows, head_dim)
    state_spec = pl.BlockSpec((1,) + state_shape[1:], lambda i, *_: (i, 0, 0, 0))
    work = slot_count * 4 * local_heads * span_len * span_len

    def attend(covers, parts, sources, state=(), hops=None):
        first_call, last_call = not state, hops is not None
        hops = hops or []
        own_sources = lax.dynamic_index_in_dim(
            jnp.asarray(sources, jnp.int32), inst_index, 1, False
        )
        numbers = (
            prompt_spans, prompt_tail, span_plan, decode_owner,
            jnp.concatenate([jnp.stack([inst_index, tp_index]).astype(jnp.int32), own_sources]),
        )
        kernel = functools.partial(
            attend_kernel,
            covers=covers,
            hops=[name for name, _ in hops],
            parts=[name for name, _ in parts],
            first_call=first_call,
            last_call=last_call,
            inst_size=inst_size,
            tp_size=tp_size,
            kv_local=kv_local,
            per_head=per_head,
            head_dim=head_dim,
            span_len=span_len,
            slot_count=slot_count,
            longest=longest,
        )
        scratch = [
            pltpu.SMEM((span_total,), jnp.int32),
            pltpu.SMEM((span_total,), jnp.int32),
            pltpu.VMEM((span_total, kv_local, span_len, width), jnp.bfloat16),
            pltpu.VMEM((kv_local, rows, 2 * span_len), jnp.float32),
            pltpu.VMEM((kv_local, rows, 2 * span_len), jnp.bfloat16),
            pltpu.VMEM((kv_local, rows, 2 * head_dim), jnp.float32),
            pltpu.VMEM((kv_local, rows, head_dim), jnp.float32),
            pltpu.SemaphoreType.DMA((len(parts), max(len(x[0][0]) for x in parts))),
        ]
        if last_call:
            scratch += [
                pltpu.VMEM((kv_heads, slice_len, width), jnp.bfloat16),
                pltpu.SemaphoreType.DMA((longest,)),
            ]
            out_specs = [by_slot, anywhere]
            out_shape = [
                jax.ShapeDtypeStruct(queries.shape, jnp.bfloat16),
                jax.ShapeDtypeStruct((longest, kv_heads, slice_len, width), jnp.bfloat16),
            ]
        else:
            out_specs = [state_spec] * 2
            out_shape = [jax.ShapeDtypeStruct(state_shape, jnp.float32)] * 2
        return pl.pallas_call(
            kernel,
            grid_spec=pltpu.PrefetchScalarGridSpec(
                num_scalar_prefetch=len(numbers),
                grid=(slot_count,),
                in_specs=[by_slot] + [state_spec] * len(state)
                + [anywhere] * (len(hops) + len(parts)),
                out_specs=out_specs,
                scratch_shapes=scratch,
            ),
            out_shape=out_shape,
            cost_estimate=pl.CostEstimate(
                flops=4 * work * head_dim, bytes_accessed=8 << 20, transcendentals=work
            ),
            compiler_params=pltpu.CompilerParams(vmem_limit_bytes=40 << 20),
        )(
            *numbers, queries, *state, *[x for _, x in hops], *[x for _, x in parts],
        )

    state, left, hops = move_pages(kv_new, kv_local, attend)
    return tuple(attend(*left, state, hops))


def solution(mesh):
    placed = (
        P(("groups", "inst"), None, "tp"),
        P(("groups", "inst"), None, "tp", None),
        P("groups"),
        P("groups"),
        P("groups"),
        P("groups"),
    )
    return jax.shard_map(
        body,
        mesh=mesh,
        in_specs=placed,
        out_specs=(P(("groups", "inst"), None, "tp"), P(("groups", "inst"), None, "tp", None)),
        check_vma=False,
    )
```

time: 66.3 us -> 78.5 us (1.18)
  the two profiles are of different devices: /device:TPU:5 before, /device:TPU:0 now
where the time goes in v5:
time: 78.5 us; the launch traced here: 79 us
  waiting for transfers between devices  36.2 us (46%)
  starting transfers between devices  17.9 us (23%)
  Pallas kernels  15.6 us (20%)
  local copies, waits for them, and re-layouts  8.18 us (10%)
  between operations  0.91 us (1%)
    ppermute x6, waiting for transfers between devices, along(): return lax.ppermute(x, 'inst', pairs)  20.3 us
    ppermute x15, waiting for transfers between devices, exchange(): sent = lax.ppermute(sent, 'tp', [(t, t ^ j) for t in range(tp_size)])  15.9 us
    pallas_call x2, Pallas kernels, attend(): pl.pallas_call(kernel, grid_spec=pltpu.PrefetchScalarGridSpec(num_scalar_...  15.6 us
    ppermute x15, starting transfers between devices, exchange(): sent = lax.ppermute(sent, 'tp', [(t, t ^ j) for t in range(tp_size)])  9.42 us
    ppermute x6, starting transfers between devices, along(): return lax.ppermute(x, 'inst', pairs)  8.45 us
    unnamed x14, local copies, waits for them, and re-layouts  6.17 us
  transfers between devices with their start and end apart: 21, of which 10 were waited for; matrix products, arithmetic and copies ran while one was open for 3% of the time, Pallas kernels for 8%

profile of v5, /device:TPU:0, one launch (start us, length us, event | category | flops | bytes accessed | tf_op | source)
XLA Modules:
  0.0 79.0 jit_solution(17595141302661389590)
XLA Ops:
  0.6 3.1 %collective-permute-start.3 = (bf16[4,8,32,256]{3,2,1,0:T(8,128)(2,1)}, bf16[4,8,32,256]{3,2,1,0:T(8,128)(2,1)S(1)}, u32[]{:S(2)}, u32[]{:S(2)}) collective-permute-start(bf16[4,8,32,256]{3,2,1,0:T(8,128)(2,1)} %refs_3_.1), channel_id=1, source_target_pairs={{0,4},{4,0},{8,12},{12,8},{1,5},{5,1},{9,13},{13,9},{2,6},{6,2},{1... | collective-permute-start | bytes 1572872 | tf_op jit(solution)/shard_map/ppermute | solution.py:282
  4.5 1.1 %constant_dynamic-slice_fusion.15 = (bf16[4,2,32,256]{3,2,1,0:T(8,128)(2,1)S(1)}, bf16[4,2,32,256]{3,2,1,0:T(8,128)(2,1)S(1)}, bf16[4,2,32,256]{3,2,1,0:T(8,128)(2,1)S(1)}, bf16[4,2,32,256]{3,2,1,0:T(8,128)(2,1)S(1)}) fusion(bf16[4,8,32,256]{3,2,1,0:T(8,128)(2,1)} %refs_3_.1, s32[]{:T(128)S(6)} %select_n.91, s32[]{:T(128)S(6)} %select_n.89, ...), kind=kLoop, calls=%fused_computation.18 | loop fusion | bytes 1048592 | tf_op jit(solution)/shard_map/dynamic_slice | solution.py:289
  6.4 0.9 %collective-permute-start.1 = (bf16[4,2,32,256]{3,2,1,0:T(8,128)(2,1)S(1)}, bf16[4,2,32,256]{3,2,1,0:T(8,128)(2,1)S(1)}, u32[]{:S(2)}, u32[]{:S(2)}) collective-permute-start(bf16[4,2,32,256]{3,2,1,0:T(8,128)(2,1)S(1)} %get-tuple-element.31), channel_id=1, source_target_pairs={{0,2},{1,3},{2,0},{3,1},{4,6},{5,7},{6,4},{7,5},{8,10},{9,11},{10,... | collective-permute-start | bytes 393224 | tf_op jit(solution)/shard_map/ppermute | solution.py:292
  7.6 3.9 %collective-permute-done.2.refs_4_ = bf16[4,2,32,256]{3,2,1,0:T(8,128)(2,1)S(1)} collective-permute-done((bf16[4,2,32,256]{3,2,1,0:T(8,128)(2,1)S(1)}, bf16[4,2,32,256]{3,2,1,0:T(8,128)(2,1)S(1)}, u32[]{:S(2)}, u32[]{:S(2)}) %collective-permute-start.2) | collective-permute-done | bytes 131104 | tf_op jit(solution)/shard_map/ppermute | solution.py:292
  11.5 2.9 %collective-permute-done.1.refs_3_ = bf16[4,2,32,256]{3,2,1,0:T(8,128)(2,1)S(1)} collective-permute-done((bf16[4,2,32,256]{3,2,1,0:T(8,128)(2,1)S(1)}, bf16[4,2,32,256]{3,2,1,0:T(8,128)(2,1)S(1)}, u32[]{:S(2)}, u32[]{:S(2)}) %collective-permute-start.1) | collective-permute-done | bytes 131104 | tf_op jit(solution)/shard_map/ppermute | solution.py:292
  14.3 1.5 %collective-permute-done.3.refs_6_ = bf16[4,8,32,256]{3,2,1,0:T(8,128)(2,1)S(1)} collective-permute-done((bf16[4,8,32,256]{3,2,1,0:T(8,128)(2,1)}, bf16[4,8,32,256]{3,2,1,0:T(8,128)(2,1)S(1)}, u32[]{:S(2)}, u32[]{:S(2)}) %collective-permute-start.3) | collective-permute-done | bytes 524320 | tf_op jit(solution)/shard_map/ppermute | solution.py:282
  16.9 1.5 %collective-permute-start.6 = (bf16[4,2,32,256]{3,2,1,0:T(8,128)(2,1)S(1)}, bf16[4,2,32,256]{3,2,1,0:T(8,128)(2,1)S(1)}, u32[]{:S(2)}, u32[]{:S(2)}) collective-permute-start(bf16[4,2,32,256]{3,2,1,0:T(8,128)(2,1)S(1)} %get-tuple-element.27), channel_id=1, source_target_pairs={{0,2},{1,3},{2,0},{3,1},{4,6},{5,7},{6,4},{7,5},{8,10},{9,11},{10,... | collective-permute-start | bytes 393224 | tf_op jit(solution)/shard_map/ppermute | solution.py:292
  19.2 1.3 %collective-permute-start.11 = (bf16[4,8,32,256]{3,2,1,0:T(8,128)(2,1)S(1)}, bf16[4,8,32,256]{3,2,1,0:T(8,128)(2,1)S(1)}, u32[]{:S(2)}, u32[]{:S(2)}) collective-permute-start(bf16[4,8,32,256]{3,2,1,0:T(8,128)(2,1)S(1)} %collective-permute-done.4.refs_7_), channel_id=1, source_target_pairs={{4,0},{8,12},{5,1},{9,13},{6,2},{10,14},{7,3},{11,15},{20,16},{24,... | collective-permute-start | bytes 1572872 | tf_op jit(solution)/shard_map/ppermute | solution.py:282
  20.6 1.7 %collective-permute-done.7.refs_8_ = bf16[4,2,32,256]{3,2,1,0:T(8,128)(2,1)S(1)} collective-permute-done((bf16[4,2,32,256]{3,2,1,0:T(8,128)(2,1)S(1)}, bf16[4,2,32,256]{3,2,1,0:T(8,128)(2,1)S(1)}, u32[]{:S(2)}, u32[]{:S(2)}) %collective-permute-start.7) | collective-permute-done | bytes 131104 | tf_op jit(solution)/shard_map/ppermute | solution.py:292
  22.3 3.0 %collective-permute-done.6.refs_7_ = bf16[4,2,32,256]{3,2,1,0:T(8,128)(2,1)S(1)} collective-permute-done((bf16[4,2,32,256]{3,2,1,0:T(8,128)(2,1)S(1)}, bf16[4,2,32,256]{3,2,1,0:T(8,128)(2,1)S(1)}, u32[]{:S(2)}, u32[]{:S(2)}) %collective-permute-start.6) | collective-permute-done | bytes 131104 | tf_op jit(solution)/shard_map/ppermute | solution.py:292
  25.3 1.6 %copy-done.1 = bf16[4,128,2048]{2,1,0:T(8,128)(2,1)S(1)} copy-done((bf16[4,128,2048]{2,1,0:T(8,128)(2,1)S(1)}, bf16[4,128,2048]{2,1,0:T(8,128)(2,1)}, u32[]{:S(2)}) %copy-start.1) | copy-done | bytes 2097176
  29.5 6.5 %shard_map.95 = (f32[4,2,1024,128]{3,2,1,0:T(8,128)S(1)}, f32[4,2,1024,128]{3,2,1,0:T(8,128)S(1)}) custom-call(s32[4]{0:T(128)S(1)} %copy-done.3, s32[4]{0:T(128)S(1)} %copy-done.4, s32[16]{0:T(128)S(1)} %copy-done.5, s32[4]{0:T(128)S(1)} %copy-done.6, s32[10]{0:T(128)S(1)} %pad_add_fusion.place_at_ref, bf16[4,128,2048]{2,1,0:T(8,128)(2,1)S(1)} %copy-done.1, ...), custom_call_target="tpu_custom_call" | custom-call | flops 2147483648 | bytes 8388608 | tf_op jit(solution)/shard_map/pallas_call | solution.py:406
  36.1 1.9 %copy-done = f32[4,2,1024,128]{3,2,1,0:T(8,128)} copy-done((f32[4,2,1024,128]{3,2,1,0:T(8,128)}, f32[4,2,1024,128]{3,2,1,0:T(8,128)S(1)}, u32[]{:S(2)}) %copy-start) | copy-done | bytes 4194328
  38.1 1.4 %collective-permute-start.9 = (bf16[2,8,32,256]{3,2,1,0:T(8,128)(2,1)S(1)}, bf16[2,8,32,256]{3,2,1,0:T(8,128)(2,1)S(1)}, u32[]{:S(2)}, u32[]{:S(2)}) collective-permute-start(bf16[2,8,32,256]{3,2,1,0:T(8,128)(2,1)S(1)} %get-tuple-element.15), channel_id=1, source_target_pairs={{4,0},{8,12},{5,1},{9,13},{6,2},{10,14},{7,3},{11,15},{20,16},{24,... | collective-permute-start | bytes 786440 | tf_op jit(solution)/shard_map/ppermute | solution.py:282
  39.5 1.3 %collective-permute-start.10 = (bf16[2,8,32,256]{3,2,1,0:T(8,128)(2,1)S(1)}, bf16[2,8,32,256]{3,2,1,0:T(8,128)(2,1)S(1)}, u32[]{:S(2)}, u32[]{:S(2)}) collective-permute-start(bf16[2,8,32,256]{3,2,1,0:T(8,128)(2,1)S(1)} %get-tuple-element.16), channel_id=1, source_target_pairs={{4,0},{8,12},{5,1},{9,13},{6,2},{10,14},{7,3},{11,15},{20,16},{24,... | collective-permute-start | bytes 786440 | tf_op jit(solution)/shard_map/ppermute | solution.py:282
  41.2 1.3 %collective-permute-start.13 = (bf16[4,2,32,256]{3,2,1,0:T(8,128)(2,1)S(1)}, bf16[4,2,32,256]{3,2,1,0:T(8,128)(2,1)S(1)}, u32[]{:S(2)}, u32[]{:S(2)}) collective-permute-start(bf16[4,2,32,256]{3,2,1,0:T(8,128)(2,1)S(1)} %get-tuple-element.21), channel_id=1, source_target_pairs={{0,2},{1,3},{2,0},{3,1},{4,6},{5,7},{6,4},{7,5},{8,10},{9,11},{10,... | collective-permute-start | bytes 393224 | tf_op jit(solution)/shard_map/ppermute | solution.py:292
  42.9 18.8 %collective-permute-done.10.refs_5_ = bf16[2,8,32,256]{3,2,1,0:T(8,128)(2,1)S(1)} collective-permute-done((bf16[2,8,32,256]{3,2,1,0:T(8,128)(2,1)S(1)}, bf16[2,8,32,256]{3,2,1,0:T(8,128)(2,1)S(1)}, u32[]{:S(2)}, u32[]{:S(2)}) %collective-permute-start.10) | collective-permute-done | bytes 262176 | tf_op jit(solution)/shard_map/ppermute | solution.py:282
  61.9 1.2 %collective-permute-start.16 = (bf16[2,2,32,256]{3,2,1,0:T(8,128)(2,1)S(1)}, bf16[2,2,32,256]{3,2,1,0:T(8,128)(2,1)S(1)}, u32[]{:S(2)}, u32[]{:S(2)}) collective-permute-start(bf16[2,2,32,256]{3,2,1,0:T(8,128)(2,1)S(1)} %get-tuple-element.39), channel_id=1, source_target_pairs={{0,2},{1,3},{2,0},{3,1},{4,6},{5,7},{6,4},{7,5},{8,10},{9,11},{10,... | collective-permute-start | bytes 196616 | tf_op jit(solution)/shard_map/ppermute | solution.py:292
  64.2 1.3 %collective-permute-start.19 = (bf16[2,2,32,256]{3,2,1,0:T(8,128)(2,1)S(1)}, bf16[2,2,32,256]{3,2,1,0:T(8,128)(2,1)S(1)}, u32[]{:S(2)}, u32[]{:S(2)}) collective-permute-start(bf16[2,2,32,256]{3,2,1,0:T(8,128)(2,1)S(1)} %get-tuple-element.35), channel_id=1, source_target_pairs={{0,2},{1,3},{2,0},{3,1},{4,6},{5,7},{6,4},{7,5},{8,10},{9,11},{10,... | collective-permute-start | bytes 196616 | tf_op jit(solution)/shard_map/ppermute | solution.py:292
  65.5 0.8 %collective-permute-done.17.refs_17_ = bf16[2,2,32,256]{3,2,1,0:T(8,128)(2,1)S(1)} collective-permute-done((bf16[2,2,32,256]{3,2,1,0:T(8,128)(2,1)S(1)}, bf16[2,2,32,256]{3,2,1,0:T(8,128)(2,1)S(1)}, u32[]{:S(2)}, u32[]{:S(2)}) %collective-permute-start.17) | collective-permute-done | bytes 65568 | tf_op jit(solution)/shard_map/ppermute | solution.py:292
  66.3 0.8 %collective-permute-done.16.refs_16_ = bf16[2,2,32,256]{3,2,1,0:T(8,128)(2,1)S(1)} collective-permute-done((bf16[2,2,32,256]{3,2,1,0:T(8,128)(2,1)S(1)}, bf16[2,2,32,256]{3,2,1,0:T(8,128)(2,1)S(1)}, u32[]{:S(2)}, u32[]{:S(2)}) %collective-permute-start.16) | collective-permute-done | bytes 65568 | tf_op jit(solution)/shard_map/ppermute | solution.py:292
  67.1 2.0 %collective-permute-done.20.refs_21_ = bf16[2,2,32,256]{3,2,1,0:T(8,128)(2,1)S(1)} collective-permute-done((bf16[2,2,32,256]{3,2,1,0:T(8,128)(2,1)S(1)}, bf16[2,2,32,256]{3,2,1,0:T(8,128)(2,1)S(1)}, u32[]{:S(2)}, u32[]{:S(2)}) %collective-permute-start.20) | collective-permute-done | bytes 65568 | tf_op jit(solution)/shard_map/ppermute | solution.py:292
  69.1 0.8 %collective-permute-done.19.refs_20_ = bf16[2,2,32,256]{3,2,1,0:T(8,128)(2,1)S(1)} collective-permute-done((bf16[2,2,32,256]{3,2,1,0:T(8,128)(2,1)S(1)}, bf16[2,2,32,256]{3,2,1,0:T(8,128)(2,1)S(1)}, u32[]{:S(2)}, u32[]{:S(2)}) %collective-permute-start.19) | collective-permute-done | bytes 65568 | tf_op jit(solution)/shard_map/ppermute | solution.py:292
  70.0 9.1 %shard_map.96 = (bf16[4,128,2048]{2,1,0:T(8,128)(2,1)}, bf16[8,8,32,256]{3,2,1,0:T(8,128)(2,1)}) custom-call(s32[4]{0:T(128)S(1)} %copy-done.3, s32[4]{0:T(128)S(1)} %copy-done.4, s32[16]{0:T(128)S(1)} %copy-done.5, s32[4]{0:T(128)S(1)} %copy-done.6, s32[10]{0:T(128)S(1)} %pad_add_fusion.place_at_ref, bf16[4,128,2048]{2,1,0:T(8,128)(2,1)S(1)} %copy-done.1, ...), custom_call_target="tpu_custom_call" | custom-call | flops 2147483648 | bytes 8388608 | tf_op jit(solution)/shard_map/pallas_call | solution.py:406
  (45 shorter events, 8.3 us)
Async XLA Ops:
  0.6 15.2 %collective-permute-start.3 = (bf16[4,8,32,256]{3,2,1,0:T(8,128)(2,1)}, bf16[4,8,32,256]{3,2,1,0:T(8,128)(2,1)S(1)}, u32[]{:S(2)}, u32[]{:S(2)}) collective-permute-start(bf16[4,8,32,256]{3,2,1,0:T(8,128)(2,1)} %refs_3_.1), channel_id=1, source_target_pairs={{0,4},{4,0},{8,12},{12,8},{1,5},{5,1},{9,13},{13,9},{2,6},{6,2},{1... | collective-permute-start | bytes 1572872 | tf_op jit(solution)/shard_map/ppermute | solution.py:282
  3.7 12.1 %collective-permute-start.4 = (bf16[4,8,32,256]{3,2,1,0:T(8,128)(2,1)}, bf16[4,8,32,256]{3,2,1,0:T(8,128)(2,1)S(1)}, u32[]{:S(2)}, u32[]{:S(2)}) collective-permute-start(bf16[4,8,32,256]{3,2,1,0:T(8,128)(2,1)} %refs_3_.1), channel_id=1, source_target_pairs={{4,8},{8,4},{5,9},{9,5},{6,10},{10,6},{7,11},{11,7},{20,24},{24,20... | collective-permute-start | bytes 1572872 | tf_op jit(solution)/shard_map/ppermute | solution.py:282
  5.7 5.8 %collective-permute-start.2 = (bf16[4,2,32,256]{3,2,1,0:T(8,128)(2,1)S(1)}, bf16[4,2,32,256]{3,2,1,0:T(8,128)(2,1)S(1)}, u32[]{:S(2)}, u32[]{:S(2)}) collective-permute-start(bf16[4,2,32,256]{3,2,1,0:T(8,128)(2,1)S(1)} %get-tuple-element.30), channel_id=1, source_target_pairs={{0,3},{1,2},{2,1},{3,0},{4,7},{5,6},{6,5},{7,4},{8,11},{9,10},{10,... | collective-permute-start | bytes 393224 | tf_op jit(solution)/shard_map/ppermute | solution.py:292
  6.4 8.0 %collective-permute-start.1 = (bf16[4,2,32,256]{3,2,1,0:T(8,128)(2,1)S(1)}, bf16[4,2,32,256]{3,2,1,0:T(8,128)(2,1)S(1)}, u32[]{:S(2)}, u32[]{:S(2)}) collective-permute-start(bf16[4,2,32,256]{3,2,1,0:T(8,128)(2,1)S(1)} %get-tuple-element.31), channel_id=1, source_target_pairs={{0,2},{1,3},{2,0},{3,1},{4,6},{5,7},{6,4},{7,5},{8,10},{9,11},{10,... | collective-permute-start | bytes 393224 | tf_op jit(solution)/shard_map/ppermute | solution.py:292
  7.3 7.0 %collective-permute-start = (bf16[4,2,32,256]{3,2,1,0:T(8,128)(2,1)S(1)}, bf16[4,2,32,256]{3,2,1,0:T(8,128)(2,1)S(1)}, u32[]{:S(2)}, u32[]{:S(2)}) collective-permute-start(bf16[4,2,32,256]{3,2,1,0:T(8,128)(2,1)S(1)} %get-tuple-element.32), channel_id=1, source_target_pairs={{0,1},{1,0},{2,3},{3,2},{4,5},{5,4},{6,7},{7,6},{8,9},{9,8},{10,11... | collective-permute-start | bytes 393224 | tf_op jit(solution)/shard_map/ppermute | solution.py:292
  15.9 22.2 %collective-permute-start.8 = (bf16[4,8,32,256]{3,2,1,0:T(8,128)(2,1)S(1)}, bf16[4,8,32,256]{3,2,1,0:T(8,128)(2,1)S(1)}, u32[]{:S(2)}, u32[]{:S(2)}) collective-permute-start(bf16[4,8,32,256]{3,2,1,0:T(8,128)(2,1)S(1)} %collective-permute-done.3.refs_6_), channel_id=1, source_target_pairs={{4,8},{8,4},{5,9},{9,5},{6,10},{10,6},{7,11},{11,7},{20,24},{24,20... | collective-permute-start | bytes 1572872 | tf_op jit(solution)/shard_map/ppermute | solution.py:282
  16.6 5.7 %collective-permute-start.7 = (bf16[4,2,32,256]{3,2,1,0:T(8,128)(2,1)S(1)}, bf16[4,2,32,256]{3,2,1,0:T(8,128)(2,1)S(1)}, u32[]{:S(2)}, u32[]{:S(2)}) collective-permute-start(bf16[4,2,32,256]{3,2,1,0:T(8,128)(2,1)S(1)} %get-tuple-element.26), channel_id=1, source_target_pairs={{0,3},{1,2},{2,1},{3,0},{4,7},{5,6},{6,5},{7,4},{8,11},{9,10},{10,... | collective-permute-start | bytes 393224 | tf_op jit(solution)/shard_map/ppermute | solution.py:292
  16.9 8.4 %collective-permute-start.6 = (bf16[4,2,32,256]{3,2,1,0:T(8,128)(2,1)S(1)}, bf16[4,2,32,256]{3,2,1,0:T(8,128)(2,1)S(1)}, u32[]{:S(2)}, u32[]{:S(2)}) collective-permute-start(bf16[4,2,32,256]{3,2,1,0:T(8,128)(2,1)S(1)} %get-tuple-element.27), channel_id=1, source_target_pairs={{0,2},{1,3},{2,0},{3,1},{4,6},{5,7},{6,4},{7,5},{8,10},{9,11},{10,... | collective-permute-start | bytes 393224 | tf_op jit(solution)/shard_map/ppermute | solution.py:292
  18.4 6.9 %collective-permute-start.5 = (bf16[4,2,32,256]{3,2,1,0:T(8,128)(2,1)S(1)}, bf16[4,2,32,256]{3,2,1,0:T(8,128)(2,1)S(1)}, u32[]{:S(2)}, u32[]{:S(2)}) collective-permute-start(bf16[4,2,32,256]{3,2,1,0:T(8,128)(2,1)S(1)} %get-tuple-element.28), channel_id=1, source_target_pairs={{0,1},{1,0},{2,3},{3,2},{4,5},{5,4},{6,7},{7,6},{8,9},{9,8},{10,11... | collective-permute-start | bytes 393224 | tf_op jit(solution)/shard_map/ppermute | solution.py:292
  19.2 21.6 %collective-permute-start.11 = (bf16[4,8,32,256]{3,2,1,0:T(8,128)(2,1)S(1)}, bf16[4,8,32,256]{3,2,1,0:T(8,128)(2,1)S(1)}, u32[]{:S(2)}, u32[]{:S(2)}) collective-permute-start(bf16[4,8,32,256]{3,2,1,0:T(8,128)(2,1)S(1)} %collective-permute-done.4.refs_7_), channel_id=1, source_target_pairs={{4,0},{8,12},{5,1},{9,13},{6,2},{10,14},{7,3},{11,15},{20,16},{24,... | collective-permute-start | bytes 1572872 | tf_op jit(solution)/shard_map/ppermute | solution.py:282
  25.3 1.6 %copy-start.1 = (bf16[4,128,2048]{2,1,0:T(8,128)(2,1)S(1)}, bf16[4,128,2048]{2,1,0:T(8,128)(2,1)}, u32[]{:S(2)}) copy-start(bf16[4,128,2048]{2,1,0:T(8,128)(2,1)} %refs_0_.3) | copy-start | bytes 6291460
  36.1 2.0 %copy-start = (f32[4,2,1024,128]{3,2,1,0:T(8,128)}, f32[4,2,1024,128]{3,2,1,0:T(8,128)S(1)}, u32[]{:S(2)}) copy-start(f32[4,2,1024,128]{3,2,1,0:T(8,128)S(1)} %get-tuple-element.13.refs_2_) | copy-start | bytes 12582916
  38.0 31.9 %copy-start.2 = (bf16[4,8,32,256]{3,2,1,0:T(8,128)(2,1)S(1)}, bf16[4,8,32,256]{3,2,1,0:T(8,128)(2,1)}, u32[]{:S(2)}) copy-start(bf16[4,8,32,256]{3,2,1,0:T(8,128)(2,1)} %refs_3_.1) | copy-start | bytes 1572868
  38.1 23.7 %collective-permute-start.9 = (bf16[2,8,32,256]{3,2,1,0:T(8,128)(2,1)S(1)}, bf16[2,8,32,256]{3,2,1,0:T(8,128)(2,1)S(1)}, u32[]{:S(2)}, u32[]{:S(2)}) collective-permute-start(bf16[2,8,32,256]{3,2,1,0:T(8,128)(2,1)S(1)} %get-tuple-element.15), channel_id=1, source_target_pairs={{4,0},{8,12},{5,1},{9,13},{6,2},{10,14},{7,3},{11,15},{20,16},{24,... | collective-permute-start | bytes 786440 | tf_op jit(solution)/shard_map/ppermute | solution.py:282
  39.5 22.2 %collective-permute-start.10 = (bf16[2,8,32,256]{3,2,1,0:T(8,128)(2,1)S(1)}, bf16[2,8,32,256]{3,2,1,0:T(8,128)(2,1)S(1)}, u32[]{:S(2)}, u32[]{:S(2)}) collective-permute-start(bf16[2,8,32,256]{3,2,1,0:T(8,128)(2,1)S(1)} %get-tuple-element.16), channel_id=1, source_target_pairs={{4,0},{8,12},{5,1},{9,13},{6,2},{10,14},{7,3},{11,15},{20,16},{24,... | collective-permute-start | bytes 786440 | tf_op jit(solution)/shard_map/ppermute | solution.py:282
  40.9 20.8 %collective-permute-start.14 = (bf16[4,2,32,256]{3,2,1,0:T(8,128)(2,1)S(1)}, bf16[4,2,32,256]{3,2,1,0:T(8,128)(2,1)S(1)}, u32[]{:S(2)}, u32[]{:S(2)}) collective-permute-start(bf16[4,2,32,256]{3,2,1,0:T(8,128)(2,1)S(1)} %get-tuple-element.20), channel_id=1, source_target_pairs={{0,3},{1,2},{2,1},{3,0},{4,7},{5,6},{6,5},{7,4},{8,11},{9,10},{10,... | collective-permute-start | bytes 393224 | tf_op jit(solution)/shard_map/ppermute | solution.py:292
  41.2 20.5 %collective-permute-start.13 = (bf16[4,2,32,256]{3,2,1,0:T(8,128)(2,1)S(1)}, bf16[4,2,32,256]{3,2,1,0:T(8,128)(2,1)S(1)}, u32[]{:S(2)}, u32[]{:S(2)}) collective-permute-start(bf16[4,2,32,256]{3,2,1,0:T(8,128)(2,1)S(1)} %get-tuple-element.21), channel_id=1, source_target_pairs={{0,2},{1,3},{2,0},{3,1},{4,6},{5,7},{6,4},{7,5},{8,10},{9,11},{10,... | collective-permute-start | bytes 393224 | tf_op jit(solution)/shard_map/ppermute | solution.py:292
  42.5 19.2 %collective-permute-start.12 = (bf16[4,2,32,256]{3,2,1,0:T(8,128)(2,1)S(1)}, bf16[4,2,32,256]{3,2,1,0:T(8,128)(2,1)S(1)}, u32[]{:S(2)}, u32[]{:S(2)}) collective-permute-start(bf16[4,2,32,256]{3,2,1,0:T(8,128)(2,1)S(1)} %get-tuple-element.22), channel_id=1, source_target_pairs={{0,1},{1,0},{2,3},{3,2},{4,5},{5,4},{6,7},{7,6},{8,9},{9,8},{10,11... | collective-permute-start | bytes 393224 | tf_op jit(solution)/shard_map/ppermute | solution.py:292
  61.8 4.5 %collective-permute-start.17 = (bf16[2,2,32,256]{3,2,1,0:T(8,128)(2,1)S(1)}, bf16[2,2,32,256]{3,2,1,0:T(8,128)(2,1)S(1)}, u32[]{:S(2)}, u32[]{:S(2)}) collective-permute-start(bf16[2,2,32,256]{3,2,1,0:T(8,128)(2,1)S(1)} %get-tuple-element.38), channel_id=1, source_target_pairs={{0,3},{1,2},{2,1},{3,0},{4,7},{5,6},{6,5},{7,4},{8,11},{9,10},{10,... | collective-permute-start | bytes 196616 | tf_op jit(solution)/shard_map/ppermute | solution.py:292
  61.9 5.2 %collective-permute-start.16 = (bf16[2,2,32,256]{3,2,1,0:T(8,128)(2,1)S(1)}, bf16[2,2,32,256]{3,2,1,0:T(8,128)(2,1)S(1)}, u32[]{:S(2)}, u32[]{:S(2)}) collective-permute-start(bf16[2,2,32,256]{3,2,1,0:T(8,128)(2,1)S(1)} %get-tuple-element.39), channel_id=1, source_target_pairs={{0,2},{1,3},{2,0},{3,1},{4,6},{5,7},{6,4},{7,5},{8,10},{9,11},{10,... | collective-permute-start | bytes 196616 | tf_op jit(solution)/shard_map/ppermute | solution.py:292
  63.1 4.1 %collective-permute-start.15 = (bf16[2,2,32,256]{3,2,1,0:T(8,128)(2,1)S(1)}, bf16[2,2,32,256]{3,2,1,0:T(8,128)(2,1)S(1)}, u32[]{:S(2)}, u32[]{:S(2)}) collective-permute-start(bf16[2,2,32,256]{3,2,1,0:T(8,128)(2,1)S(1)} %get-tuple-element.40), channel_id=1, source_target_pairs={{0,1},{1,0},{2,3},{3,2},{4,5},{5,4},{6,7},{7,6},{8,9},{9,8},{10,11... | collective-permute-start | bytes 196616 | tf_op jit(solution)/shard_map/ppermute | solution.py:292
  63.8 5.3 %collective-permute-start.20 = (bf16[2,2,32,256]{3,2,1,0:T(8,128)(2,1)S(1)}, bf16[2,2,32,256]{3,2,1,0:T(8,128)(2,1)S(1)}, u32[]{:S(2)}, u32[]{:S(2)}) collective-permute-start(bf16[2,2,32,256]{3,2,1,0:T(8,128)(2,1)S(1)} %get-tuple-element.34), channel_id=1, source_target_pairs={{0,3},{1,2},{2,1},{3,0},{4,7},{5,6},{6,5},{7,4},{8,11},{9,10},{10,... | collective-permute-start | bytes 196616 | tf_op jit(solution)/shard_map/ppermute | solution.py:292
  64.2 5.7 %collective-permute-start.19 = (bf16[2,2,32,256]{3,2,1,0:T(8,128)(2,1)S(1)}, bf16[2,2,32,256]{3,2,1,0:T(8,128)(2,1)S(1)}, u32[]{:S(2)}, u32[]{:S(2)}) collective-permute-start(bf16[2,2,32,256]{3,2,1,0:T(8,128)(2,1)S(1)} %get-tuple-element.35), channel_id=1, source_target_pairs={{0,2},{1,3},{2,0},{3,1},{4,6},{5,7},{6,4},{7,5},{8,10},{9,11},{10,... | collective-permute-start | bytes 196616 | tf_op jit(solution)/shard_map/ppermute | solution.py:292
  66.3 3.7 %collective-permute-start.18 = (bf16[2,2,32,256]{3,2,1,0:T(8,128)(2,1)S(1)}, bf16[2,2,32,256]{3,2,1,0:T(8,128)(2,1)S(1)}, u32[]{:S(2)}, u32[]{:S(2)}) collective-permute-start(bf16[2,2,32,256]{3,2,1,0:T(8,128)(2,1)S(1)} %get-tuple-element.36), channel_id=1, source_target_pairs={{0,1},{1,0},{2,3},{3,2},{4,5},{5,4},{6,7},{7,6},{8,9},{9,8},{10,11... | collective-permute-start | bytes 196616 | tf_op jit(solution)/shard_map/ppermute | solution.py:292
  (4 other events, 2.6 us)

commit v6 on v5

--- a/solution.py
+++ b/solution.py
@@ -11,12 +11,21 @@
 HEADS = 64
 KVH = 8
 LOG2E = 1.4426950408889634
+STEP = 4
+
+
+class Part:
+    def __init__(self, ref, start):
+        self.ref, self.start = ref, start
+
+    def __getitem__(self, at):
+        return self.ref[self.start + at]
 
 
 def attend_kernel(
-    spans_ref, tail_ref, plan_ref, owner_ref, place_at_ref, *refs,
+    numbers_ref, *refs,
     covers, hops, parts, first_call, last_call,
-    inst_size, tp_size, kv_local, per_head, head_dim, span_len, slot_count, longest,
+    inst_size, tp_size, kv_local, per_head, head_dim, span_len, slot_count, longest, prompt_count,
 ):
     refs = list(refs)
 
@@ -32,15 +41,20 @@
     if last_call:
         out_ref, cache_ref = take(2)
     else:
-        out_ref, next_total_ref = take(2)
+        out_ref, next_total_ref, mark_ref = take(3)
+        mark_ref[...] = jnp.zeros_like(mark_ref)
     place_ref, list_ref, kv_ref, s_ref, p_ref, acc_ref, max_ref, part_sems = take(8)
     if last_call:
         zero_ref, page_sems = take(2)
     step = pl.program_id(0)
+    span_total = slot_count * inst_size
+    spans_ref = Part(numbers_ref, 0)
+    tail_ref = Part(numbers_ref, prompt_count)
+    owner_ref = Part(numbers_ref, 2 * prompt_count)
+    plan_ref = Part(numbers_ref, 3 * prompt_count)
+    place_at_ref = Part(numbers_ref, 3 * prompt_count + span_total)
     inst = place_at_ref[0]
     tp = place_at_ref[1]
-    prompt_count = spans_ref.shape[0]
-    span_total = slot_count * inst_size
     slice_len = span_len // tp_size
     scale = LOG2E / math.sqrt(head_dim)
 
@@ -195,13 +209,13 @@
                     old = acc_ref[g, at] * jnp.concatenate([rescales[h], rescales[h]], axis=1)
                 acc_ref[g, at] = old + mixed[at]
 
-    def pairs(begin):
-        def pair(j, unused):
-            at = begin + 2 * j
-            attend([list_ref[at], list_ref[at + 1]], "here")
+    def rest(begin):
+        def block(j, unused):
+            at = begin + STEP * j
+            attend([list_ref[at + n] for n in range(STEP)], "here")
             return unused
 
-        lax.fori_loop(0, (count - begin) // 2, pair, 0)
+        lax.fori_loop(0, (count - begin) // STEP, block, 0)
 
     live = lax.broadcasted_iota(jnp.int32, (span_len, head_dim), 0) < live_rows
 
@@ -224,20 +238,16 @@
                     next_total_ref[0, g, at] = max_ref[g, at] + jnp.log(total) * LOG2E
 
     if first_call:
-        odd = lax.rem(count, 2)
-
-        @pl.when(odd == 0)
-        def _():
-            attend([own], "start")
-
-        @pl.when(odd == 1)
-        def _():
-            attend([list_ref[0], own], "start")
-
-        pairs(odd)
+        over = lax.rem(count, STEP)
+        for n in range(STEP):
+            @pl.when(over == n)
+            def _():
+                attend([list_ref[m] for m in range(n)] + [own], "start")
+
+        rest(over)
         finish()
     else:
-        used = 2 - lax.rem(count, 2)
+        over = lax.rem(count + STEP - 1, STEP) + 1
 
         @pl.when(count == 0)
         def _():
@@ -247,15 +257,12 @@
 
         @pl.when(count > 0)
         def _():
-            @pl.when(used == 1)
-            def _():
-                attend([list_ref[0]], "given")
-
-            @pl.when(used == 2)
-            def _():
-                attend([list_ref[0], list_ref[1]], "given")
-
-            pairs(used)
+            for n in range(1, STEP + 1):
+                @pl.when(over == n)
+                def _():
+                    attend([list_ref[m] for m in range(n)], "given")
+
+            rest(over)
             finish()
 
     if last_call:
@@ -316,18 +323,19 @@
     crossed = along(outer_on, [(1, 2), (2, 1)])
     inner_ends = along(inner_on, [(1, 0), (2, 3)])
     waiting = exchange(((1, 0, whole), outer_on))
+    names, arrays = zip(*parts)
+    *state, mark = attend([0, 1], list(zip(names, after(arrays, [crossed, inner_ends]))), sources)
     early = len(parts)
-    state = attend([0, 1], parts, sources)
     crossed_on = after([crossed], waiting)[0]
     crossed_half = lax.optimization_barrier([crossed_on[:half], crossed_on[half:]])
     crossed_ends = [along(x, [(1, 0), (2, 3)]) for x in crossed_half]
     two = jnp.where(middle, inner, inner_ends)
     waiting = exchange(((second, 0, whole), two))
-    waiting = waiting + list(state)
+    waiting = waiting + [mark]
     for n in range(2):
         three = jnp.where(middle, crossed_half[n], crossed_ends[n])
         three = after([three], waiting)[0]
-        exchange(((third, n * half, half), three))
+        waiting = exchange(((third, n * half, half), three))
         hops.append(((5, n * half, half), crossed_ends[n]))
     for hop, x in enumerate((outer, inner, crossed, inner_ends), 1):
         hops.append(((hop, 0, whole), x))
@@ -360,10 +368,10 @@
         own_sources = lax.dynamic_index_in_dim(
             jnp.asarray(sources, jnp.int32), inst_index, 1, False
         )
-        numbers = (
-            prompt_spans, prompt_tail, span_plan, decode_owner,
-            jnp.concatenate([jnp.stack([inst_index, tp_index]).astype(jnp.int32), own_sources]),
-        )
+        numbers = jnp.concatenate([
+            prompt_spans, prompt_tail, decode_owner, span_plan,
+            jnp.stack([inst_index, tp_index]).astype(jnp.int32), own_sources,
+        ])
         kernel = functools.partial(
             attend_kernel,
             covers=covers,
@@ -379,13 +387,14 @@
             span_len=span_len,
             slot_count=slot_count,
             longest=longest,
+            prompt_count=prompt_spans.shape[0],
         )
         scratch = [
             pltpu.SMEM((span_total,), jnp.int32),
             pltpu.SMEM((span_total,), jnp.int32),
             pltpu.VMEM((span_total, kv_local, span_len, width), jnp.bfloat16),
-            pltpu.VMEM((kv_local, rows, 2 * span_len), jnp.float32),
-            pltpu.VMEM((kv_local, rows, 2 * span_len), jnp.bfloat16),
+            pltpu.VMEM((kv_local, rows, STEP * span_len), jnp.float32),
+            pltpu.VMEM((kv_local, rows, STEP * span_len), jnp.bfloat16),
             pltpu.VMEM((kv_local, rows, 2 * head_dim), jnp.float32),
             pltpu.VMEM((kv_local, rows, head_dim), jnp.float32),
             pltpu.SemaphoreType.DMA((len(parts), max(len(x[0][0]) for x in parts))),
@@ -401,12 +410,13 @@
                 jax.ShapeDtypeStruct((longest, kv_heads, slice_len, width), jnp.bfloat16),
             ]
         else:
-            out_specs = [state_spec] * 2
+            out_specs = [state_spec] * 2 + [pl.BlockSpec((8, 128), lambda i, *_: (0, 0))]
             out_shape = [jax.ShapeDtypeStruct(state_shape, jnp.float32)] * 2
+            out_shape += [jax.ShapeDtypeStruct((8, 128), jnp.float32)]
         return pl.pallas_call(
             kernel,
             grid_spec=pltpu.PrefetchScalarGridSpec(
-                num_scalar_prefetch=len(numbers),
+                num_scalar_prefetch=1,
                 grid=(slot_count,),
                 in_specs=[by_slot] + [state_spec] * len(state)
                 + [anywhere] * (len(hops) + len(parts)),
@@ -419,7 +429,7 @@
             ),
             compiler_params=pltpu.CompilerParams(vmem_limit_bytes=40 << 20),
         )(
-            *numbers, queries, *state, *[x for _, x in hops], *[x for _, x in parts],
+            numbers, queries, *state, *[x for _, x in hops], *[x for _, x in parts],
         )
 
     state, left, hops = move_pages(kv_new, kv_local, attend)

time: 78.5 us -> 72.2 us (0.920)
  the two profiles are of different devices: /device:TPU:0 before, /device:TPU:5 now
where the time goes in v6:
time: 72.2 us; the launch traced here: 71.7 us
  waiting for transfers between devices  26.6 us (37%)
  starting transfers between devices  21.4 us (30%)
  Pallas kernels  17.8 us (25%)
  local copies, waits for them, and re-layouts  4.74 us (7%)
  between operations  1.04 us (1%)
    ppermute x15, waiting for transfers between devices, exchange(): sent = lax.ppermute(sent, 'tp', [(t, t ^ j) for t in range(tp_size)])  18.2 us
    pallas_call x2, Pallas kernels, attend(): pl.pallas_call(kernel, grid_spec=pltpu.PrefetchScalarGridSpec(num_scalar_...  17.8 us
    ppermute x15, starting transfers between devices, exchange(): sent = lax.ppermute(sent, 'tp', [(t, t ^ j) for t in range(tp_size)])  14.8 us
    ppermute x6, waiting for transfers between devices, along(): return lax.ppermute(x, 'inst', pairs)  8.38 us
    ppermute x6, starting transfers between devices, along(): return lax.ppermute(x, 'inst', pairs)  6.59 us
    unnamed x6, local copies, waits for them, and re-layouts  1.95 us
  transfers between devices with their start and end apart: 21, of which 12 were waited for; matrix products, arithmetic and copies ran while one was open for 4% of the time, Pallas kernels for 13%

profile of v6, /device:TPU:5, one launch (start us, length us, event | category | flops | bytes accessed | tf_op | source)
XLA Modules:
  0.0 71.7 jit_solution(8218619325675269995)
XLA Ops:
  0.6 1.4 %collective-permute-start.3 = (bf16[4,8,32,256]{3,2,1,0:T(8,128)(2,1)}, bf16[4,8,32,256]{3,2,1,0:T(8,128)(2,1)S(1)}, u32[]{:S(2)}, u32[]{:S(2)}) collective-permute-start(bf16[4,8,32,256]{3,2,1,0:T(8,128)(2,1)} %refs_3_.1), channel_id=1, source_target_pairs={{0,4},{4,0},{8,12},{12,8},{1,5},{5,1},{9,13},{13,9},{2,6},{6,2},{1... | collective-permute-start | bytes 1572872 | tf_op jit(solution)/shard_map/ppermute | solution.py:289
  2.8 1.1 %constant_dynamic-slice_fusion.15 = (bf16[4,2,32,256]{3,2,1,0:T(8,128)(2,1)S(1)}, bf16[4,2,32,256]{3,2,1,0:T(8,128)(2,1)S(1)}, bf16[4,2,32,256]{3,2,1,0:T(8,128)(2,1)S(1)}, bf16[4,2,32,256]{3,2,1,0:T(8,128)(2,1)S(1)}) fusion(bf16[4,8,32,256]{3,2,1,0:T(8,128)(2,1)} %refs_3_.1, s32[]{:T(128)S(6)} %select_n.91, s32[]{:T(128)S(6)} %select_n.89, ...), kind=kLoop, calls=%fused_computation.18 | loop fusion | bytes 1048592 | tf_op jit(solution)/shard_map/dynamic_slice | solution.py:296
  3.9 2.1 %collective-permute-start.2 = (bf16[4,2,32,256]{3,2,1,0:T(8,128)(2,1)S(1)}, bf16[4,2,32,256]{3,2,1,0:T(8,128)(2,1)S(1)}, u32[]{:S(2)}, u32[]{:S(2)}) collective-permute-start(bf16[4,2,32,256]{3,2,1,0:T(8,128)(2,1)S(1)} %get-tuple-element.46), channel_id=1, source_target_pairs={{0,3},{1,2},{2,1},{3,0},{4,7},{5,6},{6,5},{7,4},{8,11},{9,10},{10,... | collective-permute-start | bytes 393224 | tf_op jit(solution)/shard_map/ppermute | solution.py:299
  6.5 3.9 %collective-permute-done.2.refs_4_ = bf16[4,2,32,256]{3,2,1,0:T(8,128)(2,1)S(1)} collective-permute-done((bf16[4,2,32,256]{3,2,1,0:T(8,128)(2,1)S(1)}, bf16[4,2,32,256]{3,2,1,0:T(8,128)(2,1)S(1)}, u32[]{:S(2)}, u32[]{:S(2)}) %collective-permute-start.2) | collective-permute-done | bytes 131104 | tf_op jit(solution)/shard_map/ppermute | solution.py:299
  10.4 2.7 %collective-permute-done.1.refs_3_ = bf16[4,2,32,256]{3,2,1,0:T(8,128)(2,1)S(1)} collective-permute-done((bf16[4,2,32,256]{3,2,1,0:T(8,128)(2,1)S(1)}, bf16[4,2,32,256]{3,2,1,0:T(8,128)(2,1)S(1)}, u32[]{:S(2)}, u32[]{:S(2)}) %collective-permute-start.1) | collective-permute-done | bytes 131104 | tf_op jit(solution)/shard_map/ppermute | solution.py:299
  14.4 1.3 %collective-permute-start.9 = (bf16[4,8,32,256]{3,2,1,0:T(8,128)(2,1)S(1)}, bf16[4,8,32,256]{3,2,1,0:T(8,128)(2,1)S(1)}, u32[]{:S(2)}, u32[]{:S(2)}) collective-permute-start(bf16[4,8,32,256]{3,2,1,0:T(8,128)(2,1)S(1)} %collective-permute-done.4.refs_7_), channel_id=1, source_target_pairs={{4,0},{8,12},{5,1},{9,13},{6,2},{10,14},{7,3},{11,15},{20,16},{24,... | collective-permute-start | bytes 1572872 | tf_op jit(solution)/shard_map/ppermute | solution.py:289
  15.8 2.7 %collective-permute-start.7 = (bf16[4,2,32,256]{3,2,1,0:T(8,128)(2,1)S(1)}, bf16[4,2,32,256]{3,2,1,0:T(8,128)(2,1)S(1)}, u32[]{:S(2)}, u32[]{:S(2)}) collective-permute-start(bf16[4,2,32,256]{3,2,1,0:T(8,128)(2,1)S(1)} %get-tuple-element.42), channel_id=1, source_target_pairs={{0,3},{1,2},{2,1},{3,0},{4,7},{5,6},{6,5},{7,4},{8,11},{9,10},{10,... | collective-permute-start | bytes 393224 | tf_op jit(solution)/shard_map/ppermute | solution.py:299
  20.4 2.3 %collective-permute-done.7.refs_8_ = bf16[4,2,32,256]{3,2,1,0:T(8,128)(2,1)S(1)} collective-permute-done((bf16[4,2,32,256]{3,2,1,0:T(8,128)(2,1)S(1)}, bf16[4,2,32,256]{3,2,1,0:T(8,128)(2,1)S(1)}, u32[]{:S(2)}, u32[]{:S(2)}) %collective-permute-start.7) | collective-permute-done | bytes 131104 | tf_op jit(solution)/shard_map/ppermute | solution.py:299
  22.7 2.8 %collective-permute-done.6.refs_7_ = bf16[4,2,32,256]{3,2,1,0:T(8,128)(2,1)S(1)} collective-permute-done((bf16[4,2,32,256]{3,2,1,0:T(8,128)(2,1)S(1)}, bf16[4,2,32,256]{3,2,1,0:T(8,128)(2,1)S(1)}, u32[]{:S(2)}, u32[]{:S(2)}) %collective-permute-start.6) | collective-permute-done | bytes 131104 | tf_op jit(solution)/shard_map/ppermute | solution.py:299
  25.6 1.3 %collective-permute-start.10 = (bf16[2,8,32,256]{3,2,1,0:T(8,128)(2,1)S(1)}, bf16[2,8,32,256]{3,2,1,0:T(8,128)(2,1)S(1)}, u32[]{:S(2)}, u32[]{:S(2)}) collective-permute-start(bf16[2,8,32,256]{3,2,1,0:T(8,128)(2,1)S(1)} %get-tuple-element.32), channel_id=1, source_target_pairs={{4,0},{8,12},{5,1},{9,13},{6,2},{10,14},{7,3},{11,15},{20,16},{24,... | collective-permute-start | bytes 786440 | tf_op jit(solution)/shard_map/ppermute | solution.py:289
  26.9 5.5 %collective-permute-done.9.refs_9_ = bf16[4,8,32,256]{3,2,1,0:T(8,128)(2,1)S(1)} collective-permute-done((bf16[4,8,32,256]{3,2,1,0:T(8,128)(2,1)S(1)}, bf16[4,8,32,256]{3,2,1,0:T(8,128)(2,1)S(1)}, u32[]{:S(2)}, u32[]{:S(2)}) %collective-permute-start.9) | collective-permute-done | bytes 524320 | tf_op jit(solution)/shard_map/ppermute | solution.py:289
  32.5 4.2 %collective-permute-start.14 = (bf16[4,2,32,256]{3,2,1,0:T(8,128)(2,1)S(1)}, bf16[4,2,32,256]{3,2,1,0:T(8,128)(2,1)S(1)}, u32[]{:S(2)}, u32[]{:S(2)}) collective-permute-start(bf16[4,2,32,256]{3,2,1,0:T(8,128)(2,1)S(1)} %get-tuple-element.36), channel_id=1, source_target_pairs={{0,3},{1,2},{2,1},{3,0},{4,7},{5,6},{6,5},{7,4},{8,11},{9,10},{10,... | collective-permute-start | bytes 393224 | tf_op jit(solution)/shard_map/ppermute | solution.py:299
  37.2 1.3 %collective-permute-start.11 = (bf16[2,8,32,256]{3,2,1,0:T(8,128)(2,1)S(1)}, bf16[2,8,32,256]{3,2,1,0:T(8,128)(2,1)S(1)}, u32[]{:S(2)}, u32[]{:S(2)}) collective-permute-start(bf16[2,8,32,256]{3,2,1,0:T(8,128)(2,1)S(1)} %get-tuple-element.33), channel_id=1, source_target_pairs={{4,0},{8,12},{5,1},{9,13},{6,2},{10,14},{7,3},{11,15},{20,16},{24,... | collective-permute-start | bytes 786440 | tf_op jit(solution)/shard_map/ppermute | solution.py:289
  38.5 0.9 %collective-permute-done.10.refs_4_ = bf16[2,8,32,256]{3,2,1,0:T(8,128)(2,1)S(1)} collective-permute-done((bf16[2,8,32,256]{3,2,1,0:T(8,128)(2,1)S(1)}, bf16[2,8,32,256]{3,2,1,0:T(8,128)(2,1)S(1)}, u32[]{:S(2)}, u32[]{:S(2)}) %collective-permute-start.10) | collective-permute-done | bytes 262176 | tf_op jit(solution)/shard_map/ppermute | solution.py:289
  39.4 1.6 %collective-permute-done.14.refs_13_ = bf16[4,2,32,256]{3,2,1,0:T(8,128)(2,1)S(1)} collective-permute-done((bf16[4,2,32,256]{3,2,1,0:T(8,128)(2,1)S(1)}, bf16[4,2,32,256]{3,2,1,0:T(8,128)(2,1)S(1)}, u32[]{:S(2)}, u32[]{:S(2)}) %collective-permute-start.14) | collective-permute-done | bytes 131104 | tf_op jit(solution)/shard_map/ppermute | solution.py:299
  41.0 2.3 %collective-permute-done.13.refs_12_ = bf16[4,2,32,256]{3,2,1,0:T(8,128)(2,1)S(1)} collective-permute-done((bf16[4,2,32,256]{3,2,1,0:T(8,128)(2,1)S(1)}, bf16[4,2,32,256]{3,2,1,0:T(8,128)(2,1)S(1)}, u32[]{:S(2)}, u32[]{:S(2)}) %collective-permute-start.13) | collective-permute-done | bytes 131104 | tf_op jit(solution)/shard_map/ppermute | solution.py:299
  43.4 2.0 %collective-permute-start.16 = (bf16[2,2,32,256]{3,2,1,0:T(8,128)(2,1)S(1)}, bf16[2,2,32,256]{3,2,1,0:T(8,128)(2,1)S(1)}, u32[]{:S(2)}, u32[]{:S(2)}) collective-permute-start(bf16[2,2,32,256]{3,2,1,0:T(8,128)(2,1)S(1)} %get-tuple-element.55), channel_id=1, source_target_pairs={{0,2},{1,3},{2,0},{3,1},{4,6},{5,7},{6,4},{7,5},{8,10},{9,11},{10,... | collective-permute-start | bytes 196616 | tf_op jit(solution)/shard_map/ppermute | solution.py:299
  45.6 1.4 %collective-permute-done.11.refs_5_ = bf16[2,8,32,256]{3,2,1,0:T(8,128)(2,1)S(1)} collective-permute-done((bf16[2,8,32,256]{3,2,1,0:T(8,128)(2,1)S(1)}, bf16[2,8,32,256]{3,2,1,0:T(8,128)(2,1)S(1)}, u32[]{:S(2)}, u32[]{:S(2)}) %collective-permute-start.11) | collective-permute-done | bytes 262176 | tf_op jit(solution)/shard_map/ppermute | solution.py:289
  47.0 1.1 %collective-permute-done.17.refs_17_ = bf16[2,2,32,256]{3,2,1,0:T(8,128)(2,1)S(1)} collective-permute-done((bf16[2,2,32,256]{3,2,1,0:T(8,128)(2,1)S(1)}, bf16[2,2,32,256]{3,2,1,0:T(8,128)(2,1)S(1)}, u32[]{:S(2)}, u32[]{:S(2)}) %collective-permute-start.17) | collective-permute-done | bytes 65568 | tf_op jit(solution)/shard_map/ppermute | solution.py:299
  48.1 1.4 %collective-permute-done.16.refs_16_ = bf16[2,2,32,256]{3,2,1,0:T(8,128)(2,1)S(1)} collective-permute-done((bf16[2,2,32,256]{3,2,1,0:T(8,128)(2,1)S(1)}, bf16[2,2,32,256]{3,2,1,0:T(8,128)(2,1)S(1)}, u32[]{:S(2)}, u32[]{:S(2)}) %collective-permute-start.16) | collective-permute-done | bytes 65568 | tf_op jit(solution)/shard_map/ppermute | solution.py:299
  49.9 1.4 %collective-permute-start.19 = (bf16[2,2,32,256]{3,2,1,0:T(8,128)(2,1)S(1)}, bf16[2,2,32,256]{3,2,1,0:T(8,128)(2,1)S(1)}, u32[]{:S(2)}, u32[]{:S(2)}) collective-permute-start(bf16[2,2,32,256]{3,2,1,0:T(8,128)(2,1)S(1)} %get-tuple-element.51), channel_id=1, source_target_pairs={{0,2},{1,3},{2,0},{3,1},{4,6},{5,7},{6,4},{7,5},{8,10},{9,11},{10,... | collective-permute-start | bytes 196616 | tf_op jit(solution)/shard_map/ppermute | solution.py:299
  51.7 9.5 %shard_map.95 = (f32[4,2,1024,128]{3,2,1,0:T(8,128)S(1)}, f32[4,2,1024,128]{3,2,1,0:T(8,128)S(1)}, f32[8,128]{1,0:T(8,128)}) custom-call(s32[38]{0:T(128)S(1)} %concatenate.6.numbers_ref, bf16[4,128,2048]{2,1,0:T(8,128)(2,1)S(1)} %copy-done.2, bf16[4,2,32,256]{3,2,1,0:T(8,128)(2,1)S(1)} %get-tuple-element.21.refs_1_, ...), custom_call_target="tpu_custom_call" | custom-call | flops 2147483648 | bytes 8388608 | tf_op jit(solution)/shard_map/pallas_call | solution.py:416
  61.2 1.9 %copy-done = f32[4,2,1024,128]{3,2,1,0:T(8,128)} copy-done((f32[4,2,1024,128]{3,2,1,0:T(8,128)}, f32[4,2,1024,128]{3,2,1,0:T(8,128)S(1)}, u32[]{:S(2)}) %copy-start) | copy-done | bytes 4194328
  63.2 8.4 %shard_map.96 = (bf16[4,128,2048]{2,1,0:T(8,128)(2,1)}, bf16[8,8,32,256]{3,2,1,0:T(8,128)(2,1)}) custom-call(s32[38]{0:T(128)S(1)} %concatenate.6.numbers_ref, bf16[4,128,2048]{2,1,0:T(8,128)(2,1)S(1)} %copy-done.2, f32[4,2,1024,128]{3,2,1,0:T(8,128)S(1)} %get-tuple-element.29.refs_1_, f32[4,2,1024,128]{3,2,1,0:T(8,128)} %copy-done, ...), custom_call_target="tpu_custom_call" | custom-call | flops 2147483648 | bytes 8388608 | tf_op jit(solution)/shard_map/pallas_call | solution.py:416
  (37 shorter events, 6.1 us)
Async XLA Ops:
  0.6 13.1 %collective-permute-start.3 = (bf16[4,8,32,256]{3,2,1,0:T(8,128)(2,1)}, bf16[4,8,32,256]{3,2,1,0:T(8,128)(2,1)S(1)}, u32[]{:S(2)}, u32[]{:S(2)}) collective-permute-start(bf16[4,8,32,256]{3,2,1,0:T(8,128)(2,1)} %refs_3_.1), channel_id=1, source_target_pairs={{0,4},{4,0},{8,12},{12,8},{1,5},{5,1},{9,13},{13,9},{2,6},{6,2},{1... | collective-permute-start | bytes 1572872 | tf_op jit(solution)/shard_map/ppermute | solution.py:289
  2.0 11.7 %collective-permute-start.4 = (bf16[4,8,32,256]{3,2,1,0:T(8,128)(2,1)}, bf16[4,8,32,256]{3,2,1,0:T(8,128)(2,1)S(1)}, u32[]{:S(2)}, u32[]{:S(2)}) collective-permute-start(bf16[4,8,32,256]{3,2,1,0:T(8,128)(2,1)} %refs_3_.1), channel_id=1, source_target_pairs={{4,8},{8,4},{5,9},{9,5},{6,10},{10,6},{7,11},{11,7},{20,24},{24,20... | collective-permute-start | bytes 1572872 | tf_op jit(solution)/shard_map/ppermute | solution.py:289
  3.9 6.5 %collective-permute-start.2 = (bf16[4,2,32,256]{3,2,1,0:T(8,128)(2,1)S(1)}, bf16[4,2,32,256]{3,2,1,0:T(8,128)(2,1)S(1)}, u32[]{:S(2)}, u32[]{:S(2)}) collective-permute-start(bf16[4,2,32,256]{3,2,1,0:T(8,128)(2,1)S(1)} %get-tuple-element.46), channel_id=1, source_target_pairs={{0,3},{1,2},{2,1},{3,0},{4,7},{5,6},{6,5},{7,4},{8,11},{9,10},{10,... | collective-permute-start | bytes 393224 | tf_op jit(solution)/shard_map/ppermute | solution.py:299
  6.1 7.1 %collective-permute-start.1 = (bf16[4,2,32,256]{3,2,1,0:T(8,128)(2,1)S(1)}, bf16[4,2,32,256]{3,2,1,0:T(8,128)(2,1)S(1)}, u32[]{:S(2)}, u32[]{:S(2)}) collective-permute-start(bf16[4,2,32,256]{3,2,1,0:T(8,128)(2,1)S(1)} %get-tuple-element.47), channel_id=1, source_target_pairs={{0,2},{1,3},{2,0},{3,1},{4,6},{5,7},{6,4},{7,5},{8,10},{9,11},{10,... | collective-permute-start | bytes 393224 | tf_op jit(solution)/shard_map/ppermute | solution.py:299
  6.3 6.8 %collective-permute-start = (bf16[4,2,32,256]{3,2,1,0:T(8,128)(2,1)S(1)}, bf16[4,2,32,256]{3,2,1,0:T(8,128)(2,1)S(1)}, u32[]{:S(2)}, u32[]{:S(2)}) collective-permute-start(bf16[4,2,32,256]{3,2,1,0:T(8,128)(2,1)S(1)} %get-tuple-element.48), channel_id=1, source_target_pairs={{0,1},{1,0},{2,3},{3,2},{4,5},{5,4},{6,7},{7,6},{8,9},{9,8},{10,11... | collective-permute-start | bytes 393224 | tf_op jit(solution)/shard_map/ppermute | solution.py:299
  13.7 11.8 %collective-permute-start.8 = (bf16[4,8,32,256]{3,2,1,0:T(8,128)(2,1)S(1)}, bf16[4,8,32,256]{3,2,1,0:T(8,128)(2,1)S(1)}, u32[]{:S(2)}, u32[]{:S(2)}) collective-permute-start(bf16[4,8,32,256]{3,2,1,0:T(8,128)(2,1)S(1)} %collective-permute-done.3.refs_6_), channel_id=1, source_target_pairs={{4,8},{8,4},{5,9},{9,5},{6,10},{10,6},{7,11},{11,7},{20,24},{24,20... | collective-permute-start | bytes 1572872 | tf_op jit(solution)/shard_map/ppermute | solution.py:289
  14.4 18.0 %collective-permute-start.9 = (bf16[4,8,32,256]{3,2,1,0:T(8,128)(2,1)S(1)}, bf16[4,8,32,256]{3,2,1,0:T(8,128)(2,1)S(1)}, u32[]{:S(2)}, u32[]{:S(2)}) collective-permute-start(bf16[4,8,32,256]{3,2,1,0:T(8,128)(2,1)S(1)} %collective-permute-done.4.refs_7_), channel_id=1, source_target_pairs={{4,0},{8,12},{5,1},{9,13},{6,2},{10,14},{7,3},{11,15},{20,16},{24,... | collective-permute-start | bytes 1572872 | tf_op jit(solution)/shard_map/ppermute | solution.py:289
  15.8 7.0 %collective-permute-start.7 = (bf16[4,2,32,256]{3,2,1,0:T(8,128)(2,1)S(1)}, bf16[4,2,32,256]{3,2,1,0:T(8,128)(2,1)S(1)}, u32[]{:S(2)}, u32[]{:S(2)}) collective-permute-start(bf16[4,2,32,256]{3,2,1,0:T(8,128)(2,1)S(1)} %get-tuple-element.42), channel_id=1, source_target_pairs={{0,3},{1,2},{2,1},{3,0},{4,7},{5,6},{6,5},{7,4},{8,11},{9,10},{10,... | collective-permute-start | bytes 393224 | tf_op jit(solution)/shard_map/ppermute | solution.py:299
  18.5 7.1 %collective-permute-start.6 = (bf16[4,2,32,256]{3,2,1,0:T(8,128)(2,1)S(1)}, bf16[4,2,32,256]{3,2,1,0:T(8,128)(2,1)S(1)}, u32[]{:S(2)}, u32[]{:S(2)}) collective-permute-start(bf16[4,2,32,256]{3,2,1,0:T(8,128)(2,1)S(1)} %get-tuple-element.43), channel_id=1, source_target_pairs={{0,2},{1,3},{2,0},{3,1},{4,6},{5,7},{6,4},{7,5},{8,10},{9,11},{10,... | collective-permute-start | bytes 393224 | tf_op jit(solution)/shard_map/ppermute | solution.py:299
  18.7 6.8 %collective-permute-start.5 = (bf16[4,2,32,256]{3,2,1,0:T(8,128)(2,1)S(1)}, bf16[4,2,32,256]{3,2,1,0:T(8,128)(2,1)S(1)}, u32[]{:S(2)}, u32[]{:S(2)}) collective-permute-start(bf16[4,2,32,256]{3,2,1,0:T(8,128)(2,1)S(1)} %get-tuple-element.44), channel_id=1, source_target_pairs={{0,1},{1,0},{2,3},{3,2},{4,5},{5,4},{6,7},{7,6},{8,9},{9,8},{10,11... | collective-permute-start | bytes 393224 | tf_op jit(solution)/shard_map/ppermute | solution.py:299
  20.4 31.3 %copy-start.2 = (bf16[4,128,2048]{2,1,0:T(8,128)(2,1)S(1)}, bf16[4,128,2048]{2,1,0:T(8,128)(2,1)}, u32[]{:S(2)}) copy-start(bf16[4,128,2048]{2,1,0:T(8,128)(2,1)} %refs_0_.3) | copy-start | bytes 6291460
  25.6 13.8 %collective-permute-start.10 = (bf16[2,8,32,256]{3,2,1,0:T(8,128)(2,1)S(1)}, bf16[2,8,32,256]{3,2,1,0:T(8,128)(2,1)S(1)}, u32[]{:S(2)}, u32[]{:S(2)}) collective-permute-start(bf16[2,8,32,256]{3,2,1,0:T(8,128)(2,1)S(1)} %get-tuple-element.32), channel_id=1, source_target_pairs={{4,0},{8,12},{5,1},{9,13},{6,2},{10,14},{7,3},{11,15},{20,16},{24,... | collective-permute-start | bytes 786440 | tf_op jit(solution)/shard_map/ppermute | solution.py:289
  32.5 8.5 %collective-permute-start.14 = (bf16[4,2,32,256]{3,2,1,0:T(8,128)(2,1)S(1)}, bf16[4,2,32,256]{3,2,1,0:T(8,128)(2,1)S(1)}, u32[]{:S(2)}, u32[]{:S(2)}) collective-permute-start(bf16[4,2,32,256]{3,2,1,0:T(8,128)(2,1)S(1)} %get-tuple-element.36), channel_id=1, source_target_pairs={{0,3},{1,2},{2,1},{3,0},{4,7},{5,6},{6,5},{7,4},{8,11},{9,10},{10,... | collective-permute-start | bytes 393224 | tf_op jit(solution)/shard_map/ppermute | solution.py:299
  36.7 6.6 %collective-permute-start.13 = (bf16[4,2,32,256]{3,2,1,0:T(8,128)(2,1)S(1)}, bf16[4,2,32,256]{3,2,1,0:T(8,128)(2,1)S(1)}, u32[]{:S(2)}, u32[]{:S(2)}) collective-permute-start(bf16[4,2,32,256]{3,2,1,0:T(8,128)(2,1)S(1)} %get-tuple-element.37), channel_id=1, source_target_pairs={{0,2},{1,3},{2,0},{3,1},{4,6},{5,7},{6,4},{7,5},{8,10},{9,11},{10,... | collective-permute-start | bytes 393224 | tf_op jit(solution)/shard_map/ppermute | solution.py:299
  36.8 6.6 %collective-permute-start.12 = (bf16[4,2,32,256]{3,2,1,0:T(8,128)(2,1)S(1)}, bf16[4,2,32,256]{3,2,1,0:T(8,128)(2,1)S(1)}, u32[]{:S(2)}, u32[]{:S(2)}) collective-permute-start(bf16[4,2,32,256]{3,2,1,0:T(8,128)(2,1)S(1)} %get-tuple-element.38), channel_id=1, source_target_pairs={{0,1},{1,0},{2,3},{3,2},{4,5},{5,4},{6,7},{7,6},{8,9},{9,8},{10,11... | collective-permute-start | bytes 393224 | tf_op jit(solution)/shard_map/ppermute | solution.py:299
  37.2 9.8 %collective-permute-start.11 = (bf16[2,8,32,256]{3,2,1,0:T(8,128)(2,1)S(1)}, bf16[2,8,32,256]{3,2,1,0:T(8,128)(2,1)S(1)}, u32[]{:S(2)}, u32[]{:S(2)}) collective-permute-start(bf16[2,8,32,256]{3,2,1,0:T(8,128)(2,1)S(1)} %get-tuple-element.33), channel_id=1, source_target_pairs={{4,0},{8,12},{5,1},{9,13},{6,2},{10,14},{7,3},{11,15},{20,16},{24,... | collective-permute-start | bytes 786440 | tf_op jit(solution)/shard_map/ppermute | solution.py:289
  43.4 4.7 %collective-permute-start.17 = (bf16[2,2,32,256]{3,2,1,0:T(8,128)(2,1)S(1)}, bf16[2,2,32,256]{3,2,1,0:T(8,128)(2,1)S(1)}, u32[]{:S(2)}, u32[]{:S(2)}) collective-permute-start(bf16[2,2,32,256]{3,2,1,0:T(8,128)(2,1)S(1)} %get-tuple-element.54), channel_id=1, source_target_pairs={{0,3},{1,2},{2,1},{3,0},{4,7},{5,6},{6,5},{7,4},{8,11},{9,10},{10,... | collective-permute-start | bytes 196616 | tf_op jit(solution)/shard_map/ppermute | solution.py:299
  43.4 6.0 %collective-permute-start.16 = (bf16[2,2,32,256]{3,2,1,0:T(8,128)(2,1)S(1)}, bf16[2,2,32,256]{3,2,1,0:T(8,128)(2,1)S(1)}, u32[]{:S(2)}, u32[]{:S(2)}) collective-permute-start(bf16[2,2,32,256]{3,2,1,0:T(8,128)(2,1)S(1)} %get-tuple-element.55), channel_id=1, source_target_pairs={{0,2},{1,3},{2,0},{3,1},{4,6},{5,7},{6,4},{7,5},{8,10},{9,11},{10,... | collective-permute-start | bytes 196616 | tf_op jit(solution)/shard_map/ppermute | solution.py:299
  45.4 4.0 %collective-permute-start.15 = (bf16[2,2,32,256]{3,2,1,0:T(8,128)(2,1)S(1)}, bf16[2,2,32,256]{3,2,1,0:T(8,128)(2,1)S(1)}, u32[]{:S(2)}, u32[]{:S(2)}) collective-permute-start(bf16[2,2,32,256]{3,2,1,0:T(8,128)(2,1)S(1)} %get-tuple-element.56), channel_id=1, source_target_pairs={{0,1},{1,0},{2,3},{3,2},{4,5},{5,4},{6,7},{7,6},{8,9},{9,8},{10,11... | collective-permute-start | bytes 196616 | tf_op jit(solution)/shard_map/ppermute | solution.py:299
  49.5 13.7 %copy-start.1 = (bf16[4,8,32,256]{3,2,1,0:T(8,128)(2,1)S(1)}, bf16[4,8,32,256]{3,2,1,0:T(8,128)(2,1)}, u32[]{:S(2)}) copy-start(bf16[4,8,32,256]{3,2,1,0:T(8,128)(2,1)} %refs_3_.1) | copy-start | bytes 1572868
  49.5 13.7 %collective-permute-start.20 = (bf16[2,2,32,256]{3,2,1,0:T(8,128)(2,1)S(1)}, bf16[2,2,32,256]{3,2,1,0:T(8,128)(2,1)S(1)}, u32[]{:S(2)}, u32[]{:S(2)}) collective-permute-start(bf16[2,2,32,256]{3,2,1,0:T(8,128)(2,1)S(1)} %get-tuple-element.50), channel_id=1, source_target_pairs={{0,3},{1,2},{2,1},{3,0},{4,7},{5,6},{6,5},{7,4},{8,11},{9,10},{10,... | collective-permute-start | bytes 196616 | tf_op jit(solution)/shard_map/ppermute | solution.py:299
  49.9 13.2 %collective-permute-start.19 = (bf16[2,2,32,256]{3,2,1,0:T(8,128)(2,1)S(1)}, bf16[2,2,32,256]{3,2,1,0:T(8,128)(2,1)S(1)}, u32[]{:S(2)}, u32[]{:S(2)}) collective-permute-start(bf16[2,2,32,256]{3,2,1,0:T(8,128)(2,1)S(1)} %get-tuple-element.51), channel_id=1, source_target_pairs={{0,2},{1,3},{2,0},{3,1},{4,6},{5,7},{6,4},{7,5},{8,10},{9,11},{10,... | collective-permute-start | bytes 196616 | tf_op jit(solution)/shard_map/ppermute | solution.py:299
  51.3 11.8 %collective-permute-start.18 = (bf16[2,2,32,256]{3,2,1,0:T(8,128)(2,1)S(1)}, bf16[2,2,32,256]{3,2,1,0:T(8,128)(2,1)S(1)}, u32[]{:S(2)}, u32[]{:S(2)}) collective-permute-start(bf16[2,2,32,256]{3,2,1,0:T(8,128)(2,1)S(1)} %get-tuple-element.52), channel_id=1, source_target_pairs={{0,1},{1,0},{2,3},{3,2},{4,5},{5,4},{6,7},{7,6},{8,9},{9,8},{10,11... | collective-permute-start | bytes 196616 | tf_op jit(solution)/shard_map/ppermute | solution.py:299
  61.2 2.0 %copy-start = (f32[4,2,1024,128]{3,2,1,0:T(8,128)}, f32[4,2,1024,128]{3,2,1,0:T(8,128)S(1)}, u32[]{:S(2)}) copy-start(f32[4,2,1024,128]{3,2,1,0:T(8,128)S(1)} %get-tuple-element.30.refs_2_) | copy-start | bytes 12582916

commit v7 on v6

--- a/solution.py
+++ b/solution.py
@@ -12,6 +12,7 @@
 KVH = 8
 LOG2E = 1.4426950408889634
 STEP = 4
+TOGETHER = 4
 
 
 class Part:
@@ -24,7 +25,7 @@
 
 def attend_kernel(
     numbers_ref, *refs,
-    covers, hops, parts, first_call, last_call,
+    covers, hops, parts, later, first_call, last_call,
     inst_size, tp_size, kv_local, per_head, head_dim, span_len, slot_count, longest, prompt_count,
 ):
     refs = list(refs)
@@ -38,10 +39,12 @@
     mixed_ref, total_ref = (None, None) if first_call else take(2)
     hop_refs = take(len(hops))
     part_refs = take(len(parts))
+    take(later)
     if last_call:
         out_ref, cache_ref = take(2)
     else:
         out_ref, next_total_ref, mark_ref = take(3)
+        next_total_ref[...] = jnp.zeros_like(next_total_ref)
         mark_ref[...] = jnp.zeros_like(mark_ref)
     place_ref, list_ref, kv_ref, s_ref, p_ref, acc_ref, max_ref, part_sems = take(8)
     if last_call:
@@ -143,41 +146,40 @@
     row_ids = lax.broadcasted_iota(jnp.int32, (span_len, span_len), 0)
     col_ids = lax.broadcasted_iota(jnp.int32, (span_len, span_len), 1)
     causal = row_ids >= col_ids
+    lane_ids = lax.broadcasted_iota(jnp.int32, (span_len, head_dim), 1)
+    heads = kv_local * per_head
+    together = math.gcd(per_head, TOGETHER)
+
+    def lanes_of(head):
+        return pl.ds(pl.multiple_of(head * head_dim, head_dim), head_dim)
 
     def rows_of(h):
         return slice(h * span_len, (h + 1) * span_len)
 
-    def key_block(pages, g):
-        return jnp.concatenate([kv_ref[page, g, :, :head_dim] for page in pages], axis=0)
-
-    def value_block(pages, g):
-        return jnp.concatenate(
-            [
-                jnp.concatenate([kv_ref[page, g, :, head_dim:], ones], axis=1)
-                for page in pages
-            ],
-            axis=0,
-        )
-
     def attend(pages, since):
         wide = len(pages) * span_len
-        for g in range(kv_local):
-            q = jnp.concatenate(
+
+        def some_heads(c, unused):
+            head0 = c * together
+            g = head0 // per_head
+            keys = jnp.concatenate([kv_ref[page, g, :, :head_dim] for page in pages], axis=0)
+            values = jnp.concatenate(
                 [
-                    q_ref[0, :, (g * per_head + h) * head_dim:(g * per_head + h + 1) * head_dim]
-                    for h in range(per_head)
+                    jnp.concatenate([kv_ref[page, g, :, head_dim:], ones], axis=1)
+                    for page in pages
                 ],
                 axis=0,
             )
-            s_ref[g, :, :wide] = lax.dot_general(
-                q, key_block(pages, g), (((1,), (1,)), ((), ())),
-                preferred_element_type=jnp.float32,
+            q = jnp.concatenate(
+                [q_ref[0, :, lanes_of(head0 + h)] for h in range(together)], axis=0
             )
-        for g in range(kv_local):
+            s_ref[:, :wide] = lax.dot_general(
+                q, keys, (((1,), (1,)), ((), ())), preferred_element_type=jnp.float32
+            )
             rescales = []
-            for h in range(per_head):
-                at = rows_of(h)
-                s = s_ref[g, at, :wide] * scale
+            for h in range(together):
+                head = head0 + h
+                s = s_ref[rows_of(h), :wide] * scale
                 if since == "start":
                     own_part = jnp.where(causal, s[:, wide - span_len:], -1e30)
                     if len(pages) > 1:
@@ -188,26 +190,35 @@
                 if since == "start":
                     top = jnp.broadcast_to(top, (span_len, head_dim))
                 else:
-                    old = total_ref[0, g, at] if since == "given" else max_ref[g, at]
+                    if since == "given":
+                        old = jnp.broadcast_to(
+                            jnp.sum(
+                                jnp.where(lane_ids == head, total_ref[0], 0.0),
+                                axis=1, keepdims=True,
+                            ),
+                            (span_len, head_dim),
+                        )
+                    else:
+                        old = max_ref[head]
                     top = jnp.maximum(old, top)
                     rescales.append(jnp.exp2(old - top))
-                max_ref[g, at] = top
-                p_ref[g, at, :wide] = jnp.exp2(
+                max_ref[head] = top
+                p_ref[rows_of(h), :wide] = jnp.exp2(
                     s - jnp.concatenate([top] * len(pages), axis=1)
                 ).astype(jnp.bfloat16)
-            mixed = jnp.dot(
-                p_ref[g, :, :wide], value_block(pages, g), preferred_element_type=jnp.float32
-            )
-            if since == "start":
-                acc_ref[g] = mixed
-                continue
-            for h in range(per_head):
-                at = rows_of(h)
+            mixed = jnp.dot(p_ref[:, :wide], values, preferred_element_type=jnp.float32)
+            for h in range(together):
+                head = head0 + h
+                new = mixed[rows_of(h)]
                 if since == "given":
-                    old = jnp.concatenate([mixed_ref[0, g, at] * rescales[h], rescales[h]], axis=1)
-                else:
-                    old = acc_ref[g, at] * jnp.concatenate([rescales[h], rescales[h]], axis=1)
-                acc_ref[g, at] = old + mixed[at]
+                    given = mixed_ref[0, :, lanes_of(head)].astype(jnp.float32)
+                    new = new + jnp.concatenate([given * rescales[h], rescales[h]], axis=1)
+                elif since == "here":
+                    new = new + acc_ref[head] * jnp.concatenate([rescales[h]] * 2, axis=1)
+                acc_ref[head] = new
+            return unused
+
+        lax.fori_loop(0, heads // together, some_heads, 0)
 
     def rest(begin):
         def block(j, unused):
@@ -219,23 +230,20 @@
 
     live = lax.broadcasted_iota(jnp.int32, (span_len, head_dim), 0) < live_rows
 
-    def put_out(g, h, mixed):
-        head = g * per_head + h
-        out_ref[0, :, head * head_dim:(head + 1) * head_dim] = jnp.where(
-            live, mixed, 0.0
-        ).astype(jnp.bfloat16)
-
     def finish():
-        for g in range(kv_local):
-            for h in range(per_head):
-                at = rows_of(h)
-                total = acc_ref[g, at, head_dim:]
-                mixed = acc_ref[g, at, :head_dim] / total
-                if last_call:
-                    put_out(g, h, mixed)
-                else:
-                    out_ref[0, g, at] = mixed
-                    next_total_ref[0, g, at] = max_ref[g, at] + jnp.log(total) * LOG2E
+        def one_head(head, unused):
+            total = acc_ref[head, :, head_dim:]
+            mixed = acc_ref[head, :, :head_dim] / total
+            if last_call:
+                mixed = jnp.where(live, mixed, 0.0)
+            else:
+                next_total_ref[0] = jnp.where(
+                    lane_ids == head, max_ref[head] + jnp.log(total) * LOG2E, next_total_ref[0]
+                )
+            out_ref[0, :, lanes_of(head)] = mixed.astype(jnp.bfloat16)
+            return unused
+
+        lax.fori_loop(0, heads, one_head, 0)
 
     if first_call:
         over = lax.rem(count, STEP)
@@ -251,9 +259,12 @@
 
         @pl.when(count == 0)
         def _():
-            for g in range(kv_local):
-                for h in range(per_head):
-                    put_out(g, h, mixed_ref[0, g, rows_of(h)])
+            def one_head(head, unused):
+                given = mixed_ref[0, :, lanes_of(head)]
+                out_ref[0, :, lanes_of(head)] = jnp.where(live, given, jnp.zeros_like(given))
+                return unused
+
+            lax.fori_loop(0, heads, one_head, 0)
 
         @pl.when(count > 0)
         def _():
@@ -288,11 +299,11 @@
     def along(x, pairs):
         return lax.ppermute(x, "inst", pairs)
 
-    def exchange(*pieces):
+    def exchange(*pieces, zero=0):
         names = [name for name, _ in pieces]
         found = []
         for j in range(tp_size):
-            head = ((tp ^ j) * kv_heads) // tp_size
+            head = ((tp ^ j) * kv_heads) // tp_size + zero
             sent = [lax.dynamic_slice_in_dim(x, head, kv_local, 1) for _, x in pieces]
             sent = jnp.concatenate(sent, axis=0) if len(sent) > 1 else sent[0]
             if j:
@@ -323,19 +334,17 @@
     crossed = along(outer_on, [(1, 2), (2, 1)])
     inner_ends = along(inner_on, [(1, 0), (2, 3)])
     waiting = exchange(((1, 0, whole), outer_on))
-    names, arrays = zip(*parts)
-    *state, mark = attend([0, 1], list(zip(names, after(arrays, [crossed, inner_ends]))), sources)
-    early = len(parts)
     crossed_on = after([crossed], waiting)[0]
     crossed_half = lax.optimization_barrier([crossed_on[:half], crossed_on[half:]])
     crossed_ends = [along(x, [(1, 0), (2, 3)]) for x in crossed_half]
+    early = len(parts)
     two = jnp.where(middle, inner, inner_ends)
     waiting = exchange(((second, 0, whole), two))
-    waiting = waiting + [mark]
+    *state, mark = attend([0, 1], parts[:early], sources, later=[waiting[0], *crossed_half])
     for n in range(2):
         three = jnp.where(middle, crossed_half[n], crossed_ends[n])
         three = after([three], waiting)[0]
-        waiting = exchange(((third, n * half, half), three))
+        waiting = exchange(((third, n * half, half), three), zero=mark[0, 0])
         hops.append(((5, n * half, half), crossed_ends[n]))
     for hop, x in enumerate((outer, inner, crossed, inner_ends), 1):
         hops.append(((hop, 0, whole), x))
@@ -357,12 +366,12 @@
     longest = span_total // 2
     anywhere = pl.BlockSpec(memory_space=pl.ANY)
     by_slot = pl.BlockSpec((1, span_len, row_width), lambda i, *_: (i, 0, 0))
-    rows = per_head * span_len
-    state_shape = (slot_count, kv_local, rows, head_dim)
-    state_spec = pl.BlockSpec((1,) + state_shape[1:], lambda i, *_: (i, 0, 0, 0))
+    rows = math.gcd(per_head, TOGETHER) * span_len
+    total_spec = pl.BlockSpec((1, span_len, head_dim), lambda i, *_: (i, 0, 0))
+    state_specs = [by_slot, total_spec]
     work = slot_count * 4 * local_heads * span_len * span_len
 
-    def attend(covers, parts, sources, state=(), hops=None):
+    def attend(covers, parts, sources, state=(), hops=None, later=()):
         first_call, last_call = not state, hops is not None
         hops = hops or []
         own_sources = lax.dynamic_index_in_dim(
@@ -377,6 +386,7 @@
             covers=covers,
             hops=[name for name, _ in hops],
             parts=[name for name, _ in parts],
+            later=len(later),
             first_call=first_call,
             last_call=last_call,
             inst_size=inst_size,
@@ -393,10 +403,10 @@
             pltpu.SMEM((span_total,), jnp.int32),
             pltpu.SMEM((span_total,), jnp.int32),
             pltpu.VMEM((span_total, kv_local, span_len, width), jnp.bfloat16),
-            pltpu.VMEM((kv_local, rows, STEP * span_len), jnp.float32),
-            pltpu.VMEM((kv_local, rows, STEP * span_len), jnp.bfloat16),
-            pltpu.VMEM((kv_local, rows, 2 * head_dim), jnp.float32),
-            pltpu.VMEM((kv_local, rows, head_dim), jnp.float32),
+            pltpu.VMEM((rows, STEP * span_len), jnp.float32),
+            pltpu.VMEM((rows, STEP * span_len), jnp.bfloat16),
+            pltpu.VMEM((local_heads, span_len, 2 * head_dim), jnp.float32),
+            pltpu.VMEM((local_heads, span_len, head_dim), jnp.float32),
             pltpu.SemaphoreType.DMA((len(parts), max(len(x[0][0]) for x in parts))),
         ]
         if last_call:
@@ -410,16 +420,19 @@
                 jax.ShapeDtypeStruct((longest, kv_heads, slice_len, width), jnp.bfloat16),
             ]
         else:
-            out_specs = [state_spec] * 2 + [pl.BlockSpec((8, 128), lambda i, *_: (0, 0))]
-            out_shape = [jax.ShapeDtypeStruct(state_shape, jnp.float32)] * 2
-            out_shape += [jax.ShapeDtypeStruct((8, 128), jnp.float32)]
+            out_specs = state_specs + [pl.BlockSpec((8, 128), lambda i, *_: (0, 0))]
+            out_shape = [
+                jax.ShapeDtypeStruct(queries.shape, jnp.bfloat16),
+                jax.ShapeDtypeStruct((slot_count, span_len, head_dim), jnp.float32),
+                jax.ShapeDtypeStruct((8, 128), jnp.int32),
+            ]
         return pl.pallas_call(
             kernel,
             grid_spec=pltpu.PrefetchScalarGridSpec(
                 num_scalar_prefetch=1,
                 grid=(slot_count,),
-                in_specs=[by_slot] + [state_spec] * len(state)
-                + [anywhere] * (len(hops) + len(parts)),
+                in_specs=[by_slot] + (state_specs if state else [])
+                + [anywhere] * (len(hops) + len(parts) + len(later)),
                 out_specs=out_specs,
                 scratch_shapes=scratch,
             ),
@@ -430,6 +443,7 @@
             compiler_params=pltpu.CompilerParams(vmem_limit_bytes=40 << 20),
         )(
             numbers, queries, *state, *[x for _, x in hops], *[x for _, x in parts],
+            *later,
         )
 
     state, left, hops = move_pages(kv_new, kv_local, attend)

time: 72.2 us -> 99.9 us (1.38)
  the two profiles are of different devices: /device:TPU:5 before, /device:TPU:0 now
where the time goes in v7:
time: 99.9 us; the launch traced here: 99.8 us
  waiting for transfers between devices  29 us (29%)
  Pallas kernels  28.1 us (28%)
  starting transfers between devices  18.7 us (19%)
  local copies, waits for them, and re-layouts  18.4 us (18%)
  between operations  3.51 us (4%)
  other arithmetic  2.11 us (2%)
    pallas_call x2, Pallas kernels, attend(): pl.pallas_call(kernel, grid_spec=pltpu.PrefetchScalarGridSpec(num_scalar_...  28.1 us
    ppermute x15, waiting for transfers between devices, exchange(): sent = lax.ppermute(sent, 'tp', [(t, t ^ j) for t in range(tp_size)])  25 us
    unnamed x50, local copies, waits for them, and re-layouts  10.5 us
    ppermute x15, starting transfers between devices, exchange(): sent = lax.ppermute(sent, 'tp', [(t, t ^ j) for t in range(tp_size)])  9.48 us
    ppermute x6, starting transfers between devices, along(): return lax.ppermute(x, 'inst', pairs)  9.24 us
    ppermute x6, waiting for transfers between devices, along(): return lax.ppermute(x, 'inst', pairs)  3.99 us
    dynamic_slice x5, local copies, waits for them, and re-layouts, exchange(): sent = [lax.dynamic_slice_in_dim(x, head, kv_local, 1) for _, x in pieces]  3.47 us
  transfers between devices with their start and end apart: 21, of which 11 were waited for; matrix products, arithmetic and copies ran while one was open for 10% of the time, Pallas kernels for 13%

profile of v7, /device:TPU:0, one launch (start us, length us, event | category | flops | bytes accessed | tf_op | source)
XLA Modules:
  0.0 99.8 jit_solution(16942075602973520127)
XLA Ops:
  0.7 3.1 %collective-permute-start.3 = (bf16[4,8,32,256]{3,2,1,0:T(8,128)(2,1)}, bf16[4,8,32,256]{3,2,1,0:T(8,128)(2,1)S(1)}, u32[]{:S(2)}, u32[]{:S(2)}) collective-permute-start(bf16[4,8,32,256]{3,2,1,0:T(8,128)(2,1)} %refs_3_.1), channel_id=1, source_target_pairs={{0,4},{4,0},{8,12},{12,8},{1,5},{5,1},{9,13},{13,9},{2,6},{6,2},{1... | collective-permute-start | bytes 1572872 | tf_op jit(solution)/shard_map/ppermute | solution.py:300
  4.5 1.8 %constant_dynamic-slice_fusion.15 = (bf16[4,2,32,256]{3,2,1,0:T(8,128)(2,1)S(1)}, bf16[4,2,32,256]{3,2,1,0:T(8,128)(2,1)S(1)}, bf16[4,2,32,256]{3,2,1,0:T(8,128)(2,1)S(1)}, bf16[4,2,32,256]{3,2,1,0:T(8,128)(2,1)}) fusion(bf16[4,8,32,256]{3,2,1,0:T(8,128)(2,1)} %refs_3_.1, s32[]{:T(128)S(6)} %select_n.99, s32[]{:T(128)S(6)} %select_n.97, s32[]{:T(128)S(6)} %select_n.95, ...), kind=kLoop, calls=%fused_computation.18 | loop fusion | bytes 1048592 | tf_op jit(solution)/shard_map/dynamic_slice | solution.py:307
  8.2 3.9 %collective-permute-done.2.refs_4_ = bf16[4,2,32,256]{3,2,1,0:T(8,128)(2,1)S(1)} collective-permute-done((bf16[4,2,32,256]{3,2,1,0:T(8,128)(2,1)S(1)}, bf16[4,2,32,256]{3,2,1,0:T(8,128)(2,1)S(1)}, u32[]{:S(2)}, u32[]{:S(2)}) %collective-permute-start.2) | collective-permute-done | bytes 131104 | tf_op jit(solution)/shard_map/ppermute | solution.py:310
  12.8 2.2 %collective-permute-done.1.refs_3_ = bf16[4,2,32,256]{3,2,1,0:T(8,128)(2,1)S(1)} collective-permute-done((bf16[4,2,32,256]{3,2,1,0:T(8,128)(2,1)S(1)}, bf16[4,2,32,256]{3,2,1,0:T(8,128)(2,1)S(1)}, u32[]{:S(2)}, u32[]{:S(2)}) %collective-permute-start.1) | collective-permute-done | bytes 131104 | tf_op jit(solution)/shard_map/ppermute | solution.py:310
  16.3 1.5 %collective-permute-start.9 = (bf16[4,8,32,256]{3,2,1,0:T(8,128)(2,1)S(1)}, bf16[4,8,32,256]{3,2,1,0:T(8,128)(2,1)}, u32[]{:S(2)}, u32[]{:S(2)}) collective-permute-start(bf16[4,8,32,256]{3,2,1,0:T(8,128)(2,1)S(1)} %collective-permute-done.3.refs_6_), channel_id=1, source_target_pairs={{4,8},{8,4},{5,9},{9,5},{6,10},{10,6},{7,11},{11,7},{20,24},{24,20... | collective-permute-start | bytes 1572872 | tf_op jit(solution)/shard_map/ppermute | solution.py:300
  17.8 1.3 %collective-permute-start.8 = (bf16[4,8,32,256]{3,2,1,0:T(8,128)(2,1)S(1)}, bf16[4,8,32,256]{3,2,1,0:T(8,128)(2,1)}, u32[]{:S(2)}, u32[]{:S(2)}) collective-permute-start(bf16[4,8,32,256]{3,2,1,0:T(8,128)(2,1)S(1)} %collective-permute-done.4.refs_7_), channel_id=1, source_target_pairs={{4,0},{8,12},{5,1},{9,13},{6,2},{10,14},{7,3},{11,15},{20,16},{24,... | collective-permute-start | bytes 1572872 | tf_op jit(solution)/shard_map/ppermute | solution.py:300
  23.7 2.0 %collective-permute-done.7.refs_8_ = bf16[4,2,32,256]{3,2,1,0:T(8,128)(2,1)S(1)} collective-permute-done((bf16[4,2,32,256]{3,2,1,0:T(8,128)(2,1)}, bf16[4,2,32,256]{3,2,1,0:T(8,128)(2,1)S(1)}, u32[]{:S(2)}, u32[]{:S(2)}) %collective-permute-start.7) | collective-permute-done | bytes 131104 | tf_op jit(solution)/shard_map/ppermute | solution.py:310
  25.7 3.1 %collective-permute-done.6.refs_7_ = bf16[4,2,32,256]{3,2,1,0:T(8,128)(2,1)S(1)} collective-permute-done((bf16[4,2,32,256]{3,2,1,0:T(8,128)(2,1)}, bf16[4,2,32,256]{3,2,1,0:T(8,128)(2,1)S(1)}, u32[]{:S(2)}, u32[]{:S(2)}) %collective-permute-start.6) | collective-permute-done | bytes 131104 | tf_op jit(solution)/shard_map/ppermute | solution.py:310
  28.7 2.0 %fusion.1 = (bf16[2,8,32,256]{3,2,1,0:T(8,128)(2,1)}, bf16[2,8,32,256]{3,2,1,0:T(8,128)(2,1)}) fusion(bf16[4,8,32,256]{3,2,1,0:T(8,128)(2,1)} %collective-permute-done.9.refs_8_), kind=kLoop, calls=%fused_computation.25 | loop fusion | bytes 1048576 | tf_op jit(solution)/shard_map/slice | solution.py:338
  30.7 1.4 %collective-permute-start.10 = (bf16[2,8,32,256]{3,2,1,0:T(8,128)(2,1)}, bf16[2,8,32,256]{3,2,1,0:T(8,128)(2,1)S(1)}, u32[]{:S(2)}, u32[]{:S(2)}) collective-permute-start(bf16[2,8,32,256]{3,2,1,0:T(8,128)(2,1)} %get-tuple-element.15.refs_10_), channel_id=1, source_target_pairs={{4,0},{8,12},{5,1},{9,13},{6,2},{10,14},{7,3},{11,15},{20,16},{24,... | collective-permute-start | bytes 786440 | tf_op jit(solution)/shard_map/ppermute | solution.py:300
  32.1 4.0 %collective-permute-done.8.refs_9_ = bf16[4,8,32,256]{3,2,1,0:T(8,128)(2,1)} collective-permute-done((bf16[4,8,32,256]{3,2,1,0:T(8,128)(2,1)S(1)}, bf16[4,8,32,256]{3,2,1,0:T(8,128)(2,1)}, u32[]{:S(2)}, u32[]{:S(2)}) %collective-permute-start.8) | collective-permute-done | bytes 524320 | tf_op jit(solution)/shard_map/ppermute | solution.py:300
  38.0 1.3 %collective-permute-start.11 = (bf16[2,8,32,256]{3,2,1,0:T(8,128)(2,1)}, bf16[2,8,32,256]{3,2,1,0:T(8,128)(2,1)}, u32[]{:S(2)}, u32[]{:S(2)}) collective-permute-start(bf16[2,8,32,256]{3,2,1,0:T(8,128)(2,1)} %get-tuple-element.16.refs_11_), channel_id=1, source_target_pairs={{4,0},{8,12},{5,1},{9,13},{6,2},{10,14},{7,3},{11,15},{20,16},{24,... | collective-permute-start | bytes 786440 | tf_op jit(solution)/shard_map/ppermute | solution.py:300
  43.9 13.1 %shard_map.95 = (bf16[4,128,2048]{2,1,0:T(8,128)(2,1)S(1)}, f32[4,128,128]{2,1,0:T(8,128)S(1)}, s32[8,128]{1,0:T(8,128)S(1)}) custom-call(s32[38]{0:T(128)S(1)} %concatenate.6.numbers_ref, bf16[4,128,2048]{2,1,0:T(8,128)(2,1)S(1)} %copy-done, bf16[4,2,32,256]{3,2,1,0:T(8,128)(2,1)S(1)} %copy-done.8, bf16[4,2,32,256]{3,2,1,0:T(8,128)(2,1)S(1)} %copy-done.15, ...), custom_call_target="tpu_custom_call" | custom-call | flops 2147483648 | bytes 8388608 | tf_op jit(solution)/shard_map/pallas_call | solution.py:429
  57.0 1.3 %copy-done.1 = bf16[4,128,2048]{2,1,0:T(8,128)(2,1)} copy-done((bf16[4,128,2048]{2,1,0:T(8,128)(2,1)}, bf16[4,128,2048]{2,1,0:T(8,128)(2,1)S(1)}, u32[]{:S(2)}) %copy-start.1) | copy-done | bytes 2097176
  62.2 1.6 %collective-permute-start.13 = (bf16[4,2,32,256]{3,2,1,0:T(8,128)(2,1)}, bf16[4,2,32,256]{3,2,1,0:T(8,128)(2,1)}, u32[]{:S(2)}, u32[]{:S(2)}) collective-permute-start(bf16[4,2,32,256]{3,2,1,0:T(8,128)(2,1)} %get-tuple-element.23), channel_id=1, source_target_pairs={{0,2},{1,3},{2,0},{3,1},{4,6},{5,7},{6,4},{7,5},{8,10},{9,11},{10,... | collective-permute-start | bytes 393224 | tf_op jit(solution)/shard_map/ppermute | solution.py:310
  64.1 4.2 %collective-permute-done.14.refs_13_ = bf16[4,2,32,256]{3,2,1,0:T(8,128)(2,1)} collective-permute-done((bf16[4,2,32,256]{3,2,1,0:T(8,128)(2,1)}, bf16[4,2,32,256]{3,2,1,0:T(8,128)(2,1)}, u32[]{:S(2)}, u32[]{:S(2)}) %collective-permute-start.14) | collective-permute-done | bytes 131104 | tf_op jit(solution)/shard_map/ppermute | solution.py:310
  68.2 2.9 %collective-permute-done.13.refs_12_ = bf16[4,2,32,256]{3,2,1,0:T(8,128)(2,1)} collective-permute-done((bf16[4,2,32,256]{3,2,1,0:T(8,128)(2,1)}, bf16[4,2,32,256]{3,2,1,0:T(8,128)(2,1)}, u32[]{:S(2)}, u32[]{:S(2)}) %collective-permute-start.13) | collective-permute-done | bytes 131104 | tf_op jit(solution)/shard_map/ppermute | solution.py:310
  71.2 1.7 %collective-permute-start.16 = (bf16[2,2,32,256]{3,2,1,0:T(8,128)(2,1)S(1)}, bf16[2,2,32,256]{3,2,1,0:T(8,128)(2,1)S(1)}, u32[]{:S(2)}, u32[]{:S(2)}) collective-permute-start(bf16[2,2,32,256]{3,2,1,0:T(8,128)(2,1)S(1)} %get-tuple-element.41), channel_id=1, source_target_pairs={{0,2},{1,3},{2,0},{3,1},{4,6},{5,7},{6,4},{7,5},{8,10},{9,11},{10,... | collective-permute-start | bytes 196616 | tf_op jit(solution)/shard_map/ppermute | solution.py:310
  74.0 1.3 %collective-permute-done.17.refs_17_ = bf16[2,2,32,256]{3,2,1,0:T(8,128)(2,1)S(1)} collective-permute-done((bf16[2,2,32,256]{3,2,1,0:T(8,128)(2,1)S(1)}, bf16[2,2,32,256]{3,2,1,0:T(8,128)(2,1)S(1)}, u32[]{:S(2)}, u32[]{:S(2)}) %collective-permute-start.17) | collective-permute-done | bytes 65568 | tf_op jit(solution)/shard_map/ppermute | solution.py:310
  75.3 1.7 %collective-permute-done.16.refs_16_ = bf16[2,2,32,256]{3,2,1,0:T(8,128)(2,1)S(1)} collective-permute-done((bf16[2,2,32,256]{3,2,1,0:T(8,128)(2,1)S(1)}, bf16[2,2,32,256]{3,2,1,0:T(8,128)(2,1)S(1)}, u32[]{:S(2)}, u32[]{:S(2)}) %collective-permute-start.16) | collective-permute-done | bytes 65568 | tf_op jit(solution)/shard_map/ppermute | solution.py:310
  77.1 1.5 %collective-permute-start.19 = (bf16[2,2,32,256]{3,2,1,0:T(8,128)(2,1)S(1)}, bf16[2,2,32,256]{3,2,1,0:T(8,128)(2,1)S(1)}, u32[]{:S(2)}, u32[]{:S(2)}) collective-permute-start(bf16[2,2,32,256]{3,2,1,0:T(8,128)(2,1)S(1)} %get-tuple-element.37), channel_id=1, source_target_pairs={{0,2},{1,3},{2,0},{3,1},{4,6},{5,7},{6,4},{7,5},{8,10},{9,11},{10,... | collective-permute-start | bytes 196616 | tf_op jit(solution)/shard_map/ppermute | solution.py:310
  78.9 2.5 %collective-permute-done.20.refs_21_ = bf16[2,2,32,256]{3,2,1,0:T(8,128)(2,1)S(1)} collective-permute-done((bf16[2,2,32,256]{3,2,1,0:T(8,128)(2,1)S(1)}, bf16[2,2,32,256]{3,2,1,0:T(8,128)(2,1)S(1)}, u32[]{:S(2)}, u32[]{:S(2)}) %collective-permute-start.20) | collective-permute-done | bytes 65568 | tf_op jit(solution)/shard_map/ppermute | solution.py:310
  81.4 1.5 %collective-permute-done.19.refs_20_ = bf16[2,2,32,256]{3,2,1,0:T(8,128)(2,1)S(1)} collective-permute-done((bf16[2,2,32,256]{3,2,1,0:T(8,128)(2,1)S(1)}, bf16[2,2,32,256]{3,2,1,0:T(8,128)(2,1)S(1)}, u32[]{:S(2)}, u32[]{:S(2)}) %collective-permute-start.19) | collective-permute-done | bytes 65568 | tf_op jit(solution)/shard_map/ppermute | solution.py:310
  84.9 14.9 %shard_map.96 = (bf16[4,128,2048]{2,1,0:T(8,128)(2,1)}, bf16[8,8,32,256]{3,2,1,0:T(8,128)(2,1)}) custom-call(s32[38]{0:T(128)S(1)} %concatenate.6.numbers_ref, bf16[4,128,2048]{2,1,0:T(8,128)(2,1)S(1)} %copy-done, bf16[4,128,2048]{2,1,0:T(8,128)(2,1)S(1)} %copy-done.2, f32[4,128,128]{2,1,0:T(8,128)S(1)} %copy-done.7, bf16[4,8,32,256]{3,2,1,0:T(8,128)(2,1)S(1)} %copy-done.3, ...), custom_call_target="tpu_custom_call" | custom-call | flops 2147483648 | bytes 8388608 | tf_op jit(solution)/shard_map/pallas_call | solution.py:429
  (82 shorter events, 20.9 us)
Async XLA Ops:
  0.6 22.3 %copy-start.24 = (s32[4]{0:T(128)S(1)}, s32[4]{0:T(128)}, u32[]{:S(2)}) copy-start(s32[4]{0:T(128)} %param.13) | copy-start | bytes 52
  0.6 22.3 %copy-start.23 = (s32[4]{0:T(128)S(1)}, s32[4]{0:T(128)}, u32[]{:S(2)}) copy-start(s32[4]{0:T(128)} %param.11) | copy-start | bytes 52
  0.7 15.6 %collective-permute-start.3 = (bf16[4,8,32,256]{3,2,1,0:T(8,128)(2,1)}, bf16[4,8,32,256]{3,2,1,0:T(8,128)(2,1)S(1)}, u32[]{:S(2)}, u32[]{:S(2)}) collective-permute-start(bf16[4,8,32,256]{3,2,1,0:T(8,128)(2,1)} %refs_3_.1), channel_id=1, source_target_pairs={{0,4},{4,0},{8,12},{12,8},{1,5},{5,1},{9,13},{13,9},{2,6},{6,2},{1... | collective-permute-start | bytes 1572872 | tf_op jit(solution)/shard_map/ppermute | solution.py:300
  3.7 12.5 %collective-permute-start.4 = (bf16[4,8,32,256]{3,2,1,0:T(8,128)(2,1)}, bf16[4,8,32,256]{3,2,1,0:T(8,128)(2,1)S(1)}, u32[]{:S(2)}, u32[]{:S(2)}) collective-permute-start(bf16[4,8,32,256]{3,2,1,0:T(8,128)(2,1)} %refs_3_.1), channel_id=1, source_target_pairs={{4,8},{8,4},{5,9},{9,5},{6,10},{10,6},{7,11},{11,7},{20,24},{24,20... | collective-permute-start | bytes 1572872 | tf_op jit(solution)/shard_map/ppermute | solution.py:300
  6.4 5.8 %collective-permute-start.2 = (bf16[4,2,32,256]{3,2,1,0:T(8,128)(2,1)S(1)}, bf16[4,2,32,256]{3,2,1,0:T(8,128)(2,1)S(1)}, u32[]{:S(2)}, u32[]{:S(2)}) collective-permute-start(bf16[4,2,32,256]{3,2,1,0:T(8,128)(2,1)S(1)} %get-tuple-element.32), channel_id=1, source_target_pairs={{0,3},{1,2},{2,1},{3,0},{4,7},{5,6},{6,5},{7,4},{8,11},{9,10},{10,... | collective-permute-start | bytes 393224 | tf_op jit(solution)/shard_map/ppermute | solution.py:310
  7.0 8.0 %collective-permute-start.1 = (bf16[4,2,32,256]{3,2,1,0:T(8,128)(2,1)S(1)}, bf16[4,2,32,256]{3,2,1,0:T(8,128)(2,1)S(1)}, u32[]{:S(2)}, u32[]{:S(2)}) collective-permute-start(bf16[4,2,32,256]{3,2,1,0:T(8,128)(2,1)S(1)} %get-tuple-element.33), channel_id=1, source_target_pairs={{0,2},{1,3},{2,0},{3,1},{4,6},{5,7},{6,4},{7,5},{8,10},{9,11},{10,... | collective-permute-start | bytes 393224 | tf_op jit(solution)/shard_map/ppermute | solution.py:310
  7.9 7.7 %collective-permute-start = (bf16[4,2,32,256]{3,2,1,0:T(8,128)(2,1)S(1)}, bf16[4,2,32,256]{3,2,1,0:T(8,128)(2,1)S(1)}, u32[]{:S(2)}, u32[]{:S(2)}) collective-permute-start(bf16[4,2,32,256]{3,2,1,0:T(8,128)(2,1)S(1)} %get-tuple-element.34), channel_id=1, source_target_pairs={{0,1},{1,0},{2,3},{3,2},{4,5},{5,4},{6,7},{7,6},{8,9},{9,8},{10,11... | collective-permute-start | bytes 393224 | tf_op jit(solution)/shard_map/ppermute | solution.py:310
  16.3 12.5 %collective-permute-start.9 = (bf16[4,8,32,256]{3,2,1,0:T(8,128)(2,1)S(1)}, bf16[4,8,32,256]{3,2,1,0:T(8,128)(2,1)}, u32[]{:S(2)}, u32[]{:S(2)}) collective-permute-start(bf16[4,8,32,256]{3,2,1,0:T(8,128)(2,1)S(1)} %collective-permute-done.3.refs_6_), channel_id=1, source_target_pairs={{4,8},{8,4},{5,9},{9,5},{6,10},{10,6},{7,11},{11,7},{20,24},{24,20... | collective-permute-start | bytes 1572872 | tf_op jit(solution)/shard_map/ppermute | solution.py:300
  17.8 18.4 %collective-permute-start.8 = (bf16[4,8,32,256]{3,2,1,0:T(8,128)(2,1)S(1)}, bf16[4,8,32,256]{3,2,1,0:T(8,128)(2,1)}, u32[]{:S(2)}, u32[]{:S(2)}) collective-permute-start(bf16[4,8,32,256]{3,2,1,0:T(8,128)(2,1)S(1)} %collective-permute-done.4.refs_7_), channel_id=1, source_target_pairs={{4,0},{8,12},{5,1},{9,13},{6,2},{10,14},{7,3},{11,15},{20,16},{24,... | collective-permute-start | bytes 1572872 | tf_op jit(solution)/shard_map/ppermute | solution.py:300
  19.9 5.8 %collective-permute-start.7 = (bf16[4,2,32,256]{3,2,1,0:T(8,128)(2,1)}, bf16[4,2,32,256]{3,2,1,0:T(8,128)(2,1)S(1)}, u32[]{:S(2)}, u32[]{:S(2)}) collective-permute-start(bf16[4,2,32,256]{3,2,1,0:T(8,128)(2,1)} %get-tuple-element.28), channel_id=1, source_target_pairs={{0,3},{1,2},{2,1},{3,0},{4,7},{5,6},{6,5},{7,4},{8,11},{9,10},{10,... | collective-permute-start | bytes 393224 | tf_op jit(solution)/shard_map/ppermute | solution.py:310
  20.9 7.9 %collective-permute-start.6 = (bf16[4,2,32,256]{3,2,1,0:T(8,128)(2,1)}, bf16[4,2,32,256]{3,2,1,0:T(8,128)(2,1)S(1)}, u32[]{:S(2)}, u32[]{:S(2)}) collective-permute-start(bf16[4,2,32,256]{3,2,1,0:T(8,128)(2,1)} %get-tuple-element.29), channel_id=1, source_target_pairs={{0,2},{1,3},{2,0},{3,1},{4,6},{5,7},{6,4},{7,5},{8,10},{9,11},{10,... | collective-permute-start | bytes 393224 | tf_op jit(solution)/shard_map/ppermute | solution.py:310
  21.6 7.1 %collective-permute-start.5 = (bf16[4,2,32,256]{3,2,1,0:T(8,128)(2,1)}, bf16[4,2,32,256]{3,2,1,0:T(8,128)(2,1)S(1)}, u32[]{:S(2)}, u32[]{:S(2)}) collective-permute-start(bf16[4,2,32,256]{3,2,1,0:T(8,128)(2,1)} %get-tuple-element.30), channel_id=1, source_target_pairs={{0,1},{1,0},{2,3},{3,2},{4,5},{5,4},{6,7},{7,6},{8,9},{9,8},{10,11... | collective-permute-start | bytes 393224 | tf_op jit(solution)/shard_map/ppermute | solution.py:310
  30.7 33.3 %collective-permute-start.10 = (bf16[2,8,32,256]{3,2,1,0:T(8,128)(2,1)}, bf16[2,8,32,256]{3,2,1,0:T(8,128)(2,1)S(1)}, u32[]{:S(2)}, u32[]{:S(2)}) collective-permute-start(bf16[2,8,32,256]{3,2,1,0:T(8,128)(2,1)} %get-tuple-element.15.refs_10_), channel_id=1, source_target_pairs={{4,0},{8,12},{5,1},{9,13},{6,2},{10,14},{7,3},{11,15},{20,16},{24,... | collective-permute-start | bytes 786440 | tf_op jit(solution)/shard_map/ppermute | solution.py:300
  38.0 35.0 %collective-permute-start.11 = (bf16[2,8,32,256]{3,2,1,0:T(8,128)(2,1)}, bf16[2,8,32,256]{3,2,1,0:T(8,128)(2,1)}, u32[]{:S(2)}, u32[]{:S(2)}) collective-permute-start(bf16[2,8,32,256]{3,2,1,0:T(8,128)(2,1)} %get-tuple-element.16.refs_11_), channel_id=1, source_target_pairs={{4,0},{8,12},{5,1},{9,13},{6,2},{10,14},{7,3},{11,15},{20,16},{24,... | collective-permute-start | bytes 786440 | tf_op jit(solution)/shard_map/ppermute | solution.py:300
  59.0 23.9 %copy-start.3 = (bf16[4,8,32,256]{3,2,1,0:T(8,128)(2,1)S(1)}, bf16[4,8,32,256]{3,2,1,0:T(8,128)(2,1)}, u32[]{:S(2)}) copy-start(bf16[4,8,32,256]{3,2,1,0:T(8,128)(2,1)} %refs_3_.1) | copy-start | bytes 1572868
  62.1 6.1 %collective-permute-start.14 = (bf16[4,2,32,256]{3,2,1,0:T(8,128)(2,1)}, bf16[4,2,32,256]{3,2,1,0:T(8,128)(2,1)}, u32[]{:S(2)}, u32[]{:S(2)}) collective-permute-start(bf16[4,2,32,256]{3,2,1,0:T(8,128)(2,1)} %get-tuple-element.22), channel_id=1, source_target_pairs={{0,3},{1,2},{2,1},{3,0},{4,7},{5,6},{6,5},{7,4},{8,11},{9,10},{10,... | collective-permute-start | bytes 393224 | tf_op jit(solution)/shard_map/ppermute | solution.py:310
  62.2 8.9 %collective-permute-start.13 = (bf16[4,2,32,256]{3,2,1,0:T(8,128)(2,1)}, bf16[4,2,32,256]{3,2,1,0:T(8,128)(2,1)}, u32[]{:S(2)}, u32[]{:S(2)}) collective-permute-start(bf16[4,2,32,256]{3,2,1,0:T(8,128)(2,1)} %get-tuple-element.23), channel_id=1, source_target_pairs={{0,2},{1,3},{2,0},{3,1},{4,6},{5,7},{6,4},{7,5},{8,10},{9,11},{10,... | collective-permute-start | bytes 393224 | tf_op jit(solution)/shard_map/ppermute | solution.py:310
  63.7 7.4 %collective-permute-start.12 = (bf16[4,2,32,256]{3,2,1,0:T(8,128)(2,1)}, bf16[4,2,32,256]{3,2,1,0:T(8,128)(2,1)}, u32[]{:S(2)}, u32[]{:S(2)}) collective-permute-start(bf16[4,2,32,256]{3,2,1,0:T(8,128)(2,1)} %get-tuple-element.24), channel_id=1, source_target_pairs={{0,1},{1,0},{2,3},{3,2},{4,5},{5,4},{6,7},{7,6},{8,9},{9,8},{10,11... | collective-permute-start | bytes 393224 | tf_op jit(solution)/shard_map/ppermute | solution.py:310
  71.1 4.2 %collective-permute-start.17 = (bf16[2,2,32,256]{3,2,1,0:T(8,128)(2,1)S(1)}, bf16[2,2,32,256]{3,2,1,0:T(8,128)(2,1)S(1)}, u32[]{:S(2)}, u32[]{:S(2)}) collective-permute-start(bf16[2,2,32,256]{3,2,1,0:T(8,128)(2,1)S(1)} %get-tuple-element.40), channel_id=1, source_target_pairs={{0,3},{1,2},{2,1},{3,0},{4,7},{5,6},{6,5},{7,4},{8,11},{9,10},{10,... | collective-permute-start | bytes 196616 | tf_op jit(solution)/shard_map/ppermute | solution.py:310
  71.2 5.8 %collective-permute-start.16 = (bf16[2,2,32,256]{3,2,1,0:T(8,128)(2,1)S(1)}, bf16[2,2,32,256]{3,2,1,0:T(8,128)(2,1)S(1)}, u32[]{:S(2)}, u32[]{:S(2)}) collective-permute-start(bf16[2,2,32,256]{3,2,1,0:T(8,128)(2,1)S(1)} %get-tuple-element.41), channel_id=1, source_target_pairs={{0,2},{1,3},{2,0},{3,1},{4,6},{5,7},{6,4},{7,5},{8,10},{9,11},{10,... | collective-permute-start | bytes 196616 | tf_op jit(solution)/shard_map/ppermute | solution.py:310
  72.9 4.1 %collective-permute-start.15 = (bf16[2,2,32,256]{3,2,1,0:T(8,128)(2,1)S(1)}, bf16[2,2,32,256]{3,2,1,0:T(8,128)(2,1)S(1)}, u32[]{:S(2)}, u32[]{:S(2)}) collective-permute-start(bf16[2,2,32,256]{3,2,1,0:T(8,128)(2,1)S(1)} %get-tuple-element.42), channel_id=1, source_target_pairs={{0,1},{1,0},{2,3},{3,2},{4,5},{5,4},{6,7},{7,6},{8,9},{9,8},{10,11... | collective-permute-start | bytes 196616 | tf_op jit(solution)/shard_map/ppermute | solution.py:310
  77.0 4.4 %collective-permute-start.20 = (bf16[2,2,32,256]{3,2,1,0:T(8,128)(2,1)S(1)}, bf16[2,2,32,256]{3,2,1,0:T(8,128)(2,1)S(1)}, u32[]{:S(2)}, u32[]{:S(2)}) collective-permute-start(bf16[2,2,32,256]{3,2,1,0:T(8,128)(2,1)S(1)} %get-tuple-element.36), channel_id=1, source_target_pairs={{0,3},{1,2},{2,1},{3,0},{4,7},{5,6},{6,5},{7,4},{8,11},{9,10},{10,... | collective-permute-start | bytes 196616 | tf_op jit(solution)/shard_map/ppermute | solution.py:310
  77.1 5.8 %collective-permute-start.19 = (bf16[2,2,32,256]{3,2,1,0:T(8,128)(2,1)S(1)}, bf16[2,2,32,256]{3,2,1,0:T(8,128)(2,1)S(1)}, u32[]{:S(2)}, u32[]{:S(2)}) collective-permute-start(bf16[2,2,32,256]{3,2,1,0:T(8,128)(2,1)S(1)} %get-tuple-element.37), channel_id=1, source_target_pairs={{0,2},{1,3},{2,0},{3,1},{4,6},{5,7},{6,4},{7,5},{8,10},{9,11},{10,... | collective-permute-start | bytes 196616 | tf_op jit(solution)/shard_map/ppermute | solution.py:310
  78.6 4.3 %collective-permute-start.18 = (bf16[2,2,32,256]{3,2,1,0:T(8,128)(2,1)S(1)}, bf16[2,2,32,256]{3,2,1,0:T(8,128)(2,1)S(1)}, u32[]{:S(2)}, u32[]{:S(2)}) collective-permute-start(bf16[2,2,32,256]{3,2,1,0:T(8,128)(2,1)S(1)} %get-tuple-element.38), channel_id=1, source_target_pairs={{0,1},{1,0},{2,3},{3,2},{4,5},{5,4},{6,7},{7,6},{8,9},{9,8},{10,11... | collective-permute-start | bytes 196616 | tf_op jit(solution)/shard_map/ppermute | solution.py:310
  (22 other events, 140.0 us)

commit v8 on v7

--- a/solution.py
+++ b/solution.py
@@ -12,7 +12,7 @@
 KVH = 8
 LOG2E = 1.4426950408889634
 STEP = 4
-TOGETHER = 4
+VMEM_BYTES = 24 << 20
 
 
 class Part:
@@ -43,9 +43,7 @@
     if last_call:
         out_ref, cache_ref = take(2)
     else:
-        out_ref, next_total_ref, mark_ref = take(3)
-        next_total_ref[...] = jnp.zeros_like(next_total_ref)
-        mark_ref[...] = jnp.zeros_like(mark_ref)
+        out_ref, next_total_ref = take(2)
     place_ref, list_ref, kv_ref, s_ref, p_ref, acc_ref, max_ref, part_sems = take(8)
     if last_call:
         zero_ref, page_sems = take(2)
@@ -59,6 +57,7 @@
     inst = place_at_ref[0]
     tp = place_at_ref[1]
     slice_len = span_len // tp_size
+    most = min(longest, len(covers) * slot_count)
     scale = LOG2E / math.sqrt(head_dim)
 
     def part_copies(act):
@@ -147,39 +146,27 @@
     col_ids = lax.broadcasted_iota(jnp.int32, (span_len, span_len), 1)
     causal = row_ids >= col_ids
     lane_ids = lax.broadcasted_iota(jnp.int32, (span_len, head_dim), 1)
-    heads = kv_local * per_head
-    together = math.gcd(per_head, TOGETHER)
-
     def lanes_of(head):
-        return pl.ds(pl.multiple_of(head * head_dim, head_dim), head_dim)
+        return slice(head * head_dim, (head + 1) * head_dim)
 
     def rows_of(h):
         return slice(h * span_len, (h + 1) * span_len)
 
     def attend(pages, since):
         wide = len(pages) * span_len
-
-        def some_heads(c, unused):
-            head0 = c * together
-            g = head0 // per_head
+        for g in range(kv_local):
             keys = jnp.concatenate([kv_ref[page, g, :, :head_dim] for page in pages], axis=0)
-            values = jnp.concatenate(
-                [
-                    jnp.concatenate([kv_ref[page, g, :, head_dim:], ones], axis=1)
-                    for page in pages
-                ],
-                axis=0,
+            q = jnp.concatenate(
+                [q_ref[0, :, lanes_of(g * per_head + h)] for h in range(per_head)], axis=0
             )
-            q = jnp.concatenate(
-                [q_ref[0, :, lanes_of(head0 + h)] for h in range(together)], axis=0
-            )
-            s_ref[:, :wide] = lax.dot_general(
+            s_ref[g, :, :wide] = lax.dot_general(
                 q, keys, (((1,), (1,)), ((), ())), preferred_element_type=jnp.float32
             )
+        for g in range(kv_local):
             rescales = []
-            for h in range(together):
-                head = head0 + h
-                s = s_ref[rows_of(h), :wide] * scale
+            for h in range(per_head):
+                head = g * per_head + h
+                s = s_ref[g, rows_of(h), :wide] * scale
                 if since == "start":
                     own_part = jnp.where(causal, s[:, wide - span_len:], -1e30)
                     if len(pages) > 1:
@@ -192,23 +179,26 @@
                 else:
                     if since == "given":
                         old = jnp.broadcast_to(
-                            jnp.sum(
-                                jnp.where(lane_ids == head, total_ref[0], 0.0),
-                                axis=1, keepdims=True,
-                            ),
-                            (span_len, head_dim),
+                            total_ref[0, :, head:head + 1], (span_len, head_dim)
                         )
                     else:
                         old = max_ref[head]
                     top = jnp.maximum(old, top)
                     rescales.append(jnp.exp2(old - top))
                 max_ref[head] = top
-                p_ref[rows_of(h), :wide] = jnp.exp2(
+                p_ref[g, rows_of(h), :wide] = jnp.exp2(
                     s - jnp.concatenate([top] * len(pages), axis=1)
                 ).astype(jnp.bfloat16)
-            mixed = jnp.dot(p_ref[:, :wide], values, preferred_element_type=jnp.float32)
-            for h in range(together):
-                head = head0 + h
+            values = jnp.concatenate(
+                [
+                    jnp.concatenate([kv_ref[page, g, :, head_dim:], ones], axis=1)
+                    for page in pages
+                ],
+                axis=0,
+            )
+            mixed = jnp.dot(p_ref[g, :, :wide], values, preferred_element_type=jnp.float32)
+            for h in range(per_head):
+                head = g * per_head + h
                 new = mixed[rows_of(h)]
                 if since == "given":
                     given = mixed_ref[0, :, lanes_of(head)].astype(jnp.float32)
@@ -216,11 +206,11 @@
                 elif since == "here":
                     new = new + acc_ref[head] * jnp.concatenate([rescales[h]] * 2, axis=1)
                 acc_ref[head] = new
-            return unused
-
-        lax.fori_loop(0, heads // together, some_heads, 0)
 
     def rest(begin):
+        if most <= STEP:
+            return
+
         def block(j, unused):
             at = begin + STEP * j
             attend([list_ref[at + n] for n in range(STEP)], "here")
@@ -231,19 +221,19 @@
     live = lax.broadcasted_iota(jnp.int32, (span_len, head_dim), 0) < live_rows
 
     def finish():
-        def one_head(head, unused):
+        tops = jnp.zeros((span_len, head_dim), jnp.float32)
+        totals = jnp.ones((span_len, head_dim), jnp.float32)
+        for head in range(kv_local * per_head):
             total = acc_ref[head, :, head_dim:]
             mixed = acc_ref[head, :, :head_dim] / total
             if last_call:
                 mixed = jnp.where(live, mixed, 0.0)
             else:
-                next_total_ref[0] = jnp.where(
-                    lane_ids == head, max_ref[head] + jnp.log(total) * LOG2E, next_total_ref[0]
-                )
+                tops = jnp.where(lane_ids == head, max_ref[head], tops)
+                totals = jnp.where(lane_ids == head, total, totals)
             out_ref[0, :, lanes_of(head)] = mixed.astype(jnp.bfloat16)
-            return unused
-
-        lax.fori_loop(0, heads, one_head, 0)
+        if not last_call:
+            next_total_ref[0] = tops + jnp.log(totals) * LOG2E
 
     if first_call:
         over = lax.rem(count, STEP)
@@ -259,12 +249,13 @@
 
         @pl.when(count == 0)
         def _():
-            def one_head(head, unused):
-                given = mixed_ref[0, :, lanes_of(head)]
-                out_ref[0, :, lanes_of(head)] = jnp.where(live, given, jnp.zeros_like(given))
-                return unused
-
-            lax.fori_loop(0, heads, one_head, 0)
+            if last_call:
+                for head in range(kv_local * per_head):
+                    given = mixed_ref[0, :, lanes_of(head)]
+                    out_ref[0, :, lanes_of(head)] = jnp.where(live, given, jnp.zeros_like(given))
+            else:
+                out_ref[...] = mixed_ref[...]
+                next_total_ref[...] = total_ref[...]
 
         @pl.when(count > 0)
         def _():
@@ -299,11 +290,11 @@
     def along(x, pairs):
         return lax.ppermute(x, "inst", pairs)
 
-    def exchange(*pieces, zero=0):
+    def exchange(*pieces):
         names = [name for name, _ in pieces]
         found = []
         for j in range(tp_size):
-            head = ((tp ^ j) * kv_heads) // tp_size + zero
+            head = ((tp ^ j) * kv_heads) // tp_size
             sent = [lax.dynamic_slice_in_dim(x, head, kv_local, 1) for _, x in pieces]
             sent = jnp.concatenate(sent, axis=0) if len(sent) > 1 else sent[0]
             if j:
@@ -333,22 +324,26 @@
     outer_on, inner_on = after([outer, inner], waiting)
     crossed = along(outer_on, [(1, 2), (2, 1)])
     inner_ends = along(inner_on, [(1, 0), (2, 3)])
-    waiting = exchange(((1, 0, whole), outer_on))
-    crossed_on = after([crossed], waiting)[0]
+    own_parts = parts[:]
+    first_parts = exchange(((1, 0, whole), outer_on))
+    state = attend([0], own_parts, sources, later=first_parts[:1])
+    state = attend([1], parts[tp_size:], sources, state=state)
+    crossed_on = after([crossed], first_parts)[0]
     crossed_half = lax.optimization_barrier([crossed_on[:half], crossed_on[half:]])
     crossed_ends = [along(x, [(1, 0), (2, 3)]) for x in crossed_half]
-    early = len(parts)
     two = jnp.where(middle, inner, inner_ends)
     waiting = exchange(((second, 0, whole), two))
-    *state, mark = attend([0, 1], parts[:early], sources, later=[waiting[0], *crossed_half])
+    second_parts = parts[2 * tp_size:]
+    third_parts = len(parts)
+    threes = [jnp.where(middle, crossed_half[n], crossed_ends[n]) for n in range(2)]
+    waiting = exchange(((third, 0, half), after(threes[:1], waiting)[0]))
+    state = attend([second], second_parts, sources, state=state, later=waiting[:1])
+    exchange(((third, half, half), after(threes[1:], waiting)[0]))
     for n in range(2):
-        three = jnp.where(middle, crossed_half[n], crossed_ends[n])
-        three = after([three], waiting)[0]
-        waiting = exchange(((third, n * half, half), three), zero=mark[0, 0])
         hops.append(((5, n * half, half), crossed_ends[n]))
     for hop, x in enumerate((outer, inner, crossed, inner_ends), 1):
         hops.append(((hop, 0, whole), x))
-    return state, ([second, third], parts[early:], sources), hops
+    return state, ([third], parts[third_parts:], sources), hops
 
 
 def body(queries, kv_new, prompt_spans, prompt_tail, span_plan, decode_owner):
@@ -366,7 +361,7 @@
     longest = span_total // 2
     anywhere = pl.BlockSpec(memory_space=pl.ANY)
     by_slot = pl.BlockSpec((1, span_len, row_width), lambda i, *_: (i, 0, 0))
-    rows = math.gcd(per_head, TOGETHER) * span_len
+    rows = per_head * span_len
     total_spec = pl.BlockSpec((1, span_len, head_dim), lambda i, *_: (i, 0, 0))
     state_specs = [by_slot, total_spec]
     work = slot_count * 4 * local_heads * span_len * span_len
@@ -403,8 +398,8 @@
             pltpu.SMEM((span_total,), jnp.int32),
             pltpu.SMEM((span_total,), jnp.int32),
             pltpu.VMEM((span_total, kv_local, span_len, width), jnp.bfloat16),
-            pltpu.VMEM((rows, STEP * span_len), jnp.float32),
-            pltpu.VMEM((rows, STEP * span_len), jnp.bfloat16),
+            pltpu.VMEM((kv_local, rows, STEP * span_len), jnp.float32),
+            pltpu.VMEM((kv_local, rows, STEP * span_len), jnp.bfloat16),
             pltpu.VMEM((local_heads, span_len, 2 * head_dim), jnp.float32),
             pltpu.VMEM((local_heads, span_len, head_dim), jnp.float32),
             pltpu.SemaphoreType.DMA((len(parts), max(len(x[0][0]) for x in parts))),
@@ -420,11 +415,10 @@
                 jax.ShapeDtypeStruct((longest, kv_heads, slice_len, width), jnp.bfloat16),
             ]
         else:
-            out_specs = state_specs + [pl.BlockSpec((8, 128), lambda i, *_: (0, 0))]
+            out_specs = state_specs
             out_shape = [
                 jax.ShapeDtypeStruct(queries.shape, jnp.bfloat16),
                 jax.ShapeDtypeStruct((slot_count, span_len, head_dim), jnp.float32),
-                jax.ShapeDtypeStruct((8, 128), jnp.int32),
             ]
         return pl.pallas_call(
             kernel,
@@ -440,7 +434,7 @@
             cost_estimate=pl.CostEstimate(
                 flops=4 * work * head_dim, bytes_accessed=8 << 20, transcendentals=work
             ),
-            compiler_params=pltpu.CompilerParams(vmem_limit_bytes=40 << 20),
+            compiler_params=pltpu.CompilerParams(vmem_limit_bytes=VMEM_BYTES),
         )(
             numbers, queries, *state, *[x for _, x in hops], *[x for _, x in parts],
             *later,

time: 99.9 us -> 70.3 us (0.70)
  the two profiles are of different devices: /device:TPU:0 before, /device:TPU:5 now
where the time goes in v8:
time: 70.3 us; the launch traced here: 71.1 us
  waiting for transfers between devices  24.8 us (35%)
  Pallas kernels  22.1 us (31%)
  starting transfers between devices  19.4 us (28%)
  local copies, waits for them, and re-layouts  3.51 us (5%)
  between operations  1.14 us (2%)
    pallas_call x4, Pallas kernels, attend(): pl.pallas_call(kernel, grid_spec=pltpu.PrefetchScalarGridSpec(num_scalar_...  22.1 us
    ppermute x6, waiting for transfers between devices, along(): return lax.ppermute(x, 'inst', pairs)  18.6 us
    ppermute x15, starting transfers between devices, exchange(): sent = lax.ppermute(sent, 'tp', [(t, t ^ j) for t in range(tp_size)])  12.9 us
    ppermute x6, starting transfers between devices, along(): return lax.ppermute(x, 'inst', pairs)  6.58 us
    ppermute x15, waiting for transfers between devices, exchange(): sent = lax.ppermute(sent, 'tp', [(t, t ^ j) for t in range(tp_size)])  6.14 us
    dynamic_slice x5, local copies, waits for them, and re-layouts, exchange(): sent = [lax.dynamic_slice_in_dim(x, head, kv_local, 1) for _, x in pieces]  2 us
  transfers between devices with their start and end apart: 21, of which 6 were waited for; matrix products, arithmetic and copies ran while one was open for 5% of the time, Pallas kernels for 21%

profile of v8, /device:TPU:5, one launch (start us, length us, event | category | flops | bytes accessed | tf_op | source)
XLA Modules:
  0.0 71.1 jit_solution(13459155142025735567)
XLA Ops:
  0.6 1.4 %collective-permute-start.3 = (bf16[4,8,32,256]{3,2,1,0:T(8,128)(2,1)}, bf16[4,8,32,256]{3,2,1,0:T(8,128)(2,1)S(1)}, u32[]{:S(2)}, u32[]{:S(2)}) collective-permute-start(bf16[4,8,32,256]{3,2,1,0:T(8,128)(2,1)} %refs_3_.1), channel_id=1, source_target_pairs={{0,4},{4,0},{8,12},{12,8},{1,5},{5,1},{9,13},{13,9},{2,6},{6,2},{1... | collective-permute-start | bytes 1572872 | tf_op jit(solution)/shard_map/ppermute | solution.py:291
  2.8 1.9 %constant_dynamic-slice_fusion.13 = (bf16[4,2,32,256]{3,2,1,0:T(8,128)(2,1)}, bf16[4,2,32,256]{3,2,1,0:T(8,128)(2,1)}, bf16[4,2,32,256]{3,2,1,0:T(8,128)(2,1)}, bf16[4,2,32,256]{3,2,1,0:T(8,128)(2,1)S(1)}) fusion(bf16[4,8,32,256]{3,2,1,0:T(8,128)(2,1)} %refs_3_.1, s32[]{:T(128)S(6)} %select_n.93, s32[]{:T(128)S(6)} %select_n.91, s32[]{:T(128)S(6)} %select_n.89, ...), kind=kLoop, calls=%fused_computation.16 | loop fusion | bytes 1048592 | tf_op jit(solution)/shard_map/dynamic_slice | solution.py:298
  4.7 1.0 %collective-permute-start = (bf16[4,2,32,256]{3,2,1,0:T(8,128)(2,1)}, bf16[4,2,32,256]{3,2,1,0:T(8,128)(2,1)S(1)}, u32[]{:S(2)}, u32[]{:S(2)}) collective-permute-start(bf16[4,2,32,256]{3,2,1,0:T(8,128)(2,1)} %get-tuple-element.40), channel_id=1, source_target_pairs={{0,1},{1,0},{2,3},{3,2},{4,5},{5,4},{6,7},{7,6},{8,9},{9,8},{10,11... | collective-permute-start | bytes 393224 | tf_op jit(solution)/shard_map/ppermute | solution.py:301
  5.6 1.2 %collective-permute-start.1 = (bf16[4,2,32,256]{3,2,1,0:T(8,128)(2,1)}, bf16[4,2,32,256]{3,2,1,0:T(8,128)(2,1)S(1)}, u32[]{:S(2)}, u32[]{:S(2)}) collective-permute-start(bf16[4,2,32,256]{3,2,1,0:T(8,128)(2,1)} %get-tuple-element.39), channel_id=1, source_target_pairs={{0,2},{1,3},{2,0},{3,1},{4,6},{5,7},{6,4},{7,5},{8,10},{9,11},{10,... | collective-permute-start | bytes 393224 | tf_op jit(solution)/shard_map/ppermute | solution.py:301
  7.9 0.8 %concatenate.12.numbers_ref = s32[38]{0:T(128)S(1)} concatenate(s32[4]{0:T(128)} %param.12, s32[4]{0:T(128)} %param.13, s32[4]{0:T(128)} %param.15, s32[16]{0:T(128)} %param.14, s32[1]{0:T(128)} %bitcast, s32[1]{0:T(128)} %bitcast.1, s32[8]{0:T(128)S(1)} %fusion), dimensions={0} | concatenate | bytes 304 | tf_op jit(solution)/shard_map/concatenate | solution.py:375
  8.7 2.2 %collective-permute-done.1.refs_3_ = bf16[4,2,32,256]{3,2,1,0:T(8,128)(2,1)S(1)} collective-permute-done((bf16[4,2,32,256]{3,2,1,0:T(8,128)(2,1)}, bf16[4,2,32,256]{3,2,1,0:T(8,128)(2,1)S(1)}, u32[]{:S(2)}, u32[]{:S(2)}) %collective-permute-start.1) | collective-permute-done | bytes 131104 | tf_op jit(solution)/shard_map/ppermute | solution.py:301
  10.9 3.2 %collective-permute-done.2.refs_4_ = bf16[4,2,32,256]{3,2,1,0:T(8,128)(2,1)} collective-permute-done((bf16[4,2,32,256]{3,2,1,0:T(8,128)(2,1)}, bf16[4,2,32,256]{3,2,1,0:T(8,128)(2,1)}, u32[]{:S(2)}, u32[]{:S(2)}) %collective-permute-start.2) | collective-permute-done | bytes 131104 | tf_op jit(solution)/shard_map/ppermute | solution.py:301
  14.9 1.2 %collective-permute-start.5 = (bf16[4,2,32,256]{3,2,1,0:T(8,128)(2,1)S(1)}, bf16[4,2,32,256]{3,2,1,0:T(8,128)(2,1)S(1)}, u32[]{:S(2)}, u32[]{:S(2)}) collective-permute-start(bf16[4,2,32,256]{3,2,1,0:T(8,128)(2,1)S(1)} %get-tuple-element.36), channel_id=1, source_target_pairs={{0,1},{1,0},{2,3},{3,2},{4,5},{5,4},{6,7},{7,6},{8,9},{9,8},{10,11... | collective-permute-start | bytes 393224 | tf_op jit(solution)/shard_map/ppermute | solution.py:301
  16.1 1.2 %collective-permute-start.6 = (bf16[4,2,32,256]{3,2,1,0:T(8,128)(2,1)S(1)}, bf16[4,2,32,256]{3,2,1,0:T(8,128)(2,1)S(1)}, u32[]{:S(2)}, u32[]{:S(2)}) collective-permute-start(bf16[4,2,32,256]{3,2,1,0:T(8,128)(2,1)S(1)} %get-tuple-element.35), channel_id=1, source_target_pairs={{0,2},{1,3},{2,0},{3,1},{4,6},{5,7},{6,4},{7,5},{8,10},{9,11},{10,... | collective-permute-start | bytes 393224 | tf_op jit(solution)/shard_map/ppermute | solution.py:301
  17.8 1.3 %collective-permute-start.8 = (bf16[4,8,32,256]{3,2,1,0:T(8,128)(2,1)S(1)}, bf16[4,8,32,256]{3,2,1,0:T(8,128)(2,1)S(1)}, u32[]{:S(2)}, u32[]{:S(2)}) collective-permute-start(bf16[4,8,32,256]{3,2,1,0:T(8,128)(2,1)S(1)} %collective-permute-done.4.refs_7_), channel_id=1, source_target_pairs={{4,0},{8,12},{5,1},{9,13},{6,2},{10,14},{7,3},{11,15},{20,16},{24,... | collective-permute-start | bytes 1572872 | tf_op jit(solution)/shard_map/ppermute | solution.py:291
  19.1 5.9 %shard_map.113 = (bf16[4,128,2048]{2,1,0:T(8,128)(2,1)S(1)}, f32[4,128,128]{2,1,0:T(8,128)S(1)}) custom-call(s32[38]{0:T(128)S(1)} %concatenate.12.numbers_ref, bf16[4,128,2048]{2,1,0:T(8,128)(2,1)S(1)} %copy-done.1, bf16[4,2,32,256]{3,2,1,0:T(8,128)(2,1)S(1)} %get-tuple-element.41.refs_1_, bf16[4,2,32,256]{3,2,1,0:T(8,128)(2,1)S(1)} %collective-permute-done.refs_2_, ...), custom_call_target="tpu_custom_call" | custom-call | flops 2147483648 | bytes 8388608 | tf_op jit(solution)/shard_map/pallas_call | solution.py:423
  25.0 3.2 %shard_map.114 = (bf16[4,128,2048]{2,1,0:T(8,128)(2,1)S(1)}, f32[4,128,128]{2,1,0:T(8,128)S(1)}) custom-call(s32[38]{0:T(128)S(1)} %concatenate.12.numbers_ref, bf16[4,128,2048]{2,1,0:T(8,128)(2,1)S(1)} %copy-done.1, bf16[4,128,2048]{2,1,0:T(8,128)(2,1)S(1)} %get-tuple-element.16.refs_1_, f32[4,128,128]{2,1,0:T(8,128)S(1)} %get-tuple-element.17.refs_2_, ...), custom_call_target="tpu_custom_call" | custom-call | flops 2147483648 | bytes 8388608 | tf_op jit(solution)/shard_map/pallas_call | solution.py:423
  28.3 1.3 %collective-permute-start.13 = (bf16[2,8,32,256]{3,2,1,0:T(8,128)(2,1)S(1)}, bf16[2,8,32,256]{3,2,1,0:T(8,128)(2,1)S(1)}, u32[]{:S(2)}, u32[]{:S(2)}) collective-permute-start(bf16[2,8,32,256]{3,2,1,0:T(8,128)(2,1)S(1)} %get-tuple-element.22), channel_id=1, source_target_pairs={{4,0},{8,12},{5,1},{9,13},{6,2},{10,14},{7,3},{11,15},{20,16},{24,... | collective-permute-start | bytes 786440 | tf_op jit(solution)/shard_map/ppermute | solution.py:291
  29.6 8.9 %collective-permute-done.8.refs_9_ = bf16[4,8,32,256]{3,2,1,0:T(8,128)(2,1)S(1)} collective-permute-done((bf16[4,8,32,256]{3,2,1,0:T(8,128)(2,1)S(1)}, bf16[4,8,32,256]{3,2,1,0:T(8,128)(2,1)S(1)}, u32[]{:S(2)}, u32[]{:S(2)}) %collective-permute-start.8) | collective-permute-done | bytes 524320 | tf_op jit(solution)/shard_map/ppermute | solution.py:291
  38.6 0.8 %collective-permute-start.9 = (bf16[4,2,32,256]{3,2,1,0:T(8,128)(2,1)S(1)}, bf16[4,2,32,256]{3,2,1,0:T(8,128)(2,1)S(1)}, u32[]{:S(2)}, u32[]{:S(2)}) collective-permute-start(bf16[4,2,32,256]{3,2,1,0:T(8,128)(2,1)S(1)} %get-tuple-element.32), channel_id=1, source_target_pairs={{0,1},{1,0},{2,3},{3,2},{4,5},{5,4},{6,7},{7,6},{8,9},{9,8},{10,11... | collective-permute-start | bytes 393224 | tf_op jit(solution)/shard_map/ppermute | solution.py:301
  39.4 1.2 %collective-permute-start.10 = (bf16[4,2,32,256]{3,2,1,0:T(8,128)(2,1)S(1)}, bf16[4,2,32,256]{3,2,1,0:T(8,128)(2,1)S(1)}, u32[]{:S(2)}, u32[]{:S(2)}) collective-permute-start(bf16[4,2,32,256]{3,2,1,0:T(8,128)(2,1)S(1)} %get-tuple-element.31), channel_id=1, source_target_pairs={{0,2},{1,3},{2,0},{3,1},{4,6},{5,7},{6,4},{7,5},{8,10},{9,11},{10,... | collective-permute-start | bytes 393224 | tf_op jit(solution)/shard_map/ppermute | solution.py:301
  41.1 1.3 %collective-permute-start.14 = (bf16[2,8,32,256]{3,2,1,0:T(8,128)(2,1)S(1)}, bf16[2,8,32,256]{3,2,1,0:T(8,128)(2,1)S(1)}, u32[]{:S(2)}, u32[]{:S(2)}) collective-permute-start(bf16[2,8,32,256]{3,2,1,0:T(8,128)(2,1)S(1)} %get-tuple-element.26), channel_id=1, source_target_pairs={{4,0},{8,12},{5,1},{9,13},{6,2},{10,14},{7,3},{11,15},{20,16},{24,... | collective-permute-start | bytes 786440 | tf_op jit(solution)/shard_map/ppermute | solution.py:291
  42.4 6.9 %collective-permute-done.13.refs_4_ = bf16[2,8,32,256]{3,2,1,0:T(8,128)(2,1)S(1)} collective-permute-done((bf16[2,8,32,256]{3,2,1,0:T(8,128)(2,1)S(1)}, bf16[2,8,32,256]{3,2,1,0:T(8,128)(2,1)S(1)}, u32[]{:S(2)}, u32[]{:S(2)}) %collective-permute-start.13) | collective-permute-done | bytes 262176 | tf_op jit(solution)/shard_map/ppermute | solution.py:291
  49.4 1.0 %collective-permute-start.15 = (bf16[2,2,32,256]{3,2,1,0:T(8,128)(2,1)S(1)}, bf16[2,2,32,256]{3,2,1,0:T(8,128)(2,1)S(1)}, u32[]{:S(2)}, u32[]{:S(2)}) collective-permute-start(bf16[2,2,32,256]{3,2,1,0:T(8,128)(2,1)S(1)} %get-tuple-element.48), channel_id=1, source_target_pairs={{0,1},{1,0},{2,3},{3,2},{4,5},{5,4},{6,7},{7,6},{8,9},{9,8},{10,11... | collective-permute-start | bytes 196616 | tf_op jit(solution)/shard_map/ppermute | solution.py:301
  50.4 1.2 %collective-permute-start.16 = (bf16[2,2,32,256]{3,2,1,0:T(8,128)(2,1)S(1)}, bf16[2,2,32,256]{3,2,1,0:T(8,128)(2,1)S(1)}, u32[]{:S(2)}, u32[]{:S(2)}) collective-permute-start(bf16[2,2,32,256]{3,2,1,0:T(8,128)(2,1)S(1)} %get-tuple-element.47), channel_id=1, source_target_pairs={{0,2},{1,3},{2,0},{3,1},{4,6},{5,7},{6,4},{7,5},{8,10},{9,11},{10,... | collective-permute-start | bytes 196616 | tf_op jit(solution)/shard_map/ppermute | solution.py:301
  52.1 2.8 %collective-permute-done.14.refs_5_ = bf16[2,8,32,256]{3,2,1,0:T(8,128)(2,1)S(1)} collective-permute-done((bf16[2,8,32,256]{3,2,1,0:T(8,128)(2,1)S(1)}, bf16[2,8,32,256]{3,2,1,0:T(8,128)(2,1)S(1)}, u32[]{:S(2)}, u32[]{:S(2)}) %collective-permute-start.14) | collective-permute-done | bytes 262176 | tf_op jit(solution)/shard_map/ppermute | solution.py:291
  56.1 1.1 %collective-permute-start.19 = (bf16[2,2,32,256]{3,2,1,0:T(8,128)(2,1)S(1)}, bf16[2,2,32,256]{3,2,1,0:T(8,128)(2,1)S(1)}, u32[]{:S(2)}, u32[]{:S(2)}) collective-permute-start(bf16[2,2,32,256]{3,2,1,0:T(8,128)(2,1)S(1)} %get-tuple-element.43), channel_id=1, source_target_pairs={{0,2},{1,3},{2,0},{3,1},{4,6},{5,7},{6,4},{7,5},{8,10},{9,11},{10,... | collective-permute-start | bytes 196616 | tf_op jit(solution)/shard_map/ppermute | solution.py:301
  57.9 6.1 %shard_map.115 = (bf16[4,128,2048]{2,1,0:T(8,128)(2,1)S(1)}, f32[4,128,128]{2,1,0:T(8,128)S(1)}) custom-call(s32[38]{0:T(128)S(1)} %concatenate.12.numbers_ref, bf16[4,128,2048]{2,1,0:T(8,128)(2,1)S(1)} %copy-done.1, bf16[4,128,2048]{2,1,0:T(8,128)(2,1)S(1)} %get-tuple-element.18.refs_1_, f32[4,128,128]{2,1,0:T(8,128)S(1)} %get-tuple-element.19.refs_2_, ...), custom_call_target="tpu_custom_call" | custom-call | flops 2147483648 | bytes 8388608 | tf_op jit(solution)/shard_map/pallas_call | solution.py:423
  64.1 6.9 %shard_map.116 = (bf16[4,128,2048]{2,1,0:T(8,128)(2,1)}, bf16[8,8,32,256]{3,2,1,0:T(8,128)(2,1)}) custom-call(s32[38]{0:T(128)S(1)} %concatenate.12.numbers_ref, bf16[4,128,2048]{2,1,0:T(8,128)(2,1)S(1)} %copy-done.1, bf16[4,128,2048]{2,1,0:T(8,128)(2,1)S(1)} %get-tuple-element.24.refs_1_, f32[4,128,128]{2,1,0:T(8,128)S(1)} %get-tuple-element.25.refs_2_, ...), custom_call_target="tpu_custom_call" | custom-call | flops 2147483648 | bytes 8388608 | tf_op jit(solution)/shard_map/pallas_call | solution.py:423
  (37 shorter events, 6.1 us)
Async XLA Ops:
  0.6 18.4 %copy-start.1 = (bf16[4,128,2048]{2,1,0:T(8,128)(2,1)S(1)}, bf16[4,128,2048]{2,1,0:T(8,128)(2,1)}, u32[]{:S(2)}) copy-start(bf16[4,128,2048]{2,1,0:T(8,128)(2,1)} %refs_0_.7) | copy-start | bytes 6291460
  0.6 13.5 %collective-permute-start.3 = (bf16[4,8,32,256]{3,2,1,0:T(8,128)(2,1)}, bf16[4,8,32,256]{3,2,1,0:T(8,128)(2,1)S(1)}, u32[]{:S(2)}, u32[]{:S(2)}) collective-permute-start(bf16[4,8,32,256]{3,2,1,0:T(8,128)(2,1)} %refs_3_.1), channel_id=1, source_target_pairs={{0,4},{4,0},{8,12},{12,8},{1,5},{5,1},{9,13},{13,9},{2,6},{6,2},{1... | collective-permute-start | bytes 1572872 | tf_op jit(solution)/shard_map/ppermute | solution.py:291
  2.0 12.2 %collective-permute-start.4 = (bf16[4,8,32,256]{3,2,1,0:T(8,128)(2,1)}, bf16[4,8,32,256]{3,2,1,0:T(8,128)(2,1)S(1)}, u32[]{:S(2)}, u32[]{:S(2)}) collective-permute-start(bf16[4,8,32,256]{3,2,1,0:T(8,128)(2,1)} %refs_3_.1), channel_id=1, source_target_pairs={{4,8},{8,4},{5,9},{9,5},{6,10},{10,6},{7,11},{11,7},{20,24},{24,20... | collective-permute-start | bytes 1572872 | tf_op jit(solution)/shard_map/ppermute | solution.py:291
  4.7 4.1 %collective-permute-start = (bf16[4,2,32,256]{3,2,1,0:T(8,128)(2,1)}, bf16[4,2,32,256]{3,2,1,0:T(8,128)(2,1)S(1)}, u32[]{:S(2)}, u32[]{:S(2)}) collective-permute-start(bf16[4,2,32,256]{3,2,1,0:T(8,128)(2,1)} %get-tuple-element.40), channel_id=1, source_target_pairs={{0,1},{1,0},{2,3},{3,2},{4,5},{5,4},{6,7},{7,6},{8,9},{9,8},{10,11... | collective-permute-start | bytes 393224 | tf_op jit(solution)/shard_map/ppermute | solution.py:301
  5.6 5.3 %collective-permute-start.1 = (bf16[4,2,32,256]{3,2,1,0:T(8,128)(2,1)}, bf16[4,2,32,256]{3,2,1,0:T(8,128)(2,1)S(1)}, u32[]{:S(2)}, u32[]{:S(2)}) collective-permute-start(bf16[4,2,32,256]{3,2,1,0:T(8,128)(2,1)} %get-tuple-element.39), channel_id=1, source_target_pairs={{0,2},{1,3},{2,0},{3,1},{4,6},{5,7},{6,4},{7,5},{8,10},{9,11},{10,... | collective-permute-start | bytes 393224 | tf_op jit(solution)/shard_map/ppermute | solution.py:301
  6.8 7.3 %collective-permute-start.2 = (bf16[4,2,32,256]{3,2,1,0:T(8,128)(2,1)}, bf16[4,2,32,256]{3,2,1,0:T(8,128)(2,1)}, u32[]{:S(2)}, u32[]{:S(2)}) collective-permute-start(bf16[4,2,32,256]{3,2,1,0:T(8,128)(2,1)} %get-tuple-element.38), channel_id=1, source_target_pairs={{0,3},{1,2},{2,1},{3,0},{4,7},{5,6},{6,5},{7,4},{8,11},{9,10},{10,... | collective-permute-start | bytes 393224 | tf_op jit(solution)/shard_map/ppermute | solution.py:301
  14.2 14.0 %collective-permute-start.12 = (bf16[4,8,32,256]{3,2,1,0:T(8,128)(2,1)S(1)}, bf16[4,8,32,256]{3,2,1,0:T(8,128)(2,1)S(1)}, u32[]{:S(2)}, u32[]{:S(2)}) collective-permute-start(bf16[4,8,32,256]{3,2,1,0:T(8,128)(2,1)S(1)} %collective-permute-done.3.refs_6_), channel_id=1, source_target_pairs={{4,8},{8,4},{5,9},{9,5},{6,10},{10,6},{7,11},{11,7},{20,24},{24,20... | collective-permute-start | bytes 1572872 | tf_op jit(solution)/shard_map/ppermute | solution.py:291
  14.9 10.1 %collective-permute-start.5 = (bf16[4,2,32,256]{3,2,1,0:T(8,128)(2,1)S(1)}, bf16[4,2,32,256]{3,2,1,0:T(8,128)(2,1)S(1)}, u32[]{:S(2)}, u32[]{:S(2)}) collective-permute-start(bf16[4,2,32,256]{3,2,1,0:T(8,128)(2,1)S(1)} %get-tuple-element.36), channel_id=1, source_target_pairs={{0,1},{1,0},{2,3},{3,2},{4,5},{5,4},{6,7},{7,6},{8,9},{9,8},{10,11... | collective-permute-start | bytes 393224 | tf_op jit(solution)/shard_map/ppermute | solution.py:301
  16.1 8.9 %collective-permute-start.6 = (bf16[4,2,32,256]{3,2,1,0:T(8,128)(2,1)S(1)}, bf16[4,2,32,256]{3,2,1,0:T(8,128)(2,1)S(1)}, u32[]{:S(2)}, u32[]{:S(2)}) collective-permute-start(bf16[4,2,32,256]{3,2,1,0:T(8,128)(2,1)S(1)} %get-tuple-element.35), channel_id=1, source_target_pairs={{0,2},{1,3},{2,0},{3,1},{4,6},{5,7},{6,4},{7,5},{8,10},{9,11},{10,... | collective-permute-start | bytes 393224 | tf_op jit(solution)/shard_map/ppermute | solution.py:301
  17.3 7.7 %collective-permute-start.7 = (bf16[4,2,32,256]{3,2,1,0:T(8,128)(2,1)S(1)}, bf16[4,2,32,256]{3,2,1,0:T(8,128)(2,1)S(1)}, u32[]{:S(2)}, u32[]{:S(2)}) collective-permute-start(bf16[4,2,32,256]{3,2,1,0:T(8,128)(2,1)S(1)} %get-tuple-element.34), channel_id=1, source_target_pairs={{0,3},{1,2},{2,1},{3,0},{4,7},{5,6},{6,5},{7,4},{8,11},{9,10},{10,... | collective-permute-start | bytes 393224 | tf_op jit(solution)/shard_map/ppermute | solution.py:301
  17.8 20.7 %collective-permute-start.8 = (bf16[4,8,32,256]{3,2,1,0:T(8,128)(2,1)S(1)}, bf16[4,8,32,256]{3,2,1,0:T(8,128)(2,1)S(1)}, u32[]{:S(2)}, u32[]{:S(2)}) collective-permute-start(bf16[4,8,32,256]{3,2,1,0:T(8,128)(2,1)S(1)} %collective-permute-done.4.refs_7_), channel_id=1, source_target_pairs={{4,0},{8,12},{5,1},{9,13},{6,2},{10,14},{7,3},{11,15},{20,16},{24,... | collective-permute-start | bytes 1572872 | tf_op jit(solution)/shard_map/ppermute | solution.py:291
  28.3 21.0 %collective-permute-start.13 = (bf16[2,8,32,256]{3,2,1,0:T(8,128)(2,1)S(1)}, bf16[2,8,32,256]{3,2,1,0:T(8,128)(2,1)S(1)}, u32[]{:S(2)}, u32[]{:S(2)}) collective-permute-start(bf16[2,8,32,256]{3,2,1,0:T(8,128)(2,1)S(1)} %get-tuple-element.22), channel_id=1, source_target_pairs={{4,0},{8,12},{5,1},{9,13},{6,2},{10,14},{7,3},{11,15},{20,16},{24,... | collective-permute-start | bytes 786440 | tf_op jit(solution)/shard_map/ppermute | solution.py:291
  38.6 10.8 %collective-permute-start.9 = (bf16[4,2,32,256]{3,2,1,0:T(8,128)(2,1)S(1)}, bf16[4,2,32,256]{3,2,1,0:T(8,128)(2,1)S(1)}, u32[]{:S(2)}, u32[]{:S(2)}) collective-permute-start(bf16[4,2,32,256]{3,2,1,0:T(8,128)(2,1)S(1)} %get-tuple-element.32), channel_id=1, source_target_pairs={{0,1},{1,0},{2,3},{3,2},{4,5},{5,4},{6,7},{7,6},{8,9},{9,8},{10,11... | collective-permute-start | bytes 393224 | tf_op jit(solution)/shard_map/ppermute | solution.py:301
  39.4 10.0 %collective-permute-start.10 = (bf16[4,2,32,256]{3,2,1,0:T(8,128)(2,1)S(1)}, bf16[4,2,32,256]{3,2,1,0:T(8,128)(2,1)S(1)}, u32[]{:S(2)}, u32[]{:S(2)}) collective-permute-start(bf16[4,2,32,256]{3,2,1,0:T(8,128)(2,1)S(1)} %get-tuple-element.31), channel_id=1, source_target_pairs={{0,2},{1,3},{2,0},{3,1},{4,6},{5,7},{6,4},{7,5},{8,10},{9,11},{10,... | collective-permute-start | bytes 393224 | tf_op jit(solution)/shard_map/ppermute | solution.py:301
  40.6 8.7 %collective-permute-start.11 = (bf16[4,2,32,256]{3,2,1,0:T(8,128)(2,1)S(1)}, bf16[4,2,32,256]{3,2,1,0:T(8,128)(2,1)S(1)}, u32[]{:S(2)}, u32[]{:S(2)}) collective-permute-start(bf16[4,2,32,256]{3,2,1,0:T(8,128)(2,1)S(1)} %get-tuple-element.30), channel_id=1, source_target_pairs={{0,3},{1,2},{2,1},{3,0},{4,7},{5,6},{6,5},{7,4},{8,11},{9,10},{10,... | collective-permute-start | bytes 393224 | tf_op jit(solution)/shard_map/ppermute | solution.py:301
  41.1 13.8 %collective-permute-start.14 = (bf16[2,8,32,256]{3,2,1,0:T(8,128)(2,1)S(1)}, bf16[2,8,32,256]{3,2,1,0:T(8,128)(2,1)S(1)}, u32[]{:S(2)}, u32[]{:S(2)}) collective-permute-start(bf16[2,8,32,256]{3,2,1,0:T(8,128)(2,1)S(1)} %get-tuple-element.26), channel_id=1, source_target_pairs={{4,0},{8,12},{5,1},{9,13},{6,2},{10,14},{7,3},{11,15},{20,16},{24,... | collective-permute-start | bytes 786440 | tf_op jit(solution)/shard_map/ppermute | solution.py:291
  49.4 5.6 %collective-permute-start.15 = (bf16[2,2,32,256]{3,2,1,0:T(8,128)(2,1)S(1)}, bf16[2,2,32,256]{3,2,1,0:T(8,128)(2,1)S(1)}, u32[]{:S(2)}, u32[]{:S(2)}) collective-permute-start(bf16[2,2,32,256]{3,2,1,0:T(8,128)(2,1)S(1)} %get-tuple-element.48), channel_id=1, source_target_pairs={{0,1},{1,0},{2,3},{3,2},{4,5},{5,4},{6,7},{7,6},{8,9},{9,8},{10,11... | collective-permute-start | bytes 196616 | tf_op jit(solution)/shard_map/ppermute | solution.py:301
  50.4 4.6 %collective-permute-start.16 = (bf16[2,2,32,256]{3,2,1,0:T(8,128)(2,1)S(1)}, bf16[2,2,32,256]{3,2,1,0:T(8,128)(2,1)S(1)}, u32[]{:S(2)}, u32[]{:S(2)}) collective-permute-start(bf16[2,2,32,256]{3,2,1,0:T(8,128)(2,1)S(1)} %get-tuple-element.47), channel_id=1, source_target_pairs={{0,2},{1,3},{2,0},{3,1},{4,6},{5,7},{6,4},{7,5},{8,10},{9,11},{10,... | collective-permute-start | bytes 196616 | tf_op jit(solution)/shard_map/ppermute | solution.py:301
  51.6 4.0 %collective-permute-start.17 = (bf16[2,2,32,256]{3,2,1,0:T(8,128)(2,1)S(1)}, bf16[2,2,32,256]{3,2,1,0:T(8,128)(2,1)S(1)}, u32[]{:S(2)}, u32[]{:S(2)}) collective-permute-start(bf16[2,2,32,256]{3,2,1,0:T(8,128)(2,1)S(1)} %get-tuple-element.46), channel_id=1, source_target_pairs={{0,3},{1,2},{2,1},{3,0},{4,7},{5,6},{6,5},{7,4},{8,11},{9,10},{10,... | collective-permute-start | bytes 196616 | tf_op jit(solution)/shard_map/ppermute | solution.py:301
  55.7 8.4 %collective-permute-start.18 = (bf16[2,2,32,256]{3,2,1,0:T(8,128)(2,1)S(1)}, bf16[2,2,32,256]{3,2,1,0:T(8,128)(2,1)S(1)}, u32[]{:S(2)}, u32[]{:S(2)}) collective-permute-start(bf16[2,2,32,256]{3,2,1,0:T(8,128)(2,1)S(1)} %get-tuple-element.44), channel_id=1, source_target_pairs={{0,1},{1,0},{2,3},{3,2},{4,5},{5,4},{6,7},{7,6},{8,9},{9,8},{10,11... | collective-permute-start | bytes 196616 | tf_op jit(solution)/shard_map/ppermute | solution.py:301
  56.1 8.0 %collective-permute-start.19 = (bf16[2,2,32,256]{3,2,1,0:T(8,128)(2,1)S(1)}, bf16[2,2,32,256]{3,2,1,0:T(8,128)(2,1)S(1)}, u32[]{:S(2)}, u32[]{:S(2)}) collective-permute-start(bf16[2,2,32,256]{3,2,1,0:T(8,128)(2,1)S(1)} %get-tuple-element.43), channel_id=1, source_target_pairs={{0,2},{1,3},{2,0},{3,1},{4,6},{5,7},{6,4},{7,5},{8,10},{9,11},{10,... | collective-permute-start | bytes 196616 | tf_op jit(solution)/shard_map/ppermute | solution.py:301
  57.1 6.9 %collective-permute-start.20 = (bf16[2,2,32,256]{3,2,1,0:T(8,128)(2,1)S(1)}, bf16[2,2,32,256]{3,2,1,0:T(8,128)(2,1)S(1)}, u32[]{:S(2)}, u32[]{:S(2)}) collective-permute-start(bf16[2,2,32,256]{3,2,1,0:T(8,128)(2,1)S(1)} %get-tuple-element.42), channel_id=1, source_target_pairs={{0,3},{1,2},{2,1},{3,0},{4,7},{5,6},{6,5},{7,4},{8,11},{9,10},{10,... | collective-permute-start | bytes 196616 | tf_op jit(solution)/shard_map/ppermute | solution.py:301
  57.9 6.2 %copy-start = (bf16[4,8,32,256]{3,2,1,0:T(8,128)(2,1)S(1)}, bf16[4,8,32,256]{3,2,1,0:T(8,128)(2,1)}, u32[]{:S(2)}) copy-start(bf16[4,8,32,256]{3,2,1,0:T(8,128)(2,1)} %refs_3_.1) | copy-start | bytes 1572868

commit v9 on v4

v9 whole, which is shorter than its diff:
```python
import functools
import math

import jax
import jax.numpy as jnp
from jax import lax
from jax.experimental import pallas as pl
from jax.experimental.pallas import tpu as pltpu
from jax.sharding import PartitionSpec as P

HEADS = 64
KVH = 8
LOG2E = 1.4426950408889634
STEP = 8
VMEM_BYTES = 24 << 20


class Part:
    def __init__(self, ref, start):
        self.ref, self.start = ref, start

    def __getitem__(self, at):
        return self.ref[self.start + at]


def attend_kernel(
    numbers_ref, q_ref, *refs, hops, parts,
    inst_size, tp_size, kv_local, per_head, head_dim, span_len, slot_count, longest, prompt_count,
):
    hop_refs = refs[:len(hops)]
    part_refs = refs[len(hops):len(hops) + len(parts)]
    (out_ref, cache_ref, place_ref, kv_ref, s_ref, p_ref, acc_ref, max_ref, zero_ref,
     part_sems, page_sems) = refs[len(hops) + len(parts):]
    step = pl.program_id(0)
    span_total = slot_count * inst_size
    spans_ref = Part(numbers_ref, 0)
    tail_ref = Part(numbers_ref, prompt_count)
    owner_ref = Part(numbers_ref, 2 * prompt_count)
    plan_ref = Part(numbers_ref, 3 * prompt_count)
    place_at_ref = Part(numbers_ref, 3 * prompt_count + span_total)
    inst = place_at_ref[0]
    tp = place_at_ref[1]
    slice_len = span_len // tp_size
    scale = LOG2E / math.sqrt(head_dim)

    def part_copies(act):
        for n, (pieces, j) in enumerate(parts):
            at = pl.ds(pl.multiple_of((tp ^ j) * slice_len, slice_len), slice_len)
            begin = 0
            for m, (hop, first_slot, size) in enumerate(pieces):
                slots = pl.ds(place_at_ref[2 + hop] * slot_count + first_slot, size)
                act(pltpu.make_async_copy(
                    part_refs[n].at[begin:begin + size], kv_ref.at[slots, :, at],
                    part_sems.at[n, m],
                ))
                begin += size

    def cache_copies(act):
        first = jnp.int32(0)
        count = jnp.int32(0)
        start = jnp.int32(0)
        for p in range(prompt_count):
            hit = owner_ref[p] == inst
            first = jnp.where(hit, start, first)
            count = jnp.where(hit, spans_ref[p], count)
            start = start + spans_ref[p]

        def row(r, unused):
            page = place_ref[jnp.minimum(first + r, span_total - 1)]
            for n, (hop, first_slot, size) in enumerate(hops):
                source = place_at_ref[2 + hop]
                slot = page - source * slot_count - first_slot
                here = (source >= 0) & (slot >= 0) & (slot < size)

                @pl.when((r < count) & here)
                def _():
                    act(pltpu.make_async_copy(
                        hop_refs[n].at[slot], cache_ref.at[r], page_sems.at[r]
                    ))

            @pl.when(r >= count)
            def _():
                act(pltpu.make_async_copy(zero_ref, cache_ref.at[r], page_sems.at[r]))

            return unused

        lax.fori_loop(0, longest, row, 0)

    @pl.when(step == 0)
    def _():
        part_copies(lambda copy: copy.start())

        def put(g, unused):
            place_ref[plan_ref[g]] = g
            return unused

        lax.fori_loop(0, span_total, put, 0)
        zero_ref[...] = jnp.zeros_like(zero_ref)
        cache_copies(lambda copy: copy.start())
        part_copies(lambda copy: copy.wait())

    own = inst * slot_count + step
    span = plan_ref[own]
    first = jnp.int32(0)
    end = jnp.int32(0)
    length = jnp.int32(0)
    for p in range(prompt_count):
        start = end
        end = end + spans_ref[p]
        inside = (span >= start) & (span < end)
        first = jnp.where(inside, start, first)
        length = jnp.where(inside, (spans_ref[p] - 1) * span_len + tail_ref[p], length)
    count = span - first
    live_rows = length - count * span_len
    ones = jnp.ones((span_len, head_dim), jnp.bfloat16)
    row_ids = lax.broadcasted_iota(jnp.int32, (span_len, span_len), 0)
    col_ids = lax.broadcasted_iota(jnp.int32, (span_len, span_len), 1)
    causal = row_ids >= col_ids
    live = lax.broadcasted_iota(jnp.int32, (span_len, head_dim), 0) < live_rows
    one_step = longest <= STEP

    def lanes_of(head):
        return pl.ds(pl.multiple_of(head * head_dim, head_dim), head_dim)

    def rows_of(h):
        return slice(h * span_len, (h + 1) * span_len)

    def put_out(head, total):
        out_ref[0, :, lanes_of(head)] = jnp.where(
            live, total[:, :head_dim] / total[:, head_dim:], 0.0
        ).astype(jnp.bfloat16)

    def attend(pages, begin):
        wide = len(pages) * span_len

        def kv_head(g, unused):
            keys = jnp.concatenate([kv_ref[page, g, :, :head_dim] for page in pages], axis=0)
            q = jnp.concatenate(
                [q_ref[0, :, lanes_of(g * per_head + h)] for h in range(per_head)], axis=0
            )
            s_ref[:, :wide] = lax.dot_general(
                q, keys, (((1,), (1,)), ((), ())), preferred_element_type=jnp.float32
            )
            rescales = []
            for h in range(per_head):
                head = g * per_head + h
                s = s_ref[rows_of(h), :wide] * scale
                if begin:
                    own_part = jnp.where(causal, s[:, wide - span_len:], -1e30)
                    if len(pages) > 1:
                        s = jnp.concatenate([s[:, :wide - span_len], own_part], axis=1)
                    else:
                        s = own_part
                top = jnp.max(s, axis=1, keepdims=True)
                if begin:
                    top = jnp.broadcast_to(top, (span_len, head_dim))
                else:
                    old = max_ref[head]
                    top = jnp.maximum(old, top)
                    rescales.append(jnp.exp2(old - top))
                if not one_step:
                    max_ref[head] = top
                p_ref[rows_of(h), :wide] = jnp.exp2(
                    s - jnp.concatenate([top] * len(pages), axis=1)
                ).astype(jnp.bfloat16)
            values = jnp.concatenate(
                [
                    jnp.concatenate([kv_ref[page, g, :, head_dim:], ones], axis=1)
                    for page in pages
                ],
                axis=0,
            )
            mixed = jnp.dot(p_ref[:, :wide], values, preferred_element_type=jnp.float32)
            for h in range(per_head):
                head = g * per_head + h
                new = mixed[rows_of(h)]
                if one_step:
                    put_out(head, new)
                elif begin:
                    acc_ref[head] = new
                else:
                    acc_ref[head] = new + acc_ref[head] * jnp.concatenate(
                        [rescales[h]] * 2, axis=1
                    )
            return unused

        lax.fori_loop(0, kv_local, kv_head, 0)

    over = lax.rem(count, STEP)
    for n in range(STEP):
        @pl.when(over == n)
        def _():
            attend([place_ref[first + m] for m in range(n)] + [own], True)

    if not one_step:
        def block(j, unused):
            at = first + over + STEP * j
            attend([place_ref[at + n] for n in range(STEP)], False)
            return unused

        lax.fori_loop(0, count // STEP, block, 0)
        for head in range(kv_local * per_head):
            put_out(head, acc_ref[head])

    @pl.when(step == slot_count - 1)
    def _():
        cache_copies(lambda copy: copy.wait())


def after(values, earlier):
    return lax.optimization_barrier((list(values), list(earlier)))[0]


def move_pages(kv_new, kv_local):
    inst_size = lax.axis_size("inst")
    tp_size = lax.axis_size("tp")
    inst = lax.axis_index("inst")
    tp = lax.axis_index("tp")
    slot_count, kv_heads = kv_new.shape[:2]
    sources = [list(range(inst_size))]
    hops = [((0, 0, slot_count), kv_new)]
    parts = []

    def along(x, pairs):
        return lax.ppermute(x, "inst", pairs)

    def exchange(hop, x):
        found = []
        for j in range(tp_size):
            head = ((tp ^ j) * kv_heads) // tp_size
            sent = lax.dynamic_slice_in_dim(x, head, kv_local, 1)
            if j:
                sent = lax.ppermute(sent, "tp", [(t, t ^ j) for t in range(tp_size)])
            found.append((([(hop, 0, slot_count)], j), sent))
        parts.extend(found)
        return [x for _, x in found]

    if inst_size != 4:
        exchange(0, kv_new)
        for s in range(1, inst_size):
            sources.append([(i - s) % inst_size for i in range(inst_size)])
            pairs = [(i, (i + s) % inst_size) for i in range(inst_size)]
            hops.append(((s, 0, slot_count), along(kv_new, pairs)))
            exchange(s, hops[-1][1])
        return hops, parts, sources

    sources += [[2, 3, 0, 1], [1, 0, 3, 2], [3, -1, -1, 0], [-1, 2, 1, -1], [3, 2, 1, 0]]
    middle = (inst == 1) | (inst == 2)
    shifted = along(kv_new, [(0, 2), (1, 3), (2, 0), (3, 1)])
    outer = along(kv_new, [(0, 1), (1, 0), (2, 3), (3, 2)])
    waiting = exchange(0, kv_new)
    handed = along(after([shifted], waiting)[0], [(1, 0), (2, 3)])
    inner = along(jnp.where(middle, kv_new, shifted), [(1, 2), (2, 1)])
    waiting = exchange(2, outer)
    waiting = exchange(1, after([shifted], waiting)[0])
    exchange(5, after([jnp.where(middle, inner, handed)], waiting)[0])
    for hop, x in enumerate((shifted, outer, handed, inner), 1):
        hops.append(((hop, 0, slot_count), x))
    return hops, parts, sources


def body(queries, kv_new, prompt_spans, prompt_tail, span_plan, decode_owner):
    tp_size = lax.axis_size("tp")
    inst_size = lax.axis_size("inst")
    tp_index = lax.axis_index("tp")
    inst_index = lax.axis_index("inst")
    slot_count, span_len, row_width = queries.shape
    kv_heads, slice_len, width = kv_new.shape[1:]
    head_dim = width // 2
    local_heads = row_width // head_dim
    kv_local = max(1, kv_heads // tp_size)
    per_head = local_heads // kv_local
    rows = per_head * span_len
    span_total = slot_count * inst_size
    longest = span_total // 2
    hops, parts, sources = move_pages(kv_new, kv_local)
    own_sources = lax.dynamic_index_in_dim(jnp.asarray(sources, jnp.int32), inst_index, 1, False)
    numbers = jnp.concatenate([
        prompt_spans, prompt_tail, decode_owner, span_plan,
        jnp.stack([inst_index, tp_index]).astype(jnp.int32), own_sources,
    ])
    kernel = functools.partial(
        attend_kernel,
        hops=[name for name, _ in hops],
        parts=[name for name, _ in parts],
        inst_size=inst_size,
        tp_size=tp_size,
        kv_local=kv_local,
        per_head=per_head,
        head_dim=head_dim,
        span_len=span_len,
        slot_count=slot_count,
        longest=longest,
        prompt_count=prompt_spans.shape[0],
    )
    work = slot_count * span_total // 4 * local_heads * span_len * span_len
    anywhere = pl.BlockSpec(memory_space=pl.ANY)
    by_slot = pl.BlockSpec((1, span_len, row_width), lambda i, *_: (i, 0, 0))
    kept = (local_heads, span_len) if longest > STEP else (1, 8)
    return pl.pallas_call(
        kernel,
        grid_spec=pltpu.PrefetchScalarGridSpec(
            num_scalar_prefetch=1,
            grid=(slot_count,),
            in_specs=[by_slot] + [anywhere] * (len(hops) + len(parts)),
            out_specs=[by_slot, anywhere],
            scratch_shapes=[
                pltpu.SMEM((span_total,), jnp.int32),
                pltpu.VMEM((span_total, kv_local, span_len, width), jnp.bfloat16),
                pltpu.VMEM((rows, STEP * span_len), jnp.float32),
                pltpu.VMEM((rows, STEP * span_len), jnp.bfloat16),
                pltpu.VMEM(kept + (2 * head_dim,), jnp.float32),
                pltpu.VMEM(kept + (head_dim,), jnp.float32),
                pltpu.VMEM((kv_heads, slice_len, width), jnp.bfloat16),
                pltpu.SemaphoreType.DMA((len(parts), max(len(x[0][0]) for x in parts))),
                pltpu.SemaphoreType.DMA((longest,)),
            ],
        ),
        out_shape=[
            jax.ShapeDtypeStruct(queries.shape, jnp.bfloat16),
            jax.ShapeDtypeStruct((longest, kv_heads, slice_len, width), jnp.bfloat16),
        ],
        cost_estimate=pl.CostEstimate(
            flops=4 * work * head_dim, bytes_accessed=8 << 20, transcendentals=work
        ),
        compiler_params=pltpu.CompilerParams(vmem_limit_bytes=VMEM_BYTES),
    )(numbers, queries, *[x for _, x in hops], *[x for _, x in parts])


def solution(mesh):
    placed = (
        P(("groups", "inst"), None, "tp"),
        P(("groups", "inst"), None, "tp", None),
        P("groups"),
        P("groups"),
        P("groups"),
        P("groups"),
    )
    return jax.shard_map(
        body,
        mesh=mesh,
        in_specs=placed,
        out_specs=(P(("groups", "inst"), None, "tp"), P(("groups", "inst"), None, "tp", None)),
        check_vma=False,
    )
```

time: 66.3 us -> 84.4 us (1.27)
  the two profiles are of different devices: /device:TPU:5 before, /device:TPU:21 now
where the time goes in v9:
time: 84.4 us; the launch traced here: 84.9 us
  waiting for transfers between devices  33.6 us (40%)
  starting transfers between devices  17.5 us (21%)
  Pallas kernels  17.5 us (21%)
  local copies, waits for them, and re-layouts  14.4 us (17%)
  other arithmetic  1.15 us (1%)
    ppermute x12, waiting for transfers between devices, exchange(): sent = lax.ppermute(sent, 'tp', [(t, t ^ j) for t in range(tp_size)])  21.7 us
    pallas_call x1, Pallas kernels, body(): pl.pallas_call(kernel, grid_spec=pltpu.PrefetchScalarGridSpec(num_scalar_...  17.5 us
    ppermute x4, waiting for transfers between devices, along(): return lax.ppermute(x, 'inst', pairs)  11.9 us
    unnamed x34, local copies, waits for them, and re-layouts  10.3 us
    ppermute x12, starting transfers between devices, exchange(): sent = lax.ppermute(sent, 'tp', [(t, t ^ j) for t in range(tp_size)])  9.33 us
    ppermute x4, starting transfers between devices, along(): return lax.ppermute(x, 'inst', pairs)  8.16 us
    dynamic_slice x4, local copies, waits for them, and re-layouts, exchange(): sent = lax.dynamic_slice_in_dim(x, head, kv_local, 1)  2.01 us
  transfers between devices with their start and end apart: 16, of which 9 were waited for; matrix products, arithmetic and copies ran while one was open for 5% of the time, Pallas kernels for 0%

profile of v9, /device:TPU:21, one launch (start us, length us, event | category | flops | bytes accessed | tf_op | source)
XLA Modules:
  0.0 84.9 jit_solution(13611251231634407838)
XLA Ops:
  0.8 1.1 %constant_dynamic-slice_fusion.12 = (bf16[4,2,32,256]{3,2,1,0:T(8,128)(2,1)S(1)}, bf16[4,2,32,256]{3,2,1,0:T(8,128)(2,1)S(1)}, bf16[4,2,32,256]{3,2,1,0:T(8,128)(2,1)S(1)}, bf16[4,2,32,256]{3,2,1,0:T(8,128)(2,1)S(1)}) fusion(bf16[4,8,32,256]{3,2,1,0:T(8,128)(2,1)} %refs_0_.1, s32[]{:T(128)S(6)} %select_n.74, s32[]{:T(128)S(6)} %select_n.72, ...), kind=kLoop, calls=%fused_computation.14 | loop fusion | bytes 1048592 | tf_op jit(solution)/shard_map/dynamic_slice | solution.py:231
  2.0 2.0 %collective-permute-start.4 = (bf16[4,2,32,256]{3,2,1,0:T(8,128)(2,1)S(1)}, bf16[4,2,32,256]{3,2,1,0:T(8,128)(2,1)S(1)}, u32[]{:S(2)}, u32[]{:S(2)}) collective-permute-start(bf16[4,2,32,256]{3,2,1,0:T(8,128)(2,1)S(1)} %get-tuple-element.20), channel_id=1, source_target_pairs={{0,3},{1,2},{2,1},{3,0},{4,7},{5,6},{6,5},{7,4},{8,11},{9,10},{10,... | collective-permute-start | bytes 393224 | tf_op jit(solution)/shard_map/ppermute | solution.py:233
  4.5 1.3 %collective-permute-start.1 = (bf16[4,8,32,256]{3,2,1,0:T(8,128)(2,1)}, bf16[4,8,32,256]{3,2,1,0:T(8,128)(2,1)S(1)}, u32[]{:S(2)}, u32[]{:S(2)}) collective-permute-start(bf16[4,8,32,256]{3,2,1,0:T(8,128)(2,1)} %refs_0_.1), channel_id=1, source_target_pairs={{0,4},{4,0},{8,12},{12,8},{1,5},{5,1},{9,13},{13,9},{2,6},{6,2},{1... | collective-permute-start | bytes 1572872 | tf_op jit(solution)/shard_map/ppermute | solution.py:225
  5.8 2.6 %collective-permute-done.4.refs_8_ = bf16[4,2,32,256]{3,2,1,0:T(8,128)(2,1)S(1)} collective-permute-done((bf16[4,2,32,256]{3,2,1,0:T(8,128)(2,1)S(1)}, bf16[4,2,32,256]{3,2,1,0:T(8,128)(2,1)S(1)}, u32[]{:S(2)}, u32[]{:S(2)}) %collective-permute-start.4) | collective-permute-done | bytes 131104 | tf_op jit(solution)/shard_map/ppermute | solution.py:233
  8.4 2.7 %collective-permute-done.3.refs_7_ = bf16[4,2,32,256]{3,2,1,0:T(8,128)(2,1)S(1)} collective-permute-done((bf16[4,2,32,256]{3,2,1,0:T(8,128)(2,1)S(1)}, bf16[4,2,32,256]{3,2,1,0:T(8,128)(2,1)S(1)}, u32[]{:S(2)}, u32[]{:S(2)}) %collective-permute-start.3) | collective-permute-done | bytes 131104 | tf_op jit(solution)/shard_map/ppermute | solution.py:233
  11.1 11.9 %collective-permute-done.refs_1_ = bf16[4,8,32,256]{3,2,1,0:T(8,128)(2,1)S(1)} collective-permute-done((bf16[4,8,32,256]{3,2,1,0:T(8,128)(2,1)}, bf16[4,8,32,256]{3,2,1,0:T(8,128)(2,1)S(1)}, u32[]{:S(2)}, u32[]{:S(2)}) %collective-permute-start) | collective-permute-done | bytes 524320 | tf_op jit(solution)/shard_map/ppermute | solution.py:225
  23.0 1.1 %broadcast_select_fusion.1 = bf16[4,8,32,256]{3,2,1,0:T(8,128)(2,1)S(1)} fusion(bf16[4,8,32,256]{3,2,1,0:T(8,128)(2,1)} %refs_0_.1, bf16[4,8,32,256]{3,2,1,0:T(8,128)(2,1)S(1)} %collective-permute-done.refs_1_, pred[]{:T(512)S(6)} %or.3), kind=kLoop, calls=%fused_computation.1 | loop fusion | flops 262144 | bytes 1572865 | tf_op jit(solution)/shard_map/jit(_where)/select_n | solution.py:253
  24.1 5.2 %collective-permute-start.6 = (bf16[4,8,32,256]{3,2,1,0:T(8,128)(2,1)S(1)}, bf16[4,8,32,256]{3,2,1,0:T(8,128)(2,1)S(1)}, u32[]{:S(2)}, u32[]{:S(2)}) collective-permute-start(bf16[4,8,32,256]{3,2,1,0:T(8,128)(2,1)S(1)} %broadcast_select_fusion.1), channel_id=1, source_target_pairs={{4,8},{8,4},{5,9},{9,5},{6,10},{10,6},{7,11},{11,7},{20,24},{24,20... | collective-permute-start | bytes 1572872 | tf_op jit(solution)/shard_map/ppermute | solution.py:225
  29.3 1.5 %collective-permute-start.5 = (bf16[4,8,32,256]{3,2,1,0:T(8,128)(2,1)S(1)}, bf16[4,8,32,256]{3,2,1,0:T(8,128)(2,1)S(1)}, u32[]{:S(2)}, u32[]{:S(2)}) collective-permute-start(bf16[4,8,32,256]{3,2,1,0:T(8,128)(2,1)S(1)} %collective-permute-done.refs_1_), channel_id=1, source_target_pairs={{4,0},{8,12},{5,1},{9,13},{6,2},{10,14},{7,3},{11,15},{20,16},{24,... | collective-permute-start | bytes 1572872 | tf_op jit(solution)/shard_map/ppermute | solution.py:225
  30.9 2.0 %collective-permute-start.9 = (bf16[4,2,32,256]{3,2,1,0:T(8,128)(2,1)S(1)}, bf16[4,2,32,256]{3,2,1,0:T(8,128)(2,1)S(1)}, u32[]{:S(2)}, u32[]{:S(2)}) collective-permute-start(bf16[4,2,32,256]{3,2,1,0:T(8,128)(2,1)S(1)} %get-tuple-element.16), channel_id=1, source_target_pairs={{0,3},{1,2},{2,1},{3,0},{4,7},{5,6},{6,5},{7,4},{8,11},{9,10},{10,... | collective-permute-start | bytes 393224 | tf_op jit(solution)/shard_map/ppermute | solution.py:233
  33.4 3.9 %collective-permute-done.9.refs_12_ = bf16[4,2,32,256]{3,2,1,0:T(8,128)(2,1)S(1)} collective-permute-done((bf16[4,2,32,256]{3,2,1,0:T(8,128)(2,1)S(1)}, bf16[4,2,32,256]{3,2,1,0:T(8,128)(2,1)S(1)}, u32[]{:S(2)}, u32[]{:S(2)}) %collective-permute-start.9) | collective-permute-done | bytes 131104 | tf_op jit(solution)/shard_map/ppermute | solution.py:233
  37.9 2.1 %collective-permute-done.8.refs_11_ = bf16[4,2,32,256]{3,2,1,0:T(8,128)(2,1)S(1)} collective-permute-done((bf16[4,2,32,256]{3,2,1,0:T(8,128)(2,1)S(1)}, bf16[4,2,32,256]{3,2,1,0:T(8,128)(2,1)S(1)}, u32[]{:S(2)}, u32[]{:S(2)}) %collective-permute-start.8) | collective-permute-done | bytes 131104 | tf_op jit(solution)/shard_map/ppermute | solution.py:233
  40.8 1.3 %collective-permute-start.12 = (bf16[4,2,32,256]{3,2,1,0:T(8,128)(2,1)S(1)}, bf16[4,2,32,256]{3,2,1,0:T(8,128)(2,1)S(1)}, u32[]{:S(2)}, u32[]{:S(2)}) collective-permute-start(bf16[4,2,32,256]{3,2,1,0:T(8,128)(2,1)S(1)} %get-tuple-element.12), channel_id=1, source_target_pairs={{0,3},{1,2},{2,1},{3,0},{4,7},{5,6},{6,5},{7,4},{8,11},{9,10},{10,... | collective-permute-start | bytes 393224 | tf_op jit(solution)/shard_map/ppermute | solution.py:233
  43.0 3.6 %collective-permute-done.12.refs_16_ = bf16[4,2,32,256]{3,2,1,0:T(8,128)(2,1)S(1)} collective-permute-done((bf16[4,2,32,256]{3,2,1,0:T(8,128)(2,1)S(1)}, bf16[4,2,32,256]{3,2,1,0:T(8,128)(2,1)S(1)}, u32[]{:S(2)}, u32[]{:S(2)}) %collective-permute-start.12) | collective-permute-done | bytes 131104 | tf_op jit(solution)/shard_map/ppermute | solution.py:233
  47.3 1.9 %collective-permute-done.11.refs_15_ = bf16[4,2,32,256]{3,2,1,0:T(8,128)(2,1)S(1)} collective-permute-done((bf16[4,2,32,256]{3,2,1,0:T(8,128)(2,1)S(1)}, bf16[4,2,32,256]{3,2,1,0:T(8,128)(2,1)S(1)}, u32[]{:S(2)}, u32[]{:S(2)}) %collective-permute-start.11) | collective-permute-done | bytes 131104 | tf_op jit(solution)/shard_map/ppermute | solution.py:233
  51.3 1.4 %collective-permute-start.15 = (bf16[4,2,32,256]{3,2,1,0:T(8,128)(2,1)}, bf16[4,2,32,256]{3,2,1,0:T(8,128)(2,1)}, u32[]{:S(2)}, u32[]{:S(2)}) collective-permute-start(bf16[4,2,32,256]{3,2,1,0:T(8,128)(2,1)} %get-tuple-element.8), channel_id=1, source_target_pairs={{0,3},{1,2},{2,1},{3,0},{4,7},{5,6},{6,5},{7,4},{8,11},{9,10},{10,... | collective-permute-start | bytes 393224 | tf_op jit(solution)/shard_map/ppermute | solution.py:233
  53.4 1.3 %fusion = s32[6]{0:T(128)} fusion(s32[6,4]{0,1:T(4,128)} %constant.81.clone, s32[]{:T(128)S(6)} %select_n.66), kind=kLoop, calls=%fused_computation.19 | loop fusion | bytes 52 | tf_op jit(solution)/shard_map/jit(dynamic_index_in_dim)/squeeze | solution.py:277
  55.5 2.1 %collective-permute-done.15.refs_20_ = bf16[4,2,32,256]{3,2,1,0:T(8,128)(2,1)} collective-permute-done((bf16[4,2,32,256]{3,2,1,0:T(8,128)(2,1)}, bf16[4,2,32,256]{3,2,1,0:T(8,128)(2,1)}, u32[]{:S(2)}, u32[]{:S(2)}) %collective-permute-start.15) | collective-permute-done | bytes 131104 | tf_op jit(solution)/shard_map/ppermute | solution.py:233
  57.6 2.8 %collective-permute-done.14.refs_19_ = bf16[4,2,32,256]{3,2,1,0:T(8,128)(2,1)} collective-permute-done((bf16[4,2,32,256]{3,2,1,0:T(8,128)(2,1)}, bf16[4,2,32,256]{3,2,1,0:T(8,128)(2,1)}, u32[]{:S(2)}, u32[]{:S(2)}) %collective-permute-start.14) | collective-permute-done | bytes 131104 | tf_op jit(solution)/shard_map/ppermute | solution.py:233
  60.4 1.6 %copy-done.1 = bf16[4,128,2048]{2,1,0:T(8,128)(2,1)S(1)} copy-done((bf16[4,128,2048]{2,1,0:T(8,128)(2,1)S(1)}, bf16[4,128,2048]{2,1,0:T(8,128)(2,1)}, u32[]{:S(2)}) %copy-start.1) | copy-done | bytes 2097176
  62.0 0.9 %copy-done.3 = bf16[4,2,32,256]{3,2,1,0:T(8,128)(2,1)S(1)} copy-done((bf16[4,2,32,256]{3,2,1,0:T(8,128)(2,1)S(1)}, bf16[4,2,32,256]{3,2,1,0:T(8,128)(2,1)}, u32[]{:S(2)}) %copy-start.3) | copy-done | bytes 131096
  65.7 0.9 %copy-done.11 = bf16[4,2,32,256]{3,2,1,0:T(8,128)(2,1)S(1)} copy-done((bf16[4,2,32,256]{3,2,1,0:T(8,128)(2,1)S(1)}, bf16[4,2,32,256]{3,2,1,0:T(8,128)(2,1)}, u32[]{:S(2)}) %copy-start.11) | copy-done | bytes 131096
  66.6 0.9 %copy-done.13 = bf16[4,2,32,256]{3,2,1,0:T(8,128)(2,1)S(1)} copy-done((bf16[4,2,32,256]{3,2,1,0:T(8,128)(2,1)S(1)}, bf16[4,2,32,256]{3,2,1,0:T(8,128)(2,1)}, u32[]{:S(2)}) %copy-start.13) | copy-done | bytes 131096
  67.5 17.5 %shard_map.86 = (bf16[4,128,2048]{2,1,0:T(8,128)(2,1)}, bf16[8,8,32,256]{3,2,1,0:T(8,128)(2,1)}) custom-call(s32[36]{0:T(128)S(1)} %concatenate.3.numbers_ref, bf16[4,128,2048]{2,1,0:T(8,128)(2,1)S(1)} %copy-done.1, bf16[4,8,32,256]{3,2,1,0:T(8,128)(2,1)S(1)} %copy-done, bf16[4,8,32,256]{3,2,1,0:T(8,128)(2,1)S(1)} %collective-permute-done.refs_1_, ...), custom_call_target="tpu_custom_call" | custom-call | flops 2147483648 | bytes 8388608 | tf_op jit(solution)/shard_map/pallas_call | solution.py:300
  (51 shorter events, 10.4 us)
Async XLA Ops:
  0.6 22.3 %collective-permute-start = (bf16[4,8,32,256]{3,2,1,0:T(8,128)(2,1)}, bf16[4,8,32,256]{3,2,1,0:T(8,128)(2,1)S(1)}, u32[]{:S(2)}, u32[]{:S(2)}) collective-permute-start(bf16[4,8,32,256]{3,2,1,0:T(8,128)(2,1)} %refs_0_.1), channel_id=1, source_target_pairs={{0,8},{4,12},{8,0},{12,4},{1,9},{5,13},{9,1},{13,5},{2,10},{6,14},... | collective-permute-start | bytes 1572872 | tf_op jit(solution)/shard_map/ppermute | solution.py:225
  2.0 6.4 %collective-permute-start.4 = (bf16[4,2,32,256]{3,2,1,0:T(8,128)(2,1)S(1)}, bf16[4,2,32,256]{3,2,1,0:T(8,128)(2,1)S(1)}, u32[]{:S(2)}, u32[]{:S(2)}) collective-permute-start(bf16[4,2,32,256]{3,2,1,0:T(8,128)(2,1)S(1)} %get-tuple-element.20), channel_id=1, source_target_pairs={{0,3},{1,2},{2,1},{3,0},{4,7},{5,6},{6,5},{7,4},{8,11},{9,10},{10,... | collective-permute-start | bytes 393224 | tf_op jit(solution)/shard_map/ppermute | solution.py:233
  4.0 7.1 %collective-permute-start.3 = (bf16[4,2,32,256]{3,2,1,0:T(8,128)(2,1)S(1)}, bf16[4,2,32,256]{3,2,1,0:T(8,128)(2,1)S(1)}, u32[]{:S(2)}, u32[]{:S(2)}) collective-permute-start(bf16[4,2,32,256]{3,2,1,0:T(8,128)(2,1)S(1)} %get-tuple-element.21), channel_id=1, source_target_pairs={{0,2},{1,3},{2,0},{3,1},{4,6},{5,7},{6,4},{7,5},{8,10},{9,11},{10,... | collective-permute-start | bytes 393224 | tf_op jit(solution)/shard_map/ppermute | solution.py:233
  4.3 6.8 %collective-permute-start.2 = (bf16[4,2,32,256]{3,2,1,0:T(8,128)(2,1)S(1)}, bf16[4,2,32,256]{3,2,1,0:T(8,128)(2,1)S(1)}, u32[]{:S(2)}, u32[]{:S(2)}) collective-permute-start(bf16[4,2,32,256]{3,2,1,0:T(8,128)(2,1)S(1)} %get-tuple-element.22), channel_id=1, source_target_pairs={{0,1},{1,0},{2,3},{3,2},{4,5},{5,4},{6,7},{7,6},{8,9},{9,8},{10,11... | collective-permute-start | bytes 393224 | tf_op jit(solution)/shard_map/ppermute | solution.py:233
  4.5 26.3 %collective-permute-start.1 = (bf16[4,8,32,256]{3,2,1,0:T(8,128)(2,1)}, bf16[4,8,32,256]{3,2,1,0:T(8,128)(2,1)S(1)}, u32[]{:S(2)}, u32[]{:S(2)}) collective-permute-start(bf16[4,8,32,256]{3,2,1,0:T(8,128)(2,1)} %refs_0_.1), channel_id=1, source_target_pairs={{0,4},{4,0},{8,12},{12,8},{1,5},{5,1},{9,13},{13,9},{2,6},{6,2},{1... | collective-permute-start | bytes 1572872 | tf_op jit(solution)/shard_map/ppermute | solution.py:225
  24.1 18.9 %collective-permute-start.6 = (bf16[4,8,32,256]{3,2,1,0:T(8,128)(2,1)S(1)}, bf16[4,8,32,256]{3,2,1,0:T(8,128)(2,1)S(1)}, u32[]{:S(2)}, u32[]{:S(2)}) collective-permute-start(bf16[4,8,32,256]{3,2,1,0:T(8,128)(2,1)S(1)} %broadcast_select_fusion.1), channel_id=1, source_target_pairs={{4,8},{8,4},{5,9},{9,5},{6,10},{10,6},{7,11},{11,7},{20,24},{24,20... | collective-permute-start | bytes 1572872 | tf_op jit(solution)/shard_map/ppermute | solution.py:225
  29.3 13.7 %collective-permute-start.5 = (bf16[4,8,32,256]{3,2,1,0:T(8,128)(2,1)S(1)}, bf16[4,8,32,256]{3,2,1,0:T(8,128)(2,1)S(1)}, u32[]{:S(2)}, u32[]{:S(2)}) collective-permute-start(bf16[4,8,32,256]{3,2,1,0:T(8,128)(2,1)S(1)} %collective-permute-done.refs_1_), channel_id=1, source_target_pairs={{4,0},{8,12},{5,1},{9,13},{6,2},{10,14},{7,3},{11,15},{20,16},{24,... | collective-permute-start | bytes 1572872 | tf_op jit(solution)/shard_map/ppermute | solution.py:225
  30.9 23.8 %copy-start.14 = (s32[4]{0:T(128)S(1)}, s32[4]{0:T(128)}, u32[]{:S(2)}) copy-start(s32[4]{0:T(128)} %param.9) | copy-start | bytes 52
  30.9 23.8 %copy-start.15 = (s32[4]{0:T(128)S(1)}, s32[4]{0:T(128)}, u32[]{:S(2)}) copy-start(s32[4]{0:T(128)} %param.10) | copy-start | bytes 52
  30.9 23.8 %copy-start.16 = (s32[4]{0:T(128)S(1)}, s32[4]{0:T(128)}, u32[]{:S(2)}) copy-start(s32[4]{0:T(128)} %param.12) | copy-start | bytes 52
  30.9 29.5 %copy-start = (bf16[4,8,32,256]{3,2,1,0:T(8,128)(2,1)S(1)}, bf16[4,8,32,256]{3,2,1,0:T(8,128)(2,1)}, u32[]{:S(2)}) copy-start(bf16[4,8,32,256]{3,2,1,0:T(8,128)(2,1)} %refs_0_.1) | copy-start | bytes 1572868
  30.9 6.3 %collective-permute-start.9 = (bf16[4,2,32,256]{3,2,1,0:T(8,128)(2,1)S(1)}, bf16[4,2,32,256]{3,2,1,0:T(8,128)(2,1)S(1)}, u32[]{:S(2)}, u32[]{:S(2)}) collective-permute-start(bf16[4,2,32,256]{3,2,1,0:T(8,128)(2,1)S(1)} %get-tuple-element.16), channel_id=1, source_target_pairs={{0,3},{1,2},{2,1},{3,0},{4,7},{5,6},{6,5},{7,4},{8,11},{9,10},{10,... | collective-permute-start | bytes 393224 | tf_op jit(solution)/shard_map/ppermute | solution.py:233
  32.9 7.1 %collective-permute-start.8 = (bf16[4,2,32,256]{3,2,1,0:T(8,128)(2,1)S(1)}, bf16[4,2,32,256]{3,2,1,0:T(8,128)(2,1)S(1)}, u32[]{:S(2)}, u32[]{:S(2)}) collective-permute-start(bf16[4,2,32,256]{3,2,1,0:T(8,128)(2,1)S(1)} %get-tuple-element.17), channel_id=1, source_target_pairs={{0,2},{1,3},{2,0},{3,1},{4,6},{5,7},{6,4},{7,5},{8,10},{9,11},{10,... | collective-permute-start | bytes 393224 | tf_op jit(solution)/shard_map/ppermute | solution.py:233
  33.2 6.8 %collective-permute-start.7 = (bf16[4,2,32,256]{3,2,1,0:T(8,128)(2,1)S(1)}, bf16[4,2,32,256]{3,2,1,0:T(8,128)(2,1)S(1)}, u32[]{:S(2)}, u32[]{:S(2)}) collective-permute-start(bf16[4,2,32,256]{3,2,1,0:T(8,128)(2,1)S(1)} %get-tuple-element.18), channel_id=1, source_target_pairs={{0,1},{1,0},{2,3},{3,2},{4,5},{5,4},{6,7},{7,6},{8,9},{9,8},{10,11... | collective-permute-start | bytes 393224 | tf_op jit(solution)/shard_map/ppermute | solution.py:233
  40.0 9.9 %copy-start.4 = (bf16[4,2,32,256]{3,2,1,0:T(8,128)(2,1)}, bf16[4,2,32,256]{3,2,1,0:T(8,128)(2,1)S(1)}, u32[]{:S(2)}) copy-start(bf16[4,2,32,256]{3,2,1,0:T(8,128)(2,1)S(1)} %collective-permute-done.8.refs_11_) | copy-start | bytes 393220
  40.8 5.9 %collective-permute-start.12 = (bf16[4,2,32,256]{3,2,1,0:T(8,128)(2,1)S(1)}, bf16[4,2,32,256]{3,2,1,0:T(8,128)(2,1)S(1)}, u32[]{:S(2)}, u32[]{:S(2)}) collective-permute-start(bf16[4,2,32,256]{3,2,1,0:T(8,128)(2,1)S(1)} %get-tuple-element.12), channel_id=1, source_target_pairs={{0,3},{1,2},{2,1},{3,0},{4,7},{5,6},{6,5},{7,4},{8,11},{9,10},{10,... | collective-permute-start | bytes 393224 | tf_op jit(solution)/shard_map/ppermute | solution.py:233
  42.1 7.2 %collective-permute-start.11 = (bf16[4,2,32,256]{3,2,1,0:T(8,128)(2,1)S(1)}, bf16[4,2,32,256]{3,2,1,0:T(8,128)(2,1)S(1)}, u32[]{:S(2)}, u32[]{:S(2)}) collective-permute-start(bf16[4,2,32,256]{3,2,1,0:T(8,128)(2,1)S(1)} %get-tuple-element.13), channel_id=1, source_target_pairs={{0,2},{1,3},{2,0},{3,1},{4,6},{5,7},{6,4},{7,5},{8,10},{9,11},{10,... | collective-permute-start | bytes 393224 | tf_op jit(solution)/shard_map/ppermute | solution.py:233
  42.6 7.3 %collective-permute-start.10 = (bf16[4,2,32,256]{3,2,1,0:T(8,128)(2,1)S(1)}, bf16[4,2,32,256]{3,2,1,0:T(8,128)(2,1)S(1)}, u32[]{:S(2)}, u32[]{:S(2)}) collective-permute-start(bf16[4,2,32,256]{3,2,1,0:T(8,128)(2,1)S(1)} %get-tuple-element.14), channel_id=1, source_target_pairs={{0,1},{1,0},{2,3},{3,2},{4,5},{5,4},{6,7},{7,6},{8,9},{9,8},{10,11... | collective-permute-start | bytes 393224 | tf_op jit(solution)/shard_map/ppermute | solution.py:233
  51.3 6.3 %collective-permute-start.15 = (bf16[4,2,32,256]{3,2,1,0:T(8,128)(2,1)}, bf16[4,2,32,256]{3,2,1,0:T(8,128)(2,1)}, u32[]{:S(2)}, u32[]{:S(2)}) collective-permute-start(bf16[4,2,32,256]{3,2,1,0:T(8,128)(2,1)} %get-tuple-element.8), channel_id=1, source_target_pairs={{0,3},{1,2},{2,1},{3,0},{4,7},{5,6},{6,5},{7,4},{8,11},{9,10},{10,... | collective-permute-start | bytes 393224 | tf_op jit(solution)/shard_map/ppermute | solution.py:233
  52.8 7.7 %collective-permute-start.14 = (bf16[4,2,32,256]{3,2,1,0:T(8,128)(2,1)}, bf16[4,2,32,256]{3,2,1,0:T(8,128)(2,1)}, u32[]{:S(2)}, u32[]{:S(2)}) collective-permute-start(bf16[4,2,32,256]{3,2,1,0:T(8,128)(2,1)} %get-tuple-element.9), channel_id=1, source_target_pairs={{0,2},{1,3},{2,0},{3,1},{4,6},{5,7},{6,4},{7,5},{8,10},{9,11},{10,... | collective-permute-start | bytes 393224 | tf_op jit(solution)/shard_map/ppermute | solution.py:233
  53.3 7.1 %collective-permute-start.13 = (bf16[4,2,32,256]{3,2,1,0:T(8,128)(2,1)}, bf16[4,2,32,256]{3,2,1,0:T(8,128)(2,1)}, u32[]{:S(2)}, u32[]{:S(2)}) collective-permute-start(bf16[4,2,32,256]{3,2,1,0:T(8,128)(2,1)} %get-tuple-element.10), channel_id=1, source_target_pairs={{0,1},{1,0},{2,3},{3,2},{4,5},{5,4},{6,7},{7,6},{8,9},{9,8},{10,11... | collective-permute-start | bytes 393224 | tf_op jit(solution)/shard_map/ppermute | solution.py:233
  60.4 1.6 %copy-start.1 = (bf16[4,128,2048]{2,1,0:T(8,128)(2,1)S(1)}, bf16[4,128,2048]{2,1,0:T(8,128)(2,1)}, u32[]{:S(2)}) copy-start(bf16[4,128,2048]{2,1,0:T(8,128)(2,1)} %q_ref.1) | copy-start | bytes 6291460
  64.7 0.9 %copy-start.9 = (bf16[4,2,32,256]{3,2,1,0:T(8,128)(2,1)S(1)}, bf16[4,2,32,256]{3,2,1,0:T(8,128)(2,1)}, u32[]{:S(2)}) copy-start(bf16[4,2,32,256]{3,2,1,0:T(8,128)(2,1)} %copy-done.8) | copy-start | bytes 393220
  65.7 0.9 %copy-start.11 = (bf16[4,2,32,256]{3,2,1,0:T(8,128)(2,1)S(1)}, bf16[4,2,32,256]{3,2,1,0:T(8,128)(2,1)}, u32[]{:S(2)}) copy-start(bf16[4,2,32,256]{3,2,1,0:T(8,128)(2,1)} %copy-done.10) | copy-start | bytes 393220
  (9 other events, 6.9 us)

commit v10 on v9

--- a/solution.py
+++ b/solution.py
@@ -12,7 +12,7 @@
 KVH = 8
 LOG2E = 1.4426950408889634
 STEP = 8
-VMEM_BYTES = 24 << 20
+VMEM_BYTES = 40 << 20
 
 
 class Part:
@@ -120,7 +120,7 @@
     one_step = longest <= STEP
 
     def lanes_of(head):
-        return pl.ds(pl.multiple_of(head * head_dim, head_dim), head_dim)
+        return slice(head * head_dim, (head + 1) * head_dim)
 
     def rows_of(h):
         return slice(h * span_len, (h + 1) * span_len)
@@ -133,36 +133,47 @@
     def attend(pages, begin):
         wide = len(pages) * span_len
 
-        def kv_head(g, unused):
-            keys = jnp.concatenate([kv_ref[page, g, :, :head_dim] for page in pages], axis=0)
+        def cols_of(n):
+            return slice(n * span_len, (n + 1) * span_len)
+
+        for g in range(kv_local):
             q = jnp.concatenate(
                 [q_ref[0, :, lanes_of(g * per_head + h)] for h in range(per_head)], axis=0
             )
-            s_ref[:, :wide] = lax.dot_general(
-                q, keys, (((1,), (1,)), ((), ())), preferred_element_type=jnp.float32
-            )
+            for n in range(0, len(pages), 2):
+                some = pages[n:n + 2]
+                keys = jnp.concatenate([kv_ref[p, g, :, :head_dim] for p in some], axis=0)
+                s = lax.dot_general(
+                    q, keys, (((1,), (1,)), ((), ())), preferred_element_type=jnp.float32
+                )
+                for m in range(len(some)):
+                    if begin and n + m == len(pages) - 1:
+                        for h in range(per_head):
+                            s_ref[g, rows_of(h), cols_of(n + m)] = jnp.where(
+                                causal, s[rows_of(h), cols_of(m)], -1e30
+                            )
+                    else:
+                        s_ref[g, :, cols_of(n + m)] = s[:, cols_of(m)]
+        for g in range(kv_local):
             rescales = []
             for h in range(per_head):
                 head = g * per_head + h
-                s = s_ref[rows_of(h), :wide] * scale
-                if begin:
-                    own_part = jnp.where(causal, s[:, wide - span_len:], -1e30)
-                    if len(pages) > 1:
-                        s = jnp.concatenate([s[:, :wide - span_len], own_part], axis=1)
-                    else:
-                        s = own_part
-                top = jnp.max(s, axis=1, keepdims=True)
-                if begin:
-                    top = jnp.broadcast_to(top, (span_len, head_dim))
-                else:
+                top = s_ref[g, rows_of(h), cols_of(0)]
+                for n in range(1, len(pages)):
+                    top = jnp.maximum(top, s_ref[g, rows_of(h), cols_of(n)])
+                top = jnp.broadcast_to(
+                    jnp.max(top, axis=1, keepdims=True) * scale, (span_len, head_dim)
+                )
+                if not begin:
                     old = max_ref[head]
                     top = jnp.maximum(old, top)
                     rescales.append(jnp.exp2(old - top))
                 if not one_step:
                     max_ref[head] = top
-                p_ref[rows_of(h), :wide] = jnp.exp2(
-                    s - jnp.concatenate([top] * len(pages), axis=1)
-                ).astype(jnp.bfloat16)
+                for n in range(len(pages)):
+                    p_ref[g, rows_of(h), cols_of(n)] = jnp.exp2(
+                        s_ref[g, rows_of(h), cols_of(n)] * scale - top
+                    ).astype(jnp.bfloat16)
             values = jnp.concatenate(
                 [
                     jnp.concatenate([kv_ref[page, g, :, head_dim:], ones], axis=1)
@@ -170,7 +181,7 @@
                 ],
                 axis=0,
             )
-            mixed = jnp.dot(p_ref[:, :wide], values, preferred_element_type=jnp.float32)
+            mixed = jnp.dot(p_ref[g, :, :wide], values, preferred_element_type=jnp.float32)
             for h in range(per_head):
                 head = g * per_head + h
                 new = mixed[rows_of(h)]
@@ -182,9 +193,6 @@
                     acc_ref[head] = new + acc_ref[head] * jnp.concatenate(
                         [rescales[h]] * 2, axis=1
                     )
-            return unused
-
-        lax.fori_loop(0, kv_local, kv_head, 0)
 
     over = lax.rem(count, STEP)
     for n in range(STEP):
@@ -244,17 +252,20 @@
             exchange(s, hops[-1][1])
         return hops, parts, sources
 
-    sources += [[2, 3, 0, 1], [1, 0, 3, 2], [3, -1, -1, 0], [-1, 2, 1, -1], [3, 2, 1, 0]]
+    sources += [[1, 0, 3, 2], [-1, 2, 1, -1], [-1, 3, 0, -1], [2, -1, -1, 1], [3, -1, -1, 0]]
+    sources += [[2, 2, 1, 1], [3, 3, 0, 0]]
     middle = (inst == 1) | (inst == 2)
-    shifted = along(kv_new, [(0, 2), (1, 3), (2, 0), (3, 1)])
     outer = along(kv_new, [(0, 1), (1, 0), (2, 3), (3, 2)])
+    inner = along(kv_new, [(1, 2), (2, 1)])
     waiting = exchange(0, kv_new)
-    handed = along(after([shifted], waiting)[0], [(1, 0), (2, 3)])
-    inner = along(jnp.where(middle, kv_new, shifted), [(1, 2), (2, 1)])
-    waiting = exchange(2, outer)
-    waiting = exchange(1, after([shifted], waiting)[0])
-    exchange(5, after([jnp.where(middle, inner, handed)], waiting)[0])
-    for hop, x in enumerate((shifted, outer, handed, inner), 1):
+    outer_on, inner_on = after([outer, inner], waiting)
+    crossed = along(outer_on, [(1, 2), (2, 1)])
+    inner_ends = along(inner_on, [(1, 0), (2, 3)])
+    waiting = exchange(1, outer_on)
+    crossed_ends = along(after([crossed], waiting)[0], [(1, 0), (2, 3)])
+    waiting = exchange(6, jnp.where(middle, inner, inner_ends))
+    exchange(7, after([jnp.where(middle, crossed, crossed_ends)], waiting)[0])
+    for hop, x in enumerate((outer, inner, crossed, inner_ends, crossed_ends), 1):
         hops.append(((hop, 0, slot_count), x))
     return hops, parts, sources
 
@@ -294,7 +305,7 @@
         prompt_count=prompt_spans.shape[0],
     )
     work = slot_count * span_total // 4 * local_heads * span_len * span_len
-    anywhere = pl.BlockSpec(memory_space=pl.ANY)
+    outside = pl.BlockSpec(memory_space=pltpu.HBM)
     by_slot = pl.BlockSpec((1, span_len, row_width), lambda i, *_: (i, 0, 0))
     kept = (local_heads, span_len) if longest > STEP else (1, 8)
     return pl.pallas_call(
@@ -302,13 +313,13 @@
         grid_spec=pltpu.PrefetchScalarGridSpec(
             num_scalar_prefetch=1,
             grid=(slot_count,),
-            in_specs=[by_slot] + [anywhere] * (len(hops) + len(parts)),
-            out_specs=[by_slot, anywhere],
+            in_specs=[by_slot] + [outside] * (len(hops) + len(parts)),
+            out_specs=[by_slot, outside],
             scratch_shapes=[
                 pltpu.SMEM((span_total,), jnp.int32),
                 pltpu.VMEM((span_total, kv_local, span_len, width), jnp.bfloat16),
-                pltpu.VMEM((rows, STEP * span_len), jnp.float32),
-                pltpu.VMEM((rows, STEP * span_len), jnp.bfloat16),
+                pltpu.VMEM((kv_local, rows, STEP * span_len), jnp.float32),
+                pltpu.VMEM((kv_local, rows, STEP * span_len), jnp.bfloat16),
                 pltpu.VMEM(kept + (2 * head_dim,), jnp.float32),
                 pltpu.VMEM(kept + (head_dim,), jnp.float32),
                 pltpu.VMEM((kv_heads, slice_len, width), jnp.bfloat16),

time: 84.4 us -> 80.8 us (0.957)
  the two profiles are of different devices: /device:TPU:21 before, /device:TPU:5 now
where the time goes in v10:
time: 80.8 us; the launch traced here: 79.4 us
  waiting for transfers between devices  25.7 us (32%)
  starting transfers between devices  20.9 us (26%)
  local copies, waits for them, and re-layouts  20.6 us (25%)
  Pallas kernels  11.2 us (14%)
  between operations  0.95 us (1%)
    unnamed x48, local copies, waits for them, and re-layouts  16.5 us
    ppermute x12, waiting for transfers between devices, exchange(): sent = lax.ppermute(sent, 'tp', [(t, t ^ j) for t in range(tp_size)])  15.9 us
    ppermute x12, starting transfers between devices, exchange(): sent = lax.ppermute(sent, 'tp', [(t, t ^ j) for t in range(tp_size)])  13.1 us
    pallas_call x1, Pallas kernels, body(): pl.pallas_call(kernel, grid_spec=pltpu.PrefetchScalarGridSpec(num_scalar_...  11.2 us
    ppermute x5, waiting for transfers between devices, along(): return lax.ppermute(x, 'inst', pairs)  9.79 us
    ppermute x5, starting transfers between devices, along(): return lax.ppermute(x, 'inst', pairs)  7.83 us
    dynamic_slice x4, local copies, waits for them, and re-layouts, exchange(): sent = lax.dynamic_slice_in_dim(x, head, kv_local, 1)  2.02 us
  transfers between devices with their start and end apart: 17, of which 8 were waited for; matrix products, arithmetic and copies ran while one was open for 4% of the time, Pallas kernels for 0%

profile of v10, /device:TPU:5, one launch (start us, length us, event | category | flops | bytes accessed | tf_op | source)
XLA Modules:
  0.0 79.4 jit_solution(8512689360782708182)
XLA Ops:
  1.3 3.9 %collective-permute-start = (bf16[4,8,32,256]{3,2,1,0:T(8,128)(2,1)}, bf16[4,8,32,256]{3,2,1,0:T(8,128)(2,1)S(1)}, u32[]{:S(2)}, u32[]{:S(2)}) collective-permute-start(bf16[4,8,32,256]{3,2,1,0:T(8,128)(2,1)} %refs_0_.1), channel_id=1, source_target_pairs={{0,4},{4,0},{8,12},{12,8},{1,5},{5,1},{9,13},{13,9},{2,6},{6,2},{1... | collective-permute-start | bytes 1572872 | tf_op jit(solution)/shard_map/ppermute | solution.py:233
  5.2 1.1 %constant_dynamic-slice_fusion.12 = (bf16[4,2,32,256]{3,2,1,0:T(8,128)(2,1)S(1)}, bf16[4,2,32,256]{3,2,1,0:T(8,128)(2,1)S(1)}, bf16[4,2,32,256]{3,2,1,0:T(8,128)(2,1)S(1)}, bf16[4,2,32,256]{3,2,1,0:T(8,128)(2,1)S(1)}) fusion(bf16[4,8,32,256]{3,2,1,0:T(8,128)(2,1)} %refs_0_.1, s32[]{:T(128)S(6)} %select_n.74, s32[]{:T(128)S(6)} %select_n.72, ...), kind=kLoop, calls=%fused_computation.14 | loop fusion | bytes 1048592 | tf_op jit(solution)/shard_map/dynamic_slice | solution.py:239
  6.3 2.4 %collective-permute-start.4 = (bf16[4,2,32,256]{3,2,1,0:T(8,128)(2,1)S(1)}, bf16[4,2,32,256]{3,2,1,0:T(8,128)(2,1)S(1)}, u32[]{:S(2)}, u32[]{:S(2)}) collective-permute-start(bf16[4,2,32,256]{3,2,1,0:T(8,128)(2,1)S(1)} %get-tuple-element.22), channel_id=1, source_target_pairs={{0,3},{1,2},{2,1},{3,0},{4,7},{5,6},{6,5},{7,4},{8,11},{9,10},{10,... | collective-permute-start | bytes 393224 | tf_op jit(solution)/shard_map/ppermute | solution.py:241
  9.2 3.9 %collective-permute-done.4.refs_9_ = bf16[4,2,32,256]{3,2,1,0:T(8,128)(2,1)S(1)} collective-permute-done((bf16[4,2,32,256]{3,2,1,0:T(8,128)(2,1)S(1)}, bf16[4,2,32,256]{3,2,1,0:T(8,128)(2,1)S(1)}, u32[]{:S(2)}, u32[]{:S(2)}) %collective-permute-start.4) | collective-permute-done | bytes 131104 | tf_op jit(solution)/shard_map/ppermute | solution.py:241
  13.7 2.1 %collective-permute-done.3.refs_8_ = bf16[4,2,32,256]{3,2,1,0:T(8,128)(2,1)S(1)} collective-permute-done((bf16[4,2,32,256]{3,2,1,0:T(8,128)(2,1)S(1)}, bf16[4,2,32,256]{3,2,1,0:T(8,128)(2,1)S(1)}, u32[]{:S(2)}, u32[]{:S(2)}) %collective-permute-start.3) | collective-permute-done | bytes 131104 | tf_op jit(solution)/shard_map/ppermute | solution.py:241
  17.8 1.3 %collective-permute-start.6 = (bf16[4,8,32,256]{3,2,1,0:T(8,128)(2,1)S(1)}, bf16[4,8,32,256]{3,2,1,0:T(8,128)(2,1)S(1)}, u32[]{:S(2)}, u32[]{:S(2)}) collective-permute-start(bf16[4,8,32,256]{3,2,1,0:T(8,128)(2,1)S(1)} %collective-permute-done.1.refs_2_), channel_id=1, source_target_pairs={{4,0},{8,12},{5,1},{9,13},{6,2},{10,14},{7,3},{11,15},{20,16},{24,... | collective-permute-start | bytes 1572872 | tf_op jit(solution)/shard_map/ppermute | solution.py:233
  19.2 2.3 %collective-permute-start.9 = (bf16[4,2,32,256]{3,2,1,0:T(8,128)(2,1)S(1)}, bf16[4,2,32,256]{3,2,1,0:T(8,128)(2,1)S(1)}, u32[]{:S(2)}, u32[]{:S(2)}) collective-permute-start(bf16[4,2,32,256]{3,2,1,0:T(8,128)(2,1)S(1)} %get-tuple-element.18), channel_id=1, source_target_pairs={{0,3},{1,2},{2,1},{3,0},{4,7},{5,6},{6,5},{7,4},{8,11},{9,10},{10,... | collective-permute-start | bytes 393224 | tf_op jit(solution)/shard_map/ppermute | solution.py:241
  22.0 3.9 %collective-permute-done.9.refs_13_ = bf16[4,2,32,256]{3,2,1,0:T(8,128)(2,1)S(1)} collective-permute-done((bf16[4,2,32,256]{3,2,1,0:T(8,128)(2,1)S(1)}, bf16[4,2,32,256]{3,2,1,0:T(8,128)(2,1)S(1)}, u32[]{:S(2)}, u32[]{:S(2)}) %collective-permute-start.9) | collective-permute-done | bytes 131104 | tf_op jit(solution)/shard_map/ppermute | solution.py:241
  26.5 2.1 %collective-permute-done.8.refs_12_ = bf16[4,2,32,256]{3,2,1,0:T(8,128)(2,1)S(1)} collective-permute-done((bf16[4,2,32,256]{3,2,1,0:T(8,128)(2,1)S(1)}, bf16[4,2,32,256]{3,2,1,0:T(8,128)(2,1)S(1)}, u32[]{:S(2)}, u32[]{:S(2)}) %collective-permute-start.8) | collective-permute-done | bytes 131104 | tf_op jit(solution)/shard_map/ppermute | solution.py:241
  29.9 1.3 %collective-permute-start.10 = (bf16[4,8,32,256]{3,2,1,0:T(8,128)(2,1)S(1)}, bf16[4,8,32,256]{3,2,1,0:T(8,128)(2,1)S(1)}, u32[]{:S(2)}, u32[]{:S(2)}) collective-permute-start(bf16[4,8,32,256]{3,2,1,0:T(8,128)(2,1)S(1)} %collective-permute-done.5.refs_3_), channel_id=1, source_target_pairs={{4,0},{8,12},{5,1},{9,13},{6,2},{10,14},{7,3},{11,15},{20,16},{24,... | collective-permute-start | bytes 1572872 | tf_op jit(solution)/shard_map/ppermute | solution.py:233
  31.6 3.9 %collective-permute-start.13 = (bf16[4,2,32,256]{3,2,1,0:T(8,128)(2,1)S(1)}, bf16[4,2,32,256]{3,2,1,0:T(8,128)(2,1)S(1)}, u32[]{:S(2)}, u32[]{:S(2)}) collective-permute-start(bf16[4,2,32,256]{3,2,1,0:T(8,128)(2,1)S(1)} %get-tuple-element.14), channel_id=1, source_target_pairs={{0,3},{1,2},{2,1},{3,0},{4,7},{5,6},{6,5},{7,4},{8,11},{9,10},{10,... | collective-permute-start | bytes 393224 | tf_op jit(solution)/shard_map/ppermute | solution.py:241
  36.0 9.5 %collective-permute-done.10.refs_5_ = bf16[4,8,32,256]{3,2,1,0:T(8,128)(2,1)S(1)} collective-permute-done((bf16[4,8,32,256]{3,2,1,0:T(8,128)(2,1)S(1)}, bf16[4,8,32,256]{3,2,1,0:T(8,128)(2,1)S(1)}, u32[]{:S(2)}, u32[]{:S(2)}) %collective-permute-start.10) | collective-permute-done | bytes 524320 | tf_op jit(solution)/shard_map/ppermute | solution.py:233
  48.3 1.9 %collective-permute-start.16 = (bf16[4,2,32,256]{3,2,1,0:T(8,128)(2,1)}, bf16[4,2,32,256]{3,2,1,0:T(8,128)(2,1)}, u32[]{:S(2)}, u32[]{:S(2)}) collective-permute-start(bf16[4,2,32,256]{3,2,1,0:T(8,128)(2,1)} %get-tuple-element.10), channel_id=1, source_target_pairs={{0,3},{1,2},{2,1},{3,0},{4,7},{5,6},{6,5},{7,4},{8,11},{9,10},{10,... | collective-permute-start | bytes 393224 | tf_op jit(solution)/shard_map/ppermute | solution.py:241
  50.2 1.1 %collective-permute-start.15 = (bf16[4,2,32,256]{3,2,1,0:T(8,128)(2,1)}, bf16[4,2,32,256]{3,2,1,0:T(8,128)(2,1)}, u32[]{:S(2)}, u32[]{:S(2)}) collective-permute-start(bf16[4,2,32,256]{3,2,1,0:T(8,128)(2,1)} %get-tuple-element.11), channel_id=1, source_target_pairs={{0,2},{1,3},{2,0},{3,1},{4,6},{5,7},{6,4},{7,5},{8,10},{9,11},{10,... | collective-permute-start | bytes 393224 | tf_op jit(solution)/shard_map/ppermute | solution.py:241
  51.4 1.3 %fusion = s32[8]{0:T(128)} fusion(s32[8,4]{0,1:T(4,128)} %constant.81.clone, s32[]{:T(128)S(6)} %select_n.66), kind=kLoop, calls=%fused_computation.19 | loop fusion | bytes 68 | tf_op jit(solution)/shard_map/jit(dynamic_index_in_dim)/squeeze | solution.py:288
  54.1 3.3 %collective-permute-done.15.refs_20_ = bf16[4,2,32,256]{3,2,1,0:T(8,128)(2,1)} collective-permute-done((bf16[4,2,32,256]{3,2,1,0:T(8,128)(2,1)}, bf16[4,2,32,256]{3,2,1,0:T(8,128)(2,1)}, u32[]{:S(2)}, u32[]{:S(2)}) %collective-permute-start.15) | collective-permute-done | bytes 131104 | tf_op jit(solution)/shard_map/ppermute | solution.py:241
  58.3 1.6 %copy-done.2 = bf16[4,128,2048]{2,1,0:T(8,128)(2,1)S(1)} copy-done((bf16[4,128,2048]{2,1,0:T(8,128)(2,1)S(1)}, bf16[4,128,2048]{2,1,0:T(8,128)(2,1)}, u32[]{:S(2)}) %copy-start.2) | copy-done | bytes 2097176
  59.9 0.9 %copy-done.4 = bf16[4,2,32,256]{3,2,1,0:T(8,128)(2,1)S(1)} copy-done((bf16[4,2,32,256]{3,2,1,0:T(8,128)(2,1)S(1)}, bf16[4,2,32,256]{3,2,1,0:T(8,128)(2,1)}, u32[]{:S(2)}) %copy-start.4) | copy-done | bytes 131096
  60.8 0.9 %copy-done.6 = bf16[4,2,32,256]{3,2,1,0:T(8,128)(2,1)S(1)} copy-done((bf16[4,2,32,256]{3,2,1,0:T(8,128)(2,1)S(1)}, bf16[4,2,32,256]{3,2,1,0:T(8,128)(2,1)}, u32[]{:S(2)}) %copy-start.6) | copy-done | bytes 131096
  61.7 0.9 %copy-done.8 = bf16[4,2,32,256]{3,2,1,0:T(8,128)(2,1)S(1)} copy-done((bf16[4,2,32,256]{3,2,1,0:T(8,128)(2,1)S(1)}, bf16[4,2,32,256]{3,2,1,0:T(8,128)(2,1)}, u32[]{:S(2)}) %copy-start.8) | copy-done | bytes 131096
  62.6 0.9 %copy-done.10 = bf16[4,2,32,256]{3,2,1,0:T(8,128)(2,1)S(1)} copy-done((bf16[4,2,32,256]{3,2,1,0:T(8,128)(2,1)S(1)}, bf16[4,2,32,256]{3,2,1,0:T(8,128)(2,1)}, u32[]{:S(2)}) %copy-start.10) | copy-done | bytes 131096
  63.5 0.9 %copy-done.12 = bf16[4,2,32,256]{3,2,1,0:T(8,128)(2,1)S(1)} copy-done((bf16[4,2,32,256]{3,2,1,0:T(8,128)(2,1)S(1)}, bf16[4,2,32,256]{3,2,1,0:T(8,128)(2,1)}, u32[]{:S(2)}) %copy-start.12) | copy-done | bytes 131096
  64.4 0.9 %copy-done.14 = bf16[4,2,32,256]{3,2,1,0:T(8,128)(2,1)S(1)} copy-done((bf16[4,2,32,256]{3,2,1,0:T(8,128)(2,1)S(1)}, bf16[4,2,32,256]{3,2,1,0:T(8,128)(2,1)}, u32[]{:S(2)}) %copy-start.14) | copy-done | bytes 131096
  68.1 11.2 %shard_map.86 = (bf16[4,128,2048]{2,1,0:T(8,128)(2,1)}, bf16[8,8,32,256]{3,2,1,0:T(8,128)(2,1)}) custom-call(s32[38]{0:T(128)S(1)} %concatenate.3.numbers_ref, bf16[4,128,2048]{2,1,0:T(8,128)(2,1)S(1)} %copy-done.2, bf16[4,8,32,256]{3,2,1,0:T(8,128)(2,1)S(1)} %copy-done, bf16[4,8,32,256]{3,2,1,0:T(8,128)(2,1)S(1)} %collective-permute-done.refs_1_, ...), custom_call_target="tpu_custom_call" | custom-call | flops 2147483648 | bytes 8388608 | tf_op jit(solution)/shard_map/pallas_call | solution.py:311
  (67 shorter events, 15.1 us)
Async XLA Ops:
  0.6 16.5 %collective-permute-start.1 = (bf16[4,8,32,256]{3,2,1,0:T(8,128)(2,1)}, bf16[4,8,32,256]{3,2,1,0:T(8,128)(2,1)S(1)}, u32[]{:S(2)}, u32[]{:S(2)}) collective-permute-start(bf16[4,8,32,256]{3,2,1,0:T(8,128)(2,1)} %refs_0_.1), channel_id=1, source_target_pairs={{4,8},{8,4},{5,9},{9,5},{6,10},{10,6},{7,11},{11,7},{20,24},{24,20... | collective-permute-start | bytes 1572872 | tf_op jit(solution)/shard_map/ppermute | solution.py:233
  1.3 15.8 %collective-permute-start = (bf16[4,8,32,256]{3,2,1,0:T(8,128)(2,1)}, bf16[4,8,32,256]{3,2,1,0:T(8,128)(2,1)S(1)}, u32[]{:S(2)}, u32[]{:S(2)}) collective-permute-start(bf16[4,8,32,256]{3,2,1,0:T(8,128)(2,1)} %refs_0_.1), channel_id=1, source_target_pairs={{0,4},{4,0},{8,12},{12,8},{1,5},{5,1},{9,13},{13,9},{2,6},{6,2},{1... | collective-permute-start | bytes 1572872 | tf_op jit(solution)/shard_map/ppermute | solution.py:233
  6.3 6.7 %collective-permute-start.4 = (bf16[4,2,32,256]{3,2,1,0:T(8,128)(2,1)S(1)}, bf16[4,2,32,256]{3,2,1,0:T(8,128)(2,1)S(1)}, u32[]{:S(2)}, u32[]{:S(2)}) collective-permute-start(bf16[4,2,32,256]{3,2,1,0:T(8,128)(2,1)S(1)} %get-tuple-element.22), channel_id=1, source_target_pairs={{0,3},{1,2},{2,1},{3,0},{4,7},{5,6},{6,5},{7,4},{8,11},{9,10},{10,... | collective-permute-start | bytes 393224 | tf_op jit(solution)/shard_map/ppermute | solution.py:241
  8.7 7.1 %collective-permute-start.3 = (bf16[4,2,32,256]{3,2,1,0:T(8,128)(2,1)S(1)}, bf16[4,2,32,256]{3,2,1,0:T(8,128)(2,1)S(1)}, u32[]{:S(2)}, u32[]{:S(2)}) collective-permute-start(bf16[4,2,32,256]{3,2,1,0:T(8,128)(2,1)S(1)} %get-tuple-element.23), channel_id=1, source_target_pairs={{0,2},{1,3},{2,0},{3,1},{4,6},{5,7},{6,4},{7,5},{8,10},{9,11},{10,... | collective-permute-start | bytes 393224 | tf_op jit(solution)/shard_map/ppermute | solution.py:241
  9.0 7.5 %collective-permute-start.2 = (bf16[4,2,32,256]{3,2,1,0:T(8,128)(2,1)S(1)}, bf16[4,2,32,256]{3,2,1,0:T(8,128)(2,1)S(1)}, u32[]{:S(2)}, u32[]{:S(2)}) collective-permute-start(bf16[4,2,32,256]{3,2,1,0:T(8,128)(2,1)S(1)} %get-tuple-element.24), channel_id=1, source_target_pairs={{0,1},{1,0},{2,3},{3,2},{4,5},{5,4},{6,7},{7,6},{8,9},{9,8},{10,11... | collective-permute-start | bytes 393224 | tf_op jit(solution)/shard_map/ppermute | solution.py:241
  17.1 12.8 %collective-permute-start.5 = (bf16[4,8,32,256]{3,2,1,0:T(8,128)(2,1)S(1)}, bf16[4,8,32,256]{3,2,1,0:T(8,128)(2,1)S(1)}, u32[]{:S(2)}, u32[]{:S(2)}) collective-permute-start(bf16[4,8,32,256]{3,2,1,0:T(8,128)(2,1)S(1)} %collective-permute-done.refs_1_), channel_id=1, source_target_pairs={{4,8},{8,4},{5,9},{9,5},{6,10},{10,6},{7,11},{11,7},{20,24},{24,20... | collective-permute-start | bytes 1572872 | tf_op jit(solution)/shard_map/ppermute | solution.py:233
  17.8 13.6 %collective-permute-start.6 = (bf16[4,8,32,256]{3,2,1,0:T(8,128)(2,1)S(1)}, bf16[4,8,32,256]{3,2,1,0:T(8,128)(2,1)S(1)}, u32[]{:S(2)}, u32[]{:S(2)}) collective-permute-start(bf16[4,8,32,256]{3,2,1,0:T(8,128)(2,1)S(1)} %collective-permute-done.1.refs_2_), channel_id=1, source_target_pairs={{4,0},{8,12},{5,1},{9,13},{6,2},{10,14},{7,3},{11,15},{20,16},{24,... | collective-permute-start | bytes 1572872 | tf_op jit(solution)/shard_map/ppermute | solution.py:233
  19.2 6.7 %collective-permute-start.9 = (bf16[4,2,32,256]{3,2,1,0:T(8,128)(2,1)S(1)}, bf16[4,2,32,256]{3,2,1,0:T(8,128)(2,1)S(1)}, u32[]{:S(2)}, u32[]{:S(2)}) collective-permute-start(bf16[4,2,32,256]{3,2,1,0:T(8,128)(2,1)S(1)} %get-tuple-element.18), channel_id=1, source_target_pairs={{0,3},{1,2},{2,1},{3,0},{4,7},{5,6},{6,5},{7,4},{8,11},{9,10},{10,... | collective-permute-start | bytes 393224 | tf_op jit(solution)/shard_map/ppermute | solution.py:241
  21.5 7.1 %collective-permute-start.8 = (bf16[4,2,32,256]{3,2,1,0:T(8,128)(2,1)S(1)}, bf16[4,2,32,256]{3,2,1,0:T(8,128)(2,1)S(1)}, u32[]{:S(2)}, u32[]{:S(2)}) collective-permute-start(bf16[4,2,32,256]{3,2,1,0:T(8,128)(2,1)S(1)} %get-tuple-element.19), channel_id=1, source_target_pairs={{0,2},{1,3},{2,0},{3,1},{4,6},{5,7},{6,4},{7,5},{8,10},{9,11},{10,... | collective-permute-start | bytes 393224 | tf_op jit(solution)/shard_map/ppermute | solution.py:241
  21.8 7.5 %collective-permute-start.7 = (bf16[4,2,32,256]{3,2,1,0:T(8,128)(2,1)S(1)}, bf16[4,2,32,256]{3,2,1,0:T(8,128)(2,1)S(1)}, u32[]{:S(2)}, u32[]{:S(2)}) collective-permute-start(bf16[4,2,32,256]{3,2,1,0:T(8,128)(2,1)S(1)} %get-tuple-element.20), channel_id=1, source_target_pairs={{0,1},{1,0},{2,3},{3,2},{4,5},{5,4},{6,7},{7,6},{8,9},{9,8},{10,11... | collective-permute-start | bytes 393224 | tf_op jit(solution)/shard_map/ppermute | solution.py:241
  29.9 15.6 %collective-permute-start.10 = (bf16[4,8,32,256]{3,2,1,0:T(8,128)(2,1)S(1)}, bf16[4,8,32,256]{3,2,1,0:T(8,128)(2,1)S(1)}, u32[]{:S(2)}, u32[]{:S(2)}) collective-permute-start(bf16[4,8,32,256]{3,2,1,0:T(8,128)(2,1)S(1)} %collective-permute-done.5.refs_3_), channel_id=1, source_target_pairs={{4,0},{8,12},{5,1},{9,13},{6,2},{10,14},{7,3},{11,15},{20,16},{24,... | collective-permute-start | bytes 1572872 | tf_op jit(solution)/shard_map/ppermute | solution.py:233
  31.5 21.1 %copy-start.21 = (s32[4]{0:T(128)S(1)}, s32[4]{0:T(128)}, u32[]{:S(2)}) copy-start(s32[4]{0:T(128)} %param.9) | copy-start | bytes 52
  31.5 21.1 %copy-start.22 = (s32[4]{0:T(128)S(1)}, s32[4]{0:T(128)}, u32[]{:S(2)}) copy-start(s32[4]{0:T(128)} %param.10) | copy-start | bytes 52
  31.5 21.1 %copy-start.23 = (s32[4]{0:T(128)S(1)}, s32[4]{0:T(128)}, u32[]{:S(2)}) copy-start(s32[4]{0:T(128)} %param.12) | copy-start | bytes 52
  31.6 25.9 %copy-start = (bf16[4,8,32,256]{3,2,1,0:T(8,128)(2,1)S(1)}, bf16[4,8,32,256]{3,2,1,0:T(8,128)(2,1)}, u32[]{:S(2)}) copy-start(bf16[4,8,32,256]{3,2,1,0:T(8,128)(2,1)} %refs_0_.1) | copy-start | bytes 1572868
  31.6 13.9 %collective-permute-start.13 = (bf16[4,2,32,256]{3,2,1,0:T(8,128)(2,1)S(1)}, bf16[4,2,32,256]{3,2,1,0:T(8,128)(2,1)S(1)}, u32[]{:S(2)}, u32[]{:S(2)}) collective-permute-start(bf16[4,2,32,256]{3,2,1,0:T(8,128)(2,1)S(1)} %get-tuple-element.14), channel_id=1, source_target_pairs={{0,3},{1,2},{2,1},{3,0},{4,7},{5,6},{6,5},{7,4},{8,11},{9,10},{10,... | collective-permute-start | bytes 393224 | tf_op jit(solution)/shard_map/ppermute | solution.py:241
  35.5 10.7 %collective-permute-start.12 = (bf16[4,2,32,256]{3,2,1,0:T(8,128)(2,1)S(1)}, bf16[4,2,32,256]{3,2,1,0:T(8,128)(2,1)S(1)}, u32[]{:S(2)}, u32[]{:S(2)}) collective-permute-start(bf16[4,2,32,256]{3,2,1,0:T(8,128)(2,1)S(1)} %get-tuple-element.15), channel_id=1, source_target_pairs={{0,2},{1,3},{2,0},{3,1},{4,6},{5,7},{6,4},{7,5},{8,10},{9,11},{10,... | collective-permute-start | bytes 393224 | tf_op jit(solution)/shard_map/ppermute | solution.py:241
  35.8 11.1 %collective-permute-start.11 = (bf16[4,2,32,256]{3,2,1,0:T(8,128)(2,1)S(1)}, bf16[4,2,32,256]{3,2,1,0:T(8,128)(2,1)S(1)}, u32[]{:S(2)}, u32[]{:S(2)}) collective-permute-start(bf16[4,2,32,256]{3,2,1,0:T(8,128)(2,1)S(1)} %get-tuple-element.16), channel_id=1, source_target_pairs={{0,1},{1,0},{2,3},{3,2},{4,5},{5,4},{6,7},{7,6},{8,9},{9,8},{10,11... | collective-permute-start | bytes 393224 | tf_op jit(solution)/shard_map/ppermute | solution.py:241
  48.3 5.8 %collective-permute-start.16 = (bf16[4,2,32,256]{3,2,1,0:T(8,128)(2,1)}, bf16[4,2,32,256]{3,2,1,0:T(8,128)(2,1)}, u32[]{:S(2)}, u32[]{:S(2)}) collective-permute-start(bf16[4,2,32,256]{3,2,1,0:T(8,128)(2,1)} %get-tuple-element.10), channel_id=1, source_target_pairs={{0,3},{1,2},{2,1},{3,0},{4,7},{5,6},{6,5},{7,4},{8,11},{9,10},{10,... | collective-permute-start | bytes 393224 | tf_op jit(solution)/shard_map/ppermute | solution.py:241
  50.2 7.2 %collective-permute-start.15 = (bf16[4,2,32,256]{3,2,1,0:T(8,128)(2,1)}, bf16[4,2,32,256]{3,2,1,0:T(8,128)(2,1)}, u32[]{:S(2)}, u32[]{:S(2)}) collective-permute-start(bf16[4,2,32,256]{3,2,1,0:T(8,128)(2,1)} %get-tuple-element.11), channel_id=1, source_target_pairs={{0,2},{1,3},{2,0},{3,1},{4,6},{5,7},{6,4},{7,5},{8,10},{9,11},{10,... | collective-permute-start | bytes 393224 | tf_op jit(solution)/shard_map/ppermute | solution.py:241
  51.4 6.1 %collective-permute-start.14 = (bf16[4,2,32,256]{3,2,1,0:T(8,128)(2,1)}, bf16[4,2,32,256]{3,2,1,0:T(8,128)(2,1)}, u32[]{:S(2)}, u32[]{:S(2)}) collective-permute-start(bf16[4,2,32,256]{3,2,1,0:T(8,128)(2,1)} %get-tuple-element.12), channel_id=1, source_target_pairs={{0,1},{1,0},{2,3},{3,2},{4,5},{5,4},{6,7},{7,6},{8,9},{9,8},{10,11... | collective-permute-start | bytes 393224 | tf_op jit(solution)/shard_map/ppermute | solution.py:241
  57.4 0.9 %copy-start.1 = (bf16[4,2,32,256]{3,2,1,0:T(8,128)(2,1)S(1)}, bf16[4,2,32,256]{3,2,1,0:T(8,128)(2,1)}, u32[]{:S(2)}) copy-start(bf16[4,2,32,256]{3,2,1,0:T(8,128)(2,1)} %get-tuple-element.13.refs_18_) | copy-start | bytes 393220
  58.3 1.6 %copy-start.2 = (bf16[4,128,2048]{2,1,0:T(8,128)(2,1)S(1)}, bf16[4,128,2048]{2,1,0:T(8,128)(2,1)}, u32[]{:S(2)}) copy-start(bf16[4,128,2048]{2,1,0:T(8,128)(2,1)} %q_ref.1) | copy-start | bytes 6291460
  60.8 0.9 %copy-start.6 = (bf16[4,2,32,256]{3,2,1,0:T(8,128)(2,1)S(1)}, bf16[4,2,32,256]{3,2,1,0:T(8,128)(2,1)}, u32[]{:S(2)}) copy-start(bf16[4,2,32,256]{3,2,1,0:T(8,128)(2,1)} %copy-done.5) | copy-start | bytes 393220
  (17 other events, 13.1 us)

commit v11 on v8

--- a/solution.py
+++ b/solution.py
@@ -23,9 +23,57 @@
         return self.ref[self.start + at]
 
 
+def place_kernel(numbers_ref, *refs, hops, slot_count, span_total, longest, prompt_count):
+    hop_refs = refs[:len(hops)]
+    cache_ref, place_ref, stage_ref, sems, out_sem = refs[len(hops):]
+    spans_ref = Part(numbers_ref, 0)
+    owner_ref = Part(numbers_ref, 2 * prompt_count)
+    plan_ref = Part(numbers_ref, 3 * prompt_count)
+    place_at_ref = Part(numbers_ref, 3 * prompt_count + span_total)
+    inst = place_at_ref[0]
+    first, count, start = jnp.int32(0), jnp.int32(0), jnp.int32(0)
+    for p in range(prompt_count):
+        hit = owner_ref[p] == inst
+        first = jnp.where(hit, start, first)
+        count = jnp.where(hit, spans_ref[p], count)
+        start = start + spans_ref[p]
+
+    def put(g, unused):
+        place_ref[plan_ref[g]] = g
+        return unused
+
+    lax.fori_loop(0, span_total, put, 0)
+
+    def copies(act, fill):
+        def row(r, unused):
+            page = place_ref[jnp.minimum(first + r, span_total - 1)]
+            for n, hop in enumerate(hops):
+                source = place_at_ref[2 + hop]
+                slot = page - source * slot_count
+
+                @pl.when((r < count) & (source >= 0) & (slot >= 0) & (slot < slot_count))
+                def _():
+                    act(pltpu.make_async_copy(hop_refs[n].at[slot], stage_ref.at[r], sems.at[r]))
+
+            if fill:
+                @pl.when(r >= count)
+                def _():
+                    stage_ref[r] = jnp.zeros(stage_ref.shape[1:], stage_ref.dtype)
+
+            return unused
+
+        lax.fori_loop(0, longest, row, 0)
+
+    copies(lambda copy: copy.start(), True)
+    copies(lambda copy: copy.wait(), False)
+    out = pltpu.make_async_copy(stage_ref, cache_ref, out_sem)
+    out.start()
+    out.wait()
+
+
 def attend_kernel(
     numbers_ref, *refs,
-    covers, hops, parts, later, first_call, last_call,
+    covers, parts, later, first_call, last_call,
     inst_size, tp_size, kv_local, per_head, head_dim, span_len, slot_count, longest, prompt_count,
 ):
     refs = list(refs)
@@ -37,16 +85,12 @@
 
     (q_ref,) = take(1)
     mixed_ref, total_ref = (None, None) if first_call else take(2)
-    hop_refs = take(len(hops))
     part_refs = take(len(parts))
     take(later)
-    if last_call:
-        out_ref, cache_ref = take(2)
-    else:
-        out_ref, next_total_ref = take(2)
+    (out_ref,) = take(1)
+    if not last_call:
+        (next_total_ref,) = take(1)
     place_ref, list_ref, kv_ref, s_ref, p_ref, acc_ref, max_ref, part_sems = take(8)
-    if last_call:
-        zero_ref, page_sems = take(2)
     step = pl.program_id(0)
     span_total = slot_count * inst_size
     spans_ref = Part(numbers_ref, 0)
@@ -61,47 +105,10 @@
     scale = LOG2E / math.sqrt(head_dim)
 
     def part_copies(act):
-        for n, (pieces, j) in enumerate(parts):
+        for n, (hop, j) in enumerate(parts):
+            slots = pl.ds(place_at_ref[2 + hop] * slot_count, slot_count)
             at = pl.ds(pl.multiple_of((tp ^ j) * slice_len, slice_len), slice_len)
-            begin = 0
-            for m, (hop, first_slot, size) in enumerate(pieces):
-                slots = pl.ds(place_at_ref[2 + hop] * slot_count + first_slot, size)
-                act(pltpu.make_async_copy(
-                    part_refs[n].at[begin:begin + size], kv_ref.at[slots, :, at],
-                    part_sems.at[n, m],
-                ))
-                begin += size
-
-    def cache_copies(act):
-        first = jnp.int32(0)
-        count = jnp.int32(0)
-        start = jnp.int32(0)
-        for p in range(prompt_count):
-            hit = owner_ref[p] == inst
-            first = jnp.where(hit, start, first)
-            count = jnp.where(hit, spans_ref[p], count)
-            start = start + spans_ref[p]
-
-        def row(r, unused):
-            page = place_ref[jnp.minimum(first + r, span_total - 1)]
-            for n, (hop, first_slot, size) in enumerate(hops):
-                source = place_at_ref[2 + hop]
-                slot = page - source * slot_count - first_slot
-                here = (source >= 0) & (slot >= 0) & (slot < size)
-
-                @pl.when((r < count) & here)
-                def _():
-                    act(pltpu.make_async_copy(
-                        hop_refs[n].at[slot], cache_ref.at[r], page_sems.at[r]
-                    ))
-
-            @pl.when(r >= count)
-            def _():
-                act(pltpu.make_async_copy(zero_ref, cache_ref.at[r], page_sems.at[r]))
-
-            return unused
-
-        lax.fori_loop(0, longest, row, 0)
+            act(pltpu.make_async_copy(part_refs[n], kv_ref.at[slots, :, at], part_sems.at[n]))
 
     @pl.when(step == 0)
     def _():
@@ -112,9 +119,6 @@
             return unused
 
         lax.fori_loop(0, span_total, put, 0)
-        if last_call:
-            zero_ref[...] = jnp.zeros_like(zero_ref)
-            cache_copies(lambda copy: copy.start())
         part_copies(lambda copy: copy.wait())
 
     own = inst * slot_count + step
@@ -225,7 +229,8 @@
         totals = jnp.ones((span_len, head_dim), jnp.float32)
         for head in range(kv_local * per_head):
             total = acc_ref[head, :, head_dim:]
-            mixed = acc_ref[head, :, :head_dim] / total
+            inverse = pl.reciprocal(total, approx=True)
+            mixed = acc_ref[head, :, :head_dim] * (inverse * (2.0 - total * inverse))
             if last_call:
                 mixed = jnp.where(live, mixed, 0.0)
             else:
@@ -267,12 +272,6 @@
             rest(over)
             finish()
 
-    if last_call:
-        @pl.when(step == slot_count - 1)
-        def _():
-            cache_copies(lambda copy: copy.wait())
-
-
 def after(values, earlier):
     return lax.optimization_barrier((list(values), list(earlier)))[0]
 
@@ -284,66 +283,52 @@
     tp = lax.axis_index("tp")
     slot_count, kv_heads = kv_new.shape[:2]
     sources = [list(range(inst_size))]
-    hops = [((0, 0, slot_count), kv_new)]
+    hops = [(0, kv_new)]
     parts = []
 
     def along(x, pairs):
         return lax.ppermute(x, "inst", pairs)
 
-    def exchange(*pieces):
-        names = [name for name, _ in pieces]
+    def exchange(hop, x):
         found = []
         for j in range(tp_size):
             head = ((tp ^ j) * kv_heads) // tp_size
-            sent = [lax.dynamic_slice_in_dim(x, head, kv_local, 1) for _, x in pieces]
-            sent = jnp.concatenate(sent, axis=0) if len(sent) > 1 else sent[0]
+            sent = lax.dynamic_slice_in_dim(x, head, kv_local, 1)
             if j:
                 sent = lax.ppermute(sent, "tp", [(t, t ^ j) for t in range(tp_size)])
-            found.append(((names, j), sent))
+            found.append(((hop, j), sent))
         parts.extend(found)
         return [x for _, x in found]
 
     if inst_size != 4:
-        exchange(hops[0])
+        exchange(0, kv_new)
         for s in range(1, inst_size):
             sources.append([(i - s) % inst_size for i in range(inst_size)])
             pairs = [(i, (i + s) % inst_size) for i in range(inst_size)]
-            hops.append(((s, 0, slot_count), along(kv_new, pairs)))
-            exchange(hops[-1])
+            hops.append((s, along(kv_new, pairs)))
+            exchange(s, hops[-1][1])
         return [], (list(range(inst_size)), parts, sources), hops
 
+    sources += [[1, 0, 3, 2], [-1, 2, 1, -1], [-1, 3, 0, -1], [2, -1, -1, 1], [3, -1, -1, 0]]
+    sources += [[2, 2, 1, 1], [3, 3, 0, 0]]
     middle = (inst == 1) | (inst == 2)
-    sources += [[1, 0, 3, 2], [-1, 2, 1, -1], [-1, 3, 0, -1], [2, -1, -1, 1], [3, -1, -1, 0]]
-    second, third = 6, 7
-    sources += [[2, 2, 1, 1], [3, 3, 0, 0]]
-    whole = slot_count
-    half = slot_count // 2
     outer = along(kv_new, [(0, 1), (1, 0), (2, 3), (3, 2)])
     inner = along(kv_new, [(1, 2), (2, 1)])
-    waiting = exchange(hops[0])
+    waiting = exchange(0, kv_new)
     outer_on, inner_on = after([outer, inner], waiting)
     crossed = along(outer_on, [(1, 2), (2, 1)])
     inner_ends = along(inner_on, [(1, 0), (2, 3)])
-    own_parts = parts[:]
-    first_parts = exchange(((1, 0, whole), outer_on))
-    state = attend([0], own_parts, sources, later=first_parts[:1])
-    state = attend([1], parts[tp_size:], sources, state=state)
-    crossed_on = after([crossed], first_parts)[0]
-    crossed_half = lax.optimization_barrier([crossed_on[:half], crossed_on[half:]])
-    crossed_ends = [along(x, [(1, 0), (2, 3)]) for x in crossed_half]
-    two = jnp.where(middle, inner, inner_ends)
-    waiting = exchange(((second, 0, whole), two))
-    second_parts = parts[2 * tp_size:]
-    third_parts = len(parts)
-    threes = [jnp.where(middle, crossed_half[n], crossed_ends[n]) for n in range(2)]
-    waiting = exchange(((third, 0, half), after(threes[:1], waiting)[0]))
-    state = attend([second], second_parts, sources, state=state, later=waiting[:1])
-    exchange(((third, half, half), after(threes[1:], waiting)[0]))
-    for n in range(2):
-        hops.append(((5, n * half, half), crossed_ends[n]))
-    for hop, x in enumerate((outer, inner, crossed, inner_ends), 1):
-        hops.append(((hop, 0, whole), x))
-    return state, ([third], parts[third_parts:], sources), hops
+    waiting = exchange(1, outer_on)
+    crossed_ends = along(after([crossed], waiting)[0], [(1, 0), (2, 3)])
+    first_parts = parts[:]
+    second = exchange(6, jnp.where(middle, inner, inner_ends))
+    second_parts = parts[len(first_parts):]
+    state = attend([0, 1], first_parts, sources, later=[second[0], crossed])
+    third = exchange(7, after([jnp.where(middle, crossed, crossed_ends)], second)[0])
+    third_parts = parts[len(first_parts) + len(second_parts):]
+    state = attend([6], second_parts, sources, state=state, later=third[:1])
+    hops += enumerate((outer, inner, crossed, inner_ends, crossed_ends), 1)
+    return state, ([7], third_parts, sources), hops
 
 
 def body(queries, kv_new, prompt_spans, prompt_tail, span_plan, decode_owner):
@@ -366,20 +351,21 @@
     state_specs = [by_slot, total_spec]
     work = slot_count * 4 * local_heads * span_len * span_len
 
-    def attend(covers, parts, sources, state=(), hops=None, later=()):
-        first_call, last_call = not state, hops is not None
-        hops = hops or []
+    def numbers_of(sources):
         own_sources = lax.dynamic_index_in_dim(
             jnp.asarray(sources, jnp.int32), inst_index, 1, False
         )
-        numbers = jnp.concatenate([
+        return jnp.concatenate([
             prompt_spans, prompt_tail, decode_owner, span_plan,
             jnp.stack([inst_index, tp_index]).astype(jnp.int32), own_sources,
         ])
+
+    def attend(covers, parts, sources, state=(), later=(), last_call=False):
+        first_call = not state
+        numbers = numbers_of(sources)
         kernel = functools.partial(
             attend_kernel,
             covers=covers,
-            hops=[name for name, _ in hops],
             parts=[name for name, _ in parts],
             later=len(later),
             first_call=first_call,
@@ -402,31 +388,20 @@
             pltpu.VMEM((kv_local, rows, STEP * span_len), jnp.bfloat16),
             pltpu.VMEM((local_heads, span_len, 2 * head_dim), jnp.float32),
             pltpu.VMEM((local_heads, span_len, head_dim), jnp.float32),
-            pltpu.SemaphoreType.DMA((len(parts), max(len(x[0][0]) for x in parts))),
+            pltpu.SemaphoreType.DMA((len(parts),)),
         ]
-        if last_call:
-            scratch += [
-                pltpu.VMEM((kv_heads, slice_len, width), jnp.bfloat16),
-                pltpu.SemaphoreType.DMA((longest,)),
-            ]
-            out_specs = [by_slot, anywhere]
-            out_shape = [
-                jax.ShapeDtypeStruct(queries.shape, jnp.bfloat16),
-                jax.ShapeDtypeStruct((longest, kv_heads, slice_len, width), jnp.bfloat16),
-            ]
-        else:
-            out_specs = state_specs
-            out_shape = [
-                jax.ShapeDtypeStruct(queries.shape, jnp.bfloat16),
-                jax.ShapeDtypeStruct((slot_count, span_len, head_dim), jnp.float32),
-            ]
+        out_specs = [by_slot] if last_call else state_specs
+        out_shape = [
+            jax.ShapeDtypeStruct(queries.shape, jnp.bfloat16),
+            jax.ShapeDtypeStruct((slot_count, span_len, head_dim), jnp.float32),
+        ][:len(out_specs)]
         return pl.pallas_call(
             kernel,
             grid_spec=pltpu.PrefetchScalarGridSpec(
                 num_scalar_prefetch=1,
                 grid=(slot_count,),
                 in_specs=[by_slot] + (state_specs if state else [])
-                + [anywhere] * (len(hops) + len(parts) + len(later)),
+                + [anywhere] * (len(parts) + len(later)),
                 out_specs=out_specs,
                 scratch_shapes=scratch,
             ),
@@ -436,12 +411,37 @@
             ),
             compiler_params=pltpu.CompilerParams(vmem_limit_bytes=VMEM_BYTES),
         )(
-            numbers, queries, *state, *[x for _, x in hops], *[x for _, x in parts],
-            *later,
+            numbers, queries, *state, *[x for _, x in parts], *later,
         )
 
     state, left, hops = move_pages(kv_new, kv_local, attend)
-    return tuple(attend(*left, state, hops))
+    page_shape = (kv_heads, slice_len, width)
+    owner_cache = pl.pallas_call(
+        functools.partial(
+            place_kernel,
+            hops=[name for name, _ in hops],
+            slot_count=slot_count,
+            span_total=span_total,
+            longest=longest,
+            prompt_count=prompt_spans.shape[0],
+        ),
+        grid_spec=pltpu.PrefetchScalarGridSpec(
+            num_scalar_prefetch=1,
+            grid=(1,),
+            in_specs=[anywhere] * len(hops),
+            out_specs=anywhere,
+            scratch_shapes=[
+                pltpu.SMEM((span_total,), jnp.int32),
+                pltpu.VMEM((longest,) + page_shape, jnp.bfloat16),
+                pltpu.SemaphoreType.DMA((longest,)),
+                pltpu.SemaphoreType.DMA,
+            ],
+        ),
+        out_shape=jax.ShapeDtypeStruct((longest,) + page_shape, jnp.bfloat16),
+        cost_estimate=pl.CostEstimate(flops=0, bytes_accessed=8 << 20, transcendentals=0),
+    )(numbers_of(left[2]), *[x for _, x in hops])
+    (attended,) = attend(*left, state, last_call=True)
+    return attended, owner_cache
 
 
 def solution(mesh):

time: 70.3 us -> 70.1 us (level)
  waiting for transfers between devices: 24.8 us -> 18 us
  local copies, waits for them, and re-layouts: 3.51 us -> 8.9 us
  other arithmetic: 0.13 us -> 1.16 us
  Pallas kernels: 22.1 us -> 23.1 us
  starting transfers between devices: 19.4 us -> 18.6 us
    ppermute x6 -> x5, waiting for transfers between devices: 18.6 us -> 6.29 us  [along(): return lax.ppermute(x, 'inst', pairs)]
    ppermute x15 -> x12, waiting for transfers between devices: 6.14 us -> 11.7 us  [exchange(): sent = lax.ppermute(sent, 'tp', [(t, t ^ j) for t in range(tp_size)])]
    pallas_call x0 -> x1, Pallas kernels: none -> 3.08 us  [body(): pl.pallas_call(functools.partial(place_kernel, hops=[name for name, _ in...]
    unnamed x4 -> x40, local copies, waits for them, and re-layouts: 0.01 us -> 3 us
    pallas_call x4 -> x3, Pallas kernels: 22.1 us -> 20 us  [attend(): pl.pallas_call(kernel, grid_spec=pltpu.PrefetchScalarGridSpec(num_scalar_...]
    dynamic_slice x5 -> x4, local copies, waits for them, and re-layouts: 2 us -> 3.97 us  [exchange(): sent = lax.dynamic_slice_in_dim(x, head, kv_local, 1)]
    select_n x3 -> x2, other arithmetic: 0.13 us -> 1.16 us  [the longest x1 1.1 us: move_pages(): second = exchange(6, jnp.where(middle, inner, inner_ends))]
    ppermute x15 -> x12, starting transfers between devices: 12.9 us -> 12.3 us  [exchange(): sent = lax.ppermute(sent, 'tp', [(t, t ^ j) for t in range(tp_size)])]
  transfers between devices with their start and end apart: 21 -> 17, of which waited for: 6 -> 6; matrix products, arithmetic and copies ran while one was open for 5% -> 9% of each run, Pallas kernels for 21% -> 22%
where the time goes in v11:
time: 70.1 us; the launch traced here: 70.9 us
  Pallas kernels  23.1 us (33%)
  starting transfers between devices  18.6 us (27%)
  waiting for transfers between devices  18 us (26%)
  local copies, waits for them, and re-layouts  8.9 us (13%)
  other arithmetic  1.16 us (2%)
  between operations  1.13 us (2%)
    pallas_call x3, Pallas kernels, attend(): pl.pallas_call(kernel, grid_spec=pltpu.PrefetchScalarGridSpec(num_scalar_...  20 us
    ppermute x12, starting transfers between devices, exchange(): sent = lax.ppermute(sent, 'tp', [(t, t ^ j) for t in range(tp_size)])  12.3 us
    ppermute x12, waiting for transfers between devices, exchange(): sent = lax.ppermute(sent, 'tp', [(t, t ^ j) for t in range(tp_size)])  11.7 us
    ppermute x5, waiting for transfers between devices, along(): return lax.ppermute(x, 'inst', pairs)  6.29 us
    ppermute x5, starting transfers between devices, along(): return lax.ppermute(x, 'inst', pairs)  6.27 us
    dynamic_slice x4, local copies, waits for them, and re-layouts, exchange(): sent = lax.dynamic_slice_in_dim(x, head, kv_local, 1)  3.97 us
    pallas_call x1, Pallas kernels, body(): pl.pallas_call(functools.partial(place_kernel, hops=[name for name, _ in...  3.08 us
    unnamed x40, local copies, waits for them, and re-layouts  3 us
  transfers between devices with their start and end apart: 17, of which 6 were waited for; matrix products, arithmetic and copies ran while one was open for 9% of the time, Pallas kernels for 22%

profile of v11, /device:TPU:5, one launch (start us, length us, event | category | flops | bytes accessed | tf_op | source)
XLA Modules:
  0.0 70.9 jit_solution(17296320925249030681)
XLA Ops:
  0.7 1.4 %collective-permute-start.3 = (bf16[4,8,32,256]{3,2,1,0:T(8,128)(2,1)}, bf16[4,8,32,256]{3,2,1,0:T(8,128)(2,1)}, u32[]{:S(2)}, u32[]{:S(2)}) collective-permute-start(bf16[4,8,32,256]{3,2,1,0:T(8,128)(2,1)} %refs_0_.7), channel_id=1, source_target_pairs={{0,4},{4,0},{8,12},{12,8},{1,5},{5,1},{9,13},{13,9},{2,6},{6,2},{1... | collective-permute-start | bytes 1572872 | tf_op jit(solution)/shard_map/ppermute | solution.py:290
  2.0 1.5 %collective-permute-start.4 = (bf16[4,8,32,256]{3,2,1,0:T(8,128)(2,1)}, bf16[4,8,32,256]{3,2,1,0:T(8,128)(2,1)}, u32[]{:S(2)}, u32[]{:S(2)}) collective-permute-start(bf16[4,8,32,256]{3,2,1,0:T(8,128)(2,1)} %refs_0_.7), channel_id=1, source_target_pairs={{4,8},{8,4},{5,9},{9,5},{6,10},{10,6},{7,11},{11,7},{20,24},{24,20... | collective-permute-start | bytes 1572872 | tf_op jit(solution)/shard_map/ppermute | solution.py:290
  3.5 1.1 %constant_dynamic-slice_fusion.10 = (bf16[4,2,32,256]{3,2,1,0:T(8,128)(2,1)S(1)}, bf16[4,2,32,256]{3,2,1,0:T(8,128)(2,1)S(1)}, bf16[4,2,32,256]{3,2,1,0:T(8,128)(2,1)S(1)}, bf16[4,2,32,256]{3,2,1,0:T(8,128)(2,1)S(1)}) fusion(bf16[4,8,32,256]{3,2,1,0:T(8,128)(2,1)} %refs_0_.7, s32[]{:T(128)S(6)} %select_n.77, s32[]{:T(128)S(6)} %select_n.75, ...), kind=kLoop, calls=%fused_computation.12 | loop fusion | bytes 1048592 | tf_op jit(solution)/shard_map/dynamic_slice | solution.py:296
  4.7 2.1 %collective-permute-start.2 = (bf16[4,2,32,256]{3,2,1,0:T(8,128)(2,1)S(1)}, bf16[4,2,32,256]{3,2,1,0:T(8,128)(2,1)S(1)}, u32[]{:S(2)}, u32[]{:S(2)}) collective-permute-start(bf16[4,2,32,256]{3,2,1,0:T(8,128)(2,1)S(1)} %get-tuple-element.30), channel_id=1, source_target_pairs={{0,3},{1,2},{2,1},{3,0},{4,7},{5,6},{6,5},{7,4},{8,11},{9,10},{10,... | collective-permute-start | bytes 393224 | tf_op jit(solution)/shard_map/ppermute | solution.py:298
  7.3 4.0 %collective-permute-done.2.refs_4_ = bf16[4,2,32,256]{3,2,1,0:T(8,128)(2,1)S(1)} collective-permute-done((bf16[4,2,32,256]{3,2,1,0:T(8,128)(2,1)S(1)}, bf16[4,2,32,256]{3,2,1,0:T(8,128)(2,1)S(1)}, u32[]{:S(2)}, u32[]{:S(2)}) %collective-permute-start.2) | collective-permute-done | bytes 131104 | tf_op jit(solution)/shard_map/ppermute | solution.py:298
  11.2 2.7 %collective-permute-done.1.refs_3_ = bf16[4,2,32,256]{3,2,1,0:T(8,128)(2,1)S(1)} collective-permute-done((bf16[4,2,32,256]{3,2,1,0:T(8,128)(2,1)S(1)}, bf16[4,2,32,256]{3,2,1,0:T(8,128)(2,1)S(1)}, u32[]{:S(2)}, u32[]{:S(2)}) %collective-permute-start.1) | collective-permute-done | bytes 131104 | tf_op jit(solution)/shard_map/ppermute | solution.py:298
  14.7 1.3 %collective-permute-start.8 = (bf16[4,8,32,256]{3,2,1,0:T(8,128)(2,1)}, bf16[4,8,32,256]{3,2,1,0:T(8,128)(2,1)}, u32[]{:S(2)}, u32[]{:S(2)}) collective-permute-start(bf16[4,8,32,256]{3,2,1,0:T(8,128)(2,1)} %collective-permute-done.4.refs_2_), channel_id=1, source_target_pairs={{4,0},{8,12},{5,1},{9,13},{6,2},{10,14},{7,3},{11,15},{20,16},{24,... | collective-permute-start | bytes 1572872 | tf_op jit(solution)/shard_map/ppermute | solution.py:290
  16.0 1.9 %constant_dynamic-slice_fusion.6 = (bf16[4,2,32,256]{3,2,1,0:T(8,128)(2,1)}, bf16[4,2,32,256]{3,2,1,0:T(8,128)(2,1)}, bf16[4,2,32,256]{3,2,1,0:T(8,128)(2,1)}, bf16[4,2,32,256]{3,2,1,0:T(8,128)(2,1)S(1)}) fusion(bf16[4,8,32,256]{3,2,1,0:T(8,128)(2,1)} %collective-permute-done.3.refs_1_, s32[]{:T(128)S(6)} %select_n.77, s32[]{:T(128)S(6)} %select_n.75, ...), kind=kLoop, calls=%fused_computation.8 | loop fusion | bytes 1048592 | tf_op jit(solution)/shard_map/dynamic_slice | solution.py:296
  17.8 2.5 %collective-permute-start.7 = (bf16[4,2,32,256]{3,2,1,0:T(8,128)(2,1)}, bf16[4,2,32,256]{3,2,1,0:T(8,128)(2,1)S(1)}, u32[]{:S(2)}, u32[]{:S(2)}) collective-permute-start(bf16[4,2,32,256]{3,2,1,0:T(8,128)(2,1)} %get-tuple-element.26), channel_id=1, source_target_pairs={{0,3},{1,2},{2,1},{3,0},{4,7},{5,6},{6,5},{7,4},{8,11},{9,10},{10,... | collective-permute-start | bytes 393224 | tf_op jit(solution)/shard_map/ppermute | solution.py:298
  20.8 1.2 %fusion = s32[8]{0:T(128)} fusion(s32[8,4]{0,1:T(4,128)} %constant.87.clone, s32[]{:T(128)S(6)} %select_n.69), kind=kLoop, calls=%fused_computation.19 | loop fusion | bytes 68 | tf_op jit(solution)/shard_map/jit(dynamic_index_in_dim)/squeeze | solution.py:355
  22.7 2.1 %collective-permute-done.7.refs_8_ = bf16[4,2,32,256]{3,2,1,0:T(8,128)(2,1)S(1)} collective-permute-done((bf16[4,2,32,256]{3,2,1,0:T(8,128)(2,1)}, bf16[4,2,32,256]{3,2,1,0:T(8,128)(2,1)S(1)}, u32[]{:S(2)}, u32[]{:S(2)}) %collective-permute-start.7) | collective-permute-done | bytes 131104 | tf_op jit(solution)/shard_map/ppermute | solution.py:298
  24.8 2.9 %collective-permute-done.6.refs_7_ = bf16[4,2,32,256]{3,2,1,0:T(8,128)(2,1)S(1)} collective-permute-done((bf16[4,2,32,256]{3,2,1,0:T(8,128)(2,1)}, bf16[4,2,32,256]{3,2,1,0:T(8,128)(2,1)S(1)}, u32[]{:S(2)}, u32[]{:S(2)}) %collective-permute-start.6) | collective-permute-done | bytes 131104 | tf_op jit(solution)/shard_map/ppermute | solution.py:298
  28.4 1.4 %collective-permute-start.13 = (bf16[4,8,32,256]{3,2,1,0:T(8,128)(2,1)S(1)}, bf16[4,8,32,256]{3,2,1,0:T(8,128)(2,1)S(1)}, u32[]{:S(2)}, u32[]{:S(2)}) collective-permute-start(bf16[4,8,32,256]{3,2,1,0:T(8,128)(2,1)S(1)} %collective-permute-done.9.refs_10_.refs_3_), channel_id=1, source_target_pairs={{4,0},{8,12},{5,1},{9,13},{6,2},{10,14},{7,3},{11,15},{20,16},{24,... | collective-permute-start | bytes 1572872 | tf_op jit(solution)/shard_map/ppermute | solution.py:290
  29.8 3.0 %collective-permute-done.8.refs_4_ = bf16[4,8,32,256]{3,2,1,0:T(8,128)(2,1)} collective-permute-done((bf16[4,8,32,256]{3,2,1,0:T(8,128)(2,1)}, bf16[4,8,32,256]{3,2,1,0:T(8,128)(2,1)}, u32[]{:S(2)}, u32[]{:S(2)}) %collective-permute-start.8) | collective-permute-done | bytes 524320 | tf_op jit(solution)/shard_map/ppermute | solution.py:290
  32.9 1.1 %broadcast_select_fusion.1 = bf16[4,8,32,256]{3,2,1,0:T(8,128)(2,1)S(1)} fusion(bf16[4,8,32,256]{3,2,1,0:T(8,128)(2,1)} %collective-permute-done.4.refs_2_, bf16[4,8,32,256]{3,2,1,0:T(8,128)(2,1)} %collective-permute-done.8.refs_4_, pred[]{:T(512)S(6)} %or.3), kind=kLoop, calls=%fused_computation.1 | loop fusion | flops 262144 | bytes 1572865 | tf_op jit(solution)/shard_map/jit(_where)/select_n | solution.py:324
  34.0 3.9 %collective-permute-start.12 = (bf16[4,2,32,256]{3,2,1,0:T(8,128)(2,1)S(1)}, bf16[4,2,32,256]{3,2,1,0:T(8,128)(2,1)S(1)}, u32[]{:S(2)}, u32[]{:S(2)}) collective-permute-start(bf16[4,2,32,256]{3,2,1,0:T(8,128)(2,1)S(1)} %get-tuple-element.22), channel_id=1, source_target_pairs={{0,3},{1,2},{2,1},{3,0},{4,7},{5,6},{6,5},{7,4},{8,11},{9,10},{10,... | collective-permute-start | bytes 393224 | tf_op jit(solution)/shard_map/ppermute | solution.py:298
  38.5 7.2 %shard_map.113 = (bf16[4,128,2048]{2,1,0:T(8,128)(2,1)S(1)}, f32[4,128,128]{2,1,0:T(8,128)S(1)}) custom-call(s32[38]{0:T(128)S(1)} %concatenate.12.numbers_ref, bf16[4,128,2048]{2,1,0:T(8,128)(2,1)S(1)} %copy-done.3, bf16[4,2,32,256]{3,2,1,0:T(8,128)(2,1)S(1)} %get-tuple-element.33.refs_1_, bf16[4,2,32,256]{3,2,1,0:T(8,128)(2,1)S(1)} %collective-permute-done.refs_2_, ...), custom_call_target="tpu_custom_call" | custom-call | flops 2147483648 | bytes 8388608 | tf_op jit(solution)/shard_map/pallas_call | solution.py:398
  46.4 3.2 %collective-permute-done.13.refs_5_ = bf16[4,8,32,256]{3,2,1,0:T(8,128)(2,1)S(1)} collective-permute-done((bf16[4,8,32,256]{3,2,1,0:T(8,128)(2,1)S(1)}, bf16[4,8,32,256]{3,2,1,0:T(8,128)(2,1)S(1)}, u32[]{:S(2)}, u32[]{:S(2)}) %collective-permute-start.13) | collective-permute-done | bytes 524320 | tf_op jit(solution)/shard_map/ppermute | solution.py:290
  49.8 0.9 %constant_dynamic-slice_fusion.14 = (bf16[4,2,32,256]{3,2,1,0:T(8,128)(2,1)}, bf16[4,2,32,256]{3,2,1,0:T(8,128)(2,1)}, bf16[4,2,32,256]{3,2,1,0:T(8,128)(2,1)}, bf16[4,2,32,256]{3,2,1,0:T(8,128)(2,1)S(1)}) fusion(bf16[4,8,32,256]{3,2,1,0:T(8,128)(2,1)S(1)} %broadcast_select_fusion, s32[]{:T(128)S(6)} %select_n.77, s32[]{:T(128)S(6)} %select_n.75, ...), kind=kLoop, calls=%fused_computation.16 | loop fusion | bytes 1048592 | tf_op jit(solution)/shard_map/dynamic_slice | solution.py:296
  51.6 1.5 %collective-permute-start.15 = (bf16[4,2,32,256]{3,2,1,0:T(8,128)(2,1)}, bf16[4,2,32,256]{3,2,1,0:T(8,128)(2,1)S(1)}, u32[]{:S(2)}, u32[]{:S(2)}) collective-permute-start(bf16[4,2,32,256]{3,2,1,0:T(8,128)(2,1)} %get-tuple-element.19), channel_id=1, source_target_pairs={{0,2},{1,3},{2,0},{3,1},{4,6},{5,7},{6,4},{7,5},{8,10},{9,11},{10,... | collective-permute-start | bytes 393224 | tf_op jit(solution)/shard_map/ppermute | solution.py:298
  53.2 3.1 %shard_map.116 = bf16[8,8,32,256]{3,2,1,0:T(8,128)(2,1)} custom-call(s32[38]{0:T(128)} %copy-done.1, bf16[4,8,32,256]{3,2,1,0:T(8,128)(2,1)} %refs_0_.7, bf16[4,8,32,256]{3,2,1,0:T(8,128)(2,1)} %collective-permute-done.3.refs_1_, bf16[4,8,32,256]{3,2,1,0:T(8,128)(2,1)} %collective-permute-done.4.refs_2_, bf16[4,8,32,256]{3,2,1,0:T(8,128)(2,1)} %copy-done, ...), custom_call_target="tpu_custom_call" | custom-call | bytes 8388608 | tf_op jit(solution)/shard_map/pallas_call | solution.py:419
  56.4 1.6 %copy-done.13 = bf16[4,128,2048]{2,1,0:T(8,128)(2,1)S(1)} copy-done((bf16[4,128,2048]{2,1,0:T(8,128)(2,1)S(1)}, bf16[4,128,2048]{2,1,0:T(8,128)(2,1)}, u32[]{:S(2)}) %copy-start.13) | copy-done | bytes 2097176
  57.9 5.5 %shard_map.114 = (bf16[4,128,2048]{2,1,0:T(8,128)(2,1)S(1)}, f32[4,128,128]{2,1,0:T(8,128)S(1)}) custom-call(s32[38]{0:T(128)S(1)} %copy-done.2, bf16[4,128,2048]{2,1,0:T(8,128)(2,1)S(1)} %copy-done.3, bf16[4,128,2048]{2,1,0:T(8,128)(2,1)S(1)} %copy-done.13, f32[4,128,128]{2,1,0:T(8,128)S(1)} %copy-done.15, ...), custom_call_target="tpu_custom_call" | custom-call | flops 2147483648 | bytes 8388608 | tf_op jit(solution)/shard_map/pallas_call | solution.py:398
  63.4 7.3 %shard_map.115 = bf16[4,128,2048]{2,1,0:T(8,128)(2,1)} custom-call(s32[38]{0:T(128)S(1)} %copy-done.2, bf16[4,128,2048]{2,1,0:T(8,128)(2,1)S(1)} %copy-done.3, bf16[4,128,2048]{2,1,0:T(8,128)(2,1)S(1)} %get-tuple-element.16.refs_1_, f32[4,128,128]{2,1,0:T(8,128)S(1)} %get-tuple-element.17.refs_2_, ...), custom_call_target="tpu_custom_call" | custom-call | flops 2147483648 | bytes 8388608 | tf_op jit(solution)/shard_map/pallas_call | solution.py:398
  (62 shorter events, 5.3 us)
Async XLA Ops:
  0.6 21.3 %copy-start.19 = (s32[4]{0:T(128)S(1)}, s32[4]{0:T(128)}, u32[]{:S(2)}) copy-start(s32[4]{0:T(128)} %param.15) | copy-start | bytes 52
  0.6 21.3 %copy-start.18 = (s32[4]{0:T(128)S(1)}, s32[4]{0:T(128)}, u32[]{:S(2)}) copy-start(s32[4]{0:T(128)} %param.13) | copy-start | bytes 52
  0.7 21.3 %copy-start.17 = (s32[4]{0:T(128)S(1)}, s32[4]{0:T(128)}, u32[]{:S(2)}) copy-start(s32[4]{0:T(128)} %param.12) | copy-start | bytes 52
  0.7 13.3 %collective-permute-start.3 = (bf16[4,8,32,256]{3,2,1,0:T(8,128)(2,1)}, bf16[4,8,32,256]{3,2,1,0:T(8,128)(2,1)}, u32[]{:S(2)}, u32[]{:S(2)}) collective-permute-start(bf16[4,8,32,256]{3,2,1,0:T(8,128)(2,1)} %refs_0_.7), channel_id=1, source_target_pairs={{0,4},{4,0},{8,12},{12,8},{1,5},{5,1},{9,13},{13,9},{2,6},{6,2},{1... | collective-permute-start | bytes 1572872 | tf_op jit(solution)/shard_map/ppermute | solution.py:290
  2.0 11.9 %collective-permute-start.4 = (bf16[4,8,32,256]{3,2,1,0:T(8,128)(2,1)}, bf16[4,8,32,256]{3,2,1,0:T(8,128)(2,1)}, u32[]{:S(2)}, u32[]{:S(2)}) collective-permute-start(bf16[4,8,32,256]{3,2,1,0:T(8,128)(2,1)} %refs_0_.7), channel_id=1, source_target_pairs={{4,8},{8,4},{5,9},{9,5},{6,10},{10,6},{7,11},{11,7},{20,24},{24,20... | collective-permute-start | bytes 1572872 | tf_op jit(solution)/shard_map/ppermute | solution.py:290
  4.7 33.8 %copy-start.3 = (bf16[4,128,2048]{2,1,0:T(8,128)(2,1)S(1)}, bf16[4,128,2048]{2,1,0:T(8,128)(2,1)}, u32[]{:S(2)}) copy-start(bf16[4,128,2048]{2,1,0:T(8,128)(2,1)} %refs_0_.6) | copy-start | bytes 6291460
  4.7 6.6 %collective-permute-start.2 = (bf16[4,2,32,256]{3,2,1,0:T(8,128)(2,1)S(1)}, bf16[4,2,32,256]{3,2,1,0:T(8,128)(2,1)S(1)}, u32[]{:S(2)}, u32[]{:S(2)}) collective-permute-start(bf16[4,2,32,256]{3,2,1,0:T(8,128)(2,1)S(1)} %get-tuple-element.30), channel_id=1, source_target_pairs={{0,3},{1,2},{2,1},{3,0},{4,7},{5,6},{6,5},{7,4},{8,11},{9,10},{10,... | collective-permute-start | bytes 393224 | tf_op jit(solution)/shard_map/ppermute | solution.py:298
  6.8 7.2 %collective-permute-start.1 = (bf16[4,2,32,256]{3,2,1,0:T(8,128)(2,1)S(1)}, bf16[4,2,32,256]{3,2,1,0:T(8,128)(2,1)S(1)}, u32[]{:S(2)}, u32[]{:S(2)}) collective-permute-start(bf16[4,2,32,256]{3,2,1,0:T(8,128)(2,1)S(1)} %get-tuple-element.31), channel_id=1, source_target_pairs={{0,2},{1,3},{2,0},{3,1},{4,6},{5,7},{6,4},{7,5},{8,10},{9,11},{10,... | collective-permute-start | bytes 393224 | tf_op jit(solution)/shard_map/ppermute | solution.py:298
  7.0 6.9 %collective-permute-start = (bf16[4,2,32,256]{3,2,1,0:T(8,128)(2,1)S(1)}, bf16[4,2,32,256]{3,2,1,0:T(8,128)(2,1)S(1)}, u32[]{:S(2)}, u32[]{:S(2)}) collective-permute-start(bf16[4,2,32,256]{3,2,1,0:T(8,128)(2,1)S(1)} %get-tuple-element.32), channel_id=1, source_target_pairs={{0,1},{1,0},{2,3},{3,2},{4,5},{5,4},{6,7},{7,6},{8,9},{9,8},{10,11... | collective-permute-start | bytes 393224 | tf_op jit(solution)/shard_map/ppermute | solution.py:298
  14.0 14.4 %collective-permute-start.9 = (bf16[4,8,32,256]{3,2,1,0:T(8,128)(2,1)}, bf16[4,8,32,256]{3,2,1,0:T(8,128)(2,1)S(1)}, u32[]{:S(2)}, u32[]{:S(2)}) collective-permute-start(bf16[4,8,32,256]{3,2,1,0:T(8,128)(2,1)} %collective-permute-done.3.refs_1_), channel_id=1, source_target_pairs={{4,8},{8,4},{5,9},{9,5},{6,10},{10,6},{7,11},{11,7},{20,24},{24,20... | collective-permute-start | bytes 1572872 | tf_op jit(solution)/shard_map/ppermute | solution.py:290
  14.7 18.2 %collective-permute-start.8 = (bf16[4,8,32,256]{3,2,1,0:T(8,128)(2,1)}, bf16[4,8,32,256]{3,2,1,0:T(8,128)(2,1)}, u32[]{:S(2)}, u32[]{:S(2)}) collective-permute-start(bf16[4,8,32,256]{3,2,1,0:T(8,128)(2,1)} %collective-permute-done.4.refs_2_), channel_id=1, source_target_pairs={{4,0},{8,12},{5,1},{9,13},{6,2},{10,14},{7,3},{11,15},{20,16},{24,... | collective-permute-start | bytes 1572872 | tf_op jit(solution)/shard_map/ppermute | solution.py:290
  17.8 7.0 %collective-permute-start.7 = (bf16[4,2,32,256]{3,2,1,0:T(8,128)(2,1)}, bf16[4,2,32,256]{3,2,1,0:T(8,128)(2,1)S(1)}, u32[]{:S(2)}, u32[]{:S(2)}) collective-permute-start(bf16[4,2,32,256]{3,2,1,0:T(8,128)(2,1)} %get-tuple-element.26), channel_id=1, source_target_pairs={{0,3},{1,2},{2,1},{3,0},{4,7},{5,6},{6,5},{7,4},{8,11},{9,10},{10,... | collective-permute-start | bytes 393224 | tf_op jit(solution)/shard_map/ppermute | solution.py:298
  20.3 7.4 %collective-permute-start.6 = (bf16[4,2,32,256]{3,2,1,0:T(8,128)(2,1)}, bf16[4,2,32,256]{3,2,1,0:T(8,128)(2,1)S(1)}, u32[]{:S(2)}, u32[]{:S(2)}) collective-permute-start(bf16[4,2,32,256]{3,2,1,0:T(8,128)(2,1)} %get-tuple-element.27), channel_id=1, source_target_pairs={{0,2},{1,3},{2,0},{3,1},{4,6},{5,7},{6,4},{7,5},{8,10},{9,11},{10,... | collective-permute-start | bytes 393224 | tf_op jit(solution)/shard_map/ppermute | solution.py:298
  20.6 7.8 %collective-permute-start.5 = (bf16[4,2,32,256]{3,2,1,0:T(8,128)(2,1)}, bf16[4,2,32,256]{3,2,1,0:T(8,128)(2,1)}, u32[]{:S(2)}, u32[]{:S(2)}) collective-permute-start(bf16[4,2,32,256]{3,2,1,0:T(8,128)(2,1)} %get-tuple-element.28), channel_id=1, source_target_pairs={{0,1},{1,0},{2,3},{3,2},{4,5},{5,4},{6,7},{7,6},{8,9},{9,8},{10,11... | collective-permute-start | bytes 393224 | tf_op jit(solution)/shard_map/ppermute | solution.py:298
  22.7 23.0 %copy-start.1 = (s32[38]{0:T(128)}, s32[38]{0:T(128)S(1)}, u32[]{:S(2)}) copy-start(s32[38]{0:T(128)S(1)} %concatenate.12.numbers_ref) | copy-start | bytes 460
  28.4 10.1 %copy-start.5 = (bf16[4,2,32,256]{3,2,1,0:T(8,128)(2,1)S(1)}, bf16[4,2,32,256]{3,2,1,0:T(8,128)(2,1)}, u32[]{:S(2)}) copy-start(bf16[4,2,32,256]{3,2,1,0:T(8,128)(2,1)} %copy-done.4) | copy-start | bytes 393220
  28.4 21.3 %copy-start = (bf16[4,8,32,256]{3,2,1,0:T(8,128)(2,1)}, bf16[4,8,32,256]{3,2,1,0:T(8,128)(2,1)S(1)}, u32[]{:S(2)}) copy-start(bf16[4,8,32,256]{3,2,1,0:T(8,128)(2,1)S(1)} %collective-permute-done.9.refs_10_.refs_3_) | copy-start | bytes 1572868
  28.4 21.3 %collective-permute-start.13 = (bf16[4,8,32,256]{3,2,1,0:T(8,128)(2,1)S(1)}, bf16[4,8,32,256]{3,2,1,0:T(8,128)(2,1)S(1)}, u32[]{:S(2)}, u32[]{:S(2)}) collective-permute-start(bf16[4,8,32,256]{3,2,1,0:T(8,128)(2,1)S(1)} %collective-permute-done.9.refs_10_.refs_3_), channel_id=1, source_target_pairs={{4,0},{8,12},{5,1},{9,13},{6,2},{10,14},{7,3},{11,15},{20,16},{24,... | collective-permute-start | bytes 1572872 | tf_op jit(solution)/shard_map/ppermute | solution.py:290
  34.0 15.7 %collective-permute-start.12 = (bf16[4,2,32,256]{3,2,1,0:T(8,128)(2,1)S(1)}, bf16[4,2,32,256]{3,2,1,0:T(8,128)(2,1)S(1)}, u32[]{:S(2)}, u32[]{:S(2)}) collective-permute-start(bf16[4,2,32,256]{3,2,1,0:T(8,128)(2,1)S(1)} %get-tuple-element.22), channel_id=1, source_target_pairs={{0,3},{1,2},{2,1},{3,0},{4,7},{5,6},{6,5},{7,4},{8,11},{9,10},{10,... | collective-permute-start | bytes 393224 | tf_op jit(solution)/shard_map/ppermute | solution.py:298
  38.0 11.8 %collective-permute-start.11 = (bf16[4,2,32,256]{3,2,1,0:T(8,128)(2,1)S(1)}, bf16[4,2,32,256]{3,2,1,0:T(8,128)(2,1)S(1)}, u32[]{:S(2)}, u32[]{:S(2)}) collective-permute-start(bf16[4,2,32,256]{3,2,1,0:T(8,128)(2,1)S(1)} %get-tuple-element.23), channel_id=1, source_target_pairs={{0,2},{1,3},{2,0},{3,1},{4,6},{5,7},{6,4},{7,5},{8,10},{9,11},{10,... | collective-permute-start | bytes 393224 | tf_op jit(solution)/shard_map/ppermute | solution.py:298
  38.2 11.5 %collective-permute-start.10 = (bf16[4,2,32,256]{3,2,1,0:T(8,128)(2,1)S(1)}, bf16[4,2,32,256]{3,2,1,0:T(8,128)(2,1)S(1)}, u32[]{:S(2)}, u32[]{:S(2)}) collective-permute-start(bf16[4,2,32,256]{3,2,1,0:T(8,128)(2,1)S(1)} %get-tuple-element.24), channel_id=1, source_target_pairs={{0,1},{1,0},{2,3},{3,2},{4,5},{5,4},{6,7},{7,6},{8,9},{9,8},{10,11... | collective-permute-start | bytes 393224 | tf_op jit(solution)/shard_map/ppermute | solution.py:298
  50.7 12.7 %collective-permute-start.16 = (bf16[4,2,32,256]{3,2,1,0:T(8,128)(2,1)}, bf16[4,2,32,256]{3,2,1,0:T(8,128)(2,1)S(1)}, u32[]{:S(2)}, u32[]{:S(2)}) collective-permute-start(bf16[4,2,32,256]{3,2,1,0:T(8,128)(2,1)} %get-tuple-element.18), channel_id=1, source_target_pairs={{0,3},{1,2},{2,1},{3,0},{4,7},{5,6},{6,5},{7,4},{8,11},{9,10},{10,... | collective-permute-start | bytes 393224 | tf_op jit(solution)/shard_map/ppermute | solution.py:298
  51.6 11.9 %collective-permute-start.15 = (bf16[4,2,32,256]{3,2,1,0:T(8,128)(2,1)}, bf16[4,2,32,256]{3,2,1,0:T(8,128)(2,1)S(1)}, u32[]{:S(2)}, u32[]{:S(2)}) collective-permute-start(bf16[4,2,32,256]{3,2,1,0:T(8,128)(2,1)} %get-tuple-element.19), channel_id=1, source_target_pairs={{0,2},{1,3},{2,0},{3,1},{4,6},{5,7},{6,4},{7,5},{8,10},{9,11},{10,... | collective-permute-start | bytes 393224 | tf_op jit(solution)/shard_map/ppermute | solution.py:298
  53.1 10.3 %collective-permute-start.14 = (bf16[4,2,32,256]{3,2,1,0:T(8,128)(2,1)}, bf16[4,2,32,256]{3,2,1,0:T(8,128)(2,1)S(1)}, u32[]{:S(2)}, u32[]{:S(2)}) collective-permute-start(bf16[4,2,32,256]{3,2,1,0:T(8,128)(2,1)} %get-tuple-element.20), channel_id=1, source_target_pairs={{0,1},{1,0},{2,3},{3,2},{4,5},{5,4},{6,7},{7,6},{8,9},{9,8},{10,11... | collective-permute-start | bytes 393224 | tf_op jit(solution)/shard_map/ppermute | solution.py:298
  (13 other events, 38.8 us)

commit v12 on v11

--- a/solution.py
+++ b/solution.py
@@ -12,7 +12,7 @@
 KVH = 8
 LOG2E = 1.4426950408889634
 STEP = 4
-VMEM_BYTES = 24 << 20
+VMEM_BYTES = 18 << 20
 
 
 class Part:
@@ -156,31 +156,62 @@
     def rows_of(h):
         return slice(h * span_len, (h + 1) * span_len)
 
+    single = most <= STEP
+    live = lax.broadcasted_iota(jnp.int32, (span_len, head_dim), 0) < live_rows
+
+    def put_out(head, total):
+        inverse = pl.reciprocal(total[:, head_dim:], approx=True)
+        inverse = inverse * (2.0 - total[:, head_dim:] * inverse)
+        mixed = (total[:, :head_dim] * inverse).astype(jnp.bfloat16)
+        if last_call:
+            mixed = jnp.where(live, mixed, jnp.zeros_like(mixed))
+        out_ref[0, :, lanes_of(head)] = mixed
+
+    def put_totals(tops, totals):
+        if last_call:
+            return
+        top, total = tops[0], totals[0]
+        for head in range(1, kv_local * per_head):
+            top = jnp.where(lane_ids == head, tops[head], top)
+            total = jnp.where(lane_ids == head, totals[head], total)
+        next_total_ref[0] = top + jnp.log(total) * LOG2E
+
     def attend(pages, since):
         wide = len(pages) * span_len
+
+        def cols_of(n):
+            return slice(n * span_len, (n + 1) * span_len)
+
         for g in range(kv_local):
-            keys = jnp.concatenate([kv_ref[page, g, :, :head_dim] for page in pages], axis=0)
             q = jnp.concatenate(
                 [q_ref[0, :, lanes_of(g * per_head + h)] for h in range(per_head)], axis=0
             )
-            s_ref[g, :, :wide] = lax.dot_general(
-                q, keys, (((1,), (1,)), ((), ())), preferred_element_type=jnp.float32
-            )
+            for n in range(0, len(pages), 2):
+                some = pages[n:n + 2]
+                keys = jnp.concatenate([kv_ref[p, g, :, :head_dim] for p in some], axis=0)
+                s = lax.dot_general(
+                    q, keys, (((1,), (1,)), ((), ())), preferred_element_type=jnp.float32
+                )
+                for m in range(len(some)):
+                    if since == "start" and n + m == len(pages) - 1:
+                        for h in range(per_head):
+                            s_ref[g, rows_of(h), cols_of(n + m)] = jnp.where(
+                                causal, s[rows_of(h), cols_of(m)], -1e30
+                            )
+                    else:
+                        s_ref[g, :, cols_of(n + m)] = s[:, cols_of(m)]
+        tops, totals = [], []
         for g in range(kv_local):
             rescales = []
             for h in range(per_head):
                 head = g * per_head + h
-                s = s_ref[g, rows_of(h), :wide] * scale
-                if since == "start":
-                    own_part = jnp.where(causal, s[:, wide - span_len:], -1e30)
-                    if len(pages) > 1:
-                        s = jnp.concatenate([s[:, :wide - span_len], own_part], axis=1)
-                    else:
-                        s = own_part
-                top = jnp.max(s, axis=1, keepdims=True)
-                if since == "start":
-                    top = jnp.broadcast_to(top, (span_len, head_dim))
-                else:
+                top = s_ref[g, rows_of(h), cols_of(0)]
+                for n in range(1, len(pages)):
+                    top = jnp.maximum(top, s_ref[g, rows_of(h), cols_of(n)])
+                top = jnp.broadcast_to(
+                    jnp.max(top, axis=1, keepdims=True) * scale, (span_len, head_dim)
+                )
+                if since != "start":
                     if since == "given":
                         old = jnp.broadcast_to(
                             total_ref[0, :, head:head + 1], (span_len, head_dim)
@@ -189,10 +220,14 @@
                         old = max_ref[head]
                     top = jnp.maximum(old, top)
                     rescales.append(jnp.exp2(old - top))
-                max_ref[head] = top
-                p_ref[g, rows_of(h), :wide] = jnp.exp2(
-                    s - jnp.concatenate([top] * len(pages), axis=1)
-                ).astype(jnp.bfloat16)
+                if single:
+                    tops.append(top)
+                else:
+                    max_ref[head] = top
+                for n in range(len(pages)):
+                    p_ref[g, rows_of(h), cols_of(n)] = jnp.exp2(
+                        s_ref[g, rows_of(h), cols_of(n)] * scale - top
+                    ).astype(jnp.bfloat16)
             values = jnp.concatenate(
                 [
                     jnp.concatenate([kv_ref[page, g, :, head_dim:], ones], axis=1)
@@ -209,10 +244,16 @@
                     new = new + jnp.concatenate([given * rescales[h], rescales[h]], axis=1)
                 elif since == "here":
                     new = new + acc_ref[head] * jnp.concatenate([rescales[h]] * 2, axis=1)
-                acc_ref[head] = new
+                if single:
+                    put_out(head, new)
+                    totals.append(new[:, head_dim:])
+                else:
+                    acc_ref[head] = new
+        if single:
+            put_totals(tops, totals)
 
     def rest(begin):
-        if most <= STEP:
+        if single:
             return
 
         def block(j, unused):
@@ -222,23 +263,13 @@
 
         lax.fori_loop(0, (count - begin) // STEP, block, 0)
 
-    live = lax.broadcasted_iota(jnp.int32, (span_len, head_dim), 0) < live_rows
-
     def finish():
-        tops = jnp.zeros((span_len, head_dim), jnp.float32)
-        totals = jnp.ones((span_len, head_dim), jnp.float32)
-        for head in range(kv_local * per_head):
-            total = acc_ref[head, :, head_dim:]
-            inverse = pl.reciprocal(total, approx=True)
-            mixed = acc_ref[head, :, :head_dim] * (inverse * (2.0 - total * inverse))
-            if last_call:
-                mixed = jnp.where(live, mixed, 0.0)
-            else:
-                tops = jnp.where(lane_ids == head, max_ref[head], tops)
-                totals = jnp.where(lane_ids == head, total, totals)
-            out_ref[0, :, lanes_of(head)] = mixed.astype(jnp.bfloat16)
-        if not last_call:
-            next_total_ref[0] = tops + jnp.log(totals) * LOG2E
+        if single:
+            return
+        heads = range(kv_local * per_head)
+        for head in heads:
+            put_out(head, acc_ref[head])
+        put_totals([max_ref[head] for head in heads], [acc_ref[head, :, head_dim:] for head in heads])
 
     if first_call:
         over = lax.rem(count, STEP)
@@ -318,15 +349,17 @@
     outer_on, inner_on = after([outer, inner], waiting)
     crossed = along(outer_on, [(1, 2), (2, 1)])
     inner_ends = along(inner_on, [(1, 0), (2, 3)])
+    own_parts = parts[:]
     waiting = exchange(1, outer_on)
+    first_parts = parts[len(own_parts):]
+    state = attend([0], own_parts, sources, later=waiting[:1])
     crossed_ends = along(after([crossed], waiting)[0], [(1, 0), (2, 3)])
-    first_parts = parts[:]
     second = exchange(6, jnp.where(middle, inner, inner_ends))
-    second_parts = parts[len(first_parts):]
-    state = attend([0, 1], first_parts, sources, later=[second[0], crossed])
+    second_parts = parts[2 * tp_size:]
+    state = attend([1], first_parts, sources, state=state, later=[second[0], crossed])
     third = exchange(7, after([jnp.where(middle, crossed, crossed_ends)], second)[0])
-    third_parts = parts[len(first_parts) + len(second_parts):]
-    state = attend([6], second_parts, sources, state=state, later=third[:1])
+    third_parts = parts[3 * tp_size:]
+    state = attend([6], second_parts, sources, state=state)
     hops += enumerate((outer, inner, crossed, inner_ends, crossed_ends), 1)
     return state, ([7], third_parts, sources), hops
 
@@ -380,14 +413,16 @@
             longest=longest,
             prompt_count=prompt_spans.shape[0],
         )
+        single = min(longest, len(covers) * slot_count) <= STEP
+        kept = (1, 8) if single else (local_heads, span_len)
         scratch = [
             pltpu.SMEM((span_total,), jnp.int32),
             pltpu.SMEM((span_total,), jnp.int32),
             pltpu.VMEM((span_total, kv_local, span_len, width), jnp.bfloat16),
             pltpu.VMEM((kv_local, rows, STEP * span_len), jnp.float32),
             pltpu.VMEM((kv_local, rows, STEP * span_len), jnp.bfloat16),
-            pltpu.VMEM((local_heads, span_len, 2 * head_dim), jnp.float32),
-            pltpu.VMEM((local_heads, span_len, head_dim), jnp.float32),
+            pltpu.VMEM(kept + (2 * head_dim,), jnp.float32),
+            pltpu.VMEM(kept + (head_dim,), jnp.float32),
             pltpu.SemaphoreType.DMA((len(parts),)),
         ]
         out_specs = [by_slot] if last_call else state_specs

time: 70.1 us -> 70.8 us (level)
  the two profiles are of different devices: /device:TPU:5 before, /device:TPU:0 now
where the time goes in v12:
time: 70.8 us; the launch traced here: 71.5 us
  Pallas kernels  24 us (34%)
  waiting for transfers between devices  21.3 us (30%)
  starting transfers between devices  15.7 us (22%)
  local copies, waits for them, and re-layouts  8.3 us (12%)
  other arithmetic  1.17 us (2%)
  between operations  1.05 us (1%)
    pallas_call x4, Pallas kernels, attend(): pl.pallas_call(kernel, grid_spec=pltpu.PrefetchScalarGridSpec(num_scalar_...  21 us
    ppermute x5, waiting for transfers between devices, along(): return lax.ppermute(x, 'inst', pairs)  13.1 us
    ppermute x12, waiting for transfers between devices, exchange(): sent = lax.ppermute(sent, 'tp', [(t, t ^ j) for t in range(tp_size)])  8.16 us
    ppermute x5, starting transfers between devices, along(): return lax.ppermute(x, 'inst', pairs)  8.01 us
    ppermute x12, starting transfers between devices, exchange(): sent = lax.ppermute(sent, 'tp', [(t, t ^ j) for t in range(tp_size)])  7.65 us
    unnamed x16, local copies, waits for them, and re-layouts  3.73 us
    dynamic_slice x4, local copies, waits for them, and re-layouts, exchange(): sent = lax.dynamic_slice_in_dim(x, head, kv_local, 1)  3.1 us
    pallas_call x1, Pallas kernels, body(): pl.pallas_call(functools.partial(place_kernel, hops=[name for name, _ in...  3.01 us
  transfers between devices with their start and end apart: 17, of which 6 were waited for; matrix products, arithmetic and copies ran while one was open for 7% of the time, Pallas kernels for 24%

profile of v12, /device:TPU:0, one launch (start us, length us, event | category | flops | bytes accessed | tf_op | source)
XLA Modules:
  0.0 71.5 jit_solution(10817346159710670150)
XLA Ops:
  0.6 3.1 %collective-permute-start.3 = (bf16[4,8,32,256]{3,2,1,0:T(8,128)(2,1)}, bf16[4,8,32,256]{3,2,1,0:T(8,128)(2,1)S(1)}, u32[]{:S(2)}, u32[]{:S(2)}) collective-permute-start(bf16[4,8,32,256]{3,2,1,0:T(8,128)(2,1)} %refs_0_.9), channel_id=1, source_target_pairs={{0,4},{4,0},{8,12},{12,8},{1,5},{5,1},{9,13},{13,9},{2,6},{6,2},{1... | collective-permute-start | bytes 1572872 | tf_op jit(solution)/shard_map/ppermute | solution.py:321
  3.7 1.5 %collective-permute-start.4 = (bf16[4,8,32,256]{3,2,1,0:T(8,128)(2,1)}, bf16[4,8,32,256]{3,2,1,0:T(8,128)(2,1)}, u32[]{:S(2)}, u32[]{:S(2)}) collective-permute-start(bf16[4,8,32,256]{3,2,1,0:T(8,128)(2,1)} %refs_0_.9), channel_id=1, source_target_pairs={{4,8},{8,4},{5,9},{9,5},{6,10},{10,6},{7,11},{11,7},{20,24},{24,20... | collective-permute-start | bytes 1572872 | tf_op jit(solution)/shard_map/ppermute | solution.py:321
  5.2 1.1 %constant_dynamic-slice_fusion.9 = (bf16[4,2,32,256]{3,2,1,0:T(8,128)(2,1)S(1)}, bf16[4,2,32,256]{3,2,1,0:T(8,128)(2,1)S(1)}, bf16[4,2,32,256]{3,2,1,0:T(8,128)(2,1)S(1)}, bf16[4,2,32,256]{3,2,1,0:T(8,128)(2,1)S(1)}) fusion(bf16[4,8,32,256]{3,2,1,0:T(8,128)(2,1)} %refs_0_.9, s32[]{:T(128)S(6)} %select_n.78, s32[]{:T(128)S(6)} %select_n.76, s32[]{:T(128)S(6)} %select_n.74, ...), kind=kLoop, calls=%fused_computation.11 | loop fusion | bytes 1048592 | tf_op jit(solution)/shard_map/dynamic_slice | solution.py:327
  7.1 0.9 %collective-permute-start.1 = (bf16[4,2,32,256]{3,2,1,0:T(8,128)(2,1)S(1)}, bf16[4,2,32,256]{3,2,1,0:T(8,128)(2,1)S(1)}, u32[]{:S(2)}, u32[]{:S(2)}) collective-permute-start(bf16[4,2,32,256]{3,2,1,0:T(8,128)(2,1)S(1)} %get-tuple-element.35), channel_id=1, source_target_pairs={{0,2},{1,3},{2,0},{3,1},{4,6},{5,7},{6,4},{7,5},{8,10},{9,11},{10,... | collective-permute-start | bytes 393224 | tf_op jit(solution)/shard_map/ppermute | solution.py:329
  8.3 3.9 %collective-permute-done.2.refs_4_ = bf16[4,2,32,256]{3,2,1,0:T(8,128)(2,1)S(1)} collective-permute-done((bf16[4,2,32,256]{3,2,1,0:T(8,128)(2,1)S(1)}, bf16[4,2,32,256]{3,2,1,0:T(8,128)(2,1)S(1)}, u32[]{:S(2)}, u32[]{:S(2)}) %collective-permute-start.2) | collective-permute-done | bytes 131104 | tf_op jit(solution)/shard_map/ppermute | solution.py:329
  12.2 2.9 %collective-permute-done.1.refs_3_ = bf16[4,2,32,256]{3,2,1,0:T(8,128)(2,1)S(1)} collective-permute-done((bf16[4,2,32,256]{3,2,1,0:T(8,128)(2,1)S(1)}, bf16[4,2,32,256]{3,2,1,0:T(8,128)(2,1)S(1)}, u32[]{:S(2)}, u32[]{:S(2)}) %collective-permute-start.1) | collective-permute-done | bytes 131104 | tf_op jit(solution)/shard_map/ppermute | solution.py:329
  15.0 0.8 %collective-permute-done.3.refs_1_ = bf16[4,8,32,256]{3,2,1,0:T(8,128)(2,1)S(1)} collective-permute-done((bf16[4,8,32,256]{3,2,1,0:T(8,128)(2,1)}, bf16[4,8,32,256]{3,2,1,0:T(8,128)(2,1)S(1)}, u32[]{:S(2)}, u32[]{:S(2)}) %collective-permute-start.3) | collective-permute-done | bytes 524320 | tf_op jit(solution)/shard_map/ppermute | solution.py:321
  17.4 1.3 %collective-permute-start.8 = (bf16[4,8,32,256]{3,2,1,0:T(8,128)(2,1)}, bf16[4,8,32,256]{3,2,1,0:T(8,128)(2,1)}, u32[]{:S(2)}, u32[]{:S(2)}) collective-permute-start(bf16[4,8,32,256]{3,2,1,0:T(8,128)(2,1)} %collective-permute-done.4.refs_2_), channel_id=1, source_target_pairs={{4,0},{8,12},{5,1},{9,13},{6,2},{10,14},{7,3},{11,15},{20,16},{24,... | collective-permute-start | bytes 1572872 | tf_op jit(solution)/shard_map/ppermute | solution.py:321
  20.2 1.1 %constant_dynamic-slice_fusion.5 = (bf16[4,2,32,256]{3,2,1,0:T(8,128)(2,1)S(1)}, bf16[4,2,32,256]{3,2,1,0:T(8,128)(2,1)S(1)}, bf16[4,2,32,256]{3,2,1,0:T(8,128)(2,1)S(1)}, bf16[4,2,32,256]{3,2,1,0:T(8,128)(2,1)S(1)}) fusion(bf16[4,8,32,256]{3,2,1,0:T(8,128)(2,1)} %copy-done.6, s32[]{:T(128)S(6)} %select_n.78, s32[]{:T(128)S(6)} %select_n.76, ...), kind=kLoop, calls=%fused_computation.7 | loop fusion | bytes 1048592 | tf_op jit(solution)/shard_map/dynamic_slice | solution.py:327
  21.6 1.5 %collective-permute-start.6 = (bf16[4,2,32,256]{3,2,1,0:T(8,128)(2,1)S(1)}, bf16[4,2,32,256]{3,2,1,0:T(8,128)(2,1)S(1)}, u32[]{:S(2)}, u32[]{:S(2)}) collective-permute-start(bf16[4,2,32,256]{3,2,1,0:T(8,128)(2,1)S(1)} %get-tuple-element.31), channel_id=1, source_target_pairs={{0,2},{1,3},{2,0},{3,1},{4,6},{5,7},{6,4},{7,5},{8,10},{9,11},{10,... | collective-permute-start | bytes 393224 | tf_op jit(solution)/shard_map/ppermute | solution.py:329
  23.2 5.3 %shard_map.122 = (bf16[4,128,2048]{2,1,0:T(8,128)(2,1)S(1)}, f32[4,128,128]{2,1,0:T(8,128)S(1)}) custom-call(s32[38]{0:T(128)S(1)} %concatenate.15.numbers_ref, bf16[4,128,2048]{2,1,0:T(8,128)(2,1)S(1)} %copy-done.3, bf16[4,2,32,256]{3,2,1,0:T(8,128)(2,1)S(1)} %get-tuple-element.37.refs_1_, bf16[4,2,32,256]{3,2,1,0:T(8,128)(2,1)S(1)} %collective-permute-done.refs_2_, ...), custom_call_target="tpu_custom_call" | custom-call | flops 2147483648 | bytes 8388608 | tf_op jit(solution)/shard_map/pallas_call | solution.py:433
  28.6 1.4 %collective-permute-done.6.refs_5_ = bf16[4,2,32,256]{3,2,1,0:T(8,128)(2,1)S(1)} collective-permute-done((bf16[4,2,32,256]{3,2,1,0:T(8,128)(2,1)S(1)}, bf16[4,2,32,256]{3,2,1,0:T(8,128)(2,1)S(1)}, u32[]{:S(2)}, u32[]{:S(2)}) %collective-permute-start.6) | collective-permute-done | bytes 131104 | tf_op jit(solution)/shard_map/ppermute | solution.py:329
  30.0 1.5 %collective-permute-start.13 = (bf16[4,8,32,256]{3,2,1,0:T(8,128)(2,1)S(1)}, bf16[4,8,32,256]{3,2,1,0:T(8,128)(2,1)S(1)}, u32[]{:S(2)}, u32[]{:S(2)}) collective-permute-start(bf16[4,8,32,256]{3,2,1,0:T(8,128)(2,1)S(1)} %collective-permute-done.9.refs_8_.refs_3_), channel_id=1, source_target_pairs={{4,0},{8,12},{5,1},{9,13},{6,2},{10,14},{7,3},{11,15},{20,16},{24,... | collective-permute-start | bytes 1572872 | tf_op jit(solution)/shard_map/ppermute | solution.py:321
  31.5 5.0 %collective-permute-done.8.refs_4_ = bf16[4,8,32,256]{3,2,1,0:T(8,128)(2,1)} collective-permute-done((bf16[4,8,32,256]{3,2,1,0:T(8,128)(2,1)}, bf16[4,8,32,256]{3,2,1,0:T(8,128)(2,1)}, u32[]{:S(2)}, u32[]{:S(2)}) %collective-permute-start.8) | collective-permute-done | bytes 524320 | tf_op jit(solution)/shard_map/ppermute | solution.py:321
  36.4 1.1 %broadcast_select_fusion.1 = bf16[4,8,32,256]{3,2,1,0:T(8,128)(2,1)S(1)} fusion(bf16[4,8,32,256]{3,2,1,0:T(8,128)(2,1)} %collective-permute-done.4.refs_2_, bf16[4,8,32,256]{3,2,1,0:T(8,128)(2,1)} %collective-permute-done.8.refs_4_, pred[]{:T(512)S(6)} %or.3), kind=kLoop, calls=%fused_computation.1 | loop fusion | flops 262144 | bytes 1572865 | tf_op jit(solution)/shard_map/jit(_where)/select_n | solution.py:357
  37.7 1.6 %collective-permute-start.11 = (bf16[4,2,32,256]{3,2,1,0:T(8,128)(2,1)S(1)}, bf16[4,2,32,256]{3,2,1,0:T(8,128)(2,1)S(1)}, u32[]{:S(2)}, u32[]{:S(2)}) collective-permute-start(bf16[4,2,32,256]{3,2,1,0:T(8,128)(2,1)S(1)} %get-tuple-element.27), channel_id=1, source_target_pairs={{0,2},{1,3},{2,0},{3,1},{4,6},{5,7},{6,4},{7,5},{8,10},{9,11},{10,... | collective-permute-start | bytes 393224 | tf_op jit(solution)/shard_map/ppermute | solution.py:329
  39.5 4.4 %shard_map.123 = (bf16[4,128,2048]{2,1,0:T(8,128)(2,1)S(1)}, f32[4,128,128]{2,1,0:T(8,128)S(1)}) custom-call(s32[38]{0:T(128)S(1)} %concatenate.15.numbers_ref, bf16[4,128,2048]{2,1,0:T(8,128)(2,1)S(1)} %copy-done.3, bf16[4,128,2048]{2,1,0:T(8,128)(2,1)S(1)} %get-tuple-element.13.refs_1_, f32[4,128,128]{2,1,0:T(8,128)S(1)} %get-tuple-element.14.refs_2_, ...), custom_call_target="tpu_custom_call" | custom-call | flops 2147483648 | bytes 8388608 | tf_op jit(solution)/shard_map/pallas_call | solution.py:433
  43.9 7.3 %collective-permute-done.13.refs_5_ = bf16[4,8,32,256]{3,2,1,0:T(8,128)(2,1)S(1)} collective-permute-done((bf16[4,8,32,256]{3,2,1,0:T(8,128)(2,1)S(1)}, bf16[4,8,32,256]{3,2,1,0:T(8,128)(2,1)S(1)}, u32[]{:S(2)}, u32[]{:S(2)}) %collective-permute-start.13) | collective-permute-done | bytes 524320 | tf_op jit(solution)/shard_map/ppermute | solution.py:321
  52.1 1.2 %collective-permute-start.15 = (bf16[4,2,32,256]{3,2,1,0:T(8,128)(2,1)}, bf16[4,2,32,256]{3,2,1,0:T(8,128)(2,1)S(1)}, u32[]{:S(2)}, u32[]{:S(2)}) collective-permute-start(bf16[4,2,32,256]{3,2,1,0:T(8,128)(2,1)} %get-tuple-element.23), channel_id=1, source_target_pairs={{0,2},{1,3},{2,0},{3,1},{4,6},{5,7},{6,4},{7,5},{8,10},{9,11},{10,... | collective-permute-start | bytes 393224 | tf_op jit(solution)/shard_map/ppermute | solution.py:329
  54.0 4.7 %shard_map.124 = (bf16[4,128,2048]{2,1,0:T(8,128)(2,1)S(1)}, f32[4,128,128]{2,1,0:T(8,128)S(1)}) custom-call(s32[38]{0:T(128)S(1)} %concatenate.15.numbers_ref, bf16[4,128,2048]{2,1,0:T(8,128)(2,1)S(1)} %copy-done.3, bf16[4,128,2048]{2,1,0:T(8,128)(2,1)S(1)} %get-tuple-element.16.refs_1_, f32[4,128,128]{2,1,0:T(8,128)S(1)} %get-tuple-element.17.refs_2_, ...), custom_call_target="tpu_custom_call" | custom-call | flops 2147483648 | bytes 8388608 | tf_op jit(solution)/shard_map/pallas_call | solution.py:433
  58.7 1.3 %copy-done.4 = bf16[4,128,2048]{2,1,0:T(8,128)(2,1)} copy-done((bf16[4,128,2048]{2,1,0:T(8,128)(2,1)}, bf16[4,128,2048]{2,1,0:T(8,128)(2,1)S(1)}, u32[]{:S(2)}) %copy-start.4) | copy-done | bytes 2097176
  60.0 3.0 %shard_map.126 = bf16[8,8,32,256]{3,2,1,0:T(8,128)(2,1)} custom-call(s32[38]{0:T(128)} %copy-done.1, bf16[4,8,32,256]{3,2,1,0:T(8,128)(2,1)} %refs_0_.9, bf16[4,8,32,256]{3,2,1,0:T(8,128)(2,1)} %copy-done.6, bf16[4,8,32,256]{3,2,1,0:T(8,128)(2,1)} %collective-permute-done.4.refs_2_, bf16[4,8,32,256]{3,2,1,0:T(8,128)(2,1)} %copy-done, ...), custom_call_target="tpu_custom_call" | custom-call | bytes 8388608 | tf_op jit(solution)/shard_map/pallas_call | solution.py:454
  63.1 1.6 %copy-done.5 = bf16[4,128,2048]{2,1,0:T(8,128)(2,1)S(1)} copy-done((bf16[4,128,2048]{2,1,0:T(8,128)(2,1)S(1)}, bf16[4,128,2048]{2,1,0:T(8,128)(2,1)}, u32[]{:S(2)}) %copy-start.5) | copy-done | bytes 2097176
  64.7 6.6 %shard_map.125 = bf16[4,128,2048]{2,1,0:T(8,128)(2,1)} custom-call(s32[38]{0:T(128)S(1)} %copy-done.2, bf16[4,128,2048]{2,1,0:T(8,128)(2,1)S(1)} %copy-done.3, bf16[4,128,2048]{2,1,0:T(8,128)(2,1)S(1)} %copy-done.5, f32[4,128,128]{2,1,0:T(8,128)S(1)} %get-tuple-element.19.refs_2_, bf16[4,2,32,256]{3,2,1,0:T(8,128)(2,1)S(1)} %get-tuple-element.25.refs_3_, ...), custom_call_target="tpu_custom_call" | custom-call | flops 2147483648 | bytes 8388608 | tf_op jit(solution)/shard_map/pallas_call | solution.py:433
  (39 shorter events, 6.4 us)
Async XLA Ops:
  0.6 22.6 %copy-start.3 = (bf16[4,128,2048]{2,1,0:T(8,128)(2,1)S(1)}, bf16[4,128,2048]{2,1,0:T(8,128)(2,1)}, u32[]{:S(2)}) copy-start(bf16[4,128,2048]{2,1,0:T(8,128)(2,1)} %refs_0_.8) | copy-start | bytes 6291460
  0.6 15.2 %collective-permute-start.3 = (bf16[4,8,32,256]{3,2,1,0:T(8,128)(2,1)}, bf16[4,8,32,256]{3,2,1,0:T(8,128)(2,1)S(1)}, u32[]{:S(2)}, u32[]{:S(2)}) collective-permute-start(bf16[4,8,32,256]{3,2,1,0:T(8,128)(2,1)} %refs_0_.9), channel_id=1, source_target_pairs={{0,4},{4,0},{8,12},{12,8},{1,5},{5,1},{9,13},{13,9},{2,6},{6,2},{1... | collective-permute-start | bytes 1572872 | tf_op jit(solution)/shard_map/ppermute | solution.py:321
  3.7 12.1 %collective-permute-start.4 = (bf16[4,8,32,256]{3,2,1,0:T(8,128)(2,1)}, bf16[4,8,32,256]{3,2,1,0:T(8,128)(2,1)}, u32[]{:S(2)}, u32[]{:S(2)}) collective-permute-start(bf16[4,8,32,256]{3,2,1,0:T(8,128)(2,1)} %refs_0_.9), channel_id=1, source_target_pairs={{4,8},{8,4},{5,9},{9,5},{6,10},{10,6},{7,11},{11,7},{20,24},{24,20... | collective-permute-start | bytes 1572872 | tf_op jit(solution)/shard_map/ppermute | solution.py:321
  6.3 5.8 %collective-permute-start.2 = (bf16[4,2,32,256]{3,2,1,0:T(8,128)(2,1)S(1)}, bf16[4,2,32,256]{3,2,1,0:T(8,128)(2,1)S(1)}, u32[]{:S(2)}, u32[]{:S(2)}) collective-permute-start(bf16[4,2,32,256]{3,2,1,0:T(8,128)(2,1)S(1)} %get-tuple-element.34), channel_id=1, source_target_pairs={{0,3},{1,2},{2,1},{3,0},{4,7},{5,6},{6,5},{7,4},{8,11},{9,10},{10,... | collective-permute-start | bytes 393224 | tf_op jit(solution)/shard_map/ppermute | solution.py:329
  7.1 8.0 %collective-permute-start.1 = (bf16[4,2,32,256]{3,2,1,0:T(8,128)(2,1)S(1)}, bf16[4,2,32,256]{3,2,1,0:T(8,128)(2,1)S(1)}, u32[]{:S(2)}, u32[]{:S(2)}) collective-permute-start(bf16[4,2,32,256]{3,2,1,0:T(8,128)(2,1)S(1)} %get-tuple-element.35), channel_id=1, source_target_pairs={{0,2},{1,3},{2,0},{3,1},{4,6},{5,7},{6,4},{7,5},{8,10},{9,11},{10,... | collective-permute-start | bytes 393224 | tf_op jit(solution)/shard_map/ppermute | solution.py:329
  8.0 7.0 %collective-permute-start = (bf16[4,2,32,256]{3,2,1,0:T(8,128)(2,1)S(1)}, bf16[4,2,32,256]{3,2,1,0:T(8,128)(2,1)S(1)}, u32[]{:S(2)}, u32[]{:S(2)}) collective-permute-start(bf16[4,2,32,256]{3,2,1,0:T(8,128)(2,1)S(1)} %get-tuple-element.36), channel_id=1, source_target_pairs={{0,1},{1,0},{2,3},{3,2},{4,5},{5,4},{6,7},{7,6},{8,9},{9,8},{10,11... | collective-permute-start | bytes 393224 | tf_op jit(solution)/shard_map/ppermute | solution.py:329
  16.7 13.3 %collective-permute-start.9 = (bf16[4,8,32,256]{3,2,1,0:T(8,128)(2,1)}, bf16[4,8,32,256]{3,2,1,0:T(8,128)(2,1)S(1)}, u32[]{:S(2)}, u32[]{:S(2)}) collective-permute-start(bf16[4,8,32,256]{3,2,1,0:T(8,128)(2,1)} %copy-done.6), channel_id=1, source_target_pairs={{4,8},{8,4},{5,9},{9,5},{6,10},{10,6},{7,11},{11,7},{20,24},{24,20... | collective-permute-start | bytes 1572872 | tf_op jit(solution)/shard_map/ppermute | solution.py:321
  17.4 19.1 %collective-permute-start.8 = (bf16[4,8,32,256]{3,2,1,0:T(8,128)(2,1)}, bf16[4,8,32,256]{3,2,1,0:T(8,128)(2,1)}, u32[]{:S(2)}, u32[]{:S(2)}) collective-permute-start(bf16[4,8,32,256]{3,2,1,0:T(8,128)(2,1)} %collective-permute-done.4.refs_2_), channel_id=1, source_target_pairs={{4,0},{8,12},{5,1},{9,13},{6,2},{10,14},{7,3},{11,15},{20,16},{24,... | collective-permute-start | bytes 1572872 | tf_op jit(solution)/shard_map/ppermute | solution.py:321
  20.1 33.8 %copy-start.1 = (s32[38]{0:T(128)}, s32[38]{0:T(128)S(1)}, u32[]{:S(2)}) copy-start(s32[38]{0:T(128)S(1)} %concatenate.15.numbers_ref) | copy-start | bytes 460
  21.3 7.3 %collective-permute-start.7 = (bf16[4,2,32,256]{3,2,1,0:T(8,128)(2,1)S(1)}, bf16[4,2,32,256]{3,2,1,0:T(8,128)(2,1)S(1)}, u32[]{:S(2)}, u32[]{:S(2)}) collective-permute-start(bf16[4,2,32,256]{3,2,1,0:T(8,128)(2,1)S(1)} %get-tuple-element.30), channel_id=1, source_target_pairs={{0,3},{1,2},{2,1},{3,0},{4,7},{5,6},{6,5},{7,4},{8,11},{9,10},{10,... | collective-permute-start | bytes 393224 | tf_op jit(solution)/shard_map/ppermute | solution.py:329
  21.6 8.4 %collective-permute-start.6 = (bf16[4,2,32,256]{3,2,1,0:T(8,128)(2,1)S(1)}, bf16[4,2,32,256]{3,2,1,0:T(8,128)(2,1)S(1)}, u32[]{:S(2)}, u32[]{:S(2)}) collective-permute-start(bf16[4,2,32,256]{3,2,1,0:T(8,128)(2,1)S(1)} %get-tuple-element.31), channel_id=1, source_target_pairs={{0,2},{1,3},{2,0},{3,1},{4,6},{5,7},{6,4},{7,5},{8,10},{9,11},{10,... | collective-permute-start | bytes 393224 | tf_op jit(solution)/shard_map/ppermute | solution.py:329
  23.1 6.9 %collective-permute-start.5 = (bf16[4,2,32,256]{3,2,1,0:T(8,128)(2,1)S(1)}, bf16[4,2,32,256]{3,2,1,0:T(8,128)(2,1)S(1)}, u32[]{:S(2)}, u32[]{:S(2)}) collective-permute-start(bf16[4,2,32,256]{3,2,1,0:T(8,128)(2,1)S(1)} %get-tuple-element.32), channel_id=1, source_target_pairs={{0,1},{1,0},{2,3},{3,2},{4,5},{5,4},{6,7},{7,6},{8,9},{9,8},{10,11... | collective-permute-start | bytes 393224 | tf_op jit(solution)/shard_map/ppermute | solution.py:329
  30.0 21.2 %copy-start = (bf16[4,8,32,256]{3,2,1,0:T(8,128)(2,1)}, bf16[4,8,32,256]{3,2,1,0:T(8,128)(2,1)S(1)}, u32[]{:S(2)}) copy-start(bf16[4,8,32,256]{3,2,1,0:T(8,128)(2,1)S(1)} %collective-permute-done.9.refs_8_.refs_3_) | copy-start | bytes 1572868
  30.0 21.2 %collective-permute-start.13 = (bf16[4,8,32,256]{3,2,1,0:T(8,128)(2,1)S(1)}, bf16[4,8,32,256]{3,2,1,0:T(8,128)(2,1)S(1)}, u32[]{:S(2)}, u32[]{:S(2)}) collective-permute-start(bf16[4,8,32,256]{3,2,1,0:T(8,128)(2,1)S(1)} %collective-permute-done.9.refs_8_.refs_3_), channel_id=1, source_target_pairs={{4,0},{8,12},{5,1},{9,13},{6,2},{10,14},{7,3},{11,15},{20,16},{24,... | collective-permute-start | bytes 1572872 | tf_op jit(solution)/shard_map/ppermute | solution.py:321
  37.6 13.7 %collective-permute-start.12 = (bf16[4,2,32,256]{3,2,1,0:T(8,128)(2,1)S(1)}, bf16[4,2,32,256]{3,2,1,0:T(8,128)(2,1)S(1)}, u32[]{:S(2)}, u32[]{:S(2)}) collective-permute-start(bf16[4,2,32,256]{3,2,1,0:T(8,128)(2,1)S(1)} %get-tuple-element.26), channel_id=1, source_target_pairs={{0,3},{1,2},{2,1},{3,0},{4,7},{5,6},{6,5},{7,4},{8,11},{9,10},{10,... | collective-permute-start | bytes 393224 | tf_op jit(solution)/shard_map/ppermute | solution.py:329
  37.7 13.6 %collective-permute-start.11 = (bf16[4,2,32,256]{3,2,1,0:T(8,128)(2,1)S(1)}, bf16[4,2,32,256]{3,2,1,0:T(8,128)(2,1)S(1)}, u32[]{:S(2)}, u32[]{:S(2)}) collective-permute-start(bf16[4,2,32,256]{3,2,1,0:T(8,128)(2,1)S(1)} %get-tuple-element.27), channel_id=1, source_target_pairs={{0,2},{1,3},{2,0},{3,1},{4,6},{5,7},{6,4},{7,5},{8,10},{9,11},{10,... | collective-permute-start | bytes 393224 | tf_op jit(solution)/shard_map/ppermute | solution.py:329
  39.2 12.1 %collective-permute-start.10 = (bf16[4,2,32,256]{3,2,1,0:T(8,128)(2,1)S(1)}, bf16[4,2,32,256]{3,2,1,0:T(8,128)(2,1)S(1)}, u32[]{:S(2)}, u32[]{:S(2)}) collective-permute-start(bf16[4,2,32,256]{3,2,1,0:T(8,128)(2,1)S(1)} %get-tuple-element.28), channel_id=1, source_target_pairs={{0,1},{1,0},{2,3},{3,2},{4,5},{5,4},{6,7},{7,6},{8,9},{9,8},{10,11... | collective-permute-start | bytes 393224 | tf_op jit(solution)/shard_map/ppermute | solution.py:329
  51.2 7.5 %copy-start.7 = (bf16[4,8,32,256]{3,2,1,0:T(8,128)(2,1)}, bf16[4,8,32,256]{3,2,1,0:T(8,128)(2,1)S(1)}, u32[]{:S(2)}) copy-start(bf16[4,8,32,256]{3,2,1,0:T(8,128)(2,1)S(1)} %collective-permute-done.13.refs_5_) | copy-start | bytes 1572868
  52.1 10.9 %collective-permute-start.16 = (bf16[4,2,32,256]{3,2,1,0:T(8,128)(2,1)}, bf16[4,2,32,256]{3,2,1,0:T(8,128)(2,1)S(1)}, u32[]{:S(2)}, u32[]{:S(2)}) collective-permute-start(bf16[4,2,32,256]{3,2,1,0:T(8,128)(2,1)} %get-tuple-element.22), channel_id=1, source_target_pairs={{0,3},{1,2},{2,1},{3,0},{4,7},{5,6},{6,5},{7,4},{8,11},{9,10},{10,... | collective-permute-start | bytes 393224 | tf_op jit(solution)/shard_map/ppermute | solution.py:329
  52.1 11.0 %collective-permute-start.15 = (bf16[4,2,32,256]{3,2,1,0:T(8,128)(2,1)}, bf16[4,2,32,256]{3,2,1,0:T(8,128)(2,1)S(1)}, u32[]{:S(2)}, u32[]{:S(2)}) collective-permute-start(bf16[4,2,32,256]{3,2,1,0:T(8,128)(2,1)} %get-tuple-element.23), channel_id=1, source_target_pairs={{0,2},{1,3},{2,0},{3,1},{4,6},{5,7},{6,4},{7,5},{8,10},{9,11},{10,... | collective-permute-start | bytes 393224 | tf_op jit(solution)/shard_map/ppermute | solution.py:329
  53.3 9.8 %collective-permute-start.14 = (bf16[4,2,32,256]{3,2,1,0:T(8,128)(2,1)S(1)}, bf16[4,2,32,256]{3,2,1,0:T(8,128)(2,1)S(1)}, u32[]{:S(2)}, u32[]{:S(2)}) collective-permute-start(bf16[4,2,32,256]{3,2,1,0:T(8,128)(2,1)S(1)} %get-tuple-element.24), channel_id=1, source_target_pairs={{0,1},{1,0},{2,3},{3,2},{4,5},{5,4},{6,7},{7,6},{8,9},{9,8},{10,11... | collective-permute-start | bytes 393224 | tf_op jit(solution)/shard_map/ppermute | solution.py:329
  58.7 1.3 %copy-start.4 = (bf16[4,128,2048]{2,1,0:T(8,128)(2,1)}, bf16[4,128,2048]{2,1,0:T(8,128)(2,1)S(1)}, u32[]{:S(2)}) copy-start(bf16[4,128,2048]{2,1,0:T(8,128)(2,1)S(1)} %get-tuple-element.18.refs_1_) | copy-start | bytes 6291460
  60.0 3.1 %copy-start.2 = (s32[38]{0:T(128)S(1)}, s32[38]{0:T(128)}, u32[]{:S(2)}) copy-start(s32[38]{0:T(128)} %copy-done.1) | copy-start | bytes 460
  63.1 1.6 %copy-start.5 = (bf16[4,128,2048]{2,1,0:T(8,128)(2,1)S(1)}, bf16[4,128,2048]{2,1,0:T(8,128)(2,1)}, u32[]{:S(2)}) copy-start(bf16[4,128,2048]{2,1,0:T(8,128)(2,1)} %copy-done.4) | copy-start | bytes 6291460
  (1 other events, 0.8 us)

commit v13 on v12

--- a/solution.py
+++ b/solution.py
@@ -15,24 +15,21 @@
 VMEM_BYTES = 18 << 20
 
 
-class Part:
-    def __init__(self, ref, start):
-        self.ref, self.start = ref, start
-
-    def __getitem__(self, at):
-        return self.ref[self.start + at]
-
-
-def place_kernel(numbers_ref, *refs, hops, slot_count, span_total, longest, prompt_count):
+def source_of(sources, hop, inst):
+    found = jnp.int32(sources[hop][0])
+    for i in range(1, len(sources[hop])):
+        found = jnp.where(inst == i, sources[hop][i], found)
+    return found
+
+
+def place_kernel(
+    spans_ref, owner_ref, plan_ref, *refs, hops, sources, slot_count, span_total, longest,
+):
     hop_refs = refs[:len(hops)]
     cache_ref, place_ref, stage_ref, sems, out_sem = refs[len(hops):]
-    spans_ref = Part(numbers_ref, 0)
-    owner_ref = Part(numbers_ref, 2 * prompt_count)
-    plan_ref = Part(numbers_ref, 3 * prompt_count)
-    place_at_ref = Part(numbers_ref, 3 * prompt_count + span_total)
-    inst = place_at_ref[0]
+    inst = lax.axis_index("inst")
     first, count, start = jnp.int32(0), jnp.int32(0), jnp.int32(0)
-    for p in range(prompt_count):
+    for p in range(spans_ref.shape[0]):
         hit = owner_ref[p] == inst
         first = jnp.where(hit, start, first)
         count = jnp.where(hit, spans_ref[p], count)
@@ -48,7 +45,7 @@
         def row(r, unused):
             page = place_ref[jnp.minimum(first + r, span_total - 1)]
             for n, hop in enumerate(hops):
-                source = place_at_ref[2 + hop]
+                source = source_of(sources, hop, inst)
                 slot = page - source * slot_count
 
                 @pl.when((r < count) & (source >= 0) & (slot >= 0) & (slot < slot_count))
@@ -72,9 +69,9 @@
 
 
 def attend_kernel(
-    numbers_ref, *refs,
-    covers, parts, later, first_call, last_call,
-    inst_size, tp_size, kv_local, per_head, head_dim, span_len, slot_count, longest, prompt_count,
+    spans_ref, tail_ref, plan_ref, *refs,
+    covers, sources, parts, later, first_call, last_call,
+    inst_size, tp_size, kv_local, per_head, head_dim, span_len, slot_count, longest,
 ):
     refs = list(refs)
 
@@ -93,20 +90,16 @@
     place_ref, list_ref, kv_ref, s_ref, p_ref, acc_ref, max_ref, part_sems = take(8)
     step = pl.program_id(0)
     span_total = slot_count * inst_size
-    spans_ref = Part(numbers_ref, 0)
-    tail_ref = Part(numbers_ref, prompt_count)
-    owner_ref = Part(numbers_ref, 2 * prompt_count)
-    plan_ref = Part(numbers_ref, 3 * prompt_count)
-    place_at_ref = Part(numbers_ref, 3 * prompt_count + span_total)
-    inst = place_at_ref[0]
-    tp = place_at_ref[1]
+    prompt_count = spans_ref.shape[0]
+    inst = lax.axis_index("inst")
+    tp = lax.axis_index("tp")
     slice_len = span_len // tp_size
     most = min(longest, len(covers) * slot_count)
     scale = LOG2E / math.sqrt(head_dim)
 
     def part_copies(act):
         for n, (hop, j) in enumerate(parts):
-            slots = pl.ds(place_at_ref[2 + hop] * slot_count, slot_count)
+            slots = pl.ds(source_of(sources, hop, inst) * slot_count, slot_count)
             at = pl.ds(pl.multiple_of((tp ^ j) * slice_len, slice_len), slice_len)
             act(pltpu.make_async_copy(part_refs[n], kv_ref.at[slots, :, at], part_sems.at[n]))
 
@@ -139,7 +132,7 @@
         source = page // slot_count
         covered = jnp.bool_(False)
         for hop in covers:
-            covered = covered | (place_at_ref[2 + hop] == source)
+            covered = covered | (source_of(sources, hop, inst) == source)
         list_ref[count] = page
         return count + covered.astype(jnp.int32)
 
@@ -353,7 +346,7 @@
     waiting = exchange(1, outer_on)
     first_parts = parts[len(own_parts):]
     state = attend([0], own_parts, sources, later=waiting[:1])
-    crossed_ends = along(after([crossed], waiting)[0], [(1, 0), (2, 3)])
+    crossed_ends = along(crossed, [(1, 0), (2, 3)])
     second = exchange(6, jnp.where(middle, inner, inner_ends))
     second_parts = parts[2 * tp_size:]
     state = attend([1], first_parts, sources, state=state, later=[second[0], crossed])
@@ -367,8 +360,6 @@
 def body(queries, kv_new, prompt_spans, prompt_tail, span_plan, decode_owner):
     tp_size = lax.axis_size("tp")
     inst_size = lax.axis_size("inst")
-    tp_index = lax.axis_index("tp")
-    inst_index = lax.axis_index("inst")
     slot_count, span_len, row_width = queries.shape
     kv_heads, slice_len, width = kv_new.shape[1:]
     head_dim = width // 2
@@ -384,21 +375,12 @@
     state_specs = [by_slot, total_spec]
     work = slot_count * 4 * local_heads * span_len * span_len
 
-    def numbers_of(sources):
-        own_sources = lax.dynamic_index_in_dim(
-            jnp.asarray(sources, jnp.int32), inst_index, 1, False
-        )
-        return jnp.concatenate([
-            prompt_spans, prompt_tail, decode_owner, span_plan,
-            jnp.stack([inst_index, tp_index]).astype(jnp.int32), own_sources,
-        ])
-
     def attend(covers, parts, sources, state=(), later=(), last_call=False):
         first_call = not state
-        numbers = numbers_of(sources)
         kernel = functools.partial(
             attend_kernel,
             covers=covers,
+            sources=sources,
             parts=[name for name, _ in parts],
             later=len(later),
             first_call=first_call,
@@ -411,7 +393,6 @@
             span_len=span_len,
             slot_count=slot_count,
             longest=longest,
-            prompt_count=prompt_spans.shape[0],
         )
         single = min(longest, len(covers) * slot_count) <= STEP
         kept = (1, 8) if single else (local_heads, span_len)
@@ -433,7 +414,7 @@
         return pl.pallas_call(
             kernel,
             grid_spec=pltpu.PrefetchScalarGridSpec(
-                num_scalar_prefetch=1,
+                num_scalar_prefetch=3,
                 grid=(slot_count,),
                 in_specs=[by_slot] + (state_specs if state else [])
                 + [anywhere] * (len(parts) + len(later)),
@@ -446,7 +427,8 @@
             ),
             compiler_params=pltpu.CompilerParams(vmem_limit_bytes=VMEM_BYTES),
         )(
-            numbers, queries, *state, *[x for _, x in parts], *later,
+            prompt_spans, prompt_tail, span_plan, queries,
+            *state, *[x for _, x in parts], *later,
         )
 
     state, left, hops = move_pages(kv_new, kv_local, attend)
@@ -455,13 +437,13 @@
         functools.partial(
             place_kernel,
             hops=[name for name, _ in hops],
+            sources=left[2],
             slot_count=slot_count,
             span_total=span_total,
             longest=longest,
-            prompt_count=prompt_spans.shape[0],
         ),
         grid_spec=pltpu.PrefetchScalarGridSpec(
-            num_scalar_prefetch=1,
+            num_scalar_prefetch=3,
             grid=(1,),
             in_specs=[anywhere] * len(hops),
             out_specs=anywhere,
@@ -474,7 +456,8 @@
         ),
         out_shape=jax.ShapeDtypeStruct((longest,) + page_shape, jnp.bfloat16),
         cost_estimate=pl.CostEstimate(flops=0, bytes_accessed=8 << 20, transcendentals=0),
-    )(numbers_of(left[2]), *[x for _, x in hops])
+        compiler_params=pltpu.CompilerParams(vmem_limit_bytes=4 << 20),
+    )(prompt_spans, decode_owner, span_plan, *[x for _, x in hops])
     (attended,) = attend(*left, state, last_call=True)
     return attended, owner_cache
 

time: 70.8 us -> 64 us (0.904); the launches traced: 71.5 us -> 63.6 us
  local copies, waits for them, and re-layouts: 8.3 us -> 2.9 us
  other arithmetic: 1.17 us -> 0.11 us
  waiting for transfers between devices: 21.3 us -> 20.4 us
  starting transfers between devices: 15.7 us -> 14.9 us
    unnamed x16 -> x12, local copies, waits for them, and re-layouts: 3.73 us -> 1.61 us
    dynamic_slice x4, local copies, waits for them, and re-layouts: 3.1 us -> 1.29 us  [exchange(): sent = lax.dynamic_slice_in_dim(x, head, kv_local, 1)]
    ppermute x12, waiting for transfers between devices: 8.16 us -> 6.77 us  [exchange(): sent = lax.ppermute(sent, 'tp', [(t, t ^ j) for t in range(tp_size)])]
    select_n x1, other arithmetic: 1.1 us -> 0.06 us  [move_pages(): second = exchange(6, jnp.where(middle, inner, inner_ends))]
    ppermute x5, starting transfers between devices: 8.01 us -> 7.22 us  [along(): return lax.ppermute(x, 'inst', pairs)]
    concatenate x1 -> x0, local copies, waits for them, and re-layouts: 0.78 us -> none  [numbers_of(): jnp.concatenate([prompt_spans, prompt_tail, decode_owner, span_plan, jnp....]
  transfers between devices with their start and end apart: 17 -> 17, of which waited for: 6 -> 5; matrix products, arithmetic and copies ran while one was open for 7% -> 2% of each run, Pallas kernels for 24% -> 29%
where the time goes in v13:
time: 64 us; the launch traced here: 63.6 us
  Pallas kernels  24.1 us (38%)
  waiting for transfers between devices  20.4 us (32%)
  starting transfers between devices  14.9 us (23%)
  local copies, waits for them, and re-layouts  2.9 us (5%)
  between operations  1.18 us (2%)
    pallas_call x4, Pallas kernels, attend(): pl.pallas_call(kernel, grid_spec=pltpu.PrefetchScalarGridSpec(num_scalar_...  21.1 us
    ppermute x5, waiting for transfers between devices, along(): return lax.ppermute(x, 'inst', pairs)  13.6 us
    ppermute x12, starting transfers between devices, exchange(): sent = lax.ppermute(sent, 'tp', [(t, t ^ j) for t in range(tp_size)])  7.7 us
    ppermute x5, starting transfers between devices, along(): return lax.ppermute(x, 'inst', pairs)  7.22 us
    ppermute x12, waiting for transfers between devices, exchange(): sent = lax.ppermute(sent, 'tp', [(t, t ^ j) for t in range(tp_size)])  6.77 us
    pallas_call x1, Pallas kernels, body(): pl.pallas_call(functools.partial(place_kernel, hops=[name for name, _ in...  3.01 us
    unnamed x12, local copies, waits for them, and re-layouts  1.61 us
    dynamic_slice x4, local copies, waits for them, and re-layouts, exchange(): sent = lax.dynamic_slice_in_dim(x, head, kv_local, 1)  1.29 us
  transfers between devices with their start and end apart: 17, of which 5 were waited for; matrix products, arithmetic and copies ran while one was open for 2% of the time, Pallas kernels for 29%

profile of v13, /device:TPU:0, one launch (start us, length us, event | category | flops | bytes accessed | tf_op | source)
XLA Modules:
  0.0 63.6 jit_solution(10963863477822350987)
XLA Ops:
  0.7 3.1 %collective-permute-start.3 = (bf16[4,8,32,256]{3,2,1,0:T(8,128)(2,1)}, bf16[4,8,32,256]{3,2,1,0:T(8,128)(2,1)S(1)}, u32[]{:S(2)}, u32[]{:S(2)}) collective-permute-start(bf16[4,8,32,256]{3,2,1,0:T(8,128)(2,1)} %refs_0_.9), channel_id=1, source_target_pairs={{0,4},{4,0},{8,12},{12,8},{1,5},{5,1},{9,13},{13,9},{2,6},{6,2},{1... | collective-permute-start | bytes 1572872 | tf_op jit(solution)/shard_map/ppermute | solution.py:314
  3.7 0.7 %collective-permute-start.4 = (bf16[4,8,32,256]{3,2,1,0:T(8,128)(2,1)}, bf16[4,8,32,256]{3,2,1,0:T(8,128)(2,1)S(1)}, u32[]{:S(2)}, u32[]{:S(2)}) collective-permute-start(bf16[4,8,32,256]{3,2,1,0:T(8,128)(2,1)} %refs_0_.9), channel_id=1, source_target_pairs={{4,8},{8,4},{5,9},{9,5},{6,10},{10,6},{7,11},{11,7},{20,24},{24,20... | collective-permute-start | bytes 1572872 | tf_op jit(solution)/shard_map/ppermute | solution.py:314
  4.5 1.1 %constant_dynamic-slice_fusion.12 = (bf16[4,2,32,256]{3,2,1,0:T(8,128)(2,1)S(1)}, bf16[4,2,32,256]{3,2,1,0:T(8,128)(2,1)S(1)}, bf16[4,2,32,256]{3,2,1,0:T(8,128)(2,1)S(1)}, bf16[4,2,32,256]{3,2,1,0:T(8,128)(2,1)S(1)}) fusion(bf16[4,8,32,256]{3,2,1,0:T(8,128)(2,1)} %refs_0_.9, s32[]{:T(128)S(6)} %select_n.69, s32[]{:T(128)S(6)} %select_n.67, ...), kind=kLoop, calls=%fused_computation.14 | loop fusion | bytes 1048592 | tf_op jit(solution)/shard_map/dynamic_slice | solution.py:320
  5.7 0.7 %collective-permute-start.2 = (bf16[4,2,32,256]{3,2,1,0:T(8,128)(2,1)S(1)}, bf16[4,2,32,256]{3,2,1,0:T(8,128)(2,1)S(1)}, u32[]{:S(2)}, u32[]{:S(2)}) collective-permute-start(bf16[4,2,32,256]{3,2,1,0:T(8,128)(2,1)S(1)} %get-tuple-element.32), channel_id=1, source_target_pairs={{0,3},{1,2},{2,1},{3,0},{4,7},{5,6},{6,5},{7,4},{8,11},{9,10},{10,... | collective-permute-start | bytes 393224 | tf_op jit(solution)/shard_map/ppermute | solution.py:322
  6.4 0.9 %collective-permute-start.1 = (bf16[4,2,32,256]{3,2,1,0:T(8,128)(2,1)S(1)}, bf16[4,2,32,256]{3,2,1,0:T(8,128)(2,1)S(1)}, u32[]{:S(2)}, u32[]{:S(2)}) collective-permute-start(bf16[4,2,32,256]{3,2,1,0:T(8,128)(2,1)S(1)} %get-tuple-element.33), channel_id=1, source_target_pairs={{0,2},{1,3},{2,0},{3,1},{4,6},{5,7},{6,4},{7,5},{8,10},{9,11},{10,... | collective-permute-start | bytes 393224 | tf_op jit(solution)/shard_map/ppermute | solution.py:322
  7.3 0.3 collective-permute-start
  7.6 3.9 %collective-permute-done.2.refs_4_ = bf16[4,2,32,256]{3,2,1,0:T(8,128)(2,1)S(1)} collective-permute-done((bf16[4,2,32,256]{3,2,1,0:T(8,128)(2,1)S(1)}, bf16[4,2,32,256]{3,2,1,0:T(8,128)(2,1)S(1)}, u32[]{:S(2)}, u32[]{:S(2)}) %collective-permute-start.2) | collective-permute-done | bytes 131104 | tf_op jit(solution)/shard_map/ppermute | solution.py:322
  11.5 2.9 %collective-permute-done.1.refs_3_ = bf16[4,2,32,256]{3,2,1,0:T(8,128)(2,1)S(1)} collective-permute-done((bf16[4,2,32,256]{3,2,1,0:T(8,128)(2,1)S(1)}, bf16[4,2,32,256]{3,2,1,0:T(8,128)(2,1)S(1)}, u32[]{:S(2)}, u32[]{:S(2)}) %collective-permute-start.1) | collective-permute-done | bytes 131104 | tf_op jit(solution)/shard_map/ppermute | solution.py:322
  14.4 1.5 %collective-permute-done.3.refs_1_ = bf16[4,8,32,256]{3,2,1,0:T(8,128)(2,1)S(1)} collective-permute-done((bf16[4,8,32,256]{3,2,1,0:T(8,128)(2,1)}, bf16[4,8,32,256]{3,2,1,0:T(8,128)(2,1)S(1)}, u32[]{:S(2)}, u32[]{:S(2)}) %collective-permute-start.3) | collective-permute-done | bytes 524320 | tf_op jit(solution)/shard_map/ppermute | solution.py:314
  15.9 0.7 %collective-permute-start.9 = (bf16[4,8,32,256]{3,2,1,0:T(8,128)(2,1)S(1)}, bf16[4,8,32,256]{3,2,1,0:T(8,128)(2,1)S(1)}, u32[]{:S(2)}, u32[]{:S(2)}) collective-permute-start(bf16[4,8,32,256]{3,2,1,0:T(8,128)(2,1)S(1)} %collective-permute-done.3.refs_1_), channel_id=1, source_target_pairs={{4,8},{8,4},{5,9},{9,5},{6,10},{10,6},{7,11},{11,7},{20,24},{24,20... | collective-permute-start | bytes 1572872 | tf_op jit(solution)/shard_map/ppermute | solution.py:314
  16.6 1.3 %collective-permute-start.8 = (bf16[4,8,32,256]{3,2,1,0:T(8,128)(2,1)S(1)}, bf16[4,8,32,256]{3,2,1,0:T(8,128)(2,1)S(1)}, u32[]{:S(2)}, u32[]{:S(2)}) collective-permute-start(bf16[4,8,32,256]{3,2,1,0:T(8,128)(2,1)S(1)} %collective-permute-done.4.refs_2_), channel_id=1, source_target_pairs={{4,0},{8,12},{5,1},{9,13},{6,2},{10,14},{7,3},{11,15},{20,16},{24,... | collective-permute-start | bytes 1572872 | tf_op jit(solution)/shard_map/ppermute | solution.py:314
  18.2 1.5 %collective-permute-start.6 = (bf16[4,2,32,256]{3,2,1,0:T(8,128)(2,1)S(1)}, bf16[4,2,32,256]{3,2,1,0:T(8,128)(2,1)S(1)}, u32[]{:S(2)}, u32[]{:S(2)}) collective-permute-start(bf16[4,2,32,256]{3,2,1,0:T(8,128)(2,1)S(1)} %get-tuple-element.29), channel_id=1, source_target_pairs={{0,2},{1,3},{2,0},{3,1},{4,6},{5,7},{6,4},{7,5},{8,10},{9,11},{10,... | collective-permute-start | bytes 393224 | tf_op jit(solution)/shard_map/ppermute | solution.py:322
  19.9 1.6 %copy-done.4 = bf16[4,128,2048]{2,1,0:T(8,128)(2,1)S(1)} copy-done((bf16[4,128,2048]{2,1,0:T(8,128)(2,1)S(1)}, bf16[4,128,2048]{2,1,0:T(8,128)(2,1)}, u32[]{:S(2)}) %copy-start.4) | copy-done | bytes 2097176
  21.5 5.2 %shard_map.77 = (bf16[4,128,2048]{2,1,0:T(8,128)(2,1)S(1)}, f32[4,128,128]{2,1,0:T(8,128)S(1)}) custom-call(s32[4]{0:T(128)S(1)} %copy-done.2, s32[4]{0:T(128)S(1)} %copy-done.5, s32[16]{0:T(128)S(1)} %copy-done.3, bf16[4,128,2048]{2,1,0:T(8,128)(2,1)S(1)} %copy-done.4, bf16[4,2,32,256]{3,2,1,0:T(8,128)(2,1)S(1)} %get-tuple-element.35.refs_1_, ...), custom_call_target="tpu_custom_call" | custom-call | flops 2147483648 | bytes 8388608 | tf_op jit(solution)/shard_map/pallas_call | solution.py:414
  26.7 1.5 %collective-permute-start.13 = (bf16[4,8,32,256]{3,2,1,0:T(8,128)(2,1)S(1)}, bf16[4,8,32,256]{3,2,1,0:T(8,128)(2,1)S(1)}, u32[]{:S(2)}, u32[]{:S(2)}) collective-permute-start(bf16[4,8,32,256]{3,2,1,0:T(8,128)(2,1)S(1)} %collective-permute-done.9.refs_8_.refs_3_), channel_id=1, source_target_pairs={{4,0},{8,12},{5,1},{9,13},{6,2},{10,14},{7,3},{11,15},{20,16},{24,... | collective-permute-start | bytes 1572872 | tf_op jit(solution)/shard_map/ppermute | solution.py:314
  28.1 7.9 %collective-permute-done.8.refs_4_ = bf16[4,8,32,256]{3,2,1,0:T(8,128)(2,1)S(1)} collective-permute-done((bf16[4,8,32,256]{3,2,1,0:T(8,128)(2,1)S(1)}, bf16[4,8,32,256]{3,2,1,0:T(8,128)(2,1)S(1)}, u32[]{:S(2)}, u32[]{:S(2)}) %collective-permute-start.8) | collective-permute-done | bytes 524320 | tf_op jit(solution)/shard_map/ppermute | solution.py:314
  36.2 1.6 %collective-permute-start.11 = (bf16[4,2,32,256]{3,2,1,0:T(8,128)(2,1)S(1)}, bf16[4,2,32,256]{3,2,1,0:T(8,128)(2,1)S(1)}, u32[]{:S(2)}, u32[]{:S(2)}) collective-permute-start(bf16[4,2,32,256]{3,2,1,0:T(8,128)(2,1)S(1)} %get-tuple-element.25), channel_id=1, source_target_pairs={{0,2},{1,3},{2,0},{3,1},{4,6},{5,7},{6,4},{7,5},{8,10},{9,11},{10,... | collective-permute-start | bytes 393224 | tf_op jit(solution)/shard_map/ppermute | solution.py:322
  38.1 5.4 %shard_map.78 = (bf16[4,128,2048]{2,1,0:T(8,128)(2,1)S(1)}, f32[4,128,128]{2,1,0:T(8,128)S(1)}) custom-call(s32[4]{0:T(128)S(1)} %copy-done.2, s32[4]{0:T(128)S(1)} %copy-done.5, s32[16]{0:T(128)S(1)} %copy-done.3, bf16[4,128,2048]{2,1,0:T(8,128)(2,1)S(1)} %copy-done.4, bf16[4,128,2048]{2,1,0:T(8,128)(2,1)S(1)} %get-tuple-element.12.refs_1_, ...), custom_call_target="tpu_custom_call" | custom-call | flops 2147483648 | bytes 8388608 | tf_op jit(solution)/shard_map/pallas_call | solution.py:414
  43.5 4.2 %collective-permute-done.13.refs_5_ = bf16[4,8,32,256]{3,2,1,0:T(8,128)(2,1)S(1)} collective-permute-done((bf16[4,8,32,256]{3,2,1,0:T(8,128)(2,1)S(1)}, bf16[4,8,32,256]{3,2,1,0:T(8,128)(2,1)S(1)}, u32[]{:S(2)}, u32[]{:S(2)}) %collective-permute-start.13) | collective-permute-done | bytes 524320 | tf_op jit(solution)/shard_map/ppermute | solution.py:314
  48.0 1.4 %collective-permute-start.15 = (bf16[4,2,32,256]{3,2,1,0:T(8,128)(2,1)S(1)}, bf16[4,2,32,256]{3,2,1,0:T(8,128)(2,1)S(1)}, u32[]{:S(2)}, u32[]{:S(2)}) collective-permute-start(bf16[4,2,32,256]{3,2,1,0:T(8,128)(2,1)S(1)} %get-tuple-element.21), channel_id=1, source_target_pairs={{0,2},{1,3},{2,0},{3,1},{4,6},{5,7},{6,4},{7,5},{8,10},{9,11},{10,... | collective-permute-start | bytes 393224 | tf_op jit(solution)/shard_map/ppermute | solution.py:322
  49.3 0.5 collective-permute-start.14
  49.8 4.7 %shard_map.79 = (bf16[4,128,2048]{2,1,0:T(8,128)(2,1)S(1)}, f32[4,128,128]{2,1,0:T(8,128)S(1)}) custom-call(s32[4]{0:T(128)S(1)} %copy-done.2, s32[4]{0:T(128)S(1)} %copy-done.5, s32[16]{0:T(128)S(1)} %copy-done.3, bf16[4,128,2048]{2,1,0:T(8,128)(2,1)S(1)} %copy-done.4, bf16[4,128,2048]{2,1,0:T(8,128)(2,1)S(1)} %get-tuple-element.15.refs_1_, ...), custom_call_target="tpu_custom_call" | custom-call | flops 2147483648 | bytes 8388608 | tf_op jit(solution)/shard_map/pallas_call | solution.py:414
  54.5 3.0 %shard_map.81 = bf16[8,8,32,256]{3,2,1,0:T(8,128)(2,1)} custom-call(s32[4]{0:T(128)S(1)} %copy-done.2, s32[4]{0:T(128)S(1)} %copy-done.1, s32[16]{0:T(128)S(1)} %copy-done.3, bf16[4,8,32,256]{3,2,1,0:T(8,128)(2,1)S(1)} %copy-done, bf16[4,8,32,256]{3,2,1,0:T(8,128)(2,1)S(1)} %collective-permute-done.3.refs_1_, ...), custom_call_target="tpu_custom_call" | custom-call | bytes 8388608 | tf_op jit(solution)/shard_map/pallas_call | solution.py:436
  57.6 5.8 %shard_map.80 = bf16[4,128,2048]{2,1,0:T(8,128)(2,1)} custom-call(s32[4]{0:T(128)S(1)} %copy-done.2, s32[4]{0:T(128)S(1)} %copy-done.5, s32[16]{0:T(128)S(1)} %copy-done.3, bf16[4,128,2048]{2,1,0:T(8,128)(2,1)S(1)} %copy-done.4, bf16[4,128,2048]{2,1,0:T(8,128)(2,1)S(1)} %get-tuple-element.17.refs_1_, f32[4,128,128]{2,1,0:T(8,128)S(1)} %get-tuple-element.18.refs_2_, ...), custom_call_target="tpu_custom_call" | custom-call | flops 2147483648 | bytes 8388608 | tf_op jit(solution)/shard_map/pallas_call | solution.py:414
  (33 shorter events, 1.2 us)
Async XLA Ops:
  0.6 19.3 %copy-start.3 = (s32[16]{0:T(128)S(1)}, s32[16]{0:T(128)}, u32[]{:S(2)}) copy-start(s32[16]{0:T(128)} %plan_ref.9) | copy-start | bytes 196
  0.6 19.3 %copy-start.2 = (s32[4]{0:T(128)S(1)}, s32[4]{0:T(128)}, u32[]{:S(2)}) copy-start(s32[4]{0:T(128)} %spans_ref.9) | copy-start | bytes 52
  0.7 19.2 %copy-start.5 = (s32[4]{0:T(128)S(1)}, s32[4]{0:T(128)}, u32[]{:S(2)}) copy-start(s32[4]{0:T(128)} %tail_ref.7) | copy-start | bytes 52
  0.7 15.2 %collective-permute-start.3 = (bf16[4,8,32,256]{3,2,1,0:T(8,128)(2,1)}, bf16[4,8,32,256]{3,2,1,0:T(8,128)(2,1)S(1)}, u32[]{:S(2)}, u32[]{:S(2)}) collective-permute-start(bf16[4,8,32,256]{3,2,1,0:T(8,128)(2,1)} %refs_0_.9), channel_id=1, source_target_pairs={{0,4},{4,0},{8,12},{12,8},{1,5},{5,1},{9,13},{13,9},{2,6},{6,2},{1... | collective-permute-start | bytes 1572872 | tf_op jit(solution)/shard_map/ppermute | solution.py:314
  3.7 12.1 %collective-permute-start.4 = (bf16[4,8,32,256]{3,2,1,0:T(8,128)(2,1)}, bf16[4,8,32,256]{3,2,1,0:T(8,128)(2,1)S(1)}, u32[]{:S(2)}, u32[]{:S(2)}) collective-permute-start(bf16[4,8,32,256]{3,2,1,0:T(8,128)(2,1)} %refs_0_.9), channel_id=1, source_target_pairs={{4,8},{8,4},{5,9},{9,5},{6,10},{10,6},{7,11},{11,7},{20,24},{24,20... | collective-permute-start | bytes 1572872 | tf_op jit(solution)/shard_map/ppermute | solution.py:314
  5.7 5.8 %collective-permute-start.2 = (bf16[4,2,32,256]{3,2,1,0:T(8,128)(2,1)S(1)}, bf16[4,2,32,256]{3,2,1,0:T(8,128)(2,1)S(1)}, u32[]{:S(2)}, u32[]{:S(2)}) collective-permute-start(bf16[4,2,32,256]{3,2,1,0:T(8,128)(2,1)S(1)} %get-tuple-element.32), channel_id=1, source_target_pairs={{0,3},{1,2},{2,1},{3,0},{4,7},{5,6},{6,5},{7,4},{8,11},{9,10},{10,... | collective-permute-start | bytes 393224 | tf_op jit(solution)/shard_map/ppermute | solution.py:322
  6.4 8.0 %collective-permute-start.1 = (bf16[4,2,32,256]{3,2,1,0:T(8,128)(2,1)S(1)}, bf16[4,2,32,256]{3,2,1,0:T(8,128)(2,1)S(1)}, u32[]{:S(2)}, u32[]{:S(2)}) collective-permute-start(bf16[4,2,32,256]{3,2,1,0:T(8,128)(2,1)S(1)} %get-tuple-element.33), channel_id=1, source_target_pairs={{0,2},{1,3},{2,0},{3,1},{4,6},{5,7},{6,4},{7,5},{8,10},{9,11},{10,... | collective-permute-start | bytes 393224 | tf_op jit(solution)/shard_map/ppermute | solution.py:322
  7.3 7.0 %collective-permute-start = (bf16[4,2,32,256]{3,2,1,0:T(8,128)(2,1)S(1)}, bf16[4,2,32,256]{3,2,1,0:T(8,128)(2,1)S(1)}, u32[]{:S(2)}, u32[]{:S(2)}) collective-permute-start(bf16[4,2,32,256]{3,2,1,0:T(8,128)(2,1)S(1)} %get-tuple-element.34), channel_id=1, source_target_pairs={{0,1},{1,0},{2,3},{3,2},{4,5},{5,4},{6,7},{7,6},{8,9},{9,8},{10,11... | collective-permute-start | bytes 393224 | tf_op jit(solution)/shard_map/ppermute | solution.py:322
  15.9 10.8 %collective-permute-start.9 = (bf16[4,8,32,256]{3,2,1,0:T(8,128)(2,1)S(1)}, bf16[4,8,32,256]{3,2,1,0:T(8,128)(2,1)S(1)}, u32[]{:S(2)}, u32[]{:S(2)}) collective-permute-start(bf16[4,8,32,256]{3,2,1,0:T(8,128)(2,1)S(1)} %collective-permute-done.3.refs_1_), channel_id=1, source_target_pairs={{4,8},{8,4},{5,9},{9,5},{6,10},{10,6},{7,11},{11,7},{20,24},{24,20... | collective-permute-start | bytes 1572872 | tf_op jit(solution)/shard_map/ppermute | solution.py:314
  16.6 19.4 %collective-permute-start.8 = (bf16[4,8,32,256]{3,2,1,0:T(8,128)(2,1)S(1)}, bf16[4,8,32,256]{3,2,1,0:T(8,128)(2,1)S(1)}, u32[]{:S(2)}, u32[]{:S(2)}) collective-permute-start(bf16[4,8,32,256]{3,2,1,0:T(8,128)(2,1)S(1)} %collective-permute-done.4.refs_2_), channel_id=1, source_target_pairs={{4,0},{8,12},{5,1},{9,13},{6,2},{10,14},{7,3},{11,15},{20,16},{24,... | collective-permute-start | bytes 1572872 | tf_op jit(solution)/shard_map/ppermute | solution.py:314
  17.9 18.3 %collective-permute-start.7 = (bf16[4,2,32,256]{3,2,1,0:T(8,128)(2,1)S(1)}, bf16[4,2,32,256]{3,2,1,0:T(8,128)(2,1)S(1)}, u32[]{:S(2)}, u32[]{:S(2)}) collective-permute-start(bf16[4,2,32,256]{3,2,1,0:T(8,128)(2,1)S(1)} %get-tuple-element.28), channel_id=1, source_target_pairs={{0,3},{1,2},{2,1},{3,0},{4,7},{5,6},{6,5},{7,4},{8,11},{9,10},{10,... | collective-permute-start | bytes 393224 | tf_op jit(solution)/shard_map/ppermute | solution.py:322
  18.2 19.5 %collective-permute-start.6 = (bf16[4,2,32,256]{3,2,1,0:T(8,128)(2,1)S(1)}, bf16[4,2,32,256]{3,2,1,0:T(8,128)(2,1)S(1)}, u32[]{:S(2)}, u32[]{:S(2)}) collective-permute-start(bf16[4,2,32,256]{3,2,1,0:T(8,128)(2,1)S(1)} %get-tuple-element.29), channel_id=1, source_target_pairs={{0,2},{1,3},{2,0},{3,1},{4,6},{5,7},{6,4},{7,5},{8,10},{9,11},{10,... | collective-permute-start | bytes 393224 | tf_op jit(solution)/shard_map/ppermute | solution.py:322
  19.7 18.3 %collective-permute-start.5 = (bf16[4,2,32,256]{3,2,1,0:T(8,128)(2,1)S(1)}, bf16[4,2,32,256]{3,2,1,0:T(8,128)(2,1)S(1)}, u32[]{:S(2)}, u32[]{:S(2)}) collective-permute-start(bf16[4,2,32,256]{3,2,1,0:T(8,128)(2,1)S(1)} %get-tuple-element.30), channel_id=1, source_target_pairs={{0,1},{1,0},{2,3},{3,2},{4,5},{5,4},{6,7},{7,6},{8,9},{9,8},{10,11... | collective-permute-start | bytes 393224 | tf_op jit(solution)/shard_map/ppermute | solution.py:322
  19.9 1.6 %copy-start.4 = (bf16[4,128,2048]{2,1,0:T(8,128)(2,1)S(1)}, bf16[4,128,2048]{2,1,0:T(8,128)(2,1)}, u32[]{:S(2)}) copy-start(bf16[4,128,2048]{2,1,0:T(8,128)(2,1)} %refs_0_.8) | copy-start | bytes 6291460
  26.7 21.1 %collective-permute-start.13 = (bf16[4,8,32,256]{3,2,1,0:T(8,128)(2,1)S(1)}, bf16[4,8,32,256]{3,2,1,0:T(8,128)(2,1)S(1)}, u32[]{:S(2)}, u32[]{:S(2)}) collective-permute-start(bf16[4,8,32,256]{3,2,1,0:T(8,128)(2,1)S(1)} %collective-permute-done.9.refs_8_.refs_3_), channel_id=1, source_target_pairs={{4,0},{8,12},{5,1},{9,13},{6,2},{10,14},{7,3},{11,15},{20,16},{24,... | collective-permute-start | bytes 1572872 | tf_op jit(solution)/shard_map/ppermute | solution.py:314
  36.1 11.7 %collective-permute-start.12 = (bf16[4,2,32,256]{3,2,1,0:T(8,128)(2,1)S(1)}, bf16[4,2,32,256]{3,2,1,0:T(8,128)(2,1)S(1)}, u32[]{:S(2)}, u32[]{:S(2)}) collective-permute-start(bf16[4,2,32,256]{3,2,1,0:T(8,128)(2,1)S(1)} %get-tuple-element.24), channel_id=1, source_target_pairs={{0,3},{1,2},{2,1},{3,0},{4,7},{5,6},{6,5},{7,4},{8,11},{9,10},{10,... | collective-permute-start | bytes 393224 | tf_op jit(solution)/shard_map/ppermute | solution.py:322
  36.2 11.6 %collective-permute-start.11 = (bf16[4,2,32,256]{3,2,1,0:T(8,128)(2,1)S(1)}, bf16[4,2,32,256]{3,2,1,0:T(8,128)(2,1)S(1)}, u32[]{:S(2)}, u32[]{:S(2)}) collective-permute-start(bf16[4,2,32,256]{3,2,1,0:T(8,128)(2,1)S(1)} %get-tuple-element.25), channel_id=1, source_target_pairs={{0,2},{1,3},{2,0},{3,1},{4,6},{5,7},{6,4},{7,5},{8,10},{9,11},{10,... | collective-permute-start | bytes 393224 | tf_op jit(solution)/shard_map/ppermute | solution.py:322
  37.8 10.1 %collective-permute-start.10 = (bf16[4,2,32,256]{3,2,1,0:T(8,128)(2,1)S(1)}, bf16[4,2,32,256]{3,2,1,0:T(8,128)(2,1)S(1)}, u32[]{:S(2)}, u32[]{:S(2)}) collective-permute-start(bf16[4,2,32,256]{3,2,1,0:T(8,128)(2,1)S(1)} %get-tuple-element.26), channel_id=1, source_target_pairs={{0,1},{1,0},{2,3},{3,2},{4,5},{5,4},{6,7},{7,6},{8,9},{9,8},{10,11... | collective-permute-start | bytes 393224 | tf_op jit(solution)/shard_map/ppermute | solution.py:322
  47.9 9.7 %collective-permute-start.16 = (bf16[4,2,32,256]{3,2,1,0:T(8,128)(2,1)S(1)}, bf16[4,2,32,256]{3,2,1,0:T(8,128)(2,1)S(1)}, u32[]{:S(2)}, u32[]{:S(2)}) collective-permute-start(bf16[4,2,32,256]{3,2,1,0:T(8,128)(2,1)S(1)} %get-tuple-element.20), channel_id=1, source_target_pairs={{0,3},{1,2},{2,1},{3,0},{4,7},{5,6},{6,5},{7,4},{8,11},{9,10},{10,... | collective-permute-start | bytes 393224 | tf_op jit(solution)/shard_map/ppermute | solution.py:322
  48.0 9.6 %collective-permute-start.15 = (bf16[4,2,32,256]{3,2,1,0:T(8,128)(2,1)S(1)}, bf16[4,2,32,256]{3,2,1,0:T(8,128)(2,1)S(1)}, u32[]{:S(2)}, u32[]{:S(2)}) collective-permute-start(bf16[4,2,32,256]{3,2,1,0:T(8,128)(2,1)S(1)} %get-tuple-element.21), channel_id=1, source_target_pairs={{0,2},{1,3},{2,0},{3,1},{4,6},{5,7},{6,4},{7,5},{8,10},{9,11},{10,... | collective-permute-start | bytes 393224 | tf_op jit(solution)/shard_map/ppermute | solution.py:322
  49.3 8.3 %collective-permute-start.14 = (bf16[4,2,32,256]{3,2,1,0:T(8,128)(2,1)S(1)}, bf16[4,2,32,256]{3,2,1,0:T(8,128)(2,1)S(1)}, u32[]{:S(2)}, u32[]{:S(2)}) collective-permute-start(bf16[4,2,32,256]{3,2,1,0:T(8,128)(2,1)S(1)} %get-tuple-element.22), channel_id=1, source_target_pairs={{0,1},{1,0},{2,3},{3,2},{4,5},{5,4},{6,7},{7,6},{8,9},{9,8},{10,11... | collective-permute-start | bytes 393224 | tf_op jit(solution)/shard_map/ppermute | solution.py:322
  49.8 4.7 %copy-start = (bf16[4,8,32,256]{3,2,1,0:T(8,128)(2,1)S(1)}, bf16[4,8,32,256]{3,2,1,0:T(8,128)(2,1)}, u32[]{:S(2)}) copy-start(bf16[4,8,32,256]{3,2,1,0:T(8,128)(2,1)} %refs_0_.9) | copy-start | bytes 1572868
  49.8 4.7 %copy-start.1 = (s32[4]{0:T(128)S(1)}, s32[4]{0:T(128)}, u32[]{:S(2)}) copy-start(s32[4]{0:T(128)} %owner_ref.1) | copy-start | bytes 52
